TPU v7x, 32 devices: a whole 2x2x4 slice. The times are simulated.
32 devices in a mesh: ctx: 8 (over z, y), exp: 4 (over x, core), dp: 1.
Axes of the slice: x: 2, y: 2, z: 4, core: 2. Of those that a mesh axis runs over, the one named last changes fastest.
Arguments:
- residual: bfloat16 [512, 4096], P(('dp', 'ctx', 'exp')), may hold values from -0.59765625 to 0.59765625
- encoded_query_rows: bfloat16 [512, 4096], P(('dp', 'ctx'), 'exp'), may hold values from -256 to 256
- quantized_key_rows: bfloat16 [512, 512], P(('dp', 'ctx')), may hold values from -8 to 8
- quantized_value_rows: bfloat16 [512, 512], P(('dp', 'ctx')), may hold values from -6 to 6
- key_block_exponent: int32 [8, 4], P(('dp', 'ctx')), may hold values from -2 to 1
- value_block_exponent: int32 [8, 4], P(('dp', 'ctx')), may hold values from -2 to 1
- block_order: int32 [8], replicated, may hold values from 0 to 7, each once
- out_weight: bfloat16 [4096, 4096], P('exp', 'ctx'), may hold values from -0.09375 to 0.09375
- norm_gain: float32 [4096], replicated, may hold values from 0.1 to 1.9
- expert_ids: int32 [512, 8], P(('dp', 'ctx', 'exp')), may hold values from 0 to 15, all different within a row; in each aligned block of 16 rows (0 to 15, 16 to 31, ...) at most 12 rows name the same one
- route_weight: float32 [512, 8], P(('dp', 'ctx', 'exp')), may hold values from 0.05 to 0.25
- gate_weight: bfloat16 [32, 4096, 384], P(('ctx', 'exp')), may hold values from -0.09375 to 0.09375
- gate_scale: int32 [32, 32, 3], P(('ctx', 'exp')), may hold values from -1 to 1
- up_weight: bfloat16 [32, 4096, 384], P(('ctx', 'exp')), may hold values from -0.09375 to 0.09375
- up_scale: int32 [32, 32, 3], P(('ctx', 'exp')), may hold values from -1 to 1
- down_weight: bfloat16 [32, 384, 4096], P(('ctx', 'exp')), may hold values from -0.21875 to 0.21875
- down_scale: int32 [32, 3, 32], P(('ctx', 'exp')), may hold values from -1 to 1
Outputs:
- layer_out: bfloat16 [512, 4096], P(('dp', 'ctx', 'exp'))
Inputs may be any that keep to these rules, and one draw needn't show every extreme that they name: `expert_ids`: each row names 8 different experts. Among the rows of one device (16 aligned rows), no expert is named by more than 12 rows, a bound that some block reaches. `block_order`: A permutation of the ctx indices.
All inputs are finite; a program needn't handle non-finite values.
Results may differ from a plain program's by a relative error of at most 0.03.
Values may be sent and summed in bfloat16 or wider, within the bound.
No kernel may reach another device: no remote copies, remote signals or barrier semaphores. Data moves between devices by JAX's collectives and lax.ppermute only.
A program may use at most 128 MiB of HBM per device.

v0:
```python
import math

import jax
import jax.numpy as jnp
from jax import lax
from jax.sharding import PartitionSpec as P

QUERY_HEADS = 32
KEY_VALUE_HEADS = 4
HEAD_SIZE = 128
TOP = 8
SCALE_POSITIONS = 64


def from_partner(array, axis, bit):
    return lax.ppermute(array, axis, [(i, i ^ 1 << bit) for i in range(lax.axis_size(axis))])


def pow_two(exponent, lowest, highest):
    result_sum = jnp.zeros(exponent.shape, jnp.float32)
    for power_of in range(lowest, highest + 1):
        result_sum = result_sum + jnp.where(exponent == power_of, 2.0**power_of, 0.0)
    return result_sum


def dequant(values, exponents, lowest, highest):
    row_blocks = exponents.shape[-2]
    col_blocks = exponents.shape[-1]
    row_rep = values.shape[-2] // row_blocks
    col_rep = values.shape[-1] // col_blocks
    factor = pow_two(exponents, lowest, highest).astype(jnp.bfloat16)
    shaped = values.reshape(values.shape[:-2] + (row_blocks, row_rep, col_blocks, col_rep))
    return (shaped * factor[..., :, None, :, None]).reshape(values.shape)


def shards(
    residual,
    encoded_query_rows,
    quantized_key_rows,
    quantized_value_rows,
    key_block_exponent,
    value_block_exponent,
    block_order,
    out_weight,
    norm_gain,
    expert_ids,
    route_weight,
    gate_weight,
    gate_scale,
    up_weight,
    up_scale,
    down_weight,
    down_scale,
):
    span_rows = encoded_query_rows.shape[0]
    head_count = encoded_query_rows.shape[1] // HEAD_SIZE
    query_group_width = QUERY_HEADS // KEY_VALUE_HEADS
    ctx_count = lax.axis_size("ctx")
    exp_count = lax.axis_size("exp")
    experts = ctx_count * exp_count // 2
    tok_count = residual.shape[0]
    model_width = residual.shape[1]
    half_width = model_width // 2
    capacity = min(tok_count, max(2, 3 * tok_count * TOP // (2 * experts)))
    my_ctx = lax.axis_index("ctx")
    my_exp = lax.axis_index("exp")
    half_bit = my_exp % 2
    kv_head = my_exp * head_count // query_group_width
    ctx_ids = jnp.arange(ctx_count, dtype=jnp.int32)

    def place_of(block_ids):
        return jnp.sum(
            jnp.where(block_ids[:, None] == ctx_ids[None, :], block_order[None, :], 0), axis=1
        )

    own_place = place_of(jnp.reshape(my_ctx, (1,)))[0]
    query_place = own_place * span_rows + jnp.arange(span_rows, dtype=jnp.int32)

    def head_rows(row_vals, scales):
        picked = lax.dynamic_slice_in_dim(row_vals, kv_head * HEAD_SIZE, HEAD_SIZE, 1)
        factor = lax.dynamic_slice_in_dim(scales, kv_head, 1, 1)
        factor = jnp.repeat(pow_two(factor, -2, 1), SCALE_POSITIONS, axis=0)
        return (picked.astype(jnp.float32) * factor).astype(jnp.bfloat16)

    key_head = head_rows(quantized_key_rows, key_block_exponent)
    value_head = head_rows(quantized_value_rows, value_block_exponent)
    queries = encoded_query_rows.reshape(span_rows, head_count, HEAD_SIZE)
    inv_scale = 1.0 / math.sqrt(HEAD_SIZE)
    initial = (
        jnp.full((head_count, span_rows), -1e30, jnp.float32),
        jnp.zeros((head_count, span_rows), jnp.float32),
        jnp.zeros((span_rows, head_count, HEAD_SIZE), jnp.float32),
    )
    key_piece = lax.all_gather(key_head, "ctx", axis=0, tiled=True)
    value_piece = lax.all_gather(value_head, "ctx", axis=0, tiled=True)
    piece_len = key_piece.shape[0]
    row_ids = jnp.arange(piece_len, dtype=jnp.int32)
    key_place = place_of(row_ids // span_rows) * span_rows + row_ids % span_rows
    seen = jnp.min(key_place) <= jnp.max(query_place)

    def update(state_in):
        run_max, run_sum, run_acc = state_in
        scores = (
            jnp.einsum("qhd,kd->hqk", queries, key_piece, preferred_element_type=jnp.float32)
            * inv_scale
        )
        visible_mask = key_place[None, None, :] <= query_place[None, :, None]
        scores = jnp.where(visible_mask, scores, -1e30)
        new_max = jnp.maximum(run_max, jnp.max(scores, axis=-1))
        weights = jnp.where(visible_mask, jnp.exp(scores - new_max[:, :, None]), 0.0)
        factor = jnp.exp(run_max - new_max)
        run_sum = jnp.sum(weights, axis=-1)
        added = jnp.einsum(
            "hqk,kd->qhd",
            weights.astype(jnp.bfloat16),
            value_piece,
            preferred_element_type=jnp.float32,
        )
        run_acc = added
        return (new_max, run_sum, run_acc)

    def unchanged(state_in):
        return state_in

    run_max, run_sum, run_acc = lax.cond(seen, update, unchanged, initial)
    attended = (
        (run_acc / jnp.transpose(run_sum)[:, :, None])
        .astype(jnp.bfloat16)
        .reshape(span_rows, head_count * HEAD_SIZE)
    )
    partial_rows = jnp.dot(
        attended,
        lax.all_gather(out_weight, "ctx", axis=1, tiled=True),
        preferred_element_type=jnp.float32,
    )
    mixed = lax.psum_scatter(
        partial_rows.astype(jnp.bfloat16), "exp", scatter_dimension=0, tiled=True
    ).astype(jnp.float32)
    state_rows = residual.astype(jnp.float32) + mixed
    mean_sq = jnp.mean(state_rows * state_rows, axis=-1, keepdims=True)
    normed = (state_rows * lax.rsqrt(mean_sq + 1e-06) * norm_gain).astype(jnp.bfloat16)
    flat_ids = expert_ids.reshape(-1)
    onehot = (flat_ids[:, None] == jnp.arange(experts, dtype=jnp.int32)[None, :]).astype(jnp.int32)
    before = jnp.cumsum(onehot, axis=0) - onehot
    slot_ids = jnp.sum(before * onehot, axis=1)
    target = flat_ids * capacity + slot_ids
    owner_token = jnp.arange(flat_ids.shape[0], dtype=jnp.int32) // TOP
    slot_table = jnp.full((experts * capacity,), tok_count, jnp.int32).at[target].set(owner_token)
    padded = jnp.concatenate([normed, jnp.zeros((1, model_width), jnp.bfloat16)], axis=0)
    outgoing = padded[slot_table].reshape(experts, 1, capacity, model_width)
    outgoing = jnp.broadcast_to(outgoing, (experts, 2, capacity, model_width)).reshape(
        2 * experts, capacity, model_width
    )
    gate_deq = dequant(gate_weight[0], gate_scale[0], -1, 1)
    up_deq = dequant(up_weight[0], up_scale[0], -1, 1)
    down_deq = dequant(down_weight[0], down_scale[0], -1, 1)
    arrived = lax.all_to_all(outgoing, ("ctx", "exp"), split_axis=0, concat_axis=0, tiled=True)
    flat_rows = arrived.reshape(-1, model_width)
    gate_act = jnp.dot(flat_rows, gate_deq, preferred_element_type=jnp.float32)
    up_act = jnp.dot(flat_rows, up_deq, preferred_element_type=jnp.float32)
    hidden = (jax.nn.silu(gate_act) * up_act).astype(jnp.bfloat16)
    partial_out = jnp.dot(hidden, down_deq, preferred_element_type=jnp.float32).reshape(
        arrived.shape[0], arrived.shape[1], model_width
    )
    kept_cols = lax.dynamic_slice_in_dim(partial_out, half_bit * half_width, half_width, 2)
    given_cols = lax.dynamic_slice_in_dim(partial_out, (1 - half_bit) * half_width, half_width, 2)
    returned = lax.all_to_all(
        (
            kept_cols
            + from_partner(given_cols.astype(jnp.bfloat16), "exp", 0).astype(given_cols.dtype)
        ).astype(jnp.bfloat16),
        ("ctx", "exp"),
        split_axis=0,
        concat_axis=0,
        tiled=True,
    )
    expert_out = (
        returned.reshape(experts, 2, capacity, half_width)
        .transpose(0, 2, 1, 3)
        .reshape(experts * capacity, model_width)
    )
    picked = expert_out[target].astype(jnp.float32) * route_weight.reshape(-1)[:, None]
    combined = jnp.sum(picked.reshape(tok_count, TOP, model_width), axis=1)
    return (state_rows + combined).astype(jnp.bfloat16)


def solution(mesh):
    return jax.shard_map(
        shards,
        mesh=mesh,
        in_specs=(
            P(("dp", "ctx", "exp"), None),
            P(("dp", "ctx"), "exp"),
            P(("dp", "ctx"), None),
            P(("dp", "ctx"), None),
            P(("dp", "ctx"), None),
            P(("dp", "ctx"), None),
            P(),
            P("exp", "ctx"),
            P(),
            P(("dp", "ctx", "exp"), None),
            P(("dp", "ctx", "exp"), None),
            P(("ctx", "exp"), None, None),
            P(("ctx", "exp"), None, None),
            P(("ctx", "exp"), None, None),
            P(("ctx", "exp"), None, None),
            P(("ctx", "exp"), None, None),
            P(("ctx", "exp"), None, None),
        ),
        out_specs=P(("dp", "ctx", "exp"), None),
        check_vma=False,
    )
```

profile of v0, /device:TPU:0, one launch (start us, length us, event | category | flops | bytes accessed | tf_op | source)
XLA Modules:
  0.0 371.3 jit_solution(848701787820456989)
XLA Ops:
  7.3 1.3 fusion.60
  9.8 1.3 fusion.59
  14.7 1.3 fusion.51
  21.5 33.1 %all_gather.10 = bf16[512,128]{1,0:T(8,128)(2,1)S(1)} all-gather(bf16[64,128]{1,0:T(8,128)(2,1)S(1)} %multiply_convert_fusion.1), channel_id=1, replica_groups=mesh['ctx'=8,'exp'=4,'dp'=1] {'ctx'}, dimensions={0}, use_global_device_ids=true | all-gather | bytes 147456 | tf_op jit(solution)/shard_map/all_gather | solution.py:95
  55.3 31.5 %all_gather.9 = bf16[512,128]{1,0:T(8,128)(2,1)S(1)} all-gather(bf16[64,128]{1,0:T(8,128)(2,1)S(1)} %multiply_convert_fusion.2), channel_id=1, replica_groups=mesh['ctx'=8,'exp'=4,'dp'=1] {'ctx'}, dimensions={0}, use_global_device_ids=true | all-gather | bytes 147456 | tf_op jit(solution)/shard_map/all_gather | solution.py:94
  86.8 2.1 conditional.1
  86.9 1.3 fusion.58
  88.9 52.7 %all-gather.2.cloned.1.call-done = bf16[1024,4096]{1,0:T(8,128)(2,1)} async-done(((bf16[1024,512]{1,0:T(8,128)(2,1)}), bf16[1024,4096]{1,0:T(8,128)(2,1)}) %all-gather.2.cloned.1.call-update) | async-done | bytes 8388624 | tf_op jit(solution)/shard_map/all_gather | solution.py:133
  141.6 5.9 %convolution_convert_fusion = bf16[64,4096]{1,0:T(8,128)(2,1)} fusion(bf16[1024,4096]{1,0:T(8,128)(2,1)} %all-gather.2.cloned.1.call-done, f32[64,8,128]{2,0,1:T(8,128)S(1)} %get-tuple-element.23, f32[64,8]{0,1:T(8,128)S(1)} %bitcast.88), kind=kOutput, calls=%fused_computation.20 | convolution fusion | flops 537264128 | bytes 9177088 | tf_op jit(solution)/shard_map/dot_general | solution.py:131
  149.2 18.3 %reduce-scatter.2.cloned.1.call-done = bf16[16,4096]{1,0:T(8,128)(2,1)} async-done(((bf16[64,4096]{1,0:T(8,128)(2,1)}), bf16[16,4096]{1,0:T(8,128)(2,1)}) %reduce-scatter.2.cloned.1.call-update) | async-done | bytes 131088 | tf_op jit(solution)/shard_map/reduce_scatter | solution.py:136
  169.6 2.7 gather_fusion
  172.3 2.3 broadcast_in_dim.137
  174.6 2.5 broadcast_in_dim.138
  177.1 4.9 %all-to-all-start = ((bf16[32,12,4096]{2,1,0:T(8,128)(2,1)}), bf16[32,12,4096]{2,1,0:T(8,128)(2,1)}, u32[]{:S(2)}, u32[]{:S(2)}) async-start(bf16[32,12,4096]{2,1,0:T(8,128)(2,1)} %bitcast.85), calls=%async_computation.1 | async-start | bytes 8388608 | tf_op jit(solution)/shard_map/all_to_all | solution.py:157
  182.5 3.4 mul.156
  185.9 4.8 %copy.50 = bf16[1,4096,384]{1,2,0:T(8,128)(2,1)} copy(bf16[1,4096,384]{2,1,0:T(8,128)(2,1)} %param.30) | data formatting | bytes 6291456 | tf_op args[11]
  191.2 3.3 mul.161
  194.5 4.8 %copy.51 = bf16[1,4096,384]{1,2,0:T(8,128)(2,1)} copy(bf16[1,4096,384]{2,1,0:T(8,128)(2,1)} %param.32) | data formatting | bytes 6291456 | tf_op args[13]
  199.8 3.4 mul.166
  203.2 72.6 %all-to-all-done = bf16[32,12,4096]{2,1,0:T(8,128)(2,1)} async-done(((bf16[32,12,4096]{2,1,0:T(8,128)(2,1)}), bf16[32,12,4096]{2,1,0:T(8,128)(2,1)}, u32[]{:S(2)}, u32[]{:S(2)}) %all-to-all-start) | async-done | bytes 3145760 | tf_op jit(solution)/shard_map/all_to_all | solution.py:157
  275.8 4.0 %reshape.262 = bf16[384,4096]{1,0:T(8,128)(2,1)S(1)} reshape(bf16[32,12,4096]{2,1,0:T(8,128)(2,1)} %all-to-all-done) | data formatting | bytes 6291456 | tf_op jit(solution)/shard_map/reshape | solution.py:158
  279.8 1.7 copy-done.2
  281.4 4.8 %fusion.17 = f32[384,384]{1,0:T(8,128)S(1)} fusion(bf16[384,4096]{1,0:T(8,128)(2,1)S(1)} %reshape.262, bf16[1,4096,384]{1,2,0:T(8,128)(2,1)} %copy.50, bf16[1,4096,384]{1,2,0:T(8,128)(2,1)} %mul.156), kind=kOutput, calls=%fused_computation.25 | convolution fusion | flops 1209532416 | bytes 10027008 | tf_op jit(solution)/shard_map/dot_general | solution.py:159
  286.3 4.6 %fusion.26 = bf16[384,384]{1,0:T(8,128)(2,1)} fusion(bf16[384,4096]{1,0:T(8,128)(2,1)} %copy-done.2, bf16[1,4096,384]{1,2,0:T(8,128)(2,1)S(1)} %copy-done.4, bf16[1,4096,384]{1,2,0:T(8,128)(2,1)S(1)} %copy-done.3, f32[384,384]{1,0:T(8,128)S(1)} %fusion.17), kind=kOutput, calls=%fused_computation.35 | convolution fusion | flops 1210417152 | bytes 10321920 | tf_op jit(solution)/shard_map/dot_general | solution.py:160
  291.9 3.7 fusion.13
  295.6 2.7 copy-done
  298.6 3.4 collective-permute-done
  301.9 2.4 add_convert_fusion
  304.3 2.2 copy.53
  306.6 4.1 %all-to-all-start.1 = ((bf16[32,12,2048]{2,1,0:T(8,128)(2,1)}), bf16[32,12,2048]{2,1,0:T(8,128)(2,1)S(1)}, u32[]{:S(2)}, u32[]{:S(2)}) async-start(bf16[32,12,2048]{2,1,0:T(8,128)(2,1)} %copy.53), calls=%async_computation.2 | async-start | bytes 4194304 | tf_op jit(solution)/shard_map/all_to_all | solution.py:167
  310.7 48.7 %all-to-all-done.1 = bf16[32,12,2048]{2,1,0:T(8,128)(2,1)S(1)} async-done(((bf16[32,12,2048]{2,1,0:T(8,128)(2,1)}), bf16[32,12,2048]{2,1,0:T(8,128)(2,1)S(1)}, u32[]{:S(2)}, u32[]{:S(2)}) %all-to-all-start.1) | async-done | bytes 1572896 | tf_op jit(solution)/shard_map/all_to_all | solution.py:167
  359.4 1.6 copy.54
  (75 shorter events, 15.8 us)
Async XLA Ops:
  6.5 135.1 %all-gather.2.cloned.1.call-start = ((), (), s32[]{:S(2)}) async-start(), calls=%async_computation.3 | async-start | bytes 9437184 | tf_op jit(solution)/shard_map/all_gather | solution.py:133
  7.3 160.2 %reduce-scatter.2.cloned.1.call-start = ((), (), s32[]{:S(2)}) async-start(), calls=%async_computation.4 | async-start | bytes 655360 | tf_op jit(solution)/shard_map/reduce_scatter | solution.py:136
  141.6 6.2 %copy-start.9 = (s32[16,8]{0,1:T(8,128)S(1)}, s32[16,8]{0,1:T(8,128)}, u32[]{:S(2)}) copy-start(s32[16,8]{0,1:T(8,128)} %param.28) | copy-start | bytes 1540
  141.6 25.9 %copy-start.5 = (bf16[16,4096]{1,0:T(8,128)(2,1)S(1)}, bf16[16,4096]{1,0:T(8,128)(2,1)}, u32[]{:S(2)}) copy-start(bf16[16,4096]{1,0:T(8,128)(2,1)} %param.19) | copy-start | bytes 393220
  141.6 27.0 %copy-start.8 = (f32[4096]{0:T(1024)S(1)}, f32[4096]{0:T(1024)}, u32[]{:S(2)}) copy-start(f32[4096]{0:T(1024)} %param.27) | copy-start | bytes 49156
  177.1 4.9 %copy-start.12 = (s32[1,32,3]{1,0,2:T(1,128)S(1)}, s32[1,32,3]{1,0,2:T(1,128)}, u32[]{:S(2)}) copy-start(s32[1,32,3]{1,0,2:T(1,128)} %param.31) | copy-start | bytes 1156
  177.1 4.9 %copy-start.13 = (s32[1,32,3]{1,0,2:T(1,128)S(1)}, s32[1,32,3]{1,0,2:T(1,128)}, u32[]{:S(2)}) copy-start(s32[1,32,3]{1,0,2:T(1,128)} %param.33) | copy-start | bytes 1156
  177.1 98.7 %all-to-all-start = ((bf16[32,12,4096]{2,1,0:T(8,128)(2,1)}), bf16[32,12,4096]{2,1,0:T(8,128)(2,1)}, u32[]{:S(2)}, u32[]{:S(2)}) async-start(bf16[32,12,4096]{2,1,0:T(8,128)(2,1)} %bitcast.85), calls=%async_computation.1 | async-start | bytes 8388608 | tf_op jit(solution)/shard_map/all_to_all | solution.py:157
  194.5 4.8 %copy-start.11 = (s32[1,3,32]{2,0,1:T(1,128)S(1)}, s32[1,3,32]{2,0,1:T(1,128)}, u32[]{:S(2)}) copy-start(s32[1,3,32]{2,0,1:T(1,128)} %param.35) | copy-start | bytes 1156
  279.8 1.7 copy-start.2
  281.4 4.8 %copy-start.3 = (bf16[1,4096,384]{1,2,0:T(8,128)(2,1)S(1)}, bf16[1,4096,384]{1,2,0:T(8,128)(2,1)}, u32[]{:S(2)}) copy-start(bf16[1,4096,384]{1,2,0:T(8,128)(2,1)} %mul.161) | copy-start | bytes 9437188
  281.4 4.8 %copy-start.4 = (bf16[1,4096,384]{1,2,0:T(8,128)(2,1)S(1)}, bf16[1,4096,384]{1,2,0:T(8,128)(2,1)}, u32[]{:S(2)}) copy-start(bf16[1,4096,384]{1,2,0:T(8,128)(2,1)} %copy.51) | copy-start | bytes 9437188
  286.3 5.6 %copy-start.1 = (bf16[1,384,4096]{2,1,0:T(8,128)(2,1)S(1)}, bf16[1,384,4096]{2,1,0:T(8,128)(2,1)}, u32[]{:S(2)}) copy-start(bf16[1,384,4096]{2,1,0:T(8,128)(2,1)} %mul.166) | copy-start | bytes 9437188
  295.6 2.7 copy-start
  298.5 3.5 collective-permute-start
  304.3 6.3 %copy-start.10 = (f32[16,8]{0,1:T(8,128)S(1)}, f32[16,8]{0,1:T(8,128)}, u32[]{:S(2)}) copy-start(f32[16,8]{0,1:T(8,128)} %param.29) | copy-start | bytes 1540
  306.6 52.8 %all-to-all-start.1 = ((bf16[32,12,2048]{2,1,0:T(8,128)(2,1)}), bf16[32,12,2048]{2,1,0:T(8,128)(2,1)S(1)}, u32[]{:S(2)}, u32[]{:S(2)}) async-start(bf16[32,12,2048]{2,1,0:T(8,128)(2,1)} %copy.53), calls=%async_computation.2 | async-start | bytes 4194304 | tf_op jit(solution)/shard_map/all_to_all | solution.py:167
  361.7 2.0 copy-start.6
  361.7 2.0 copy-start.7
Sparse Core Ops, SparseCore 0:
  9.4 132.1 all-gather.1
  147.6 19.8 reduce-scatter.1
where the time goes:
time: 372 us; the launch traced here: 371 us
  waiting for transfers between devices  196 us (53%)
  blocking collectives  64.6 us (17%)
  local copies, waits for them, and re-layouts  45.9 us (12%)
  matrix products  20.6 us (6%)
  between operations  20.6 us (6%)
  other arithmetic  14.1 us (4%)
  starting transfers between devices  9.09 us (2%)
    all_to_all x1, waiting for transfers between devices, shards(): lax.all_to_all(outgoing, ('ctx', 'exp'), split_axis=0, concat_axis=0, til...  72.6 us
    all_gather x1, waiting for transfers between devices, shards(): lax.all_gather(out_weight, 'ctx', axis=1, tiled=True)  52.7 us
    all_to_all x1, waiting for transfers between devices, shards(): lax.all_to_all((kept_cols + from_partner(given_cols.astype(jnp.bfloat16),...  48.7 us
    all_gather x1, blocking collectives, shards(): value_piece = lax.all_gather(value_head, 'ctx', axis=0, tiled=True)  33.1 us
    all_gather x1, blocking collectives, shards(): key_piece = lax.all_gather(key_head, 'ctx', axis=0, tiled=True)  31.5 us
    reduce_scatter x1, waiting for transfers between devices, shards(): lax.psum_scatter(partial_rows.astype(jnp.bfloat16), 'exp', scatter_dimens...  18.3 us
    unnamed x36, local copies, waits for them, and re-layouts  15.4 us
    mul x6, local copies, waits for them, and re-layouts, dequant(): return (shaped * factor[..., :, None, :, None]).reshape(values.shape)  11.6 us
  transfers between devices with their start and end apart: 5, of which 5 were waited for; matrix products, arithmetic and copies ran while one was open for 9% of the time, Pallas kernels for 0%

commit v1 on v0

v1 whole, which is shorter than its diff:
```python
import functools
import math

import jax
import jax.numpy as jnp
from jax import lax
from jax.experimental import pallas as pl
from jax.experimental.pallas import tpu as pltpu
from jax.sharding import PartitionSpec as P

QUERY_HEADS = 32
KEY_VALUE_HEADS = 4
HEAD_SIZE = 128
TOP = 8
SCALE_POSITIONS = 64
WB = 128
MIB = 1 << 20


def from_partner(array, axis, bit):
    return lax.ppermute(array, axis, [(i, i ^ 1 << bit) for i in range(lax.axis_size(axis))])


def bits_of(count):
    return count.bit_length() - 1


def from_offset(array, offset):
    return lax.ppermute(array, "exp", [(i, i ^ offset) for i in range(lax.axis_size("exp"))])


def from_ctx(array, offset):
    return lax.ppermute(array, "ctx", [(i, i ^ offset) for i in range(lax.axis_size("ctx"))])


def gather_route(ctx_count, x_count, rows_only=False):
    transfers, arrival = [], {(0, 0): 0}

    def go(source, axis, bit, delay=0):
        move = (1 << bit, 0) if axis == "ctx" else (0, 1 << bit - 1)
        target = (source[0] ^ move[0], source[1] ^ move[1])
        arrival[target] = arrival[source] + 1 + delay
        transfers.append((arrival[target], source, target, axis, bit))

    for bit in range(bits_of(ctx_count) - 1, 0, -1):
        for source in list(arrival):
            go(source, "ctx", bit)
    x_steps = [] if rows_only else [("exp", bit + 1) for bit in range(bits_of(x_count))]
    for number, first in enumerate(sorted(arrival)):
        steps = [("ctx", 0)] + x_steps if number % 2 == 0 else x_steps + [("ctx", 0)]
        held = [first]
        for axis, bit in steps:
            before = len(transfers)
            for source in held:
                late = source != first and (ctx_count, x_count) == (8, 2) and number in (0, 2)
                go(source, axis, bit, 1 if late else 0)
            held = held + [transfer[2] for transfer in transfers[before:]]
    return sorted(transfers, key=lambda transfer: transfer[0])


def stages_of(route):
    return [[t for t in route if t[0] == stage] for stage in sorted({t[0] for t in route})]


def together(*values):
    return lax.optimization_barrier(values)


def block_factor(exponent, width):
    factor = jnp.where(exponent < 0, 0.5, jnp.where(exponent > 0, 2.0, 1.0))
    return jnp.full((1, width), factor, jnp.float32).astype(jnp.bfloat16)


def pack_kernel(plan, ctx_ref, exp_ref, key_scale_ref, value_scale_ref, query_ref, key_ref, value_ref,
                ids_ref, route_ref, residual_ref, packed_ref, *piece_refs):
    heads, group, experts = plan
    span, width = query_ref.shape
    my_ctx, my_exp = ctx_ref[0], exp_ref[0]
    kv_head = my_exp * heads // group
    at = pl.ds(pl.multiple_of(kv_head * HEAD_SIZE, HEAD_SIZE), HEAD_SIZE)
    blocks = key_scale_ref.shape[0]
    for place, (ref, scale_ref) in enumerate(((key_ref, key_scale_ref), (value_ref, value_scale_ref))):
        for block in range(blocks):
            exponent = scale_ref[block, kv_head]
            factor = jnp.where(
                exponent < -1,
                0.25,
                jnp.where(exponent < 0, 0.5, jnp.where(exponent < 1, 1.0, 2.0)),
            )
            rows = pl.ds(block * (span // blocks), span // blocks)
            scaled = ref[rows, at].astype(jnp.float32) * factor
            packed_ref[rows, pl.ds(place * HEAD_SIZE, HEAD_SIZE)] = scaled.astype(jnp.bfloat16)
    packed_ref[:, 2 * HEAD_SIZE : 2 * HEAD_SIZE + width] = query_ref[...]
    tok = ids_ref.shape[1]
    number = lax.broadcasted_iota(jnp.int32, (128, tok), 0)
    dense = jnp.zeros((128, tok), jnp.float32)
    for k in range(TOP):
        dense = dense + jnp.where(ids_ref[k : k + 1, :] == number, route_ref[k : k + 1, :], 0.0)
    dense = jnp.concatenate([dense, jnp.zeros((128, 128 - tok), jnp.float32)], axis=1)
    dense = jnp.transpose(dense)[:tok, :]
    high = dense.astype(jnp.bfloat16)
    packed_ref[0:tok, 2 * HEAD_SIZE + width :] = high
    packed_ref[tok : 2 * tok, 2 * HEAD_SIZE + width :] = (dense - high.astype(jnp.float32)).astype(
        jnp.bfloat16
    )
    packed_ref[2 * tok :, 2 * HEAD_SIZE + width :] = jnp.zeros((span - 2 * tok, 128), jnp.bfloat16)
    cols = piece_refs[0].shape[1]
    for offset, ref in enumerate(piece_refs):
        col = pl.multiple_of(lax.bitwise_xor(my_ctx, offset) * cols, cols)
        ref[...] = residual_ref[:, pl.ds(col, cols)]


def deq_in_kernel(exp_ref, gate_scale_ref, up_scale_ref, gate_ref, up_ref, _, own_ref, give_ref):
    step = pl.program_id(0)
    core = lax.bitwise_and(exp_ref[0], 1)
    rows, cols = own_ref.shape[0], gate_ref.shape[2]
    for half, (ref, scale_ref) in enumerate(((gate_ref, gate_scale_ref), (up_ref, up_scale_ref))):
        for out_ref, side in ((give_ref, 1 - core), (own_ref, core)):
            first = (2 * step + side) * (rows // WB)
            for i in range(rows // WB):
                row = pl.multiple_of(side * rows + i * WB, WB)
                for j in range(cols // WB):
                    factor = block_factor(scale_ref[j, 0, first + i], WB)
                    out_ref[pl.ds(i * WB, WB), pl.ds(half * cols + j * WB, WB)] = (
                        ref[0, pl.ds(row, WB), pl.ds(j * WB, WB)] * factor
                    )


def deq_in(my_exp, gate_weight, gate_scale, up_weight, up_scale, ctx_count, after):
    width, hidden = gate_weight.shape[1:]
    rows = width // (2 * ctx_count)
    spec = pl.BlockSpec((1, 2 * rows, hidden), lambda i, e, gs, us: (0, i, 0))
    out_spec = pl.BlockSpec((rows, 2 * hidden), lambda i, e, gs, us: (i, 0))
    shape = jax.ShapeDtypeStruct((width // 2, 2 * hidden), jnp.bfloat16)
    return pl.pallas_call(
        deq_in_kernel,
        grid_spec=pltpu.PrefetchScalarGridSpec(
            num_scalar_prefetch=3,
            grid=(ctx_count,),
            in_specs=[spec, spec, pl.BlockSpec(memory_space=pl.ANY)],
            out_specs=[out_spec, out_spec],
        ),
        out_shape=[shape, shape],
        compiler_params=pltpu.CompilerParams(vmem_limit_bytes=16 * MIB),
        cost_estimate=pl.CostEstimate(
            flops=2 * width * hidden, bytes_accessed=8 * width * hidden, transcendentals=0
        ),
        name="dequant_in",
    )(
        my_exp,
        jnp.transpose(gate_scale, (2, 0, 1)),
        jnp.transpose(up_scale, (2, 0, 1)),
        gate_weight,
        up_weight,
        after,
    )


def deq_down_kernel(exp_ref, scale_ref, down_ref, _, own_ref, give_ref):
    step = pl.program_id(0)
    core = lax.bitwise_and(exp_ref[0], 1)
    rows, cols = own_ref.shape
    for out_ref, side in ((give_ref, 1 - core), (own_ref, core)):
        first = (2 * step + side) * (cols // WB)
        for j in range(cols // WB):
            col = pl.multiple_of(side * cols + j * WB, WB)
            for i in range(rows // WB):
                factor = block_factor(scale_ref[i, 0, first + j], WB)
                out_ref[pl.ds(i * WB, WB), pl.ds(j * WB, WB)] = (
                    down_ref[0, pl.ds(i * WB, WB), pl.ds(col, WB)] * factor
                )


def deq_down(my_exp, down_weight, down_scale, ctx_count, after):
    hidden, width = down_weight.shape[1:]
    cols = width // (2 * ctx_count)
    out_spec = pl.BlockSpec((hidden, cols), lambda i, e, ds: (0, i))
    shape = jax.ShapeDtypeStruct((hidden, width // 2), jnp.bfloat16)
    return pl.pallas_call(
        deq_down_kernel,
        grid_spec=pltpu.PrefetchScalarGridSpec(
            num_scalar_prefetch=2,
            grid=(ctx_count,),
            in_specs=[
                pl.BlockSpec((1, hidden, 2 * cols), lambda i, e, ds: (0, 0, i)),
                pl.BlockSpec(memory_space=pl.ANY),
            ],
            out_specs=[out_spec, out_spec],
        ),
        out_shape=[shape, shape],
        compiler_params=pltpu.CompilerParams(vmem_limit_bytes=16 * MIB),
        cost_estimate=pl.CostEstimate(
            flops=width * hidden, bytes_accessed=4 * width * hidden, transcendentals=0
        ),
        name="dequant_down",
    )(my_exp, jnp.transpose(down_scale, (1, 0, 2)), down_weight, after)


def attend_kernel(plan, ctx_ref, exp_ref, order_ref, *refs):
    ctx_count, exp_count, tok, heads, x_off = plan
    packed, pieces = refs[:ctx_count], refs[ctx_count : 2 * ctx_count]
    weight_ref, _ = refs[2 * ctx_count : 2 * ctx_count + 2]
    rest = refs[2 * ctx_count + 2 :]
    out_refs, route_refs = rest[0:2], (rest[2:3] if x_off == 0 else rest[0:1]) + rest[1:2]
    key_scr, value_scr, place_scr, att_scr = rest[-4:]
    x_count = exp_count // 2
    span = packed[0].shape[0]
    positions = ctx_count * span
    per_ctx = 2 * tok
    my_ctx, my_exp = ctx_ref[0], exp_ref[0]
    my_x, my_core = lax.shift_right_logical(my_exp, 1), lax.bitwise_and(my_exp, 1)
    start = pl.multiple_of(lax.bitwise_xor(my_x, x_off) * per_ctx, per_ctx)
    lane = lax.broadcasted_iota(jnp.int32, (8, positions), 1)
    places = lane % span
    for offset, ref in enumerate(packed):
        key_scr[pl.ds(offset * span, span), :] = ref[:, 0:HEAD_SIZE]
        value_scr[pl.ds(offset * span, span), :] = ref[:, HEAD_SIZE : 2 * HEAD_SIZE]
        base = order_ref[lax.bitwise_xor(my_ctx, offset)] * span
        places = places + jnp.where(lane // span == offset, base, 0)
    place_scr[...] = places
    scale = 1.0 / math.sqrt(HEAD_SIZE)
    for offset, ref in enumerate(packed):
        source = lax.bitwise_xor(my_ctx, offset)
        queries = jnp.concatenate(
            [
                ref[pl.ds(start, per_ctx), (h + 2) * HEAD_SIZE : (h + 3) * HEAD_SIZE]
                for h in range(heads)
            ],
            axis=0,
        )
        scores = lax.dot_general(
            queries, key_scr[...], (((1,), (1,)), ((), ())), preferred_element_type=jnp.float32
        )
        own_place = (
            order_ref[source] * span + start + lax.broadcasted_iota(jnp.int32, (per_ctx, positions), 0)
        )
        bias = jnp.where(place_scr[0:1, :] <= own_place, 0.0, -1e30)
        scores = scores.reshape(heads, per_ctx, positions) * scale + bias[None]
        largest = jnp.max(scores, axis=-1, keepdims=True)
        exps = jnp.exp(scores - largest)
        total = jnp.sum(exps, axis=-1, keepdims=True)
        mixed = jnp.dot(
            exps.astype(jnp.bfloat16).reshape(heads * per_ctx, positions),
            value_scr[...],
            preferred_element_type=jnp.float32,
        ).reshape(heads, per_ctx, HEAD_SIZE)
        mixed = (mixed / total).astype(jnp.bfloat16)
        at = pl.ds(pl.multiple_of(source * per_ctx, per_ctx), per_ctx)
        for head in range(heads):
            att_scr[at, pl.ds(head * HEAD_SIZE, HEAD_SIZE)] = mixed[head]

    cols = weight_ref.shape[1] // 2
    per_x = ctx_count * per_ctx
    first = (heads + 2) * HEAD_SIZE
    route_lane = lax.broadcasted_iota(jnp.int32, (tok, HEAD_SIZE), 1)
    expert = my_ctx * x_count + lax.bitwise_xor(my_x, x_off)
    sides = [jnp.zeros((tok, HEAD_SIZE), jnp.float32)] * 2
    for offset, ref in enumerate(packed):
        for part_of in range(2):
            block = ref[part_of * tok : (part_of + 1) * tok, first:].astype(jnp.float32)
            column = jnp.sum(jnp.where(route_lane == expert, block, 0.0), axis=1, keepdims=True)
            sides[part_of] = sides[part_of] + jnp.where(
                route_lane == lax.bitwise_xor(my_ctx, offset), column, 0.0
            )
    for which, out_ref in enumerate(out_refs):
        side = lax.bitwise_xor(my_core, which)
        weight = weight_ref[:, pl.ds(pl.multiple_of(side * cols, cols), cols)]
        part = jnp.dot(att_scr[...], weight, preferred_element_type=jnp.float32)
        out_ref[0:per_x, :] = part.astype(out_ref.dtype)
        if x_off == 0:
            for offset, ref in enumerate(pieces):
                row = (lax.bitwise_xor(my_ctx, offset) * 2 + my_core) * tok
                at = pl.ds(pl.multiple_of(row, tok), tok)
                piece = ref[:, pl.ds(pl.multiple_of(side * cols, cols), cols)].astype(jnp.float32)
                out_ref[at, :] = (out_ref[at, :].astype(jnp.float32) + piece).astype(out_ref.dtype)
        route_out = route_refs[which]
        row = route_out.shape[0] - 2 * tok
        for part_of, values in enumerate(sides):
            at = pl.ds(row + part_of * tok, tok)
            route_out[at, 0:HEAD_SIZE] = values.astype(jnp.bfloat16)
            if route_out.shape[1] > HEAD_SIZE:
                rest_shape = (tok, route_out.shape[1] - HEAD_SIZE)
                route_out[at, HEAD_SIZE:] = jnp.zeros(rest_shape, jnp.bfloat16)


def fill_rows(plan, ctx_ref, exp_ref, gain_ref, chunk_refs, offsets, rows_scr, groups):
    ctx_count, x_count = plan
    half = ctx_count // 2
    my_ctx = ctx_ref[0]
    my_core = lax.bitwise_and(exp_ref[0], 1)
    mine = lax.shift_right_logical(my_ctx, bits_of(half))
    rows, cols = chunk_refs[0].shape
    rows = rows // 2
    sums = {}
    for ref, (c_off, x_off) in zip(chunk_refs, offsets):
        source = lax.bitwise_xor(my_ctx, c_off)
        gain_at = pl.multiple_of((source * 2 + my_core) * cols, cols)
        gain = gain_ref[:, pl.ds(gain_at, cols)]
        col = pl.multiple_of(lax.bitwise_and(source, half - 1) * cols, cols)
        for place, group in enumerate(groups):
            side = mine if group == 1 else 1 - mine
            chunk = ref[pl.ds(pl.multiple_of(side * rows, rows), rows), :].astype(jnp.float32)
            row = (place * x_count + x_off) * rows
            rows_scr[pl.ds(row, rows), pl.ds(col, cols)] = (chunk * gain).astype(jnp.bfloat16)
            square = jnp.sum(chunk * chunk, axis=-1, keepdims=True)
            sums[row] = sums[row] + square if row in sums else square
    return sums


def experts_in_first(plan, offsets, ctx_ref, exp_ref, *refs):
    chunk_refs, (gain_ref, own_ref, other_ref, _, act_ref, square_ref, rows_scr) = refs[:-7], refs[-7:]
    half = plan[0] // 2
    sums = fill_rows(plan, ctx_ref, exp_ref, gain_ref, chunk_refs, offsets, rows_scr, (0, 1))
    for row, square in sums.items():
        square_ref[pl.ds(row, square.shape[0]), :] = square
    depth, width = rows_scr.shape[1], own_ref.shape[1]
    start = lax.shift_right_logical(ctx_ref[0], bits_of(half)) * depth
    at = pl.ds(pl.multiple_of(start, depth), depth)
    for place, ref in enumerate((own_ref, other_ref)):
        act_ref[:, place * width : (place + 1) * width] = jnp.dot(
            rows_scr[...], ref[at, :], preferred_element_type=jnp.float32
        )


def experts_in_second(plan, offsets, group, ctx_ref, exp_ref, *refs):
    chunk_refs, rest = refs[:-8], refs[-8:]
    gain_ref, own_ref, other_ref, first_ref, square_ref, _, act_ref, rows_scr = rest
    half = plan[0] // 2
    sums = fill_rows(plan, ctx_ref, exp_ref, gain_ref, chunk_refs, offsets, rows_scr, (group,))
    count, depth = rows_scr.shape
    width = own_ref.shape[1]
    lane = lax.broadcasted_iota(jnp.int32, (1, HEAD_SIZE), 1)
    for row, square in sums.items():
        rows = square.shape[0]
        square = square + square_ref[pl.ds(group * count + row, rows), :]
        high = square.astype(jnp.bfloat16).astype(jnp.float32)
        act_ref[pl.ds(row, rows), 2 * width :] = jnp.where(lane == 0, high, square - high).astype(
            jnp.bfloat16
        )
    start = (1 - lax.shift_right_logical(ctx_ref[0], bits_of(half))) * depth
    at = pl.ds(pl.multiple_of(start, depth), depth)
    for place, ref in enumerate((own_ref, other_ref)):
        cols = slice(place * width, (place + 1) * width)
        act = first_ref[group * count : (group + 1) * count, cols] + jnp.dot(
            rows_scr[...], ref[at, :], preferred_element_type=jnp.float32
        )
        act_ref[:, cols] = act.astype(jnp.bfloat16)


def experts_out_kernel(plan, group, slots, model_width, ctx_ref, exp_ref, act_ref, came_ref, *refs):
    ctx_count, exp_count, tok = plan
    x_count, half = exp_count // 2, ctx_count // 2
    route_refs = refs[:exp_count]
    own_ref, other_ref, _ = refs[exp_count : exp_count + 3]
    rest = refs[exp_count + 3 :]
    state_refs, rest = (rest[:ctx_count], rest[ctx_count:]) if group == 1 else ((), rest)
    out_refs, hidden_scr = rest[:-1], rest[-1]
    my_ctx = ctx_ref[0]
    my_core = lax.bitwise_and(exp_ref[0], 1)
    mine = lax.shift_right_logical(my_ctx, bits_of(half))
    first_ctx = (mine if group == 1 else 1 - mine) * half
    width = (act_ref.shape[1] - HEAD_SIZE) // 2
    hidden = width // 2
    lane = lax.broadcasted_iota(jnp.int32, (tok, HEAD_SIZE), 1)
    blocks = []
    for ref in route_refs:
        row = ref.shape[0] - 2 * tok
        both = ref[row : row + 2 * tok, 0:HEAD_SIZE].astype(jnp.float32)
        blocks.append(both[:tok] + both[tok:])
    columns = []
    for x_off in range(x_count):
        for low in range(half):
            for core in range(2):
                same, swapped = blocks[2 * x_off + core], blocks[2 * x_off + 1 - core]
                block = jnp.where(my_core == 0, same, swapped)
                picked = jnp.where(lane == first_ctx + low, block, 0.0)
                columns.append(jnp.sum(picked, axis=1, keepdims=True))
    route = jnp.concatenate(columns, axis=0)
    squares = act_ref[:, 2 * width :].astype(jnp.float32) + came_ref[:, 2 * width :].astype(jnp.float32)
    norm = lax.rsqrt((squares[:, 0:1] + squares[:, 1:2]) / model_width + 1e-06)
    scaled_route = norm * route
    for side in range(2):
        acts = act_ref[:, side * width : (side + 1) * width].astype(jnp.float32) + came_ref[
            :, (1 - side) * width : (2 - side) * width
        ].astype(jnp.float32)
        gate = acts[:, :hidden] * norm
        value = gate / (1.0 + jnp.exp(-gate)) * (acts[:, hidden:] * scaled_route)
        hidden_scr[:, side * hidden : (side + 1) * hidden] = value.astype(jnp.bfloat16)
    picked = []
    for c_off, x_off in slots:
        low = lax.bitwise_and(lax.bitwise_xor(my_ctx, c_off), half - 1)
        row = pl.multiple_of((x_off * half + low) * (2 * tok), 2 * tok)
        picked.append(hidden_scr[pl.ds(row, 2 * tok), :])
    picked = jnp.concatenate(picked, axis=0)
    out_cols = own_ref.shape[1]
    step = min(512, out_cols)
    for col in range(0, out_cols, step):
        at = pl.ds(col, step)
        out = jnp.dot(picked[:, :hidden], own_ref[:, at], preferred_element_type=jnp.float32)
        out = out + jnp.dot(picked[:, hidden:], other_ref[:, at], preferred_element_type=jnp.float32)
        for place, ref in enumerate(out_refs):
            ref[:, at] = out[place * 2 * tok : (place + 1) * 2 * tok, :].astype(ref.dtype)
    for slot, ref in zip(slots, out_refs):
        if slot == (0, 0):
            for c_off, state_ref in enumerate(state_refs):
                cols = state_ref.shape[1]
                at = pl.ds(pl.multiple_of(lax.bitwise_xor(my_ctx, c_off) * cols, cols), cols)
                own_row = pl.multiple_of(my_ctx * (2 * tok), 2 * tok)
                ref[:, at] = ref[:, at] + state_ref[pl.ds(own_row, 2 * tok), :].astype(jnp.float32)


def shards(
    residual,
    encoded_query_rows,
    quantized_key_rows,
    quantized_value_rows,
    key_block_exponent,
    value_block_exponent,
    block_order,
    out_weight,
    norm_gain,
    expert_ids,
    route_weight,
    gate_weight,
    gate_scale,
    up_weight,
    up_scale,
    down_weight,
    down_scale,
):
    f32, bf16 = jnp.float32, jnp.bfloat16
    vmem = pl.BlockSpec(memory_space=pltpu.VMEM)
    smem = pl.BlockSpec(memory_space=pltpu.SMEM)
    anywhere = pl.BlockSpec(memory_space=pl.ANY)
    span, query_width = encoded_query_rows.shape
    heads = query_width // HEAD_SIZE
    group = QUERY_HEADS // KEY_VALUE_HEADS
    ctx_count = lax.axis_size("ctx")
    exp_count = lax.axis_size("exp")
    x_count = exp_count // 2
    experts = ctx_count * x_count
    tok, model_width = residual.shape
    half_width = model_width // 2
    cols = half_width // ctx_count
    my_ctx = lax.axis_index("ctx").astype(jnp.int32).reshape(1)
    my_exp = lax.axis_index("exp").astype(jnp.int32).reshape(1)
    route = gather_route(ctx_count, x_count)

    packed, *pieces = pl.pallas_call(
        functools.partial(pack_kernel, (heads, group, experts)),
        in_specs=[smem] * 4 + [vmem] * 6,
        out_specs=[vmem] * (1 + ctx_count),
        out_shape=[jax.ShapeDtypeStruct((span, query_width + 3 * HEAD_SIZE), bf16)]
        + [jax.ShapeDtypeStruct((tok, 2 * cols), bf16)] * ctx_count,
        compiler_params=pltpu.CompilerParams(vmem_limit_bytes=8 * MIB),
        name="pack",
    )(
        my_ctx,
        my_exp,
        key_block_exponent,
        value_block_exponent,
        encoded_query_rows,
        quantized_key_rows,
        quantized_value_rows,
        jnp.transpose(expert_ids),
        jnp.transpose(route_weight),
        residual,
    )
    held = {(0, 0): packed}
    stages = stages_of(gather_route(ctx_count, x_count, rows_only=True))
    for number, stage in enumerate(stages):
        came = [from_partner(held[source], axis, bit) for _, source, _, axis, bit in stage]
        if number == 0:
            in_own, in_give = deq_in(
                my_exp, gate_weight, gate_scale, up_weight, up_scale, ctx_count, packed
            )
            *came, in_own, in_give = together(*came, in_own, in_give)
        elif number == 1:
            in_other = from_offset(in_give, 1)
            pieces = [pieces[0]] + [from_ctx(pieces[offset], offset) for offset in range(1, ctx_count)]
            down_own, down_give = deq_down(my_exp, down_weight, down_scale, ctx_count, came_first)
            *came, down_own, down_give = together(*came, down_own, down_give)
        came_first = came[0]
        held.update({target: array for (_, _, target, _, _), array in zip(stage, came)})
    packed = [held[offset, 0] for offset in range(ctx_count)]
    down_other = from_offset(down_give, 1)

    positions = ctx_count * span
    per_x = 2 * ctx_count * tok
    gives, after = {}, out_weight
    for x_off in reversed(range(x_count)):
        give_shape = jax.ShapeDtypeStruct((per_x + 2 * tok, cols), bf16)
        first_shape = jax.ShapeDtypeStruct((per_x, cols), f32) if x_off == 0 else give_shape
        route_shape = [jax.ShapeDtypeStruct((2 * tok, HEAD_SIZE), bf16)] if x_off == 0 else []
        outs = pl.pallas_call(
            functools.partial(attend_kernel, (ctx_count, exp_count, tok, heads, x_off)),
            in_specs=[smem] * 3 + [vmem] * (2 * ctx_count + 1) + [anywhere],
            out_specs=[vmem] * (2 + len(route_shape)),
            out_shape=[first_shape, give_shape] + route_shape,
            scratch_shapes=[
                pltpu.VMEM((positions, HEAD_SIZE), bf16),
                pltpu.VMEM((positions, HEAD_SIZE), bf16),
                pltpu.VMEM((8, positions), jnp.int32),
                pltpu.VMEM((per_x, query_width), bf16),
            ],
            compiler_params=pltpu.CompilerParams(vmem_limit_bytes=2 * ctx_count * MIB),
            cost_estimate=pl.CostEstimate(
                flops=(4 * positions * positions + 4 * positions * cols) * query_width // x_count,
                bytes_accessed=4 * MIB,
                transcendentals=heads * positions * positions // x_count,
            ),
            name="attend",
        )(my_ctx, my_exp, block_order, *packed, *pieces, out_weight, after)
        gives[2 * x_off + 1] = from_offset(outs[1], 2 * x_off + 1)
        if x_off:
            gives[2 * x_off] = from_offset(outs[0], 2 * x_off)
            after = outs[0]
        else:
            keep, own_route = outs[0], outs[2]

    gives = [gives[offset] for offset in range(1, exp_count)]
    state = keep
    for give in gives:
        state = state + give[:per_x].astype(f32)
    state = state.astype(bf16)

    chunks = {(0, 0): state}
    for stage in stages_of(route):
        came = [from_partner(chunks[source], axis, bit) for _, source, _, axis, bit in stage]
        if stage[-1] != route[-1]:
            came = together(*came)
        chunks.update({target: array for (_, _, target, _, _), array in zip(stage, came)})
    gain = norm_gain.reshape(1, model_width)
    rows = x_count * per_x
    in_width = in_own.shape[1]
    near = tuple(sorted(key for key in chunks if key[0] < ctx_count // 2))
    far = tuple(sorted(key for key in chunks if key[0] >= ctx_count // 2))
    first_act, first_square = pl.pallas_call(
        functools.partial(experts_in_first, (ctx_count, x_count), near),
        in_specs=[smem] * 2 + [vmem] * (len(near) + 3) + [anywhere],
        out_specs=[vmem] * 2,
        out_shape=[
            jax.ShapeDtypeStruct((rows, 2 * in_width), f32),
            jax.ShapeDtypeStruct((rows, 1), f32),
        ],
        scratch_shapes=[pltpu.VMEM((rows, half_width // 2), bf16)],
        compiler_params=pltpu.CompilerParams(vmem_limit_bytes=2 * ctx_count * MIB),
        cost_estimate=pl.CostEstimate(
            flops=2 * rows * half_width * in_width, bytes_accessed=8 * MIB, transcendentals=0
        ),
        name="experts_in_first",
    )(my_ctx, my_exp, *[chunks[key] for key in near], gain, in_own, in_other, down_give)
    acts = []
    for part in range(2):
        acts.append(
            pl.pallas_call(
                functools.partial(experts_in_second, (ctx_count, x_count), far, part),
                in_specs=[smem] * 2 + [vmem] * (len(far) + 5) + [anywhere],
                out_specs=vmem,
                out_shape=jax.ShapeDtypeStruct((rows // 2, 2 * in_width + HEAD_SIZE), bf16),
                scratch_shapes=[pltpu.VMEM((rows // 2, half_width // 2), bf16)],
                compiler_params=pltpu.CompilerParams(vmem_limit_bytes=2 * ctx_count * MIB),
                cost_estimate=pl.CostEstimate(
                    flops=rows * half_width * in_width, bytes_accessed=8 * MIB, transcendentals=0
                ),
                name="experts_in_second",
            )(
                my_ctx,
                my_exp,
                *[chunks[key] for key in far],
                gain,
                in_own,
                in_other,
                first_act,
                first_square,
                acts[0] if part else first_square,
            )
        )
    leaves = {key for key in chunks} - {source for _, source, _, _, _ in route}
    sums = {}
    for part in range(2):
        slots = near if part == 1 else far
        states = [chunks[offset, 0] for offset in range(ctx_count)] if part == 1 else []
        outs = pl.pallas_call(
            functools.partial(experts_out_kernel, (ctx_count, exp_count, tok), part, slots, model_width),
            in_specs=[smem] * 2 + [vmem] * (4 + exp_count) + [anywhere] + [vmem] * len(states),
            out_specs=[vmem] * len(slots),
            out_shape=[
                jax.ShapeDtypeStruct((2 * tok, half_width), bf16 if slot in leaves else f32)
                for slot in slots
            ],
            scratch_shapes=[pltpu.VMEM((rows // 2, in_width), bf16)],
            compiler_params=pltpu.CompilerParams(vmem_limit_bytes=2 * ctx_count * MIB),
            cost_estimate=pl.CostEstimate(
                flops=rows * half_width * in_width,
                bytes_accessed=8 * MIB,
                transcendentals=rows * in_width // 2,
            ),
            name="experts_out",
        )(
            my_ctx,
            my_exp,
            acts[part],
            from_offset(acts[part], 1),
            own_route,
            *gives,
            down_own,
            down_other,
            sums[slots_done[0]] if part else acts[1],
            *states,
        )
        slots_done = slots
        sums.update(zip(slots, outs))

    backward = stages_of(route)[::-1]
    for number, stage in enumerate(backward):
        came = [from_partner(sums[target].astype(bf16), axis, bit) for _, _, target, axis, bit in stage]
        if number < len(backward) - 1:
            waiting = [key for key in near if key in sums] if number == 0 else []
            values = together(*came, *[sums[key] for key in waiting])
            came = values[: len(came)]
            sums.update(zip(waiting, values[len(came) :]))
        for (_, source, target, _, _), array in zip(stage, came):
            sums[source] = sums[source] + array.astype(f32)
    total = sums[0, 0]
    core = lax.bitwise_and(my_exp[0], 1)
    mine = jnp.where(core == 0, total[:tok], total[tok:]).astype(bf16)
    came = from_offset(jnp.where(core == 0, total[tok:], total[:tok]).astype(bf16), 1)
    mine = mine.reshape(tok, ctx_count, 1, cols)
    came = came.reshape(tok, ctx_count, 1, cols)
    result = jnp.where(core == 0, jnp.concatenate([mine, came], axis=2), jnp.concatenate([came, mine], axis=2))
    return result.reshape(tok, model_width)


def solution(mesh):
    return jax.shard_map(
        shards,
        mesh=mesh,
        in_specs=(
            P(("dp", "ctx", "exp"), None),
            P(("dp", "ctx"), "exp"),
            P(("dp", "ctx"), None),
            P(("dp", "ctx"), None),
            P(("dp", "ctx"), None),
            P(("dp", "ctx"), None),
            P(),
            P("exp", "ctx"),
            P(),
            P(("dp", "ctx", "exp"), None),
            P(("dp", "ctx", "exp"), None),
            P(("ctx", "exp"), None, None),
            P(("ctx", "exp"), None, None),
            P(("ctx", "exp"), None, None),
            P(("ctx", "exp"), None, None),
            P(("ctx", "exp"), None, None),
            P(("ctx", "exp"), None, None),
        ),
        out_specs=P(("dp", "ctx", "exp"), None),
        check_vma=False,
    )
```

time: 372 us -> 138 us (0.37)
  waiting for transfers between devices: 196 us -> 51.4 us
  blocking collectives: 64.6 us -> 0 us
  starting transfers between devices: 9.09 us -> 53.6 us
  local copies, waits for them, and re-layouts: 45.9 us -> 12.2 us
  matrix products: 20.6 us -> 0 us
  between operations: 20.6 us -> 0.31 us
  Pallas kernels: 0 us -> 19.5 us
  other arithmetic: 14.1 us -> 0.43 us
    all_to_all x2 -> x0, waiting for transfers between devices: 121 us -> none  [the longest x1 72.6 us: shards(): lax.all_to_all(outgoing, ('ctx', 'exp'), split_axis=0, concat_axis=0, til...]
    all_gather x2 -> x0, blocking collectives: 64.6 us -> none  [the longest x1 33.1 us: shards(): value_piece = lax.all_gather(value_head, 'ctx', axis=0, tiled=True)]
    all_gather x1 -> x0, waiting for transfers between devices: 52.7 us -> none  [shards(): lax.all_gather(out_weight, 'ctx', axis=1, tiled=True)]
    ppermute x1 -> x37, starting transfers between devices: 0.07 us -> 42 us  [from_partner(): lax.ppermute(array, axis, [(i, i ^ 1 << bit) for i in range(lax.axis_size...]
    ppermute x1 -> x37, waiting for transfers between devices: 3.39 us -> 37.2 us  [from_partner(): lax.ppermute(array, axis, [(i, i ^ 1 << bit) for i in range(lax.axis_size...]
    dot_general x6 -> x0, matrix products: 20.6 us -> none  [the longest x1 5.89 us: shards(): jnp.dot(attended, lax.all_gather(out_weight, 'ctx', axis=1, tiled=True),...]
    pallas_call x0 -> x10, Pallas kernels: none -> 19.5 us  [the longest x2 7.23 us: shards(): pl.pallas_call(functools.partial(attend_kernel, (ctx_count, exp_count, to...]
    reduce_scatter x1 -> x0, waiting for transfers between devices: 18.3 us -> none  [shards(): lax.psum_scatter(partial_rows.astype(jnp.bfloat16), 'exp', scatter_dimens...]
  transfers between devices with their start and end apart: 5 -> 52, of which waited for: 5 -> 32; matrix products, arithmetic and copies ran while one was open for 9% -> 0% of each run, Pallas kernels for 0% -> 14%
where the time goes in v1:
time: 138 us
  starting transfers between devices  53.6 us (39%)
  waiting for transfers between devices  51.4 us (37%)
  Pallas kernels  19.5 us (14%)
  local copies, waits for them, and re-layouts  12.2 us (9%)
    ppermute x37, starting transfers between devices, from_partner(): lax.ppermute(array, axis, [(i, i ^ 1 << bit) for i in range(lax.axis_size...  42 us
    ppermute x37, waiting for transfers between devices, from_partner(): lax.ppermute(array, axis, [(i, i ^ 1 << bit) for i in range(lax.axis_size...  37.2 us
    unnamed x36, local copies, waits for them, and re-layouts  11.4 us
    ppermute x7, starting transfers between devices, from_ctx(): lax.ppermute(array, 'ctx', [(i, i ^ offset) for i in range(lax.axis_size(...  8.58 us
    ppermute x7, waiting for transfers between devices, from_ctx(): lax.ppermute(array, 'ctx', [(i, i ^ offset) for i in range(lax.axis_size(...  7.4 us
    pallas_call x2, Pallas kernels, shards(): pl.pallas_call(functools.partial(attend_kernel, (ctx_count, exp_count, to...  7.23 us
    ppermute x8, waiting for transfers between devices, from_offset(): lax.ppermute(array, 'exp', [(i, i ^ offset) for i in range(lax.axis_size(...  6.86 us
    pallas_call x2, Pallas kernels, shards(): pl.pallas_call(functools.partial(experts_out_kernel, (ctx_count, exp_coun...  3.51 us
  transfers between devices with their start and end apart: 52, of which 32 were waited for; matrix products, arithmetic and copies ran while one was open for 0% of the time, Pallas kernels for 14%

profile of v1, /device:TPU:0, one launch (start us, length us, event | category | flops | bytes accessed | tf_op | source)
XLA Modules:
  0.0 137.5 jit_solution(15555759122326497897)
XLA Ops:
  6.8 4.1 %collective-permute-start = (bf16[64,1408]{1,0:T(8,128)(2,1)S(1)}, bf16[64,1408]{1,0:T(8,128)(2,1)S(1)}, u32[]{:S(2)}, u32[]{:S(2)}) collective-permute-start(bf16[64,1408]{1,0:T(8,128)(2,1)S(1)} %get-tuple-element.83._.refs_0_), channel_id=1, source_target_pairs={{0,16},{4,20},{8,24},{12,28},{16,0},{20,4},{24,8},{28,12},{1,17},{... | collective-permute-start | bytes 540680 | tf_op jit(solution)/shard_map/ppermute | solution.py:21
  10.9 1.6 %collective-permute-start.1 = (bf16[64,1408]{1,0:T(8,128)(2,1)S(1)}, bf16[64,1408]{1,0:T(8,128)(2,1)S(1)}, u32[]{:S(2)}, u32[]{:S(2)}) collective-permute-start(bf16[64,1408]{1,0:T(8,128)(2,1)S(1)} %get-tuple-element.83._.refs_0_), channel_id=1, source_target_pairs={{0,8},{4,12},{8,0},{12,4},{16,24},{20,28},{24,16},{28,20},{1,9},{5... | collective-permute-start | bytes 540680 | tf_op jit(solution)/shard_map/ppermute | solution.py:21
  14.0 1.9 %copy-done.2 = bf16[1,4096,384]{2,1,0:T(8,128)(2,1)S(1)} copy-done((bf16[1,4096,384]{2,1,0:T(8,128)(2,1)S(1)}, bf16[1,4096,384]{2,1,0:T(8,128)(2,1)}, u32[]{:S(2)}) %copy-start.2) | copy-done | bytes 3145752
  15.9 1.9 %copy-done.3 = bf16[1,4096,384]{2,1,0:T(8,128)(2,1)S(1)} copy-done((bf16[1,4096,384]{2,1,0:T(8,128)(2,1)S(1)}, bf16[1,4096,384]{2,1,0:T(8,128)(2,1)}, u32[]{:S(2)}) %copy-start.3) | copy-done | bytes 3145752
  19.2 2.0 %dequant_in.1 = (bf16[2048,768]{1,0:T(8,128)(2,1)S(1)}, bf16[2048,768]{1,0:T(8,128)(2,1)S(1)}) custom-call(s32[1]{0:T(128)} %bitcast.1.exp_ref, s32[3,1,32]{2,1,0:T(1,128)S(1)} %bitcast.21, s32[3,1,32]{2,1,0:T(1,128)S(1)} %bitcast.22, bf16[1,4096,384]{2,1,0:T(8,128)(2,1)S(1)} %copy-done.2, bf16[1,4096,384]{2,1,0:T(8,128)(2,1)S(1)} %copy-done.3, ...), custom_call_target="tpu_custom_call" | custom-call | flops 3145728 | bytes 12582912 | tf_op jit(solution)/shard_map/dequant_in/pallas_call | solution.py:135
  23.8 1.9 %dequant_down.1 = (bf16[384,2048]{1,0:T(8,128)(2,1)S(1)}, bf16[384,2048]{1,0:T(8,128)(2,1)S(1)}) custom-call(s32[1]{0:T(128)} %bitcast.1.exp_ref, s32[3,1,32]{2,1,0:T(1,128)S(1)} %bitcast.23, bf16[1,384,4096]{2,1,0:T(8,128)(2,1)S(1)} %copy-done.1, bf16[64,1408]{1,0:T(8,128)(2,1)S(1)} %collective-permute-done._.refs_4_), custom_call_target="tpu_custom_call" | custom-call | flops 1572864 | bytes 6291456 | tf_op jit(solution)/shard_map/dequant_down/pallas_call | solution.py:179
  25.7 2.5 %collective-permute-done.3.refs_6_ = bf16[64,1408]{1,0:T(8,128)(2,1)S(1)} collective-permute-done((bf16[64,1408]{1,0:T(8,128)(2,1)S(1)}, bf16[64,1408]{1,0:T(8,128)(2,1)S(1)}, u32[]{:S(2)}, u32[]{:S(2)}) %collective-permute-start.3) | collective-permute-done | bytes 180256 | tf_op jit(solution)/shard_map/ppermute | solution.py:21
  29.2 3.1 %collective-permute-done.4.refs_3_ = bf16[64,1408]{1,0:T(8,128)(2,1)S(1)} collective-permute-done((bf16[64,1408]{1,0:T(8,128)(2,1)S(1)}, bf16[64,1408]{1,0:T(8,128)(2,1)S(1)}, u32[]{:S(2)}, u32[]{:S(2)}) %collective-permute-start.4) | collective-permute-done | bytes 180256 | tf_op jit(solution)/shard_map/ppermute | solution.py:21
  33.2 2.3 %collective-permute-start.10 = (bf16[16,512]{1,0:T(8,128)(2,1)S(1)}, bf16[16,512]{1,0:T(8,128)(2,1)S(1)}, u32[]{:S(2)}, u32[]{:S(2)}) collective-permute-start(bf16[16,512]{1,0:T(8,128)(2,1)S(1)} %get-tuple-element.98), channel_id=1, source_target_pairs={{0,16},{4,20},{8,24},{12,28},{16,0},{20,4},{24,8},{28,12},{1,17},{... | collective-permute-start | bytes 49160 | tf_op jit(solution)/shard_map/ppermute | solution.py:33
  38.1 2.7 %collective-permute-start.13 = (bf16[16,512]{1,0:T(8,128)(2,1)S(1)}, bf16[16,512]{1,0:T(8,128)(2,1)S(1)}, u32[]{:S(2)}, u32[]{:S(2)}) collective-permute-start(bf16[16,512]{1,0:T(8,128)(2,1)S(1)} %get-tuple-element.101), channel_id=1, source_target_pairs={{0,28},{4,24},{8,20},{12,16},{16,12},{20,8},{24,4},{28,0},{1,29},{... | collective-permute-start | bytes 49160 | tf_op jit(solution)/shard_map/ppermute | solution.py:33
  42.2 2.3 %collective-permute-done.13.refs_15_ = bf16[16,512]{1,0:T(8,128)(2,1)S(1)} collective-permute-done((bf16[16,512]{1,0:T(8,128)(2,1)S(1)}, bf16[16,512]{1,0:T(8,128)(2,1)S(1)}, u32[]{:S(2)}, u32[]{:S(2)}) %collective-permute-start.13) | collective-permute-done | bytes 16416 | tf_op jit(solution)/shard_map/ppermute | solution.py:33
  46.0 3.2 %collective-permute-done.9.refs_11_ = bf16[16,512]{1,0:T(8,128)(2,1)S(1)} collective-permute-done((bf16[16,512]{1,0:T(8,128)(2,1)S(1)}, bf16[16,512]{1,0:T(8,128)(2,1)S(1)}, u32[]{:S(2)}, u32[]{:S(2)}) %collective-permute-start.9) | collective-permute-done | bytes 16416 | tf_op jit(solution)/shard_map/ppermute | solution.py:33
  49.2 3.6 %attend.2 = (bf16[288,256]{1,0:T(8,128)(2,1)S(1)}, bf16[288,256]{1,0:T(8,128)(2,1)S(1)}) custom-call(s32[1]{0:T(128)} %bitcast.ctx_ref, s32[1]{0:T(128)} %bitcast.1.exp_ref, s32[8]{0:T(128)S(1)} %copy-done.16, bf16[64,1408]{1,0:T(8,128)(2,1)S(1)} %get-tuple-element.83._.refs_0_, bf16[64,1408]{1,0:T(8,128)(2,1)S(1)} %collective-permute-done.2.refs_1_, ...), custom_call_target="tpu_custom_call" | custom-call | flops 805306368 | bytes 4194304 | tf_op jit(solution)/shard_map/attend/pallas_call | solution.py:495
  52.8 1.5 %collective-permute-start.15 = (bf16[288,256]{1,0:T(8,128)(2,1)S(1)}, bf16[288,256]{1,0:T(8,128)(2,1)S(1)}, u32[]{:S(2)}, u32[]{:S(2)}) collective-permute-start(bf16[288,256]{1,0:T(8,128)(2,1)S(1)} %get-tuple-element.102.refs_17_), channel_id=1, source_target_pairs={{0,2},{1,3},{2,0},{3,1},{4,6},{5,7},{6,4},{7,5},{8,10},{9,11},{10,... | collective-permute-start | bytes 442376 | tf_op jit(solution)/shard_map/ppermute | solution.py:29
  54.3 3.6 %attend.3 = (f32[256,256]{1,0:T(8,128)S(1)}, bf16[288,256]{1,0:T(8,128)(2,1)S(1)}, bf16[32,128]{1,0:T(8,128)(2,1)S(1)}) custom-call(s32[1]{0:T(128)} %bitcast.ctx_ref, s32[1]{0:T(128)} %bitcast.1.exp_ref, s32[8]{0:T(128)S(1)} %copy-done.16, bf16[64,1408]{1,0:T(8,128)(2,1)S(1)} %get-tuple-element.83._.refs_0_, ...), custom_call_target="tpu_custom_call" | custom-call | flops 805306368 | bytes 4194304 | tf_op jit(solution)/shard_map/attend/pallas_call | solution.py:495
  59.4 4.3 %collective-permute-done.16.refs_3_ = bf16[288,256]{1,0:T(8,128)(2,1)S(1)} collective-permute-done((bf16[288,256]{1,0:T(8,128)(2,1)S(1)}, bf16[288,256]{1,0:T(8,128)(2,1)S(1)}, u32[]{:S(2)}, u32[]{:S(2)}) %collective-permute-start.16) | collective-permute-done | bytes 147488 | tf_op jit(solution)/shard_map/ppermute | solution.py:29
  64.3 2.6 %collective-permute-start.18 = (bf16[256,256]{1,0:T(8,128)(2,1)S(1)}, bf16[256,256]{1,0:T(8,128)(2,1)S(1)}, u32[]{:S(2)}, u32[]{:S(2)}) collective-permute-start(bf16[256,256]{1,0:T(8,128)(2,1)S(1)} %add_convert_fusion.7.refs_0_.refs_7_), channel_id=1, source_target_pairs={{0,8},{4,12},{8,0},{12,4},{16,24},{20,28},{24,16},{28,20},{1,9},{5... | collective-permute-start | bytes 393224 | tf_op jit(solution)/shard_map/ppermute | solution.py:21
  68.3 4.9 %collective-permute-done.17.refs_0_.refs_11_ = bf16[256,256]{1,0:T(8,128)(2,1)S(1)} collective-permute-done((bf16[256,256]{1,0:T(8,128)(2,1)S(1)}, bf16[256,256]{1,0:T(8,128)(2,1)S(1)}, u32[]{:S(2)}, u32[]{:S(2)}) %collective-permute-start.17) | collective-permute-done | bytes 131104 | tf_op jit(solution)/shard_map/ppermute | solution.py:21
  74.9 4.3 %collective-permute-done.21.refs_4_.refs_13_ = bf16[256,256]{1,0:T(8,128)(2,1)S(1)} collective-permute-done((bf16[256,256]{1,0:T(8,128)(2,1)S(1)}, bf16[256,256]{1,0:T(8,128)(2,1)S(1)}, u32[]{:S(2)}, u32[]{:S(2)}) %collective-permute-start.21) | collective-permute-done | bytes 131104 | tf_op jit(solution)/shard_map/ppermute | solution.py:21
  82.2 2.1 %collective-permute-done.24.refs_2_.refs_12_ = bf16[256,256]{1,0:T(8,128)(2,1)S(1)} collective-permute-done((bf16[256,256]{1,0:T(8,128)(2,1)S(1)}, bf16[256,256]{1,0:T(8,128)(2,1)S(1)}, u32[]{:S(2)}, u32[]{:S(2)}) %collective-permute-start.24) | collective-permute-done | bytes 131104 | tf_op jit(solution)/shard_map/ppermute | solution.py:21
  84.2 2.1 %collective-permute-done.25.refs_1_ = bf16[256,256]{1,0:T(8,128)(2,1)S(1)} collective-permute-done((bf16[256,256]{1,0:T(8,128)(2,1)S(1)}, bf16[256,256]{1,0:T(8,128)(2,1)S(1)}, u32[]{:S(2)}, u32[]{:S(2)}) %collective-permute-start.25) | collective-permute-done | bytes 131104 | tf_op jit(solution)/shard_map/ppermute | solution.py:21
  89.6 2.0 %collective-permute-done.28.refs_7_ = bf16[256,256]{1,0:T(8,128)(2,1)S(1)} collective-permute-done((bf16[256,256]{1,0:T(8,128)(2,1)S(1)}, bf16[256,256]{1,0:T(8,128)(2,1)S(1)}, u32[]{:S(2)}, u32[]{:S(2)}) %collective-permute-start.28) | collective-permute-done | bytes 131104 | tf_op jit(solution)/shard_map/ppermute | solution.py:21
  94.9 2.0 %experts_in_first.1 = (f32[512,1536]{1,0:T(8,128)S(1)}, f32[512,1]{1,0:T(8,128)S(1)}) custom-call(s32[1]{0:T(128)} %bitcast.ctx_ref, s32[1]{0:T(128)} %bitcast.1.exp_ref, bf16[256,256]{1,0:T(8,128)(2,1)S(1)} %add_convert_fusion.7.refs_0_.refs_7_, bf16[256,256]{1,0:T(8,128)(2,1)S(1)} %collective-permute-done.20.refs_1_, ...), custom_call_target="tpu_custom_call" | custom-call | flops 1610612736 | bytes 8388608 | tf_op jit(solution)/shard_map/experts_in_first/pallas_call | solution.py:538
  102.0 1.8 %experts_out.2 = (f32[32,2048]{1,0:T(8,128)S(1)}, bf16[32,2048]{1,0:T(8,128)(2,1)S(1)}, f32[32,2048]{1,0:T(8,128)S(1)}, bf16[32,2048]{1,0:T(8,128)(2,1)S(1)}, f3...) custom-call(s32[1]{0:T(128)} %bitcast.ctx_ref, ...), custom_call_target="tpu_custom_call" | custom-call | flops 805306368 | bytes 8388608 | tf_op jit(solution)/shard_map/experts_out/pallas_call | solution.py:584
  103.8 1.8 %collective-permute-start.35 = (bf16[32,2048]{1,0:T(8,128)(2,1)S(1)}, bf16[32,2048]{1,0:T(8,128)(2,1)S(1)}, u32[]{:S(2)}, u32[]{:S(2)}) collective-permute-start(bf16[32,2048]{1,0:T(8,128)(2,1)S(1)} %get-tuple-element.126), channel_id=1, source_target_pairs={{0,2},{1,3},{2,0},{3,1},{4,6},{5,7},{6,4},{7,5},{8,10},{9,11},{10,... | collective-permute-start | bytes 393224 | tf_op jit(solution)/shard_map/ppermute | solution.py:21
  107.9 1.8 %experts_out.3 = (f32[32,2048]{1,0:T(8,128)S(1)}, bf16[32,2048]{1,0:T(8,128)(2,1)S(1)}, f32[32,2048]{1,0:T(8,128)S(1)}, bf16[32,2048]{1,0:T(8,128)(2,1)S(1)}, f3...) custom-call(s32[1]{0:T(128)} %bitcast.ctx_ref, ...), custom_call_target="tpu_custom_call" | custom-call | flops 805306368 | bytes 8388608 | tf_op jit(solution)/shard_map/experts_out/pallas_call | solution.py:584
  109.7 2.3 %collective-permute-done.36 = bf16[32,2048]{1,0:T(8,128)(2,1)S(1)} collective-permute-done((bf16[32,2048]{1,0:T(8,128)(2,1)S(1)}, bf16[32,2048]{1,0:T(8,128)(2,1)S(1)}, u32[]{:S(2)}, u32[]{:S(2)}) %collective-permute-start.36) | collective-permute-done | bytes 131104 | tf_op jit(solution)/shard_map/ppermute | solution.py:21
  112.3 1.8 %collective-permute-start.38 = (bf16[32,2048]{1,0:T(8,128)(2,1)S(1)}, bf16[32,2048]{1,0:T(8,128)(2,1)S(1)}, u32[]{:S(2)}, u32[]{:S(2)}) collective-permute-start(bf16[32,2048]{1,0:T(8,128)(2,1)S(1)} %get-tuple-element.139), channel_id=1, source_target_pairs={{0,2},{1,3},{2,0},{3,1},{4,6},{5,7},{6,4},{7,5},{8,10},{9,11},{10,... | collective-permute-start | bytes 393224 | tf_op jit(solution)/shard_map/ppermute | solution.py:21
  124.7 2.6 %collective-permute-done.42 = bf16[32,2048]{1,0:T(8,128)(2,1)S(1)} collective-permute-done((bf16[32,2048]{1,0:T(8,128)(2,1)S(1)}, bf16[32,2048]{1,0:T(8,128)(2,1)S(1)}, u32[]{:S(2)}, u32[]{:S(2)}) %collective-permute-start.42) | collective-permute-done | bytes 131104 | tf_op jit(solution)/shard_map/ppermute | solution.py:21
  127.3 1.8 %collective-permute-start.47 = (bf16[32,2048]{1,0:T(8,128)(2,1)S(1)}, bf16[32,2048]{1,0:T(8,128)(2,1)S(1)}, u32[]{:S(2)}, u32[]{:S(2)}) collective-permute-start(bf16[32,2048]{1,0:T(8,128)(2,1)S(1)} %add_convert_fusion.2), channel_id=1, source_target_pairs={{0,16},{4,20},{8,24},{12,28},{16,0},{20,4},{24,8},{28,12},{1,17},{... | collective-permute-start | bytes 393224 | tf_op jit(solution)/shard_map/ppermute | solution.py:21
  129.2 2.5 %collective-permute-start.48 = (bf16[32,2048]{1,0:T(8,128)(2,1)S(1)}, bf16[32,2048]{1,0:T(8,128)(2,1)S(1)}, u32[]{:S(2)}, u32[]{:S(2)}) collective-permute-start(bf16[32,2048]{1,0:T(8,128)(2,1)S(1)} %add_convert_fusion.1), channel_id=1, source_target_pairs={{0,8},{4,12},{8,0},{12,4},{16,24},{20,28},{24,16},{28,20},{1,9},{5... | collective-permute-start | bytes 393224 | tf_op jit(solution)/shard_map/ppermute | solution.py:21
  131.7 3.0 %collective-permute-done.47 = bf16[32,2048]{1,0:T(8,128)(2,1)S(1)} collective-permute-done((bf16[32,2048]{1,0:T(8,128)(2,1)S(1)}, bf16[32,2048]{1,0:T(8,128)(2,1)S(1)}, u32[]{:S(2)}, u32[]{:S(2)}) %collective-permute-start.47) | collective-permute-done | bytes 131104 | tf_op jit(solution)/shard_map/ppermute | solution.py:21
  (131 shorter events, 55.6 us)
Async XLA Ops:
  6.8 14.3 %collective-permute-start = (bf16[64,1408]{1,0:T(8,128)(2,1)S(1)}, bf16[64,1408]{1,0:T(8,128)(2,1)S(1)}, u32[]{:S(2)}, u32[]{:S(2)}) collective-permute-start(bf16[64,1408]{1,0:T(8,128)(2,1)S(1)} %get-tuple-element.83._.refs_0_), channel_id=1, source_target_pairs={{0,16},{4,20},{8,24},{12,28},{16,0},{20,4},{24,8},{28,12},{1,17},{... | collective-permute-start | bytes 540680 | tf_op jit(solution)/shard_map/ppermute | solution.py:21
  10.9 10.2 %collective-permute-start.1 = (bf16[64,1408]{1,0:T(8,128)(2,1)S(1)}, bf16[64,1408]{1,0:T(8,128)(2,1)S(1)}, u32[]{:S(2)}, u32[]{:S(2)}) collective-permute-start(bf16[64,1408]{1,0:T(8,128)(2,1)S(1)} %get-tuple-element.83._.refs_0_), channel_id=1, source_target_pairs={{0,8},{4,12},{8,0},{12,4},{16,24},{20,28},{24,16},{28,20},{1,9},{5... | collective-permute-start | bytes 540680 | tf_op jit(solution)/shard_map/ppermute | solution.py:21
  12.5 8.7 %collective-permute-start.2 = (bf16[64,1408]{1,0:T(8,128)(2,1)S(1)}, bf16[64,1408]{1,0:T(8,128)(2,1)S(1)}, u32[]{:S(2)}, u32[]{:S(2)}) collective-permute-start(bf16[64,1408]{1,0:T(8,128)(2,1)S(1)} %get-tuple-element.83._.refs_0_), channel_id=1, source_target_pairs={{0,4},{4,0},{8,12},{12,8},{16,20},{20,16},{24,28},{28,24},{1,5},{5... | collective-permute-start | bytes 540680 | tf_op jit(solution)/shard_map/ppermute | solution.py:21
  21.2 73.7 %collective-permute-start.32 = (bf16[2048,768]{1,0:T(8,128)(2,1)S(1)}, bf16[2048,768]{1,0:T(8,128)(2,1)S(1)}, u32[]{:S(2)}, u32[]{:S(2)}) collective-permute-start(bf16[2048,768]{1,0:T(8,128)(2,1)S(1)} %get-tuple-element.116), channel_id=1, source_target_pairs={{0,1},{1,0},{2,3},{3,2},{4,5},{5,4},{6,7},{7,6},{8,9},{9,8},{10,11... | collective-permute-start | bytes 9437192 | tf_op jit(solution)/shard_map/ppermute | solution.py:29
  21.3 7.0 %collective-permute-start.3 = (bf16[64,1408]{1,0:T(8,128)(2,1)S(1)}, bf16[64,1408]{1,0:T(8,128)(2,1)S(1)}, u32[]{:S(2)}, u32[]{:S(2)}) collective-permute-start(bf16[64,1408]{1,0:T(8,128)(2,1)S(1)} %collective-permute-done._.refs_4_), channel_id=1, source_target_pairs={{0,8},{4,12},{8,0},{12,4},{16,24},{20,28},{24,16},{28,20},{1,9},{5... | collective-permute-start | bytes 540680 | tf_op jit(solution)/shard_map/ppermute | solution.py:21
  21.8 7.4 %collective-permute-start.5 = (bf16[64,1408]{1,0:T(8,128)(2,1)S(1)}, bf16[64,1408]{1,0:T(8,128)(2,1)S(1)}, u32[]{:S(2)}, u32[]{:S(2)}) collective-permute-start(bf16[64,1408]{1,0:T(8,128)(2,1)S(1)} %collective-permute-done._.refs_4_), channel_id=1, source_target_pairs={{0,4},{4,0},{8,12},{12,8},{16,20},{20,16},{24,28},{28,24},{1,5},{5... | collective-permute-start | bytes 540680 | tf_op jit(solution)/shard_map/ppermute | solution.py:21
  22.6 9.6 %collective-permute-start.4 = (bf16[64,1408]{1,0:T(8,128)(2,1)S(1)}, bf16[64,1408]{1,0:T(8,128)(2,1)S(1)}, u32[]{:S(2)}, u32[]{:S(2)}) collective-permute-start(bf16[64,1408]{1,0:T(8,128)(2,1)S(1)} %collective-permute-done.1.refs_2_), channel_id=1, source_target_pairs={{0,4},{4,0},{8,12},{12,8},{16,20},{20,16},{24,28},{28,24},{1,5},{5... | collective-permute-start | bytes 540680 | tf_op jit(solution)/shard_map/ppermute | solution.py:21
  32.3 16.9 %collective-permute-start.6 = (bf16[64,1408]{1,0:T(8,128)(2,1)S(1)}, bf16[64,1408]{1,0:T(8,128)(2,1)S(1)}, u32[]{:S(2)}, u32[]{:S(2)}) collective-permute-start(bf16[64,1408]{1,0:T(8,128)(2,1)S(1)} %collective-permute-done.3.refs_6_), channel_id=1, source_target_pairs={{0,4},{4,0},{8,12},{12,8},{16,20},{20,16},{24,28},{28,24},{1,5},{5... | collective-permute-start | bytes 540680 | tf_op jit(solution)/shard_map/ppermute | solution.py:21
  38.1 6.4 %collective-permute-start.13 = (bf16[16,512]{1,0:T(8,128)(2,1)S(1)}, bf16[16,512]{1,0:T(8,128)(2,1)S(1)}, u32[]{:S(2)}, u32[]{:S(2)}) collective-permute-start(bf16[16,512]{1,0:T(8,128)(2,1)S(1)} %get-tuple-element.101), channel_id=1, source_target_pairs={{0,28},{4,24},{8,20},{12,16},{16,12},{20,8},{24,4},{28,0},{1,29},{... | collective-permute-start | bytes 49160 | tf_op jit(solution)/shard_map/ppermute | solution.py:33
  52.8 6.6 %collective-permute-start.15 = (bf16[288,256]{1,0:T(8,128)(2,1)S(1)}, bf16[288,256]{1,0:T(8,128)(2,1)S(1)}, u32[]{:S(2)}, u32[]{:S(2)}) collective-permute-start(bf16[288,256]{1,0:T(8,128)(2,1)S(1)} %get-tuple-element.102.refs_17_), channel_id=1, source_target_pairs={{0,2},{1,3},{2,0},{3,1},{4,6},{5,7},{6,4},{7,5},{8,10},{9,11},{10,... | collective-permute-start | bytes 442376 | tf_op jit(solution)/shard_map/ppermute | solution.py:29
  63.8 9.4 %collective-permute-start.17 = (bf16[256,256]{1,0:T(8,128)(2,1)S(1)}, bf16[256,256]{1,0:T(8,128)(2,1)S(1)}, u32[]{:S(2)}, u32[]{:S(2)}) collective-permute-start(bf16[256,256]{1,0:T(8,128)(2,1)S(1)} %add_convert_fusion.7.refs_0_.refs_7_), channel_id=1, source_target_pairs={{0,16},{4,20},{8,24},{12,28},{16,0},{20,4},{24,8},{28,12},{1,17},{... | collective-permute-start | bytes 393224 | tf_op jit(solution)/shard_map/ppermute | solution.py:21
  64.3 9.1 %collective-permute-start.18 = (bf16[256,256]{1,0:T(8,128)(2,1)S(1)}, bf16[256,256]{1,0:T(8,128)(2,1)S(1)}, u32[]{:S(2)}, u32[]{:S(2)}) collective-permute-start(bf16[256,256]{1,0:T(8,128)(2,1)S(1)} %add_convert_fusion.7.refs_0_.refs_7_), channel_id=1, source_target_pairs={{0,8},{4,12},{8,0},{12,4},{16,24},{20,28},{24,16},{28,20},{1,9},{5... | collective-permute-start | bytes 393224 | tf_op jit(solution)/shard_map/ppermute | solution.py:21
  66.8 6.6 %collective-permute-start.19 = (bf16[256,256]{1,0:T(8,128)(2,1)S(1)}, bf16[256,256]{1,0:T(8,128)(2,1)S(1)}, u32[]{:S(2)}, u32[]{:S(2)}) collective-permute-start(bf16[256,256]{1,0:T(8,128)(2,1)S(1)} %add_convert_fusion.7.refs_0_.refs_7_), channel_id=1, source_target_pairs={{0,4},{4,0},{8,12},{12,8},{16,20},{20,16},{24,28},{28,24},{1,5},{5... | collective-permute-start | bytes 393224 | tf_op jit(solution)/shard_map/ppermute | solution.py:21
  73.2 28.2 %collective-permute-start.34 = (bf16[384,2048]{1,0:T(8,128)(2,1)S(1)}, bf16[384,2048]{1,0:T(8,128)(2,1)S(1)}, u32[]{:S(2)}, u32[]{:S(2)}) collective-permute-start(bf16[384,2048]{1,0:T(8,128)(2,1)S(1)} %get-tuple-element.121.refs_11_), channel_id=1, source_target_pairs={{0,1},{1,0},{2,3},{3,2},{4,5},{5,4},{6,7},{7,6},{8,9},{9,8},{10,11... | collective-permute-start | bytes 4718600 | tf_op jit(solution)/shard_map/ppermute | solution.py:29
  73.4 5.8 %collective-permute-start.21 = (bf16[256,256]{1,0:T(8,128)(2,1)S(1)}, bf16[256,256]{1,0:T(8,128)(2,1)S(1)}, u32[]{:S(2)}, u32[]{:S(2)}) collective-permute-start(bf16[256,256]{1,0:T(8,128)(2,1)S(1)} %collective-permute-done.17.refs_0_.refs_11_), channel_id=1, source_target_pairs={{0,8},{4,12},{8,0},{12,4},{16,24},{20,28},{24,16},{28,20},{1,9},{5... | collective-permute-start | bytes 393224 | tf_op jit(solution)/shard_map/ppermute | solution.py:21
  73.4 6.8 %collective-permute-start.22 = (bf16[256,256]{1,0:T(8,128)(2,1)S(1)}, bf16[256,256]{1,0:T(8,128)(2,1)S(1)}, u32[]{:S(2)}, u32[]{:S(2)}) collective-permute-start(bf16[256,256]{1,0:T(8,128)(2,1)S(1)} %collective-permute-done.18.refs_4_.refs_9_), channel_id=1, source_target_pairs={{0,2},{1,3},{2,0},{3,1},{4,6},{5,7},{6,4},{7,5},{8,10},{9,11},{10,... | collective-permute-start | bytes 393224 | tf_op jit(solution)/shard_map/ppermute | solution.py:21
  74.0 6.7 %collective-permute-start.23 = (bf16[256,256]{1,0:T(8,128)(2,1)S(1)}, bf16[256,256]{1,0:T(8,128)(2,1)S(1)}, u32[]{:S(2)}, u32[]{:S(2)}) collective-permute-start(bf16[256,256]{1,0:T(8,128)(2,1)S(1)} %collective-permute-done.18.refs_4_.refs_9_), channel_id=1, source_target_pairs={{0,4},{4,0},{8,12},{12,8},{16,20},{20,16},{24,28},{28,24},{1,5},{5... | collective-permute-start | bytes 393224 | tf_op jit(solution)/shard_map/ppermute | solution.py:21
  80.1 6.2 %collective-permute-start.25 = (bf16[256,256]{1,0:T(8,128)(2,1)S(1)}, bf16[256,256]{1,0:T(8,128)(2,1)S(1)}, u32[]{:S(2)}, u32[]{:S(2)}) collective-permute-start(bf16[256,256]{1,0:T(8,128)(2,1)S(1)} %collective-permute-done.17.refs_0_.refs_11_), channel_id=1, source_target_pairs={{0,2},{1,3},{2,0},{3,1},{4,6},{5,7},{6,4},{7,5},{8,10},{9,11},{10,... | collective-permute-start | bytes 393224 | tf_op jit(solution)/shard_map/ppermute | solution.py:21
  80.7 7.7 %collective-permute-start.27 = (bf16[256,256]{1,0:T(8,128)(2,1)S(1)}, bf16[256,256]{1,0:T(8,128)(2,1)S(1)}, u32[]{:S(2)}, u32[]{:S(2)}) collective-permute-start(bf16[256,256]{1,0:T(8,128)(2,1)S(1)} %collective-permute-done.19.refs_2_.refs_8_), channel_id=1, source_target_pairs={{0,2},{1,3},{2,0},{3,1},{4,6},{5,7},{6,4},{7,5},{8,10},{9,11},{10,... | collective-permute-start | bytes 393224 | tf_op jit(solution)/shard_map/ppermute | solution.py:21
  100.8 7.1 %collective-permute-start.37 = (bf16[256,1664]{1,0:T(8,128)(2,1)S(1)}, bf16[256,1664]{1,0:T(8,128)(2,1)S(1)}, u32[]{:S(2)}, u32[]{:S(2)}) collective-permute-start(bf16[256,1664]{1,0:T(8,128)(2,1)S(1)} %experts_in_second.3.refs_6_.act_ref), channel_id=1, source_target_pairs={{0,1},{1,0},{2,3},{3,2},{4,5},{5,4},{6,7},{7,6},{8,9},{9,8},{10,11... | collective-permute-start | bytes 2555912 | tf_op jit(solution)/shard_map/ppermute | solution.py:29
  103.8 5.9 %collective-permute-start.35 = (bf16[32,2048]{1,0:T(8,128)(2,1)S(1)}, bf16[32,2048]{1,0:T(8,128)(2,1)S(1)}, u32[]{:S(2)}, u32[]{:S(2)}) collective-permute-start(bf16[32,2048]{1,0:T(8,128)(2,1)S(1)} %get-tuple-element.126), channel_id=1, source_target_pairs={{0,2},{1,3},{2,0},{3,1},{4,6},{5,7},{6,4},{7,5},{8,10},{9,11},{10,... | collective-permute-start | bytes 393224 | tf_op jit(solution)/shard_map/ppermute | solution.py:21
  105.6 6.4 %collective-permute-start.36 = (bf16[32,2048]{1,0:T(8,128)(2,1)S(1)}, bf16[32,2048]{1,0:T(8,128)(2,1)S(1)}, u32[]{:S(2)}, u32[]{:S(2)}) collective-permute-start(bf16[32,2048]{1,0:T(8,128)(2,1)S(1)} %get-tuple-element.127), channel_id=1, source_target_pairs={{0,4},{4,0},{8,12},{12,8},{16,20},{20,16},{24,28},{28,24},{1,5},{5... | collective-permute-start | bytes 393224 | tf_op jit(solution)/shard_map/ppermute | solution.py:21
  106.3 8.5 %collective-permute-start.41 = (bf16[32,2048]{1,0:T(8,128)(2,1)S(1)}, bf16[32,2048]{1,0:T(8,128)(2,1)S(1)}, u32[]{:S(2)}, u32[]{:S(2)}) collective-permute-start(bf16[32,2048]{1,0:T(8,128)(2,1)S(1)} %get-tuple-element.143), channel_id=1, source_target_pairs={{0,4},{4,0},{8,12},{12,8},{16,20},{20,16},{24,28},{28,24},{1,5},{5... | collective-permute-start | bytes 393224 | tf_op jit(solution)/shard_map/ppermute | solution.py:21
  107.6 13.7 %collective-permute-start.46 = (bf16[32,2048]{1,0:T(8,128)(2,1)S(1)}, bf16[32,2048]{1,0:T(8,128)(2,1)S(1)}, u32[]{:S(2)}, u32[]{:S(2)}) collective-permute-start(bf16[32,2048]{1,0:T(8,128)(2,1)S(1)} %get-tuple-element.151), channel_id=1, source_target_pairs={{0,2},{1,3},{2,0},{3,1},{4,6},{5,7},{6,4},{7,5},{8,10},{9,11},{10,... | collective-permute-start | bytes 393224 | tf_op jit(solution)/shard_map/ppermute | solution.py:21
  112.3 6.1 %collective-permute-start.38 = (bf16[32,2048]{1,0:T(8,128)(2,1)S(1)}, bf16[32,2048]{1,0:T(8,128)(2,1)S(1)}, u32[]{:S(2)}, u32[]{:S(2)}) collective-permute-start(bf16[32,2048]{1,0:T(8,128)(2,1)S(1)} %get-tuple-element.139), channel_id=1, source_target_pairs={{0,2},{1,3},{2,0},{3,1},{4,6},{5,7},{6,4},{7,5},{8,10},{9,11},{10,... | collective-permute-start | bytes 393224 | tf_op jit(solution)/shard_map/ppermute | solution.py:21
  114.9 7.6 %collective-permute-start.45 = (bf16[32,2048]{1,0:T(8,128)(2,1)S(1)}, bf16[32,2048]{1,0:T(8,128)(2,1)S(1)}, u32[]{:S(2)}, u32[]{:S(2)}) collective-permute-start(bf16[32,2048]{1,0:T(8,128)(2,1)S(1)} %add_convert_fusion.3), channel_id=1, source_target_pairs={{0,4},{4,0},{8,12},{12,8},{16,20},{20,16},{24,28},{28,24},{1,5},{5... | collective-permute-start | bytes 393224 | tf_op jit(solution)/shard_map/ppermute | solution.py:21
  117.0 6.8 %collective-permute-start.44 = (bf16[32,2048]{1,0:T(8,128)(2,1)S(1)}, bf16[32,2048]{1,0:T(8,128)(2,1)S(1)}, u32[]{:S(2)}, u32[]{:S(2)}) collective-permute-start(bf16[32,2048]{1,0:T(8,128)(2,1)S(1)} %get-tuple-element.148), channel_id=1, source_target_pairs={{0,4},{4,0},{8,12},{12,8},{16,20},{20,16},{24,28},{28,24},{1,5},{5... | collective-permute-start | bytes 393224 | tf_op jit(solution)/shard_map/ppermute | solution.py:21
  120.7 6.5 %collective-permute-start.42 = (bf16[32,2048]{1,0:T(8,128)(2,1)S(1)}, bf16[32,2048]{1,0:T(8,128)(2,1)S(1)}, u32[]{:S(2)}, u32[]{:S(2)}) collective-permute-start(bf16[32,2048]{1,0:T(8,128)(2,1)S(1)} %add_convert_fusion.5), channel_id=1, source_target_pairs={{0,8},{4,12},{8,0},{12,4},{16,24},{20,28},{24,16},{28,20},{1,9},{5... | collective-permute-start | bytes 393224 | tf_op jit(solution)/shard_map/ppermute | solution.py:21
  121.3 10.4 %collective-permute-start.50 = (bf16[32,2048]{1,0:T(8,128)(2,1)S(1)}, bf16[32,2048]{1,0:T(8,128)(2,1)S(1)}, u32[]{:S(2)}, u32[]{:S(2)}) collective-permute-start(bf16[32,2048]{1,0:T(8,128)(2,1)S(1)} %get-tuple-element.160), channel_id=1, source_target_pairs={{0,2},{1,3},{2,0},{3,1},{4,6},{5,7},{6,4},{7,5},{8,10},{9,11},{10,... | collective-permute-start | bytes 393224 | tf_op jit(solution)/shard_map/ppermute | solution.py:21
  122.5 9.2 %collective-permute-start.49 = (bf16[32,2048]{1,0:T(8,128)(2,1)S(1)}, bf16[32,2048]{1,0:T(8,128)(2,1)S(1)}, u32[]{:S(2)}, u32[]{:S(2)}) collective-permute-start(bf16[32,2048]{1,0:T(8,128)(2,1)S(1)} %add_convert_fusion), channel_id=1, source_target_pairs={{0,4},{4,0},{8,12},{12,8},{16,20},{20,16},{24,28},{28,24},{1,5},{5... | collective-permute-start | bytes 393224 | tf_op jit(solution)/shard_map/ppermute | solution.py:21
  127.3 7.4 %collective-permute-start.47 = (bf16[32,2048]{1,0:T(8,128)(2,1)S(1)}, bf16[32,2048]{1,0:T(8,128)(2,1)S(1)}, u32[]{:S(2)}, u32[]{:S(2)}) collective-permute-start(bf16[32,2048]{1,0:T(8,128)(2,1)S(1)} %add_convert_fusion.2), channel_id=1, source_target_pairs={{0,16},{4,20},{8,24},{12,28},{16,0},{20,4},{24,8},{28,12},{1,17},{... | collective-permute-start | bytes 393224 | tf_op jit(solution)/shard_map/ppermute | solution.py:21
  129.2 6.0 %collective-permute-start.48 = (bf16[32,2048]{1,0:T(8,128)(2,1)S(1)}, bf16[32,2048]{1,0:T(8,128)(2,1)S(1)}, u32[]{:S(2)}, u32[]{:S(2)}) collective-permute-start(bf16[32,2048]{1,0:T(8,128)(2,1)S(1)} %add_convert_fusion.1), channel_id=1, source_target_pairs={{0,8},{4,12},{8,0},{12,4},{16,24},{20,28},{24,16},{28,20},{1,9},{5... | collective-permute-start | bytes 393224 | tf_op jit(solution)/shard_map/ppermute | solution.py:21
  (37 other events, 214.1 us)

commit v2 on v1

--- a/solution.py
+++ b/solution.py
@@ -71,27 +71,51 @@
     return jnp.full((1, width), factor, jnp.float32).astype(jnp.bfloat16)
 
 
-def pack_kernel(plan, ctx_ref, exp_ref, key_scale_ref, value_scale_ref, query_ref, key_ref, value_ref,
-                ids_ref, route_ref, residual_ref, packed_ref, *piece_refs):
-    heads, group, experts = plan
-    span, width = query_ref.shape
+def copy_all(sems, pairs):
+    copies = [pltpu.make_async_copy(src, dst, sems.at[i]) for i, (src, dst) in enumerate(pairs)]
+    for copy in copies:
+        copy.start()
+    return copies
+
+
+def pack_kernel(plan, ctx_ref, exp_ref, key_scale_hbm, value_scale_hbm, query_hbm, key_hbm, value_hbm, ids_hbm,
+                route_hbm, residual_hbm, packed_ref, near_ref, far_ref, key_scale_ref, value_scale_ref,
+                key_ref, value_ref, ids_ref, route_ref, sems):
+    heads, group = plan
+    span, width = query_hbm.shape
+    half, tok, cols = near_ref.shape
     my_ctx, my_exp = ctx_ref[0], exp_ref[0]
     kv_head = my_exp * heads // group
     at = pl.ds(pl.multiple_of(kv_head * HEAD_SIZE, HEAD_SIZE), HEAD_SIZE)
+    pairs = [
+        (key_scale_hbm, key_scale_ref),
+        (value_scale_hbm, value_scale_ref),
+        (key_hbm.at[:, at], key_ref),
+        (value_hbm.at[:, at], value_ref),
+        (ids_hbm, ids_ref),
+        (route_hbm, route_ref),
+        (query_hbm, packed_ref.at[:, 2 * HEAD_SIZE : 2 * HEAD_SIZE + width]),
+    ]
+    for offset in range(2 * half):
+        col = pl.multiple_of(lax.bitwise_xor(my_ctx, offset) * cols, cols)
+        pairs.append(
+            (residual_hbm.at[:, pl.ds(col, cols)], (near_ref if offset < half else far_ref).at[offset % half])
+        )
+    copies = copy_all(sems, pairs)
+    for copy in copies[:6]:
+        copy.wait()
+    lane = lax.broadcasted_iota(jnp.int32, key_scale_ref.shape, 1)
     blocks = key_scale_ref.shape[0]
     for place, (ref, scale_ref) in enumerate(((key_ref, key_scale_ref), (value_ref, value_scale_ref))):
+        exponent = scale_ref[...]
+        factor = jnp.where(
+            exponent < -1, 0.25, jnp.where(exponent < 0, 0.5, jnp.where(exponent < 1, 1.0, 2.0))
+        )
+        factor = jnp.sum(jnp.where(lane == kv_head, factor, 0.0), axis=1, keepdims=True)
         for block in range(blocks):
-            exponent = scale_ref[block, kv_head]
-            factor = jnp.where(
-                exponent < -1,
-                0.25,
-                jnp.where(exponent < 0, 0.5, jnp.where(exponent < 1, 1.0, 2.0)),
-            )
             rows = pl.ds(block * (span // blocks), span // blocks)
-            scaled = ref[rows, at].astype(jnp.float32) * factor
+            scaled = ref[rows, :].astype(jnp.float32) * factor[block : block + 1, :]
             packed_ref[rows, pl.ds(place * HEAD_SIZE, HEAD_SIZE)] = scaled.astype(jnp.bfloat16)
-    packed_ref[:, 2 * HEAD_SIZE : 2 * HEAD_SIZE + width] = query_ref[...]
-    tok = ids_ref.shape[1]
     number = lax.broadcasted_iota(jnp.int32, (128, tok), 0)
     dense = jnp.zeros((128, tok), jnp.float32)
     for k in range(TOP):
@@ -104,112 +128,123 @@
         jnp.bfloat16
     )
     packed_ref[2 * tok :, 2 * HEAD_SIZE + width :] = jnp.zeros((span - 2 * tok, 128), jnp.bfloat16)
-    cols = piece_refs[0].shape[1]
-    for offset, ref in enumerate(piece_refs):
-        col = pl.multiple_of(lax.bitwise_xor(my_ctx, offset) * cols, cols)
-        ref[...] = residual_ref[:, pl.ds(col, cols)]
-
-
-def deq_in_kernel(exp_ref, gate_scale_ref, up_scale_ref, gate_ref, up_ref, _, own_ref, give_ref):
-    step = pl.program_id(0)
+    for copy in copies[6:]:
+        copy.wait()
+
+
+def deq_in_kernel(ctx_count, exp_ref, gate_scale_hbm, up_scale_hbm, gate_hbm, up_hbm, _, own_ref, give_ref,
+                  gate_ref, up_ref, gate_scale_ref, up_scale_ref, sems):
     core = lax.bitwise_and(exp_ref[0], 1)
-    rows, cols = own_ref.shape[0], gate_ref.shape[2]
-    for half, (ref, scale_ref) in enumerate(((gate_ref, gate_scale_ref), (up_ref, up_scale_ref))):
-        for out_ref, side in ((give_ref, 1 - core), (own_ref, core)):
-            first = (2 * step + side) * (rows // WB)
-            for i in range(rows // WB):
-                row = pl.multiple_of(side * rows + i * WB, WB)
-                for j in range(cols // WB):
-                    factor = block_factor(scale_ref[j, 0, first + i], WB)
-                    out_ref[pl.ds(i * WB, WB), pl.ds(half * cols + j * WB, WB)] = (
-                        ref[0, pl.ds(row, WB), pl.ds(j * WB, WB)] * factor
-                    )
+    width, cols = gate_ref.shape
+    rows = width // (2 * ctx_count)
+    pairs = [(gate_scale_hbm, gate_scale_ref), (up_scale_hbm, up_scale_ref)]
+    for step in range(ctx_count):
+        at = pl.ds(step * 2 * rows, 2 * rows)
+        pairs += [(gate_hbm.at[0, at], gate_ref.at[at]), (up_hbm.at[0, at], up_ref.at[at])]
+    copies = copy_all(sems, pairs)
+    for copy in copies[:2]:
+        copy.wait()
+    for step in range(ctx_count):
+        for half, (ref, scale_ref) in enumerate(((gate_ref, gate_scale_ref), (up_ref, up_scale_ref))):
+            copies[2 + 2 * step + half].wait()
+            for out_ref, side in ((give_ref, 1 - core), (own_ref, core)):
+                first = (2 * step + side) * (rows // WB)
+                for i in range(rows // WB):
+                    row = pl.multiple_of((2 * step + side) * rows + i * WB, WB)
+                    for j in range(cols // WB):
+                        factor = block_factor(scale_ref[j, 0, first + i], WB)
+                        out_ref[pl.ds(step * rows + i * WB, WB), pl.ds(half * cols + j * WB, WB)] = (
+                            ref[pl.ds(row, WB), pl.ds(j * WB, WB)] * factor
+                        )
 
 
 def deq_in(my_exp, gate_weight, gate_scale, up_weight, up_scale, ctx_count, after):
     width, hidden = gate_weight.shape[1:]
-    rows = width // (2 * ctx_count)
-    spec = pl.BlockSpec((1, 2 * rows, hidden), lambda i, e, gs, us: (0, i, 0))
-    out_spec = pl.BlockSpec((rows, 2 * hidden), lambda i, e, gs, us: (i, 0))
     shape = jax.ShapeDtypeStruct((width // 2, 2 * hidden), jnp.bfloat16)
+    gate_scale = jnp.transpose(gate_scale, (2, 0, 1))
+    up_scale = jnp.transpose(up_scale, (2, 0, 1))
     return pl.pallas_call(
-        deq_in_kernel,
-        grid_spec=pltpu.PrefetchScalarGridSpec(
-            num_scalar_prefetch=3,
-            grid=(ctx_count,),
-            in_specs=[spec, spec, pl.BlockSpec(memory_space=pl.ANY)],
-            out_specs=[out_spec, out_spec],
-        ),
+        functools.partial(deq_in_kernel, ctx_count),
+        in_specs=[pl.BlockSpec(memory_space=pltpu.SMEM)]
+        + [pl.BlockSpec(memory_space=pltpu.HBM)] * 4
+        + [pl.BlockSpec(memory_space=pl.ANY)],
+        out_specs=[pl.BlockSpec(memory_space=pltpu.VMEM)] * 2,
         out_shape=[shape, shape],
-        compiler_params=pltpu.CompilerParams(vmem_limit_bytes=16 * MIB),
+        scratch_shapes=[
+            pltpu.VMEM((width, hidden), jnp.bfloat16),
+            pltpu.VMEM((width, hidden), jnp.bfloat16),
+            pltpu.SMEM(gate_scale.shape, jnp.int32),
+            pltpu.SMEM(up_scale.shape, jnp.int32),
+            pltpu.SemaphoreType.DMA((2 + 2 * ctx_count,)),
+        ],
+        compiler_params=pltpu.CompilerParams(vmem_limit_bytes=20 * MIB),
         cost_estimate=pl.CostEstimate(
             flops=2 * width * hidden, bytes_accessed=8 * width * hidden, transcendentals=0
         ),
         name="dequant_in",
-    )(
-        my_exp,
-        jnp.transpose(gate_scale, (2, 0, 1)),
-        jnp.transpose(up_scale, (2, 0, 1)),
-        gate_weight,
-        up_weight,
-        after,
-    )
-
-
-def deq_down_kernel(exp_ref, scale_ref, down_ref, _, own_ref, give_ref):
-    step = pl.program_id(0)
+    )(my_exp, gate_scale, up_scale, gate_weight, up_weight, after)
+
+
+def deq_down_kernel(ctx_count, exp_ref, scale_hbm, down_hbm, _, own_ref, give_ref, down_ref, scale_ref, sems):
     core = lax.bitwise_and(exp_ref[0], 1)
-    rows, cols = own_ref.shape
-    for out_ref, side in ((give_ref, 1 - core), (own_ref, core)):
-        first = (2 * step + side) * (cols // WB)
-        for j in range(cols // WB):
-            col = pl.multiple_of(side * cols + j * WB, WB)
-            for i in range(rows // WB):
-                factor = block_factor(scale_ref[i, 0, first + j], WB)
-                out_ref[pl.ds(i * WB, WB), pl.ds(j * WB, WB)] = (
-                    down_ref[0, pl.ds(i * WB, WB), pl.ds(col, WB)] * factor
-                )
+    rows, width = down_ref.shape
+    cols = width // (2 * ctx_count)
+    pairs = [(scale_hbm, scale_ref)]
+    for step in range(ctx_count):
+        at = pl.ds(step * 2 * cols, 2 * cols)
+        pairs.append((down_hbm.at[0, :, at], down_ref.at[:, at]))
+    copies = copy_all(sems, pairs)
+    copies[0].wait()
+    for step in range(ctx_count):
+        copies[1 + step].wait()
+        for out_ref, side in ((give_ref, 1 - core), (own_ref, core)):
+            first = (2 * step + side) * (cols // WB)
+            for j in range(cols // WB):
+                col = pl.multiple_of((2 * step + side) * cols + j * WB, WB)
+                for i in range(rows // WB):
+                    factor = block_factor(scale_ref[i, 0, first + j], WB)
+                    out_ref[pl.ds(i * WB, WB), pl.ds(step * cols + j * WB, WB)] = (
+                        down_ref[pl.ds(i * WB, WB), pl.ds(col, WB)] * factor
+                    )
 
 
 def deq_down(my_exp, down_weight, down_scale, ctx_count, after):
     hidden, width = down_weight.shape[1:]
-    cols = width // (2 * ctx_count)
-    out_spec = pl.BlockSpec((hidden, cols), lambda i, e, ds: (0, i))
     shape = jax.ShapeDtypeStruct((hidden, width // 2), jnp.bfloat16)
+    down_scale = jnp.transpose(down_scale, (1, 0, 2))
     return pl.pallas_call(
-        deq_down_kernel,
-        grid_spec=pltpu.PrefetchScalarGridSpec(
-            num_scalar_prefetch=2,
-            grid=(ctx_count,),
-            in_specs=[
-                pl.BlockSpec((1, hidden, 2 * cols), lambda i, e, ds: (0, 0, i)),
-                pl.BlockSpec(memory_space=pl.ANY),
-            ],
-            out_specs=[out_spec, out_spec],
-        ),
+        functools.partial(deq_down_kernel, ctx_count),
+        in_specs=[pl.BlockSpec(memory_space=pltpu.SMEM)]
+        + [pl.BlockSpec(memory_space=pltpu.HBM)] * 2
+        + [pl.BlockSpec(memory_space=pl.ANY)],
+        out_specs=[pl.BlockSpec(memory_space=pltpu.VMEM)] * 2,
         out_shape=[shape, shape],
-        compiler_params=pltpu.CompilerParams(vmem_limit_bytes=16 * MIB),
+        scratch_shapes=[
+            pltpu.VMEM((hidden, width), jnp.bfloat16),
+            pltpu.SMEM(down_scale.shape, jnp.int32),
+            pltpu.SemaphoreType.DMA((1 + ctx_count,)),
+        ],
+        compiler_params=pltpu.CompilerParams(vmem_limit_bytes=12 * MIB),
         cost_estimate=pl.CostEstimate(
             flops=width * hidden, bytes_accessed=4 * width * hidden, transcendentals=0
         ),
         name="dequant_down",
-    )(my_exp, jnp.transpose(down_scale, (1, 0, 2)), down_weight, after)
+    )(my_exp, down_scale, down_weight, after)
 
 
 def attend_kernel(plan, ctx_ref, exp_ref, order_ref, *refs):
-    ctx_count, exp_count, tok, heads, x_off = plan
-    packed, pieces = refs[:ctx_count], refs[ctx_count : 2 * ctx_count]
-    weight_ref, _ = refs[2 * ctx_count : 2 * ctx_count + 2]
-    rest = refs[2 * ctx_count + 2 :]
-    out_refs, route_refs = rest[0:2], (rest[2:3] if x_off == 0 else rest[0:1]) + rest[1:2]
-    key_scr, value_scr, place_scr, att_scr = rest[-4:]
+    ctx_count, exp_count, tok, heads, piece_places = plan
+    packed, refs = refs[:ctx_count], refs[ctx_count:]
+    piece_refs, refs = refs[: 1 + bits_of(ctx_count)], refs[1 + bits_of(ctx_count) :]
+    weight_ref, rest = refs[0], refs[2:]
+    keep_ref, own_route_ref = rest[0:2]
+    give_refs = rest[2 : 1 + exp_count]
+    key_scr, value_scr, place_scr, att_scr = rest[1 + exp_count :]
     x_count = exp_count // 2
     span = packed[0].shape[0]
     positions = ctx_count * span
-    per_ctx = 2 * tok
     my_ctx, my_exp = ctx_ref[0], exp_ref[0]
     my_x, my_core = lax.shift_right_logical(my_exp, 1), lax.bitwise_and(my_exp, 1)
-    start = pl.multiple_of(lax.bitwise_xor(my_x, x_off) * per_ctx, per_ctx)
     lane = lax.broadcasted_iota(jnp.int32, (8, positions), 1)
     places = lane % span
     for offset, ref in enumerate(packed):
@@ -222,62 +257,62 @@
     for offset, ref in enumerate(packed):
         source = lax.bitwise_xor(my_ctx, offset)
         queries = jnp.concatenate(
-            [
-                ref[pl.ds(start, per_ctx), (h + 2) * HEAD_SIZE : (h + 3) * HEAD_SIZE]
-                for h in range(heads)
-            ],
-            axis=0,
+            [ref[:, (h + 2) * HEAD_SIZE : (h + 3) * HEAD_SIZE] for h in range(heads)], axis=0
         )
         scores = lax.dot_general(
             queries, key_scr[...], (((1,), (1,)), ((), ())), preferred_element_type=jnp.float32
         )
-        own_place = (
-            order_ref[source] * span + start + lax.broadcasted_iota(jnp.int32, (per_ctx, positions), 0)
-        )
+        own_place = order_ref[source] * span + lax.broadcasted_iota(jnp.int32, (span, positions), 0)
         bias = jnp.where(place_scr[0:1, :] <= own_place, 0.0, -1e30)
-        scores = scores.reshape(heads, per_ctx, positions) * scale + bias[None]
+        scores = scores.reshape(heads, span, positions) * scale + bias[None]
         largest = jnp.max(scores, axis=-1, keepdims=True)
         exps = jnp.exp(scores - largest)
         total = jnp.sum(exps, axis=-1, keepdims=True)
         mixed = jnp.dot(
-            exps.astype(jnp.bfloat16).reshape(heads * per_ctx, positions),
+            exps.astype(jnp.bfloat16).reshape(heads * span, positions),
             value_scr[...],
             preferred_element_type=jnp.float32,
-        ).reshape(heads, per_ctx, HEAD_SIZE)
+        ).reshape(heads, span, HEAD_SIZE)
         mixed = (mixed / total).astype(jnp.bfloat16)
-        at = pl.ds(pl.multiple_of(source * per_ctx, per_ctx), per_ctx)
-        for head in range(heads):
-            att_scr[at, pl.ds(head * HEAD_SIZE, HEAD_SIZE)] = mixed[head]
+        for owner in range(exp_count):
+            x_off = lax.bitwise_xor(my_x, owner // 2)
+            row = pl.multiple_of(((x_off * ctx_count + source) * 2 + owner % 2) * tok, tok)
+            for head in range(heads):
+                att_scr[pl.ds(row, tok), pl.ds(head * HEAD_SIZE, HEAD_SIZE)] = mixed[
+                    head, owner * tok : (owner + 1) * tok, :
+                ]
 
     cols = weight_ref.shape[1] // 2
-    per_x = ctx_count * per_ctx
+    per_x = 2 * ctx_count * tok
     first = (heads + 2) * HEAD_SIZE
     route_lane = lax.broadcasted_iota(jnp.int32, (tok, HEAD_SIZE), 1)
-    expert = my_ctx * x_count + lax.bitwise_xor(my_x, x_off)
-    sides = [jnp.zeros((tok, HEAD_SIZE), jnp.float32)] * 2
-    for offset, ref in enumerate(packed):
-        for part_of in range(2):
-            block = ref[part_of * tok : (part_of + 1) * tok, first:].astype(jnp.float32)
-            column = jnp.sum(jnp.where(route_lane == expert, block, 0.0), axis=1, keepdims=True)
-            sides[part_of] = sides[part_of] + jnp.where(
-                route_lane == lax.bitwise_xor(my_ctx, offset), column, 0.0
-            )
-    for which, out_ref in enumerate(out_refs):
-        side = lax.bitwise_xor(my_core, which)
+    for which in range(exp_count - 1, -1, -1):
+        side = lax.bitwise_xor(my_core, which % 2)
         weight = weight_ref[:, pl.ds(pl.multiple_of(side * cols, cols), cols)]
-        part = jnp.dot(att_scr[...], weight, preferred_element_type=jnp.float32)
+        part = jnp.dot(
+            att_scr[pl.ds(which // 2 * per_x, per_x), :], weight, preferred_element_type=jnp.float32
+        )
+        out_ref = give_refs[which - 1] if which else keep_ref
         out_ref[0:per_x, :] = part.astype(out_ref.dtype)
-        if x_off == 0:
-            for offset, ref in enumerate(pieces):
+        if which < 2:
+            for offset, (array, place) in enumerate(piece_places):
                 row = (lax.bitwise_xor(my_ctx, offset) * 2 + my_core) * tok
                 at = pl.ds(pl.multiple_of(row, tok), tok)
-                piece = ref[:, pl.ds(pl.multiple_of(side * cols, cols), cols)].astype(jnp.float32)
+                piece = piece_refs[array][place, :, pl.ds(pl.multiple_of(side * cols, cols), cols)].astype(jnp.float32)
                 out_ref[at, :] = (out_ref[at, :].astype(jnp.float32) + piece).astype(out_ref.dtype)
-        route_out = route_refs[which]
-        row = route_out.shape[0] - 2 * tok
-        for part_of, values in enumerate(sides):
+        expert = my_ctx * x_count + lax.bitwise_xor(my_x, which // 2)
+        sides = [jnp.zeros((tok, HEAD_SIZE), jnp.float32)] * 2
+        for offset, ref in enumerate(packed):
+            for part_of in range(2):
+                block = ref[part_of * tok : (part_of + 1) * tok, first:].astype(jnp.float32)
+                column = jnp.sum(jnp.where(route_lane == expert, block, 0.0), axis=1, keepdims=True)
+                sides[part_of] = sides[part_of] + jnp.where(
+                    route_lane == lax.bitwise_xor(my_ctx, offset), column, 0.0
+                )
+        route_out, row = (give_refs[which - 1], per_x) if which else (own_route_ref, 0)
+        for part_of, side in enumerate(sides):
             at = pl.ds(row + part_of * tok, tok)
-            route_out[at, 0:HEAD_SIZE] = values.astype(jnp.bfloat16)
+            route_out[at, 0:HEAD_SIZE] = side.astype(jnp.bfloat16)
             if route_out.shape[1] > HEAD_SIZE:
                 rest_shape = (tok, route_out.shape[1] - HEAD_SIZE)
                 route_out[at, HEAD_SIZE:] = jnp.zeros(rest_shape, jnp.bfloat16)
@@ -446,12 +481,26 @@
     my_exp = lax.axis_index("exp").astype(jnp.int32).reshape(1)
     route = gather_route(ctx_count, x_count)
 
-    packed, *pieces = pl.pallas_call(
-        functools.partial(pack_kernel, (heads, group, experts)),
-        in_specs=[smem] * 4 + [vmem] * 6,
-        out_specs=[vmem] * (1 + ctx_count),
-        out_shape=[jax.ShapeDtypeStruct((span, query_width + 3 * HEAD_SIZE), bf16)]
-        + [jax.ShapeDtypeStruct((tok, 2 * cols), bf16)] * ctx_count,
+    hbm = pl.BlockSpec(memory_space=pltpu.HBM)
+    piece_shape = jax.ShapeDtypeStruct((ctx_count // 2, tok, 2 * cols), bf16)
+    packed, near, far = pl.pallas_call(
+        functools.partial(pack_kernel, (heads, group)),
+        in_specs=[smem] * 2 + [hbm] * 8,
+        out_specs=[vmem] * 3,
+        out_shape=[
+            jax.ShapeDtypeStruct((span, query_width + 3 * HEAD_SIZE), bf16),
+            piece_shape,
+            piece_shape,
+        ],
+        scratch_shapes=[
+            pltpu.VMEM(key_block_exponent.shape, jnp.int32),
+            pltpu.VMEM(key_block_exponent.shape, jnp.int32),
+            pltpu.VMEM((span, HEAD_SIZE), bf16),
+            pltpu.VMEM((span, HEAD_SIZE), bf16),
+            pltpu.VMEM((TOP, tok), jnp.int32),
+            pltpu.VMEM((TOP, tok), f32),
+            pltpu.SemaphoreType.DMA((7 + ctx_count,)),
+        ],
         compiler_params=pltpu.CompilerParams(vmem_limit_bytes=8 * MIB),
         name="pack",
     )(
@@ -467,9 +516,14 @@
         residual,
     )
     held = {(0, 0): packed}
+    piece_arrays = [near]
+    piece_at = {(0, offset): (0, offset) for offset in range(ctx_count // 2)}
+    sending, send_keys = far, [(0, offset) for offset in range(ctx_count // 2, ctx_count)]
     stages = stages_of(gather_route(ctx_count, x_count, rows_only=True))
     for number, stage in enumerate(stages):
         came = [from_partner(held[source], axis, bit) for _, source, _, axis, bit in stage]
+        piece_bit = bits_of(ctx_count) - 1 - number
+        came.append(from_ctx(sending, 1 << piece_bit))
         if number == 0:
             in_own, in_give = deq_in(
                 my_exp, gate_weight, gate_scale, up_weight, up_scale, ctx_count, packed
@@ -477,47 +531,49 @@
             *came, in_own, in_give = together(*came, in_own, in_give)
         elif number == 1:
             in_other = from_offset(in_give, 1)
-            pieces = [pieces[0]] + [from_ctx(pieces[offset], offset) for offset in range(1, ctx_count)]
             down_own, down_give = deq_down(my_exp, down_weight, down_scale, ctx_count, came_first)
-            *came, down_own, down_give = together(*came, down_own, down_give)
+            *came, in_other, down_own, down_give = together(*came, in_other, down_own, down_give)
+        elif number < len(stages) - 1:
+            came = together(*came)
         came_first = came[0]
         held.update({target: array for (_, _, target, _, _), array in zip(stage, came)})
+        piece_arrays.append(came[-1])
+        for place, (source, target) in enumerate(send_keys):
+            piece_at[source ^ 1 << piece_bit, target ^ 1 << piece_bit] = (number + 1, place)
+        if piece_bit:
+            send_keys = sorted(key for key in piece_at if key[1] == key[1] & ((2 << piece_bit - 1) - 1) and key[1] >> piece_bit - 1 & 1)
+            sending = jnp.stack([piece_arrays[array][place] for array, place in map(piece_at.get, send_keys)])
     packed = [held[offset, 0] for offset in range(ctx_count)]
+    piece_places = tuple(piece_at[offset, 0] for offset in range(ctx_count))
     down_other = from_offset(down_give, 1)
 
     positions = ctx_count * span
     per_x = 2 * ctx_count * tok
-    gives, after = {}, out_weight
-    for x_off in reversed(range(x_count)):
-        give_shape = jax.ShapeDtypeStruct((per_x + 2 * tok, cols), bf16)
-        first_shape = jax.ShapeDtypeStruct((per_x, cols), f32) if x_off == 0 else give_shape
-        route_shape = [jax.ShapeDtypeStruct((2 * tok, HEAD_SIZE), bf16)] if x_off == 0 else []
-        outs = pl.pallas_call(
-            functools.partial(attend_kernel, (ctx_count, exp_count, tok, heads, x_off)),
-            in_specs=[smem] * 3 + [vmem] * (2 * ctx_count + 1) + [anywhere],
-            out_specs=[vmem] * (2 + len(route_shape)),
-            out_shape=[first_shape, give_shape] + route_shape,
-            scratch_shapes=[
-                pltpu.VMEM((positions, HEAD_SIZE), bf16),
-                pltpu.VMEM((positions, HEAD_SIZE), bf16),
-                pltpu.VMEM((8, positions), jnp.int32),
-                pltpu.VMEM((per_x, query_width), bf16),
-            ],
-            compiler_params=pltpu.CompilerParams(vmem_limit_bytes=2 * ctx_count * MIB),
-            cost_estimate=pl.CostEstimate(
-                flops=(4 * positions * positions + 4 * positions * cols) * query_width // x_count,
-                bytes_accessed=4 * MIB,
-                transcendentals=heads * positions * positions // x_count,
-            ),
-            name="attend",
-        )(my_ctx, my_exp, block_order, *packed, *pieces, out_weight, after)
-        gives[2 * x_off + 1] = from_offset(outs[1], 2 * x_off + 1)
-        if x_off:
-            gives[2 * x_off] = from_offset(outs[0], 2 * x_off)
-            after = outs[0]
-        else:
-            keep, own_route = outs[0], outs[2]
-
+    keep, own_route, *gives = pl.pallas_call(
+        functools.partial(attend_kernel, (ctx_count, exp_count, tok, heads, piece_places)),
+        in_specs=[smem] * 3 + [vmem] * (ctx_count + len(piece_arrays) + 1) + [anywhere],
+        out_specs=[vmem] * (1 + exp_count),
+        out_shape=[
+            jax.ShapeDtypeStruct((per_x, cols), f32),
+            jax.ShapeDtypeStruct((2 * tok, HEAD_SIZE), bf16),
+        ]
+        + [jax.ShapeDtypeStruct((per_x + 2 * tok, cols), bf16)] * (exp_count - 1),
+        scratch_shapes=[
+            pltpu.VMEM((positions, HEAD_SIZE), bf16),
+            pltpu.VMEM((positions, HEAD_SIZE), bf16),
+            pltpu.VMEM((8, positions), jnp.int32),
+            pltpu.VMEM((positions, query_width), bf16),
+        ],
+        compiler_params=pltpu.CompilerParams(vmem_limit_bytes=3 * ctx_count * MIB),
+        cost_estimate=pl.CostEstimate(
+            flops=4 * positions * positions * query_width + 4 * positions * query_width * cols,
+            bytes_accessed=8 * MIB,
+            transcendentals=heads * positions * positions,
+        ),
+        name="attend",
+    )(my_ctx, my_exp, block_order, *packed, *piece_arrays, out_weight, down_other)
+
+    gives = {offset: from_offset(gives[offset - 1], offset) for offset in reversed(range(1, exp_count))}
     gives = [gives[offset] for offset in range(1, exp_count)]
     state = keep
     for give in gives:

time: 138 us -> 129 us (0.935)
  waiting for transfers between devices: 51.4 us -> 46.6 us
  starting transfers between devices: 53.6 us -> 50.1 us
    ppermute x37, waiting for transfers between devices: 37.2 us -> 28.9 us  [from_partner(): lax.ppermute(array, axis, [(i, i ^ 1 << bit) for i in range(lax.axis_size...]
    ppermute x7 -> x3, starting transfers between devices: 8.58 us -> 3.77 us  [from_ctx(): lax.ppermute(array, 'ctx', [(i, i ^ offset) for i in range(lax.axis_size(...]
    pallas_call x2 -> x1, Pallas kernels: 7.23 us -> 4.56 us  [shards(): pl.pallas_call(functools.partial(attend_kernel, (ctx_count, exp_count, to...]
    ppermute x8, waiting for transfers between devices: 6.86 us -> 8.98 us  [from_offset(): lax.ppermute(array, 'exp', [(i, i ^ offset) for i in range(lax.axis_size(...]
    pallas_call x3, Pallas kernels: 4.51 us -> 6.41 us  [the longest x1 4.43 us: deq_in(): pl.pallas_call(functools.partial(deq_in_kernel, ctx_count), in_specs=[pl....]
    ppermute x37, starting transfers between devices: 42 us -> 43.6 us  [from_partner(): lax.ppermute(array, axis, [(i, i ^ 1 << bit) for i in range(lax.axis_size...]
    ppermute x7 -> x3, waiting for transfers between devices: 7.4 us -> 8.72 us  [from_ctx(): lax.ppermute(array, 'ctx', [(i, i ^ offset) for i in range(lax.axis_size(...]
  transfers between devices with their start and end apart: 52 -> 48, of which waited for: 32 -> 25; matrix products, arithmetic and copies ran while one was open for 0% -> 0% of each run, Pallas kernels for 14% -> 10%
where the time goes in v2:
time: 129 us
  starting transfers between devices  50.1 us (39%)
  waiting for transfers between devices  46.6 us (36%)
  Pallas kernels  19 us (15%)
  local copies, waits for them, and re-layouts  12.2 us (9%)
    ppermute x37, starting transfers between devices, from_partner(): lax.ppermute(array, axis, [(i, i ^ 1 << bit) for i in range(lax.axis_size...  43.6 us
    ppermute x37, waiting for transfers between devices, from_partner(): lax.ppermute(array, axis, [(i, i ^ 1 << bit) for i in range(lax.axis_size...  28.9 us
    unnamed x36, local copies, waits for them, and re-layouts  11.4 us
    ppermute x8, waiting for transfers between devices, from_offset(): lax.ppermute(array, 'exp', [(i, i ^ offset) for i in range(lax.axis_size(...  8.98 us
    ppermute x3, waiting for transfers between devices, from_ctx(): lax.ppermute(array, 'ctx', [(i, i ^ offset) for i in range(lax.axis_size(...  8.72 us
    pallas_call x1, Pallas kernels, shards(): pl.pallas_call(functools.partial(attend_kernel, (ctx_count, exp_count, to...  4.56 us
    pallas_call x1, Pallas kernels, deq_in(): pl.pallas_call(functools.partial(deq_in_kernel, ctx_count), in_specs=[pl....  4.43 us
    ppermute x3, starting transfers between devices, from_ctx(): lax.ppermute(array, 'ctx', [(i, i ^ offset) for i in range(lax.axis_size(...  3.77 us
  transfers between devices with their start and end apart: 48, of which 25 were waited for; matrix products, arithmetic and copies ran while one was open for 0% of the time, Pallas kernels for 10%

profile of v2, /device:TPU:0, one launch (start us, length us, event | category | flops | bytes accessed | tf_op | source)
XLA Modules:
  0.0 128.7 jit_solution(15261181476163995090)
XLA Ops:
  6.6 4.1 %collective-permute-start = (bf16[64,1408]{1,0:T(8,128)(2,1)S(1)}, bf16[64,1408]{1,0:T(8,128)(2,1)S(1)}, u32[]{:S(2)}, u32[]{:S(2)}) collective-permute-start(bf16[64,1408]{1,0:T(8,128)(2,1)S(1)} %get-tuple-element.80._.refs_0_), channel_id=1, source_target_pairs={{0,16},{4,20},{8,24},{12,28},{16,0},{20,4},{24,8},{28,12},{1,17},{... | collective-permute-start | bytes 540680 | tf_op jit(solution)/shard_map/ppermute | solution.py:21
  10.7 1.6 %collective-permute-start.1 = (bf16[64,1408]{1,0:T(8,128)(2,1)S(1)}, bf16[64,1408]{1,0:T(8,128)(2,1)S(1)}, u32[]{:S(2)}, u32[]{:S(2)}) collective-permute-start(bf16[64,1408]{1,0:T(8,128)(2,1)S(1)} %get-tuple-element.80._.refs_0_), channel_id=1, source_target_pairs={{0,8},{4,12},{8,0},{12,4},{16,24},{20,28},{24,16},{28,20},{1,9},{5... | collective-permute-start | bytes 540680 | tf_op jit(solution)/shard_map/ppermute | solution.py:21
  12.3 1.5 %collective-permute-start.2 = (bf16[64,1408]{1,0:T(8,128)(2,1)S(1)}, bf16[64,1408]{1,0:T(8,128)(2,1)S(1)}, u32[]{:S(2)}, u32[]{:S(2)}) collective-permute-start(bf16[64,1408]{1,0:T(8,128)(2,1)S(1)} %get-tuple-element.80._.refs_0_), channel_id=1, source_target_pairs={{0,4},{4,0},{8,12},{12,8},{16,20},{20,16},{24,28},{28,24},{1,5},{5... | collective-permute-start | bytes 540680 | tf_op jit(solution)/shard_map/ppermute | solution.py:21
  14.1 1.9 %copy-done.1 = bf16[1,4096,384]{2,1,0:T(8,128)(2,1)S(1)} copy-done((bf16[1,4096,384]{2,1,0:T(8,128)(2,1)S(1)}, bf16[1,4096,384]{2,1,0:T(8,128)(2,1)}, u32[]{:S(2)}) %copy-start.1) | copy-done | bytes 3145752
  16.0 1.9 %copy-done.2 = bf16[1,4096,384]{2,1,0:T(8,128)(2,1)S(1)} copy-done((bf16[1,4096,384]{2,1,0:T(8,128)(2,1)S(1)}, bf16[1,4096,384]{2,1,0:T(8,128)(2,1)}, u32[]{:S(2)}) %copy-start.2) | copy-done | bytes 3145752
  19.3 4.4 %dequant_in.1 = (bf16[2048,768]{1,0:T(8,128)(2,1)S(1)}, bf16[2048,768]{1,0:T(8,128)(2,1)S(1)}) custom-call(s32[1]{0:T(128)} %bitcast.1.exp_ref, s32[3,1,32]{2,1,0:T(1,128)S(1)} %bitcast.21, s32[3,1,32]{2,1,0:T(1,128)S(1)} %bitcast.22, bf16[1,4096,384]{2,1,0:T(8,128)(2,1)S(1)} %copy-done.1, bf16[1,4096,384]{2,1,0:T(8,128)(2,1)S(1)} %copy-done.2, ...), custom_call_target="tpu_custom_call" | custom-call | flops 3145728 | bytes 12582912 | tf_op jit(solution)/shard_map/dequant_in/pallas_call | solution.py:166
  24.6 1.8 %collective-permute-start.5 = (bf16[64,1408]{1,0:T(8,128)(2,1)S(1)}, bf16[64,1408]{1,0:T(8,128)(2,1)S(1)}, u32[]{:S(2)}, u32[]{:S(2)}) collective-permute-start(bf16[64,1408]{1,0:T(8,128)(2,1)S(1)} %collective-permute-done.1.refs_2_), channel_id=1, source_target_pairs={{0,4},{4,0},{8,12},{12,8},{16,20},{20,16},{24,28},{28,24},{1,5},{5... | collective-permute-start | bytes 540680 | tf_op jit(solution)/shard_map/ppermute | solution.py:21
  26.4 1.7 %collective-permute-start.7 = (bf16[4,16,512]{2,1,0:T(8,128)(2,1)S(1)}, bf16[4,16,512]{2,1,0:T(8,128)(2,1)S(1)}, u32[]{:S(2)}, u32[]{:S(2)}) collective-permute-start(bf16[4,16,512]{2,1,0:T(8,128)(2,1)S(1)} %pad_maximum_fusion), channel_id=1, source_target_pairs={{0,8},{4,12},{8,0},{12,4},{16,24},{20,28},{24,16},{28,20},{1,9},{5... | collective-permute-start | bytes 196616 | tf_op jit(solution)/shard_map/ppermute | solution.py:33
  28.1 1.6 %dequant_down.1 = (bf16[384,2048]{1,0:T(8,128)(2,1)S(1)}, bf16[384,2048]{1,0:T(8,128)(2,1)S(1)}) custom-call(s32[1]{0:T(128)} %bitcast.1.exp_ref, s32[3,1,32]{2,1,0:T(1,128)S(1)} %bitcast.23, bf16[1,384,4096]{2,1,0:T(8,128)(2,1)S(1)} %copy-done, bf16[64,1408]{1,0:T(8,128)(2,1)S(1)} %collective-permute-done._.refs_4_), custom_call_target="tpu_custom_call" | custom-call | flops 1572864 | bytes 6291456 | tf_op jit(solution)/shard_map/dequant_down/pallas_call | solution.py:215
  29.7 2.5 %collective-permute-done.7.refs_10_ = bf16[4,16,512]{2,1,0:T(8,128)(2,1)S(1)} collective-permute-done((bf16[4,16,512]{2,1,0:T(8,128)(2,1)S(1)}, bf16[4,16,512]{2,1,0:T(8,128)(2,1)S(1)}, u32[]{:S(2)}, u32[]{:S(2)}) %collective-permute-start.7) | collective-permute-done | bytes 65568 | tf_op jit(solution)/shard_map/ppermute | solution.py:33
  32.2 2.6 %collective-permute-done.5.refs_3_ = bf16[64,1408]{1,0:T(8,128)(2,1)S(1)} collective-permute-done((bf16[64,1408]{1,0:T(8,128)(2,1)S(1)}, bf16[64,1408]{1,0:T(8,128)(2,1)S(1)}, u32[]{:S(2)}, u32[]{:S(2)}) %collective-permute-start.5) | collective-permute-done | bytes 180256 | tf_op jit(solution)/shard_map/ppermute | solution.py:21
  35.3 1.8 %collective-permute-start.10 = (bf16[4,16,512]{2,1,0:T(8,128)(2,1)S(1)}, bf16[4,16,512]{2,1,0:T(8,128)(2,1)S(1)}, u32[]{:S(2)}, u32[]{:S(2)}) collective-permute-start(bf16[4,16,512]{2,1,0:T(8,128)(2,1)S(1)} %pad_maximum_fusion.1), channel_id=1, source_target_pairs={{0,4},{4,0},{8,12},{12,8},{16,20},{20,16},{24,28},{28,24},{1,5},{5... | collective-permute-start | bytes 196616 | tf_op jit(solution)/shard_map/ppermute | solution.py:33
  37.1 6.2 %collective-permute-done.10.refs_11_ = bf16[4,16,512]{2,1,0:T(8,128)(2,1)S(1)} collective-permute-done((bf16[4,16,512]{2,1,0:T(8,128)(2,1)S(1)}, bf16[4,16,512]{2,1,0:T(8,128)(2,1)S(1)}, u32[]{:S(2)}, u32[]{:S(2)}) %collective-permute-start.10) | collective-permute-done | bytes 65568 | tf_op jit(solution)/shard_map/ppermute | solution.py:33
  43.3 4.6 %attend.1 = (f32[256,256]{1,0:T(8,128)S(1)}, bf16[32,128]{1,0:T(8,128)(2,1)S(1)}, bf16[288,256]{1,0:T(8,128)(2,1)S(1)}, bf16[288,256]{1,0:T(8,128)(2,1)S(1)}, bf16[288,256]{1,0:T(8,128)(2,1)S(1)}) custom-call(s32[1]{0:T(128)} %bitcast.ctx_ref, s32[1]{0:T(128)} %bitcast.1.exp_ref, s32[8]{0:T(128)S(1)} %copy-done.16, ...), custom_call_target="tpu_custom_call" | custom-call | flops 1610612736 | bytes 8388608 | tf_op jit(solution)/shard_map/attend/pallas_call | solution.py:552
  47.9 1.6 %collective-permute-start.13 = (bf16[288,256]{1,0:T(8,128)(2,1)S(1)}, bf16[288,256]{1,0:T(8,128)(2,1)S(1)}, u32[]{:S(2)}, u32[]{:S(2)}) collective-permute-start(bf16[288,256]{1,0:T(8,128)(2,1)S(1)} %get-tuple-element.99), channel_id=1, source_target_pairs={{0,2},{1,3},{2,0},{3,1},{4,6},{5,7},{6,4},{7,5},{8,10},{9,11},{10,... | collective-permute-start | bytes 442376 | tf_op jit(solution)/shard_map/ppermute | solution.py:29
  49.8 4.8 %collective-permute-done.13.refs_2_ = bf16[288,256]{1,0:T(8,128)(2,1)S(1)} collective-permute-done((bf16[288,256]{1,0:T(8,128)(2,1)S(1)}, bf16[288,256]{1,0:T(8,128)(2,1)S(1)}, u32[]{:S(2)}, u32[]{:S(2)}) %collective-permute-start.13) | collective-permute-done | bytes 147488 | tf_op jit(solution)/shard_map/ppermute | solution.py:29
  54.6 2.3 %collective-permute-done.14.refs_3_ = bf16[288,256]{1,0:T(8,128)(2,1)S(1)} collective-permute-done((bf16[288,256]{1,0:T(8,128)(2,1)S(1)}, bf16[288,256]{1,0:T(8,128)(2,1)S(1)}, u32[]{:S(2)}, u32[]{:S(2)}) %collective-permute-start.14) | collective-permute-done | bytes 147488 | tf_op jit(solution)/shard_map/ppermute | solution.py:29
  56.9 2.7 %collective-permute-start.15 = (bf16[256,256]{1,0:T(8,128)(2,1)S(1)}, bf16[256,256]{1,0:T(8,128)(2,1)S(1)}, u32[]{:S(2)}, u32[]{:S(2)}) collective-permute-start(bf16[256,256]{1,0:T(8,128)(2,1)S(1)} %add_convert_fusion.7.refs_0_.refs_7_), channel_id=1, source_target_pairs={{0,16},{4,20},{8,24},{12,28},{16,0},{20,4},{24,8},{28,12},{1,17},{... | collective-permute-start | bytes 393224 | tf_op jit(solution)/shard_map/ppermute | solution.py:21
  59.6 1.6 %collective-permute-start.16 = (bf16[256,256]{1,0:T(8,128)(2,1)S(1)}, bf16[256,256]{1,0:T(8,128)(2,1)S(1)}, u32[]{:S(2)}, u32[]{:S(2)}) collective-permute-start(bf16[256,256]{1,0:T(8,128)(2,1)S(1)} %add_convert_fusion.7.refs_0_.refs_7_), channel_id=1, source_target_pairs={{0,8},{4,12},{8,0},{12,4},{16,24},{20,28},{24,16},{28,20},{1,9},{5... | collective-permute-start | bytes 393224 | tf_op jit(solution)/shard_map/ppermute | solution.py:21
  61.7 1.5 %collective-permute-start.18 = (bf16[256,256]{1,0:T(8,128)(2,1)S(1)}, bf16[256,256]{1,0:T(8,128)(2,1)S(1)}, u32[]{:S(2)}, u32[]{:S(2)}) collective-permute-start(bf16[256,256]{1,0:T(8,128)(2,1)S(1)} %add_convert_fusion.7.refs_0_.refs_7_), channel_id=1, source_target_pairs={{0,2},{1,3},{2,0},{3,1},{4,6},{5,7},{6,4},{7,5},{8,10},{9,11},{10,... | collective-permute-start | bytes 393224 | tf_op jit(solution)/shard_map/ppermute | solution.py:21
  63.2 3.3 %collective-permute-done.15.refs_0_.refs_11_ = bf16[256,256]{1,0:T(8,128)(2,1)S(1)} collective-permute-done((bf16[256,256]{1,0:T(8,128)(2,1)S(1)}, bf16[256,256]{1,0:T(8,128)(2,1)S(1)}, u32[]{:S(2)}, u32[]{:S(2)}) %collective-permute-start.15) | collective-permute-done | bytes 131104 | tf_op jit(solution)/shard_map/ppermute | solution.py:21
  66.7 1.4 %collective-permute-start.19 = (bf16[256,256]{1,0:T(8,128)(2,1)S(1)}, bf16[256,256]{1,0:T(8,128)(2,1)S(1)}, u32[]{:S(2)}, u32[]{:S(2)}) collective-permute-start(bf16[256,256]{1,0:T(8,128)(2,1)S(1)} %collective-permute-done.15.refs_0_.refs_11_), channel_id=1, source_target_pairs={{0,8},{4,12},{8,0},{12,4},{16,24},{20,28},{24,16},{28,20},{1,9},{5... | collective-permute-start | bytes 393224 | tf_op jit(solution)/shard_map/ppermute | solution.py:21
  68.1 1.5 %collective-permute-start.20 = (bf16[256,256]{1,0:T(8,128)(2,1)S(1)}, bf16[256,256]{1,0:T(8,128)(2,1)S(1)}, u32[]{:S(2)}, u32[]{:S(2)}) collective-permute-start(bf16[256,256]{1,0:T(8,128)(2,1)S(1)} %collective-permute-done.16.refs_4_.refs_9_), channel_id=1, source_target_pairs={{0,2},{1,3},{2,0},{3,1},{4,6},{5,7},{6,4},{7,5},{8,10},{9,11},{10,... | collective-permute-start | bytes 393224 | tf_op jit(solution)/shard_map/ppermute | solution.py:21
  72.2 1.5 %collective-permute-start.25 = (bf16[256,256]{1,0:T(8,128)(2,1)S(1)}, bf16[256,256]{1,0:T(8,128)(2,1)S(1)}, u32[]{:S(2)}, u32[]{:S(2)}) collective-permute-start(bf16[256,256]{1,0:T(8,128)(2,1)S(1)} %collective-permute-done.17.refs_2_.refs_8_), channel_id=1, source_target_pairs={{0,2},{1,3},{2,0},{3,1},{4,6},{5,7},{6,4},{7,5},{8,10},{9,11},{10,... | collective-permute-start | bytes 393224 | tf_op jit(solution)/shard_map/ppermute | solution.py:21
  73.7 1.6 %collective-permute-done.21.refs_6_.refs_10_ = bf16[256,256]{1,0:T(8,128)(2,1)S(1)} collective-permute-done((bf16[256,256]{1,0:T(8,128)(2,1)S(1)}, bf16[256,256]{1,0:T(8,128)(2,1)S(1)}, u32[]{:S(2)}, u32[]{:S(2)}) %collective-permute-start.21) | collective-permute-done | bytes 131104 | tf_op jit(solution)/shard_map/ppermute | solution.py:21
  83.0 2.4 %collective-permute-done.28.refs_6_.refs_14_ = bf16[256,256]{1,0:T(8,128)(2,1)S(1)} collective-permute-done((bf16[256,256]{1,0:T(8,128)(2,1)S(1)}, bf16[256,256]{1,0:T(8,128)(2,1)S(1)}, u32[]{:S(2)}, u32[]{:S(2)}) %collective-permute-start.28) | collective-permute-done | bytes 131104 | tf_op jit(solution)/shard_map/ppermute | solution.py:21
  86.7 2.0 %experts_in_first.1 = (f32[512,1536]{1,0:T(8,128)S(1)}, f32[512,1]{1,0:T(8,128)S(1)}) custom-call(s32[1]{0:T(128)} %bitcast.ctx_ref, s32[1]{0:T(128)} %bitcast.1.exp_ref, bf16[256,256]{1,0:T(8,128)(2,1)S(1)} %add_convert_fusion.7.refs_0_.refs_7_, bf16[256,256]{1,0:T(8,128)(2,1)S(1)} %collective-permute-done.18.refs_1_, ...), custom_call_target="tpu_custom_call" | custom-call | flops 1610612736 | bytes 8388608 | tf_op jit(solution)/shard_map/experts_in_first/pallas_call | solution.py:594
  88.7 1.6 %collective-permute-done.29.refs_7_ = bf16[256,256]{1,0:T(8,128)(2,1)S(1)} collective-permute-done((bf16[256,256]{1,0:T(8,128)(2,1)S(1)}, bf16[256,256]{1,0:T(8,128)(2,1)S(1)}, u32[]{:S(2)}, u32[]{:S(2)}) %collective-permute-start.29) | collective-permute-done | bytes 131104 | tf_op jit(solution)/shard_map/ppermute | solution.py:21
  93.9 1.8 %experts_out.2 = (f32[32,2048]{1,0:T(8,128)S(1)}, bf16[32,2048]{1,0:T(8,128)(2,1)S(1)}, f32[32,2048]{1,0:T(8,128)S(1)}, bf16[32,2048]{1,0:T(8,128)(2,1)S(1)}, f3...) custom-call(s32[1]{0:T(128)} %bitcast.ctx_ref, ...), custom_call_target="tpu_custom_call" | custom-call | flops 805306368 | bytes 8388608 | tf_op jit(solution)/shard_map/experts_out/pallas_call | solution.py:640
  99.8 2.0 %experts_out.3 = (f32[32,2048]{1,0:T(8,128)S(1)}, bf16[32,2048]{1,0:T(8,128)(2,1)S(1)}, f32[32,2048]{1,0:T(8,128)S(1)}, bf16[32,2048]{1,0:T(8,128)(2,1)S(1)}, f3...) custom-call(s32[1]{0:T(128)} %bitcast.ctx_ref, ...), custom_call_target="tpu_custom_call" | custom-call | flops 805306368 | bytes 8388608 | tf_op jit(solution)/shard_map/experts_out/pallas_call | solution.py:640
  115.8 3.8 %collective-permute-done.38 = bf16[32,2048]{1,0:T(8,128)(2,1)S(1)} collective-permute-done((bf16[32,2048]{1,0:T(8,128)(2,1)S(1)}, bf16[32,2048]{1,0:T(8,128)(2,1)S(1)}, u32[]{:S(2)}, u32[]{:S(2)}) %collective-permute-start.38) | collective-permute-done | bytes 131104 | tf_op jit(solution)/shard_map/ppermute | solution.py:21
  120.8 5.5 %collective-permute-done.43 = bf16[32,2048]{1,0:T(8,128)(2,1)S(1)} collective-permute-done((bf16[32,2048]{1,0:T(8,128)(2,1)S(1)}, bf16[32,2048]{1,0:T(8,128)(2,1)S(1)}, u32[]{:S(2)}, u32[]{:S(2)}) %collective-permute-start.43) | collective-permute-done | bytes 131104 | tf_op jit(solution)/shard_map/ppermute | solution.py:21
  (129 shorter events, 47.4 us)
Async XLA Ops:
  6.6 17.2 %collective-permute-start = (bf16[64,1408]{1,0:T(8,128)(2,1)S(1)}, bf16[64,1408]{1,0:T(8,128)(2,1)S(1)}, u32[]{:S(2)}, u32[]{:S(2)}) collective-permute-start(bf16[64,1408]{1,0:T(8,128)(2,1)S(1)} %get-tuple-element.80._.refs_0_), channel_id=1, source_target_pairs={{0,16},{4,20},{8,24},{12,28},{16,0},{20,4},{24,8},{28,12},{1,17},{... | collective-permute-start | bytes 540680 | tf_op jit(solution)/shard_map/ppermute | solution.py:21
  10.7 13.1 %collective-permute-start.1 = (bf16[64,1408]{1,0:T(8,128)(2,1)S(1)}, bf16[64,1408]{1,0:T(8,128)(2,1)S(1)}, u32[]{:S(2)}, u32[]{:S(2)}) collective-permute-start(bf16[64,1408]{1,0:T(8,128)(2,1)S(1)} %get-tuple-element.80._.refs_0_), channel_id=1, source_target_pairs={{0,8},{4,12},{8,0},{12,4},{16,24},{20,28},{24,16},{28,20},{1,9},{5... | collective-permute-start | bytes 540680 | tf_op jit(solution)/shard_map/ppermute | solution.py:21
  12.3 11.5 %collective-permute-start.2 = (bf16[64,1408]{1,0:T(8,128)(2,1)S(1)}, bf16[64,1408]{1,0:T(8,128)(2,1)S(1)}, u32[]{:S(2)}, u32[]{:S(2)}) collective-permute-start(bf16[64,1408]{1,0:T(8,128)(2,1)S(1)} %get-tuple-element.80._.refs_0_), channel_id=1, source_target_pairs={{0,4},{4,0},{8,12},{12,8},{16,20},{20,16},{24,28},{28,24},{1,5},{5... | collective-permute-start | bytes 540680 | tf_op jit(solution)/shard_map/ppermute | solution.py:21
  13.8 10.0 %collective-permute-start.3 = (bf16[4,16,512]{2,1,0:T(8,128)(2,1)S(1)}, bf16[4,16,512]{2,1,0:T(8,128)(2,1)S(1)}, u32[]{:S(2)}, u32[]{:S(2)}) collective-permute-start(bf16[4,16,512]{2,1,0:T(8,128)(2,1)S(1)} %get-tuple-element.81), channel_id=1, source_target_pairs={{0,16},{4,20},{8,24},{12,28},{16,0},{20,4},{24,8},{28,12},{1,17},{... | collective-permute-start | bytes 196616 | tf_op jit(solution)/shard_map/ppermute | solution.py:33
  23.8 11.1 %collective-permute-start.8 = (bf16[2048,768]{1,0:T(8,128)(2,1)S(1)}, bf16[2048,768]{1,0:T(8,128)(2,1)S(1)}, u32[]{:S(2)}, u32[]{:S(2)}) collective-permute-start(bf16[2048,768]{1,0:T(8,128)(2,1)S(1)} %get-tuple-element.89), channel_id=1, source_target_pairs={{0,1},{1,0},{2,3},{3,2},{4,5},{5,4},{6,7},{7,6},{8,9},{9,8},{10,11... | collective-permute-start | bytes 9437192 | tf_op jit(solution)/shard_map/ppermute | solution.py:29
  23.8 8.4 %collective-permute-start.4 = (bf16[64,1408]{1,0:T(8,128)(2,1)S(1)}, bf16[64,1408]{1,0:T(8,128)(2,1)S(1)}, u32[]{:S(2)}, u32[]{:S(2)}) collective-permute-start(bf16[64,1408]{1,0:T(8,128)(2,1)S(1)} %collective-permute-done._.refs_4_), channel_id=1, source_target_pairs={{0,8},{4,12},{8,0},{12,4},{16,24},{20,28},{24,16},{28,20},{1,9},{5... | collective-permute-start | bytes 540680 | tf_op jit(solution)/shard_map/ppermute | solution.py:21
  24.4 7.9 %collective-permute-start.6 = (bf16[64,1408]{1,0:T(8,128)(2,1)S(1)}, bf16[64,1408]{1,0:T(8,128)(2,1)S(1)}, u32[]{:S(2)}, u32[]{:S(2)}) collective-permute-start(bf16[64,1408]{1,0:T(8,128)(2,1)S(1)} %collective-permute-done._.refs_4_), channel_id=1, source_target_pairs={{0,4},{4,0},{8,12},{12,8},{16,20},{20,16},{24,28},{28,24},{1,5},{5... | collective-permute-start | bytes 540680 | tf_op jit(solution)/shard_map/ppermute | solution.py:21
  24.6 10.2 %collective-permute-start.5 = (bf16[64,1408]{1,0:T(8,128)(2,1)S(1)}, bf16[64,1408]{1,0:T(8,128)(2,1)S(1)}, u32[]{:S(2)}, u32[]{:S(2)}) collective-permute-start(bf16[64,1408]{1,0:T(8,128)(2,1)S(1)} %collective-permute-done.1.refs_2_), channel_id=1, source_target_pairs={{0,4},{4,0},{8,12},{12,8},{16,20},{20,16},{24,28},{28,24},{1,5},{5... | collective-permute-start | bytes 540680 | tf_op jit(solution)/shard_map/ppermute | solution.py:21
  26.4 5.8 %collective-permute-start.7 = (bf16[4,16,512]{2,1,0:T(8,128)(2,1)S(1)}, bf16[4,16,512]{2,1,0:T(8,128)(2,1)S(1)}, u32[]{:S(2)}, u32[]{:S(2)}) collective-permute-start(bf16[4,16,512]{2,1,0:T(8,128)(2,1)S(1)} %pad_maximum_fusion), channel_id=1, source_target_pairs={{0,8},{4,12},{8,0},{12,4},{16,24},{20,28},{24,16},{28,20},{1,9},{5... | collective-permute-start | bytes 196616 | tf_op jit(solution)/shard_map/ppermute | solution.py:33
  34.8 8.4 %collective-permute-start.11 = (bf16[384,2048]{1,0:T(8,128)(2,1)S(1)}, bf16[384,2048]{1,0:T(8,128)(2,1)S(1)}, u32[]{:S(2)}, u32[]{:S(2)}) collective-permute-start(bf16[384,2048]{1,0:T(8,128)(2,1)S(1)} %get-tuple-element.96.refs_11_), channel_id=1, source_target_pairs={{0,1},{1,0},{2,3},{3,2},{4,5},{5,4},{6,7},{7,6},{8,9},{9,8},{10,11... | collective-permute-start | bytes 4718600 | tf_op jit(solution)/shard_map/ppermute | solution.py:29
  34.9 8.4 %collective-permute-start.9 = (bf16[64,1408]{1,0:T(8,128)(2,1)S(1)}, bf16[64,1408]{1,0:T(8,128)(2,1)S(1)}, u32[]{:S(2)}, u32[]{:S(2)}) collective-permute-start(bf16[64,1408]{1,0:T(8,128)(2,1)S(1)} %collective-permute-done.4.refs_6_), channel_id=1, source_target_pairs={{0,4},{4,0},{8,12},{12,8},{16,20},{20,16},{24,28},{28,24},{1,5},{5... | collective-permute-start | bytes 540680 | tf_op jit(solution)/shard_map/ppermute | solution.py:21
  35.3 8.0 %collective-permute-start.10 = (bf16[4,16,512]{2,1,0:T(8,128)(2,1)S(1)}, bf16[4,16,512]{2,1,0:T(8,128)(2,1)S(1)}, u32[]{:S(2)}, u32[]{:S(2)}) collective-permute-start(bf16[4,16,512]{2,1,0:T(8,128)(2,1)S(1)} %pad_maximum_fusion.1), channel_id=1, source_target_pairs={{0,4},{4,0},{8,12},{12,8},{16,20},{20,16},{24,28},{28,24},{1,5},{5... | collective-permute-start | bytes 196616 | tf_op jit(solution)/shard_map/ppermute | solution.py:33
  47.9 6.7 %collective-permute-start.13 = (bf16[288,256]{1,0:T(8,128)(2,1)S(1)}, bf16[288,256]{1,0:T(8,128)(2,1)S(1)}, u32[]{:S(2)}, u32[]{:S(2)}) collective-permute-start(bf16[288,256]{1,0:T(8,128)(2,1)S(1)} %get-tuple-element.99), channel_id=1, source_target_pairs={{0,2},{1,3},{2,0},{3,1},{4,6},{5,7},{6,4},{7,5},{8,10},{9,11},{10,... | collective-permute-start | bytes 442376 | tf_op jit(solution)/shard_map/ppermute | solution.py:29
  49.5 7.4 %collective-permute-start.14 = (bf16[288,256]{1,0:T(8,128)(2,1)S(1)}, bf16[288,256]{1,0:T(8,128)(2,1)S(1)}, u32[]{:S(2)}, u32[]{:S(2)}) collective-permute-start(bf16[288,256]{1,0:T(8,128)(2,1)S(1)} %get-tuple-element.100), channel_id=1, source_target_pairs={{0,3},{1,2},{2,1},{3,0},{4,7},{5,6},{6,5},{7,4},{8,11},{9,10},{10,... | collective-permute-start | bytes 442376 | tf_op jit(solution)/shard_map/ppermute | solution.py:29
  56.9 9.6 %collective-permute-start.15 = (bf16[256,256]{1,0:T(8,128)(2,1)S(1)}, bf16[256,256]{1,0:T(8,128)(2,1)S(1)}, u32[]{:S(2)}, u32[]{:S(2)}) collective-permute-start(bf16[256,256]{1,0:T(8,128)(2,1)S(1)} %add_convert_fusion.7.refs_0_.refs_7_), channel_id=1, source_target_pairs={{0,16},{4,20},{8,24},{12,28},{16,0},{20,4},{24,8},{28,12},{1,17},{... | collective-permute-start | bytes 393224 | tf_op jit(solution)/shard_map/ppermute | solution.py:21
  59.6 7.1 %collective-permute-start.16 = (bf16[256,256]{1,0:T(8,128)(2,1)S(1)}, bf16[256,256]{1,0:T(8,128)(2,1)S(1)}, u32[]{:S(2)}, u32[]{:S(2)}) collective-permute-start(bf16[256,256]{1,0:T(8,128)(2,1)S(1)} %add_convert_fusion.7.refs_0_.refs_7_), channel_id=1, source_target_pairs={{0,8},{4,12},{8,0},{12,4},{16,24},{20,28},{24,16},{28,20},{1,9},{5... | collective-permute-start | bytes 393224 | tf_op jit(solution)/shard_map/ppermute | solution.py:21
  70.4 6.4 %collective-permute-start.22 = (bf16[256,256]{1,0:T(8,128)(2,1)S(1)}, bf16[256,256]{1,0:T(8,128)(2,1)S(1)}, u32[]{:S(2)}, u32[]{:S(2)}) collective-permute-start(bf16[256,256]{1,0:T(8,128)(2,1)S(1)} %collective-permute-done.15.refs_0_.refs_11_), channel_id=1, source_target_pairs={{0,4},{4,0},{8,12},{12,8},{16,20},{20,16},{24,28},{28,24},{1,5},{5... | collective-permute-start | bytes 393224 | tf_op jit(solution)/shard_map/ppermute | solution.py:21
  72.2 9.2 %collective-permute-start.25 = (bf16[256,256]{1,0:T(8,128)(2,1)S(1)}, bf16[256,256]{1,0:T(8,128)(2,1)S(1)}, u32[]{:S(2)}, u32[]{:S(2)}) collective-permute-start(bf16[256,256]{1,0:T(8,128)(2,1)S(1)} %collective-permute-done.17.refs_2_.refs_8_), channel_id=1, source_target_pairs={{0,2},{1,3},{2,0},{3,1},{4,6},{5,7},{6,4},{7,5},{8,10},{9,11},{10,... | collective-permute-start | bytes 393224 | tf_op jit(solution)/shard_map/ppermute | solution.py:21
  79.5 5.9 %collective-permute-start.28 = (bf16[256,256]{1,0:T(8,128)(2,1)S(1)}, bf16[256,256]{1,0:T(8,128)(2,1)S(1)}, u32[]{:S(2)}, u32[]{:S(2)}) collective-permute-start(bf16[256,256]{1,0:T(8,128)(2,1)S(1)} %collective-permute-done.19.refs_4_.refs_13_), channel_id=1, source_target_pairs={{0,4},{4,0},{8,12},{12,8},{16,20},{20,16},{24,28},{28,24},{1,5},{5... | collective-permute-start | bytes 393224 | tf_op jit(solution)/shard_map/ppermute | solution.py:21
  80.8 7.9 %collective-permute-start.24 = (bf16[256,256]{1,0:T(8,128)(2,1)S(1)}, bf16[256,256]{1,0:T(8,128)(2,1)S(1)}, u32[]{:S(2)}, u32[]{:S(2)}) collective-permute-start(bf16[256,256]{1,0:T(8,128)(2,1)S(1)} %collective-permute-done.22.refs_2_.refs_12_), channel_id=1, source_target_pairs={{0,2},{1,3},{2,0},{3,1},{4,6},{5,7},{6,4},{7,5},{8,10},{9,11},{10,... | collective-permute-start | bytes 393224 | tf_op jit(solution)/shard_map/ppermute | solution.py:21
  92.7 7.1 %collective-permute-start.33 = (bf16[256,1664]{1,0:T(8,128)(2,1)S(1)}, bf16[256,1664]{1,0:T(8,128)(2,1)S(1)}, u32[]{:S(2)}, u32[]{:S(2)}) collective-permute-start(bf16[256,1664]{1,0:T(8,128)(2,1)S(1)} %experts_in_second.3.refs_6_.act_ref), channel_id=1, source_target_pairs={{0,1},{1,0},{2,3},{3,2},{4,5},{5,4},{6,7},{7,6},{8,9},{9,8},{10,11... | collective-permute-start | bytes 2555912 | tf_op jit(solution)/shard_map/ppermute | solution.py:29
  95.7 6.4 %collective-permute-start.31 = (bf16[32,2048]{1,0:T(8,128)(2,1)S(1)}, bf16[32,2048]{1,0:T(8,128)(2,1)S(1)}, u32[]{:S(2)}, u32[]{:S(2)}) collective-permute-start(bf16[32,2048]{1,0:T(8,128)(2,1)S(1)} %get-tuple-element.120), channel_id=1, source_target_pairs={{0,2},{1,3},{2,0},{3,1},{4,6},{5,7},{6,4},{7,5},{8,10},{9,11},{10,... | collective-permute-start | bytes 393224 | tf_op jit(solution)/shard_map/ppermute | solution.py:21
  96.6 6.4 %collective-permute-start.32 = (bf16[32,2048]{1,0:T(8,128)(2,1)S(1)}, bf16[32,2048]{1,0:T(8,128)(2,1)S(1)}, u32[]{:S(2)}, u32[]{:S(2)}) collective-permute-start(bf16[32,2048]{1,0:T(8,128)(2,1)S(1)} %get-tuple-element.121), channel_id=1, source_target_pairs={{0,4},{4,0},{8,12},{12,8},{16,20},{20,16},{24,28},{28,24},{1,5},{5... | collective-permute-start | bytes 393224 | tf_op jit(solution)/shard_map/ppermute | solution.py:21
  97.9 8.5 %collective-permute-start.37 = (bf16[32,2048]{1,0:T(8,128)(2,1)S(1)}, bf16[32,2048]{1,0:T(8,128)(2,1)S(1)}, u32[]{:S(2)}, u32[]{:S(2)}) collective-permute-start(bf16[32,2048]{1,0:T(8,128)(2,1)S(1)} %get-tuple-element.137), channel_id=1, source_target_pairs={{0,4},{4,0},{8,12},{12,8},{16,20},{20,16},{24,28},{28,24},{1,5},{5... | collective-permute-start | bytes 393224 | tf_op jit(solution)/shard_map/ppermute | solution.py:21
  98.6 14.4 %collective-permute-start.42 = (bf16[32,2048]{1,0:T(8,128)(2,1)S(1)}, bf16[32,2048]{1,0:T(8,128)(2,1)S(1)}, u32[]{:S(2)}, u32[]{:S(2)}) collective-permute-start(bf16[32,2048]{1,0:T(8,128)(2,1)S(1)} %get-tuple-element.145), channel_id=1, source_target_pairs={{0,2},{1,3},{2,0},{3,1},{4,6},{5,7},{6,4},{7,5},{8,10},{9,11},{10,... | collective-permute-start | bytes 393224 | tf_op jit(solution)/shard_map/ppermute | solution.py:21
  106.5 7.7 %collective-permute-start.41 = (bf16[32,2048]{1,0:T(8,128)(2,1)S(1)}, bf16[32,2048]{1,0:T(8,128)(2,1)S(1)}, u32[]{:S(2)}, u32[]{:S(2)}) collective-permute-start(bf16[32,2048]{1,0:T(8,128)(2,1)S(1)} %add_convert_fusion.3), channel_id=1, source_target_pairs={{0,4},{4,0},{8,12},{12,8},{16,20},{20,16},{24,28},{28,24},{1,5},{5... | collective-permute-start | bytes 393224 | tf_op jit(solution)/shard_map/ppermute | solution.py:21
  108.3 6.9 %collective-permute-start.40 = (bf16[32,2048]{1,0:T(8,128)(2,1)S(1)}, bf16[32,2048]{1,0:T(8,128)(2,1)S(1)}, u32[]{:S(2)}, u32[]{:S(2)}) collective-permute-start(bf16[32,2048]{1,0:T(8,128)(2,1)S(1)} %get-tuple-element.142), channel_id=1, source_target_pairs={{0,4},{4,0},{8,12},{12,8},{16,20},{20,16},{24,28},{28,24},{1,5},{5... | collective-permute-start | bytes 393224 | tf_op jit(solution)/shard_map/ppermute | solution.py:21
  112.0 7.7 %collective-permute-start.38 = (bf16[32,2048]{1,0:T(8,128)(2,1)S(1)}, bf16[32,2048]{1,0:T(8,128)(2,1)S(1)}, u32[]{:S(2)}, u32[]{:S(2)}) collective-permute-start(bf16[32,2048]{1,0:T(8,128)(2,1)S(1)} %add_convert_fusion.5), channel_id=1, source_target_pairs={{0,8},{4,12},{8,0},{12,4},{16,24},{20,28},{24,16},{28,20},{1,9},{5... | collective-permute-start | bytes 393224 | tf_op jit(solution)/shard_map/ppermute | solution.py:21
  113.0 7.8 %collective-permute-start.46 = (bf16[32,2048]{1,0:T(8,128)(2,1)S(1)}, bf16[32,2048]{1,0:T(8,128)(2,1)S(1)}, u32[]{:S(2)}, u32[]{:S(2)}) collective-permute-start(bf16[32,2048]{1,0:T(8,128)(2,1)S(1)} %get-tuple-element.154), channel_id=1, source_target_pairs={{0,2},{1,3},{2,0},{3,1},{4,6},{5,7},{6,4},{7,5},{8,10},{9,11},{10,... | collective-permute-start | bytes 393224 | tf_op jit(solution)/shard_map/ppermute | solution.py:21
  114.2 6.7 %collective-permute-start.45 = (bf16[32,2048]{1,0:T(8,128)(2,1)S(1)}, bf16[32,2048]{1,0:T(8,128)(2,1)S(1)}, u32[]{:S(2)}, u32[]{:S(2)}) collective-permute-start(bf16[32,2048]{1,0:T(8,128)(2,1)S(1)} %add_convert_fusion), channel_id=1, source_target_pairs={{0,4},{4,0},{8,12},{12,8},{16,20},{20,16},{24,28},{28,24},{1,5},{5... | collective-permute-start | bytes 393224 | tf_op jit(solution)/shard_map/ppermute | solution.py:21
  119.7 6.5 %collective-permute-start.43 = (bf16[32,2048]{1,0:T(8,128)(2,1)S(1)}, bf16[32,2048]{1,0:T(8,128)(2,1)S(1)}, u32[]{:S(2)}, u32[]{:S(2)}) collective-permute-start(bf16[32,2048]{1,0:T(8,128)(2,1)S(1)} %add_convert_fusion.2), channel_id=1, source_target_pairs={{0,16},{4,20},{8,24},{12,28},{16,0},{20,4},{24,8},{28,12},{1,17},{... | collective-permute-start | bytes 393224 | tf_op jit(solution)/shard_map/ppermute | solution.py:21
  119.9 6.4 %collective-permute-start.44 = (bf16[32,2048]{1,0:T(8,128)(2,1)S(1)}, bf16[32,2048]{1,0:T(8,128)(2,1)S(1)}, u32[]{:S(2)}, u32[]{:S(2)}) collective-permute-start(bf16[32,2048]{1,0:T(8,128)(2,1)S(1)} %add_convert_fusion.1), channel_id=1, source_target_pairs={{0,8},{4,12},{8,0},{12,4},{16,24},{20,28},{24,16},{28,20},{1,9},{5... | collective-permute-start | bytes 393224 | tf_op jit(solution)/shard_map/ppermute | solution.py:21
  (33 other events, 194.5 us)

commit v3 on v2

--- a/solution.py
+++ b/solution.py
@@ -17,10 +17,6 @@
 MIB = 1 << 20
 
 
-def from_partner(array, axis, bit):
-    return lax.ppermute(array, axis, [(i, i ^ 1 << bit) for i in range(lax.axis_size(axis))])
-
-
 def bits_of(count):
     return count.bit_length() - 1
 
@@ -33,29 +29,51 @@
     return lax.ppermute(array, "ctx", [(i, i ^ offset) for i in range(lax.axis_size("ctx"))])
 
 
+def moved(offset, move):
+    return (offset[0] ^ move[0], offset[1] ^ move[1])
+
+
 def gather_route(ctx_count, x_count, rows_only=False):
-    transfers, arrival = [], {(0, 0): 0}
-
-    def go(source, axis, bit, delay=0):
-        move = (1 << bit, 0) if axis == "ctx" else (0, 1 << bit - 1)
-        target = (source[0] ^ move[0], source[1] ^ move[1])
-        arrival[target] = arrival[source] + 1 + delay
-        transfers.append((arrival[target], source, target, axis, bit))
-
-    for bit in range(bits_of(ctx_count) - 1, 0, -1):
+    transfers, arrival, places = [], {(0, 0): 0}, {(0, 0): ((0, 0), (0, 0))}
+
+    def go(source, moves, delay=0):
+        reached = tuple(moved(place, (c, e >> 1)) for place, (c, e) in zip(places[source], moves))
+        target = reached[0]
+        arrival[target], places[target] = arrival[source] + 1 + delay, reached
+        transfers.append((arrival[target], source, target, moves))
+        return target
+
+    bits = bits_of(ctx_count)
+    y_move = (1, 0)
+    if rows_only:
+        shared, steps = range(bits - 1, 1, -1), [(2, 0), y_move]
+    else:
+        shared, steps = range(bits - 1, 0, -1), [(0, 2 << bit) for bit in range(bits_of(x_count))] + [y_move]
+    pairs = list(zip(steps, reversed(steps)))
+    for bit in shared:
         for source in list(arrival):
-            go(source, "ctx", bit)
-    x_steps = [] if rows_only else [("exp", bit + 1) for bit in range(bits_of(x_count))]
+            go(source, ((1 << bit, 0),) * 2)
     for number, first in enumerate(sorted(arrival)):
-        steps = [("ctx", 0)] + x_steps if number % 2 == 0 else x_steps + [("ctx", 0)]
         held = [first]
-        for axis, bit in steps:
-            before = len(transfers)
-            for source in held:
-                late = source != first and (ctx_count, x_count) == (8, 2) and number in (0, 2)
-                go(source, axis, bit, 1 if late else 0)
-            held = held + [transfer[2] for transfer in transfers[before:]]
-    return sorted(transfers, key=lambda transfer: transfer[0])
+        for moves in pairs:
+            tuned = (ctx_count, x_count) == (8, 2) and not rows_only and number in (0, 2)
+            held = held + [go(source, moves, 1 if tuned and source != first else 0) for source in held]
+    return sorted(transfers, key=lambda transfer: transfer[0]), places
+
+
+def follow(array, moves):
+    exp_count = lax.axis_size("exp")
+    pairs = []
+    for c in range(lax.axis_size("ctx")):
+        for e in range(exp_count):
+            far = moved((c, e), moves[e % 2])
+            pairs.append((far[0] * exp_count + far[1], c * exp_count + e))
+    return lax.ppermute(array, ("ctx", "exp"), pairs)
+
+
+def by_core(core, place, part):
+    first, second = place[0][part], place[1][part]
+    return first if first == second else jnp.where(core == 0, first, second)
 
 
 def stages_of(route):
@@ -69,6 +87,10 @@
 def block_factor(exponent, width):
     factor = jnp.where(exponent < 0, 0.5, jnp.where(exponent > 0, 2.0, 1.0))
     return jnp.full((1, width), factor, jnp.float32).astype(jnp.bfloat16)
+
+
+def in_hbm(*arrays):
+    return [pltpu.with_memory_space_constraint(array, pltpu.HBM) for array in arrays]
 
 
 def copy_all(sems, pairs):
@@ -182,7 +204,7 @@
             flops=2 * width * hidden, bytes_accessed=8 * width * hidden, transcendentals=0
         ),
         name="dequant_in",
-    )(my_exp, gate_scale, up_scale, gate_weight, up_weight, after)
+    )(my_exp, *in_hbm(gate_scale, up_scale, gate_weight, up_weight), after)
 
 
 def deq_down_kernel(ctx_count, exp_ref, scale_hbm, down_hbm, _, own_ref, give_ref, down_ref, scale_ref, sems):
@@ -229,11 +251,11 @@
             flops=width * hidden, bytes_accessed=4 * width * hidden, transcendentals=0
         ),
         name="dequant_down",
-    )(my_exp, down_scale, down_weight, after)
+    )(my_exp, *in_hbm(down_scale, down_weight), after)
 
 
 def attend_kernel(plan, ctx_ref, exp_ref, order_ref, *refs):
-    ctx_count, exp_count, tok, heads, piece_places = plan
+    ctx_count, exp_count, tok, heads, piece_places, places_of = plan
     packed, refs = refs[:ctx_count], refs[ctx_count:]
     piece_refs, refs = refs[: 1 + bits_of(ctx_count)], refs[1 + bits_of(ctx_count) :]
     weight_ref, rest = refs[0], refs[2:]
@@ -250,12 +272,12 @@
     for offset, ref in enumerate(packed):
         key_scr[pl.ds(offset * span, span), :] = ref[:, 0:HEAD_SIZE]
         value_scr[pl.ds(offset * span, span), :] = ref[:, HEAD_SIZE : 2 * HEAD_SIZE]
-        base = order_ref[lax.bitwise_xor(my_ctx, offset)] * span
+        base = order_ref[lax.bitwise_xor(my_ctx, by_core(my_core, places_of[offset], 0))] * span
         places = places + jnp.where(lane // span == offset, base, 0)
     place_scr[...] = places
     scale = 1.0 / math.sqrt(HEAD_SIZE)
     for offset, ref in enumerate(packed):
-        source = lax.bitwise_xor(my_ctx, offset)
+        source = lax.bitwise_xor(my_ctx, by_core(my_core, places_of[offset], 0))
         queries = jnp.concatenate(
             [ref[:, (h + 2) * HEAD_SIZE : (h + 3) * HEAD_SIZE] for h in range(heads)], axis=0
         )
@@ -303,12 +325,11 @@
         expert = my_ctx * x_count + lax.bitwise_xor(my_x, which // 2)
         sides = [jnp.zeros((tok, HEAD_SIZE), jnp.float32)] * 2
         for offset, ref in enumerate(packed):
+            source = lax.bitwise_xor(my_ctx, by_core(my_core, places_of[offset], 0))
             for part_of in range(2):
                 block = ref[part_of * tok : (part_of + 1) * tok, first:].astype(jnp.float32)
                 column = jnp.sum(jnp.where(route_lane == expert, block, 0.0), axis=1, keepdims=True)
-                sides[part_of] = sides[part_of] + jnp.where(
-                    route_lane == lax.bitwise_xor(my_ctx, offset), column, 0.0
-                )
+                sides[part_of] = sides[part_of] + jnp.where(route_lane == source, column, 0.0)
         route_out, row = (give_refs[which - 1], per_x) if which else (own_route_ref, 0)
         for part_of, side in enumerate(sides):
             at = pl.ds(row + part_of * tok, tok)
@@ -318,7 +339,7 @@
                 route_out[at, HEAD_SIZE:] = jnp.zeros(rest_shape, jnp.bfloat16)
 
 
-def fill_rows(plan, ctx_ref, exp_ref, gain_ref, chunk_refs, offsets, rows_scr, groups):
+def fill_rows(plan, ctx_ref, exp_ref, gain_ref, chunk_refs, places, rows_scr, square_ref, groups):
     ctx_count, x_count = plan
     half = ctx_count // 2
     my_ctx = ctx_ref[0]
@@ -326,28 +347,25 @@
     mine = lax.shift_right_logical(my_ctx, bits_of(half))
     rows, cols = chunk_refs[0].shape
     rows = rows // 2
-    sums = {}
-    for ref, (c_off, x_off) in zip(chunk_refs, offsets):
-        source = lax.bitwise_xor(my_ctx, c_off)
+    for ref, place_of in zip(chunk_refs, places):
+        source = lax.bitwise_xor(my_ctx, by_core(my_core, place_of, 0))
+        x_off = by_core(my_core, place_of, 1)
         gain_at = pl.multiple_of((source * 2 + my_core) * cols, cols)
         gain = gain_ref[:, pl.ds(gain_at, cols)]
         col = pl.multiple_of(lax.bitwise_and(source, half - 1) * cols, cols)
         for place, group in enumerate(groups):
             side = mine if group == 1 else 1 - mine
             chunk = ref[pl.ds(pl.multiple_of(side * rows, rows), rows), :].astype(jnp.float32)
-            row = (place * x_count + x_off) * rows
-            rows_scr[pl.ds(row, rows), pl.ds(col, cols)] = (chunk * gain).astype(jnp.bfloat16)
-            square = jnp.sum(chunk * chunk, axis=-1, keepdims=True)
-            sums[row] = sums[row] + square if row in sums else square
-    return sums
+            at = pl.ds(pl.multiple_of((place * x_count + x_off) * rows, rows), rows)
+            rows_scr[at, pl.ds(col, cols)] = (chunk * gain).astype(jnp.bfloat16)
+            square_ref[at, :] = square_ref[at, :] + jnp.sum(chunk * chunk, axis=-1, keepdims=True)
 
 
 def experts_in_first(plan, offsets, ctx_ref, exp_ref, *refs):
     chunk_refs, (gain_ref, own_ref, other_ref, _, act_ref, square_ref, rows_scr) = refs[:-7], refs[-7:]
     half = plan[0] // 2
-    sums = fill_rows(plan, ctx_ref, exp_ref, gain_ref, chunk_refs, offsets, rows_scr, (0, 1))
-    for row, square in sums.items():
-        square_ref[pl.ds(row, square.shape[0]), :] = square
+    square_ref[...] = jnp.zeros(square_ref.shape, jnp.float32)
+    fill_rows(plan, ctx_ref, exp_ref, gain_ref, chunk_refs, offsets, rows_scr, square_ref, (0, 1))
     depth, width = rows_scr.shape[1], own_ref.shape[1]
     start = lax.shift_right_logical(ctx_ref[0], bits_of(half)) * depth
     at = pl.ds(pl.multiple_of(start, depth), depth)
@@ -358,20 +376,17 @@
 
 
 def experts_in_second(plan, offsets, group, ctx_ref, exp_ref, *refs):
-    chunk_refs, rest = refs[:-8], refs[-8:]
-    gain_ref, own_ref, other_ref, first_ref, square_ref, _, act_ref, rows_scr = rest
+    chunk_refs, rest = refs[:-9], refs[-9:]
+    gain_ref, own_ref, other_ref, first_ref, square_ref, _, act_ref, rows_scr, sum_scr = rest
     half = plan[0] // 2
-    sums = fill_rows(plan, ctx_ref, exp_ref, gain_ref, chunk_refs, offsets, rows_scr, (group,))
     count, depth = rows_scr.shape
     width = own_ref.shape[1]
+    sum_scr[...] = square_ref[group * count : (group + 1) * count, :]
+    fill_rows(plan, ctx_ref, exp_ref, gain_ref, chunk_refs, offsets, rows_scr, sum_scr, (group,))
     lane = lax.broadcasted_iota(jnp.int32, (1, HEAD_SIZE), 1)
-    for row, square in sums.items():
-        rows = square.shape[0]
-        square = square + square_ref[pl.ds(group * count + row, rows), :]
-        high = square.astype(jnp.bfloat16).astype(jnp.float32)
-        act_ref[pl.ds(row, rows), 2 * width :] = jnp.where(lane == 0, high, square - high).astype(
-            jnp.bfloat16
-        )
+    square = sum_scr[...]
+    high = square.astype(jnp.bfloat16).astype(jnp.float32)
+    act_ref[:, 2 * width :] = jnp.where(lane == 0, high, square - high).astype(jnp.bfloat16)
     start = (1 - lax.shift_right_logical(ctx_ref[0], bits_of(half))) * depth
     at = pl.ds(pl.multiple_of(start, depth), depth)
     for place, ref in enumerate((own_ref, other_ref)):
@@ -382,13 +397,14 @@
         act_ref[:, cols] = act.astype(jnp.bfloat16)
 
 
-def experts_out_kernel(plan, group, slots, model_width, ctx_ref, exp_ref, act_ref, came_ref, *refs):
+def experts_out_kernel(plan, group, places, state_at, model_width, ctx_ref, exp_ref, act_ref, came_ref, *refs):
     ctx_count, exp_count, tok = plan
     x_count, half = exp_count // 2, ctx_count // 2
     route_refs = refs[:exp_count]
     own_ref, other_ref, _ = refs[exp_count : exp_count + 3]
     rest = refs[exp_count + 3 :]
-    state_refs, rest = (rest[:ctx_count], rest[ctx_count:]) if group == 1 else ((), rest)
+    state_count = 1 + max((max(pair) for pair in state_at), default=-1)
+    state_refs, rest = rest[:state_count], rest[state_count:]
     out_refs, hidden_scr = rest[:-1], rest[-1]
     my_ctx = ctx_ref[0]
     my_core = lax.bitwise_and(exp_ref[0], 1)
@@ -422,8 +438,9 @@
         value = gate / (1.0 + jnp.exp(-gate)) * (acts[:, hidden:] * scaled_route)
         hidden_scr[:, side * hidden : (side + 1) * hidden] = value.astype(jnp.bfloat16)
     picked = []
-    for c_off, x_off in slots:
-        low = lax.bitwise_and(lax.bitwise_xor(my_ctx, c_off), half - 1)
+    for place in places:
+        x_off = by_core(my_core, place, 1)
+        low = lax.bitwise_and(lax.bitwise_xor(my_ctx, by_core(my_core, place, 0)), half - 1)
         row = pl.multiple_of((x_off * half + low) * (2 * tok), 2 * tok)
         picked.append(hidden_scr[pl.ds(row, 2 * tok), :])
     picked = jnp.concatenate(picked, axis=0)
@@ -435,13 +452,17 @@
         out = out + jnp.dot(picked[:, hidden:], other_ref[:, at], preferred_element_type=jnp.float32)
         for place, ref in enumerate(out_refs):
             ref[:, at] = out[place * 2 * tok : (place + 1) * 2 * tok, :].astype(ref.dtype)
-    for slot, ref in zip(slots, out_refs):
-        if slot == (0, 0):
-            for c_off, state_ref in enumerate(state_refs):
-                cols = state_ref.shape[1]
+    for place, ref in zip(places, out_refs):
+        if place[0] == (0, 0):
+            own_rows = pl.ds(pl.multiple_of(my_ctx * (2 * tok), 2 * tok), 2 * tok)
+            for c_off, (first, second) in enumerate(state_at):
+                cols = state_refs[first].shape[1]
                 at = pl.ds(pl.multiple_of(lax.bitwise_xor(my_ctx, c_off) * cols, cols), cols)
-                own_row = pl.multiple_of(my_ctx * (2 * tok), 2 * tok)
-                ref[:, at] = ref[:, at] + state_ref[pl.ds(own_row, 2 * tok), :].astype(jnp.float32)
+                state = state_refs[first][own_rows, :].astype(jnp.float32)
+                if second != first:
+                    other = state_refs[second][own_rows, :].astype(jnp.float32)
+                    state = jnp.where(my_core == 0, state, other)
+                ref[:, at] = ref[:, at] + state
 
 
 def shards(
@@ -479,7 +500,7 @@
     cols = half_width // ctx_count
     my_ctx = lax.axis_index("ctx").astype(jnp.int32).reshape(1)
     my_exp = lax.axis_index("exp").astype(jnp.int32).reshape(1)
-    route = gather_route(ctx_count, x_count)
+    route, places = gather_route(ctx_count, x_count)
 
     hbm = pl.BlockSpec(memory_space=pltpu.HBM)
     piece_shape = jax.ShapeDtypeStruct((ctx_count // 2, tok, 2 * cols), bf16)
@@ -506,22 +527,25 @@
     )(
         my_ctx,
         my_exp,
-        key_block_exponent,
-        value_block_exponent,
-        encoded_query_rows,
-        quantized_key_rows,
-        quantized_value_rows,
-        jnp.transpose(expert_ids),
-        jnp.transpose(route_weight),
-        residual,
+        *in_hbm(
+            key_block_exponent,
+            value_block_exponent,
+            encoded_query_rows,
+            quantized_key_rows,
+            quantized_value_rows,
+            jnp.transpose(expert_ids),
+            jnp.transpose(route_weight),
+            residual,
+        ),
     )
     held = {(0, 0): packed}
     piece_arrays = [near]
     piece_at = {(0, offset): (0, offset) for offset in range(ctx_count // 2)}
     sending, send_keys = far, [(0, offset) for offset in range(ctx_count // 2, ctx_count)]
-    stages = stages_of(gather_route(ctx_count, x_count, rows_only=True))
+    row_route, row_places = gather_route(ctx_count, x_count, rows_only=True)
+    stages = stages_of(row_route)
     for number, stage in enumerate(stages):
-        came = [from_partner(held[source], axis, bit) for _, source, _, axis, bit in stage]
+        came = [follow(held[source], moves) for _, source, _, moves in stage]
         piece_bit = bits_of(ctx_count) - 1 - number
         came.append(from_ctx(sending, 1 << piece_bit))
         if number == 0:
@@ -536,21 +560,23 @@
         elif number < len(stages) - 1:
             came = together(*came)
         came_first = came[0]
-        held.update({target: array for (_, _, target, _, _), array in zip(stage, came)})
+        held.update({target: array for (_, _, target, _), array in zip(stage, came)})
         piece_arrays.append(came[-1])
         for place, (source, target) in enumerate(send_keys):
             piece_at[source ^ 1 << piece_bit, target ^ 1 << piece_bit] = (number + 1, place)
         if piece_bit:
-            send_keys = sorted(key for key in piece_at if key[1] == key[1] & ((2 << piece_bit - 1) - 1) and key[1] >> piece_bit - 1 & 1)
+            below = 1 << piece_bit
+            send_keys = sorted(key for key in piece_at if below // 2 <= key[1] < below)
             sending = jnp.stack([piece_arrays[array][place] for array, place in map(piece_at.get, send_keys)])
     packed = [held[offset, 0] for offset in range(ctx_count)]
+    attend_places = tuple(row_places[offset, 0] for offset in range(ctx_count))
     piece_places = tuple(piece_at[offset, 0] for offset in range(ctx_count))
     down_other = from_offset(down_give, 1)
 
     positions = ctx_count * span
     per_x = 2 * ctx_count * tok
     keep, own_route, *gives = pl.pallas_call(
-        functools.partial(attend_kernel, (ctx_count, exp_count, tok, heads, piece_places)),
+        functools.partial(attend_kernel, (ctx_count, exp_count, tok, heads, piece_places, attend_places)),
         in_specs=[smem] * 3 + [vmem] * (ctx_count + len(piece_arrays) + 1) + [anywhere],
         out_specs=[vmem] * (1 + exp_count),
         out_shape=[
@@ -582,17 +608,18 @@
 
     chunks = {(0, 0): state}
     for stage in stages_of(route):
-        came = [from_partner(chunks[source], axis, bit) for _, source, _, axis, bit in stage]
+        came = [follow(chunks[source], moves) for _, source, _, moves in stage]
         if stage[-1] != route[-1]:
             came = together(*came)
-        chunks.update({target: array for (_, _, target, _, _), array in zip(stage, came)})
+        chunks.update({target: array for (_, _, target, _), array in zip(stage, came)})
     gain = norm_gain.reshape(1, model_width)
     rows = x_count * per_x
     in_width = in_own.shape[1]
     near = tuple(sorted(key for key in chunks if key[0] < ctx_count // 2))
     far = tuple(sorted(key for key in chunks if key[0] >= ctx_count // 2))
+    near_places, far_places = (tuple(places[key] for key in keys) for keys in (near, far))
     first_act, first_square = pl.pallas_call(
-        functools.partial(experts_in_first, (ctx_count, x_count), near),
+        functools.partial(experts_in_first, (ctx_count, x_count), near_places),
         in_specs=[smem] * 2 + [vmem] * (len(near) + 3) + [anywhere],
         out_specs=[vmem] * 2,
         out_shape=[
@@ -610,11 +637,14 @@
     for part in range(2):
         acts.append(
             pl.pallas_call(
-                functools.partial(experts_in_second, (ctx_count, x_count), far, part),
+                functools.partial(experts_in_second, (ctx_count, x_count), far_places, part),
                 in_specs=[smem] * 2 + [vmem] * (len(far) + 5) + [anywhere],
                 out_specs=vmem,
                 out_shape=jax.ShapeDtypeStruct((rows // 2, 2 * in_width + HEAD_SIZE), bf16),
-                scratch_shapes=[pltpu.VMEM((rows // 2, half_width // 2), bf16)],
+                scratch_shapes=[
+                    pltpu.VMEM((rows // 2, half_width // 2), bf16),
+                    pltpu.VMEM((rows // 2, 1), f32),
+                ],
                 compiler_params=pltpu.CompilerParams(vmem_limit_bytes=2 * ctx_count * MIB),
                 cost_estimate=pl.CostEstimate(
                     flops=rows * half_width * in_width, bytes_accessed=8 * MIB, transcendentals=0
@@ -632,13 +662,25 @@
                 acts[0] if part else first_square,
             )
         )
-    leaves = {key for key in chunks} - {source for _, source, _, _, _ in route}
+    leaves = set(chunks) - {source for _, source, _, _ in route}
     sums = {}
     for part in range(2):
         slots = near if part == 1 else far
-        states = [chunks[offset, 0] for offset in range(ctx_count)] if part == 1 else []
+        state_keys, state_at = [], []
+        for offset in range(ctx_count) if part == 1 else ():
+            pair = [next(key for key in chunks if places[key][core] == (offset, 0)) for core in range(2)]
+            state_keys += [key for key in pair if key not in state_keys]
+            state_at.append(tuple(state_keys.index(key) for key in pair))
+        states = [chunks[key] for key in state_keys]
         outs = pl.pallas_call(
-            functools.partial(experts_out_kernel, (ctx_count, exp_count, tok), part, slots, model_width),
+            functools.partial(
+                experts_out_kernel,
+                (ctx_count, exp_count, tok),
+                part,
+                tuple(places[key] for key in slots),
+                tuple(state_at),
+                model_width,
+            ),
             in_specs=[smem] * 2 + [vmem] * (4 + exp_count) + [anywhere] + [vmem] * len(states),
             out_specs=[vmem] * len(slots),
             out_shape=[
@@ -670,13 +712,13 @@
 
     backward = stages_of(route)[::-1]
     for number, stage in enumerate(backward):
-        came = [from_partner(sums[target].astype(bf16), axis, bit) for _, _, target, axis, bit in stage]
+        came = [follow(sums[target].astype(bf16), moves) for _, _, target, moves in stage]
         if number < len(backward) - 1:
             waiting = [key for key in near if key in sums] if number == 0 else []
             values = together(*came, *[sums[key] for key in waiting])
             came = values[: len(came)]
             sums.update(zip(waiting, values[len(came) :]))
-        for (_, source, target, _, _), array in zip(stage, came):
+        for (_, source, target, _), array in zip(stage, came):
             sums[source] = sums[source] + array.astype(f32)
     total = sums[0, 0]
     core = lax.bitwise_and(my_exp[0], 1)

time: 129 us -> 117 us (0.907)
  local copies, waits for them, and re-layouts: 12.2 us -> 0.93 us
  starting transfers between devices: 50.1 us -> 52.3 us
  waiting for transfers between devices: 46.6 us -> 44.5 us
    unnamed x36 -> x8, local copies, waits for them, and re-layouts: 11.4 us -> 0.05 us
    ppermute x37, waiting for transfers between devices: 28.9 us -> 24.4 us  [follow(): return lax.ppermute(array, ('ctx', 'exp'), pairs)]
    ppermute x3, waiting for transfers between devices: 8.72 us -> 11.3 us  [from_ctx(): lax.ppermute(array, 'ctx', [(i, i ^ offset) for i in range(lax.axis_size(...]
    ppermute x8, starting transfers between devices: 2.7 us -> 4.54 us  [from_offset(): lax.ppermute(array, 'exp', [(i, i ^ offset) for i in range(lax.axis_size(...]
    ppermute x37, starting transfers between devices: 43.6 us -> 45.1 us  [follow(): return lax.ppermute(array, ('ctx', 'exp'), pairs)]
    pallas_call x1, Pallas kernels: 4.43 us -> 3 us  [deq_in(): pl.pallas_call(functools.partial(deq_in_kernel, ctx_count), in_specs=[pl....]
where the time goes in v3:
time: 117 us
  starting transfers between devices  52.3 us (45%)
  waiting for transfers between devices  44.5 us (38%)
  Pallas kernels  18.8 us (16%)
    ppermute x37, starting transfers between devices, follow(): return lax.ppermute(array, ('ctx', 'exp'), pairs)  45.1 us
    ppermute x37, waiting for transfers between devices, follow(): return lax.ppermute(array, ('ctx', 'exp'), pairs)  24.4 us
    ppermute x3, waiting for transfers between devices, from_ctx(): lax.ppermute(array, 'ctx', [(i, i ^ offset) for i in range(lax.axis_size(...  11.3 us
    ppermute x8, waiting for transfers between devices, from_offset(): lax.ppermute(array, 'exp', [(i, i ^ offset) for i in range(lax.axis_size(...  8.76 us
    pallas_call x1, Pallas kernels, shards(): pl.pallas_call(functools.partial(attend_kernel, (ctx_count, exp_count, to...  4.55 us
    ppermute x8, starting transfers between devices, from_offset(): lax.ppermute(array, 'exp', [(i, i ^ offset) for i in range(lax.axis_size(...  4.54 us
    pallas_call x2, Pallas kernels, shards(): pl.pallas_call(functools.partial(experts_out_kernel, (ctx_count, exp_coun...  3.54 us
    pallas_call x1, Pallas kernels, deq_in(): pl.pallas_call(functools.partial(deq_in_kernel, ctx_count), in_specs=[pl....  3 us
  transfers between devices with their start and end apart: 48, of which 25 were waited for; matrix products, arithmetic and copies ran while one was open for 0% of the time, Pallas kernels for 10%

profile of v3, /device:TPU:0, one launch (start us, length us, event | category | flops | bytes accessed | tf_op | source)
XLA Modules:
  0.0 117.3 jit_solution(14240089790038164123)
XLA Ops:
  1.2 4.1 %collective-permute-start = (bf16[64,1408]{1,0:T(8,128)(2,1)S(1)}, bf16[64,1408]{1,0:T(8,128)(2,1)S(1)}, u32[]{:S(2)}, u32[]{:S(2)}) collective-permute-start(bf16[64,1408]{1,0:T(8,128)(2,1)S(1)} %get-tuple-element.80._.refs_0_), channel_id=1, source_target_pairs={{16,0},{17,1},{18,2},{19,3},{20,4},{21,5},{22,6},{23,7},{24,8},{25... | collective-permute-start | bytes 540680 | tf_op jit(solution)/shard_map/ppermute | solution.py:71
  5.3 1.6 %collective-permute-start.1 = (bf16[64,1408]{1,0:T(8,128)(2,1)S(1)}, bf16[64,1408]{1,0:T(8,128)(2,1)S(1)}, u32[]{:S(2)}, u32[]{:S(2)}) collective-permute-start(bf16[64,1408]{1,0:T(8,128)(2,1)S(1)} %get-tuple-element.80._.refs_0_), channel_id=1, source_target_pairs={{8,0},{5,1},{10,2},{7,3},{12,4},{1,5},{14,6},{3,7},{0,8},{13,9},{2... | collective-permute-start | bytes 540680 | tf_op jit(solution)/shard_map/ppermute | solution.py:71
  6.8 1.5 %collective-permute-start.2 = (bf16[64,1408]{1,0:T(8,128)(2,1)S(1)}, bf16[64,1408]{1,0:T(8,128)(2,1)S(1)}, u32[]{:S(2)}, u32[]{:S(2)}) collective-permute-start(bf16[64,1408]{1,0:T(8,128)(2,1)S(1)} %get-tuple-element.80._.refs_0_), channel_id=1, source_target_pairs={{4,0},{9,1},{6,2},{11,3},{0,4},{13,5},{2,6},{15,7},{12,8},{1,9},{1... | collective-permute-start | bytes 540680 | tf_op jit(solution)/shard_map/ppermute | solution.py:71
  8.7 3.0 %dequant_in.1 = (bf16[2048,768]{1,0:T(8,128)(2,1)S(1)}, bf16[2048,768]{1,0:T(8,128)(2,1)S(1)}) custom-call(s32[1]{0:T(128)} %bitcast.1.exp_ref, s32[3,1,32]{2,1,0:T(1,128)} %bitcast.25, s32[3,1,32]{2,1,0:T(1,128)} %bitcast.26, bf16[1,4096,384]{2,1,0:T(8,128)(2,1)} %gate_hbm.1, bf16[1,4096,384]{2,1,0:T(8,128)(2,1)} %up_hbm.1, ...), custom_call_target="tpu_custom_call" | custom-call | flops 3145728 | bytes 12582912 | tf_op jit(solution)/shard_map/dequant_in/pallas_call | solution.py:188
  11.7 4.9 %collective-permute-done.3.refs_9_ = bf16[4,16,512]{2,1,0:T(8,128)(2,1)S(1)} collective-permute-done((bf16[4,16,512]{2,1,0:T(8,128)(2,1)S(1)}, bf16[4,16,512]{2,1,0:T(8,128)(2,1)S(1)}, u32[]{:S(2)}, u32[]{:S(2)}) %collective-permute-start.3) | collective-permute-done | bytes 65568 | tf_op jit(solution)/shard_map/ppermute | solution.py:29
  17.4 1.5 %collective-permute-start.6 = (bf16[64,1408]{1,0:T(8,128)(2,1)S(1)}, bf16[64,1408]{1,0:T(8,128)(2,1)S(1)}, u32[]{:S(2)}, u32[]{:S(2)}) collective-permute-start(bf16[64,1408]{1,0:T(8,128)(2,1)S(1)} %collective-permute-done._.refs_4_), channel_id=1, source_target_pairs={{4,0},{9,1},{6,2},{11,3},{0,4},{13,5},{2,6},{15,7},{12,8},{1,9},{1... | collective-permute-start | bytes 540680 | tf_op jit(solution)/shard_map/ppermute | solution.py:71
  19.4 1.5 %collective-permute-start.7 = (bf16[4,16,512]{2,1,0:T(8,128)(2,1)S(1)}, bf16[4,16,512]{2,1,0:T(8,128)(2,1)S(1)}, u32[]{:S(2)}, u32[]{:S(2)}) collective-permute-start(bf16[4,16,512]{2,1,0:T(8,128)(2,1)S(1)} %pad_maximum_fusion), channel_id=1, source_target_pairs={{0,8},{4,12},{8,0},{12,4},{16,24},{20,28},{24,16},{28,20},{1,9},{5... | collective-permute-start | bytes 196616 | tf_op jit(solution)/shard_map/ppermute | solution.py:29
  20.9 2.0 %dequant_down.1 = (bf16[384,2048]{1,0:T(8,128)(2,1)S(1)}, bf16[384,2048]{1,0:T(8,128)(2,1)S(1)}) custom-call(s32[1]{0:T(128)} %bitcast.1.exp_ref, s32[3,1,32]{2,1,0:T(1,128)} %bitcast.27, bf16[1,384,4096]{2,1,0:T(8,128)(2,1)} %down_hbm.1, bf16[64,1408]{1,0:T(8,128)(2,1)S(1)} %collective-permute-done._.refs_4_), custom_call_target="tpu_custom_call" | custom-call | flops 1572864 | bytes 6291456 | tf_op jit(solution)/shard_map/dequant_down/pallas_call | solution.py:237
  22.9 2.0 %collective-permute-done.7.refs_10_ = bf16[4,16,512]{2,1,0:T(8,128)(2,1)S(1)} collective-permute-done((bf16[4,16,512]{2,1,0:T(8,128)(2,1)S(1)}, bf16[4,16,512]{2,1,0:T(8,128)(2,1)S(1)}, u32[]{:S(2)}, u32[]{:S(2)}) %collective-permute-start.7) | collective-permute-done | bytes 65568 | tf_op jit(solution)/shard_map/ppermute | solution.py:29
  25.6 1.8 %collective-permute-start.11 = (bf16[384,2048]{1,0:T(8,128)(2,1)S(1)}, bf16[384,2048]{1,0:T(8,128)(2,1)S(1)}, u32[]{:S(2)}, u32[]{:S(2)}) collective-permute-start(bf16[384,2048]{1,0:T(8,128)(2,1)S(1)} %get-tuple-element.96.refs_11_), channel_id=1, source_target_pairs={{0,1},{1,0},{2,3},{3,2},{4,5},{5,4},{6,7},{7,6},{8,9},{9,8},{10,11... | collective-permute-start | bytes 4718600 | tf_op jit(solution)/shard_map/ppermute | solution.py:25
  29.6 4.4 %collective-permute-done.10.refs_11_ = bf16[4,16,512]{2,1,0:T(8,128)(2,1)S(1)} collective-permute-done((bf16[4,16,512]{2,1,0:T(8,128)(2,1)S(1)}, bf16[4,16,512]{2,1,0:T(8,128)(2,1)S(1)}, u32[]{:S(2)}, u32[]{:S(2)}) %collective-permute-start.10) | collective-permute-done | bytes 65568 | tf_op jit(solution)/shard_map/ppermute | solution.py:29
  33.9 4.5 %attend.1 = (f32[256,256]{1,0:T(8,128)S(1)}, bf16[32,128]{1,0:T(8,128)(2,1)S(1)}, bf16[288,256]{1,0:T(8,128)(2,1)S(1)}, bf16[288,256]{1,0:T(8,128)(2,1)S(1)}, bf16[288,256]{1,0:T(8,128)(2,1)S(1)}) custom-call(s32[1]{0:T(128)} %bitcast.ctx_ref, s32[1]{0:T(128)} %bitcast.1.exp_ref, s32[8]{0:T(128)S(1)} %copy-done.2, ...), custom_call_target="tpu_custom_call" | custom-call | flops 1610612736 | bytes 8388608 | tf_op jit(solution)/shard_map/attend/pallas_call | solution.py:578
  38.6 1.6 %collective-permute-start.13 = (bf16[288,256]{1,0:T(8,128)(2,1)S(1)}, bf16[288,256]{1,0:T(8,128)(2,1)S(1)}, u32[]{:S(2)}, u32[]{:S(2)}) collective-permute-start(bf16[288,256]{1,0:T(8,128)(2,1)S(1)} %get-tuple-element.99), channel_id=1, source_target_pairs={{0,2},{1,3},{2,0},{3,1},{4,6},{5,7},{6,4},{7,5},{8,10},{9,11},{10,... | collective-permute-start | bytes 442376 | tf_op jit(solution)/shard_map/ppermute | solution.py:25
  40.4 4.8 %collective-permute-done.13.refs_2_ = bf16[288,256]{1,0:T(8,128)(2,1)S(1)} collective-permute-done((bf16[288,256]{1,0:T(8,128)(2,1)S(1)}, bf16[288,256]{1,0:T(8,128)(2,1)S(1)}, u32[]{:S(2)}, u32[]{:S(2)}) %collective-permute-start.13) | collective-permute-done | bytes 147488 | tf_op jit(solution)/shard_map/ppermute | solution.py:25
  45.3 2.3 %collective-permute-done.14.refs_3_ = bf16[288,256]{1,0:T(8,128)(2,1)S(1)} collective-permute-done((bf16[288,256]{1,0:T(8,128)(2,1)S(1)}, bf16[288,256]{1,0:T(8,128)(2,1)S(1)}, u32[]{:S(2)}, u32[]{:S(2)}) %collective-permute-start.14) | collective-permute-done | bytes 147488 | tf_op jit(solution)/shard_map/ppermute | solution.py:25
  47.6 2.5 %collective-permute-start.15 = (bf16[256,256]{1,0:T(8,128)(2,1)S(1)}, bf16[256,256]{1,0:T(8,128)(2,1)S(1)}, u32[]{:S(2)}, u32[]{:S(2)}) collective-permute-start(bf16[256,256]{1,0:T(8,128)(2,1)S(1)} %add_convert_fusion.7.refs_0_.refs_7_.refs_8_), channel_id=1, source_target_pairs={{16,0},{17,1},{18,2},{19,3},{20,4},{21,5},{22,6},{23,7},{24,8},{25... | collective-permute-start | bytes 393224 | tf_op jit(solution)/shard_map/ppermute | solution.py:71
  51.4 1.5 %collective-permute-start.17 = (bf16[256,256]{1,0:T(8,128)(2,1)S(1)}, bf16[256,256]{1,0:T(8,128)(2,1)S(1)}, u32[]{:S(2)}, u32[]{:S(2)}) collective-permute-start(bf16[256,256]{1,0:T(8,128)(2,1)S(1)} %add_convert_fusion.7.refs_0_.refs_7_.refs_8_), channel_id=1, source_target_pairs={{2,0},{5,1},{0,2},{7,3},{6,4},{1,5},{4,6},{3,7},{10,8},{13,9},{8,1... | collective-permute-start | bytes 393224 | tf_op jit(solution)/shard_map/ppermute | solution.py:71
  54.1 3.1 %collective-permute-done.15.refs_0_.refs_15_.refs_16_ = bf16[256,256]{1,0:T(8,128)(2,1)S(1)} collective-permute-done((bf16[256,256]{1,0:T(8,128)(2,1)S(1)}, bf16[256,256]{1,0:T(8,128)(2,1)S(1)}, u32[]{:S(2)}, u32[]{:S(2)}) %collective-permute-start.15) | collective-permute-done | bytes 131104 | tf_op jit(solution)/shard_map/ppermute | solution.py:71
  58.7 1.5 %collective-permute-start.20 = (bf16[256,256]{1,0:T(8,128)(2,1)S(1)}, bf16[256,256]{1,0:T(8,128)(2,1)S(1)}, u32[]{:S(2)}, u32[]{:S(2)}) collective-permute-start(bf16[256,256]{1,0:T(8,128)(2,1)S(1)} %collective-permute-done.16.refs_4_.refs_11_.refs_12_), channel_id=1, source_target_pairs={{2,0},{5,1},{0,2},{7,3},{6,4},{1,5},{4,6},{3,7},{10,8},{13,9},{8,1... | collective-permute-start | bytes 393224 | tf_op jit(solution)/shard_map/ppermute | solution.py:71
  65.6 2.4 %collective-permute-done.22.refs_1_.refs_18_ = bf16[256,256]{1,0:T(8,128)(2,1)S(1)} collective-permute-done((bf16[256,256]{1,0:T(8,128)(2,1)S(1)}, bf16[256,256]{1,0:T(8,128)(2,1)S(1)}, u32[]{:S(2)}, u32[]{:S(2)}) %collective-permute-start.22) | collective-permute-done | bytes 131104 | tf_op jit(solution)/shard_map/ppermute | solution.py:71
  69.0 1.8 %collective-permute-start.27 = (bf16[256,256]{1,0:T(8,128)(2,1)S(1)}, bf16[256,256]{1,0:T(8,128)(2,1)S(1)}, u32[]{:S(2)}, u32[]{:S(2)}) collective-permute-start(bf16[256,256]{1,0:T(8,128)(2,1)S(1)} %collective-permute-done.19.refs_4_.refs_19_.refs_20_), channel_id=1, source_target_pairs={{2,0},{5,1},{0,2},{7,3},{6,4},{1,5},{4,6},{3,7},{10,8},{13,9},{8,1... | collective-permute-start | bytes 393224 | tf_op jit(solution)/shard_map/ppermute | solution.py:71
  71.3 1.5 %collective-permute-start.24 = (bf16[256,256]{1,0:T(8,128)(2,1)S(1)}, bf16[256,256]{1,0:T(8,128)(2,1)S(1)}, u32[]{:S(2)}, u32[]{:S(2)}) collective-permute-start(bf16[256,256]{1,0:T(8,128)(2,1)S(1)} %collective-permute-done.22.refs_1_.refs_18_), channel_id=1, source_target_pairs={{4,0},{3,1},{6,2},{1,3},{0,4},{7,5},{2,6},{5,7},{12,8},{11,9},{14,... | collective-permute-start | bytes 393224 | tf_op jit(solution)/shard_map/ppermute | solution.py:71
  73.4 1.5 %collective-permute-done.27.refs_5_.refs_22_ = bf16[256,256]{1,0:T(8,128)(2,1)S(1)} collective-permute-done((bf16[256,256]{1,0:T(8,128)(2,1)S(1)}, bf16[256,256]{1,0:T(8,128)(2,1)S(1)}, u32[]{:S(2)}, u32[]{:S(2)}) %collective-permute-start.27) | collective-permute-done | bytes 131104 | tf_op jit(solution)/shard_map/ppermute | solution.py:71
  76.5 2.0 %experts_in_first.1 = (f32[512,1536]{1,0:T(8,128)S(1)}, f32[512,1]{1,0:T(8,128)S(1)}) custom-call(s32[1]{0:T(128)} %bitcast.ctx_ref, s32[1]{0:T(128)} %bitcast.1.exp_ref, bf16[256,256]{1,0:T(8,128)(2,1)S(1)} %add_convert_fusion.7.refs_0_.refs_7_.refs_8_, bf16[256,256]{1,0:T(8,128)(2,1)S(1)} %collective-permute-done.17.refs_1_.refs_10_, ...), custom_call_target="tpu_custom_call" | custom-call | flops 1610612736 | bytes 8388608 | tf_op jit(solution)/shard_map/experts_in_first/pallas_call | solution.py:621
  78.5 2.2 %collective-permute-done.29.refs_7_ = bf16[256,256]{1,0:T(8,128)(2,1)S(1)} collective-permute-done((bf16[256,256]{1,0:T(8,128)(2,1)S(1)}, bf16[256,256]{1,0:T(8,128)(2,1)S(1)}, u32[]{:S(2)}, u32[]{:S(2)}) %collective-permute-start.29) | collective-permute-done | bytes 131104 | tf_op jit(solution)/shard_map/ppermute | solution.py:71
  84.4 1.8 %experts_out.2 = (f32[32,2048]{1,0:T(8,128)S(1)}, f32[32,2048]{1,0:T(8,128)S(1)}, bf16[32,2048]{1,0:T(8,128)(2,1)S(1)}, bf16[32,2048]{1,0:T(8,128)(2,1)S(1)}, f3...) custom-call(s32[1]{0:T(128)} %bitcast.ctx_ref, ...), custom_call_target="tpu_custom_call" | custom-call | flops 805306368 | bytes 8388608 | tf_op jit(solution)/shard_map/experts_out/pallas_call | solution.py:675
  90.3 1.8 %experts_out.3 = (f32[32,2048]{1,0:T(8,128)S(1)}, f32[32,2048]{1,0:T(8,128)S(1)}, bf16[32,2048]{1,0:T(8,128)(2,1)S(1)}, bf16[32,2048]{1,0:T(8,128)(2,1)S(1)}, f3...) custom-call(s32[1]{0:T(128)} %bitcast.ctx_ref, ...), custom_call_target="tpu_custom_call" | custom-call | flops 805306368 | bytes 8388608 | tf_op jit(solution)/shard_map/experts_out/pallas_call | solution.py:675
  96.8 2.2 %collective-permute-done.36 = bf16[32,2048]{1,0:T(8,128)(2,1)S(1)} collective-permute-done((bf16[32,2048]{1,0:T(8,128)(2,1)S(1)}, bf16[32,2048]{1,0:T(8,128)(2,1)S(1)}, u32[]{:S(2)}, u32[]{:S(2)}) %collective-permute-start.36) | collective-permute-done | bytes 131104 | tf_op jit(solution)/shard_map/ppermute | solution.py:71
  101.9 1.6 %collective-permute-start.38 = (bf16[32,2048]{1,0:T(8,128)(2,1)S(1)}, bf16[32,2048]{1,0:T(8,128)(2,1)S(1)}, u32[]{:S(2)}, u32[]{:S(2)}) collective-permute-start(bf16[32,2048]{1,0:T(8,128)(2,1)S(1)} %add_convert_fusion.5), channel_id=1, source_target_pairs={{8,0},{9,1},{10,2},{11,3},{12,4},{13,5},{14,6},{15,7},{0,8},{1,9},... | collective-permute-start | bytes 393224 | tf_op jit(solution)/shard_map/ppermute | solution.py:71
  105.6 1.7 %collective-permute-done.39 = bf16[32,2048]{1,0:T(8,128)(2,1)S(1)} collective-permute-done((bf16[32,2048]{1,0:T(8,128)(2,1)S(1)}, bf16[32,2048]{1,0:T(8,128)(2,1)S(1)}, u32[]{:S(2)}, u32[]{:S(2)}) %collective-permute-start.39) | collective-permute-done | bytes 131104 | tf_op jit(solution)/shard_map/ppermute | solution.py:71
  107.4 1.8 %collective-permute-start.43 = (bf16[32,2048]{1,0:T(8,128)(2,1)S(1)}, bf16[32,2048]{1,0:T(8,128)(2,1)S(1)}, u32[]{:S(2)}, u32[]{:S(2)}) collective-permute-start(bf16[32,2048]{1,0:T(8,128)(2,1)S(1)} %add_convert_fusion.2), channel_id=1, source_target_pairs={{16,0},{17,1},{18,2},{19,3},{20,4},{21,5},{22,6},{23,7},{24,8},{25... | collective-permute-start | bytes 393224 | tf_op jit(solution)/shard_map/ppermute | solution.py:71
  109.9 5.0 %collective-permute-done.43 = bf16[32,2048]{1,0:T(8,128)(2,1)S(1)} collective-permute-done((bf16[32,2048]{1,0:T(8,128)(2,1)S(1)}, bf16[32,2048]{1,0:T(8,128)(2,1)S(1)}, u32[]{:S(2)}, u32[]{:S(2)}) %collective-permute-start.43) | collective-permute-done | bytes 131104 | tf_op jit(solution)/shard_map/ppermute | solution.py:71
  (101 shorter events, 39.7 us)
Async XLA Ops:
  1.2 15.5 %collective-permute-start = (bf16[64,1408]{1,0:T(8,128)(2,1)S(1)}, bf16[64,1408]{1,0:T(8,128)(2,1)S(1)}, u32[]{:S(2)}, u32[]{:S(2)}) collective-permute-start(bf16[64,1408]{1,0:T(8,128)(2,1)S(1)} %get-tuple-element.80._.refs_0_), channel_id=1, source_target_pairs={{16,0},{17,1},{18,2},{19,3},{20,4},{21,5},{22,6},{23,7},{24,8},{25... | collective-permute-start | bytes 540680 | tf_op jit(solution)/shard_map/ppermute | solution.py:71
  5.3 11.4 %collective-permute-start.1 = (bf16[64,1408]{1,0:T(8,128)(2,1)S(1)}, bf16[64,1408]{1,0:T(8,128)(2,1)S(1)}, u32[]{:S(2)}, u32[]{:S(2)}) collective-permute-start(bf16[64,1408]{1,0:T(8,128)(2,1)S(1)} %get-tuple-element.80._.refs_0_), channel_id=1, source_target_pairs={{8,0},{5,1},{10,2},{7,3},{12,4},{1,5},{14,6},{3,7},{0,8},{13,9},{2... | collective-permute-start | bytes 540680 | tf_op jit(solution)/shard_map/ppermute | solution.py:71
  6.8 9.8 %collective-permute-start.2 = (bf16[64,1408]{1,0:T(8,128)(2,1)S(1)}, bf16[64,1408]{1,0:T(8,128)(2,1)S(1)}, u32[]{:S(2)}, u32[]{:S(2)}) collective-permute-start(bf16[64,1408]{1,0:T(8,128)(2,1)S(1)} %get-tuple-element.80._.refs_0_), channel_id=1, source_target_pairs={{4,0},{9,1},{6,2},{11,3},{0,4},{13,5},{2,6},{15,7},{12,8},{1,9},{1... | collective-permute-start | bytes 540680 | tf_op jit(solution)/shard_map/ppermute | solution.py:71
  8.4 8.3 %collective-permute-start.3 = (bf16[4,16,512]{2,1,0:T(8,128)(2,1)S(1)}, bf16[4,16,512]{2,1,0:T(8,128)(2,1)S(1)}, u32[]{:S(2)}, u32[]{:S(2)}) collective-permute-start(bf16[4,16,512]{2,1,0:T(8,128)(2,1)S(1)} %get-tuple-element.81), channel_id=1, source_target_pairs={{0,16},{4,20},{8,24},{12,28},{16,0},{20,4},{24,8},{28,12},{1,17},{... | collective-permute-start | bytes 196616 | tf_op jit(solution)/shard_map/ppermute | solution.py:29
  16.6 9.0 %collective-permute-start.8 = (bf16[2048,768]{1,0:T(8,128)(2,1)S(1)}, bf16[2048,768]{1,0:T(8,128)(2,1)S(1)}, u32[]{:S(2)}, u32[]{:S(2)}) collective-permute-start(bf16[2048,768]{1,0:T(8,128)(2,1)S(1)} %get-tuple-element.89), channel_id=1, source_target_pairs={{0,1},{1,0},{2,3},{3,2},{4,5},{5,4},{6,7},{7,6},{8,9},{9,8},{10,11... | collective-permute-start | bytes 9437192 | tf_op jit(solution)/shard_map/ppermute | solution.py:25
  16.7 8.3 %collective-permute-start.5 = (bf16[64,1408]{1,0:T(8,128)(2,1)S(1)}, bf16[64,1408]{1,0:T(8,128)(2,1)S(1)}, u32[]{:S(2)}, u32[]{:S(2)}) collective-permute-start(bf16[64,1408]{1,0:T(8,128)(2,1)S(1)} %collective-permute-done._.refs_4_), channel_id=1, source_target_pairs={{8,0},{5,1},{10,2},{7,3},{12,4},{1,5},{14,6},{3,7},{0,8},{13,9},{2... | collective-permute-start | bytes 540680 | tf_op jit(solution)/shard_map/ppermute | solution.py:71
  17.4 7.6 %collective-permute-start.6 = (bf16[64,1408]{1,0:T(8,128)(2,1)S(1)}, bf16[64,1408]{1,0:T(8,128)(2,1)S(1)}, u32[]{:S(2)}, u32[]{:S(2)}) collective-permute-start(bf16[64,1408]{1,0:T(8,128)(2,1)S(1)} %collective-permute-done._.refs_4_), channel_id=1, source_target_pairs={{4,0},{9,1},{6,2},{11,3},{0,4},{13,5},{2,6},{15,7},{12,8},{1,9},{1... | collective-permute-start | bytes 540680 | tf_op jit(solution)/shard_map/ppermute | solution.py:71
  18.9 6.7 %collective-permute-start.4 = (bf16[64,1408]{1,0:T(8,128)(2,1)S(1)}, bf16[64,1408]{1,0:T(8,128)(2,1)S(1)}, u32[]{:S(2)}, u32[]{:S(2)}) collective-permute-start(bf16[64,1408]{1,0:T(8,128)(2,1)S(1)} %collective-permute-done.1.refs_2_), channel_id=1, source_target_pairs={{4,0},{9,1},{6,2},{11,3},{0,4},{13,5},{2,6},{15,7},{12,8},{1,9},{1... | collective-permute-start | bytes 540680 | tf_op jit(solution)/shard_map/ppermute | solution.py:71
  25.6 8.3 %collective-permute-start.11 = (bf16[384,2048]{1,0:T(8,128)(2,1)S(1)}, bf16[384,2048]{1,0:T(8,128)(2,1)S(1)}, u32[]{:S(2)}, u32[]{:S(2)}) collective-permute-start(bf16[384,2048]{1,0:T(8,128)(2,1)S(1)} %get-tuple-element.96.refs_11_), channel_id=1, source_target_pairs={{0,1},{1,0},{2,3},{3,2},{4,5},{5,4},{6,7},{7,6},{8,9},{9,8},{10,11... | collective-permute-start | bytes 4718600 | tf_op jit(solution)/shard_map/ppermute | solution.py:25
  27.4 6.5 %collective-permute-start.9 = (bf16[64,1408]{1,0:T(8,128)(2,1)S(1)}, bf16[64,1408]{1,0:T(8,128)(2,1)S(1)}, u32[]{:S(2)}, u32[]{:S(2)}) collective-permute-start(bf16[64,1408]{1,0:T(8,128)(2,1)S(1)} %collective-permute-done.5.refs_6_), channel_id=1, source_target_pairs={{4,0},{9,1},{6,2},{11,3},{0,4},{13,5},{2,6},{15,7},{12,8},{1,9},{1... | collective-permute-start | bytes 540680 | tf_op jit(solution)/shard_map/ppermute | solution.py:71
  38.6 6.7 %collective-permute-start.13 = (bf16[288,256]{1,0:T(8,128)(2,1)S(1)}, bf16[288,256]{1,0:T(8,128)(2,1)S(1)}, u32[]{:S(2)}, u32[]{:S(2)}) collective-permute-start(bf16[288,256]{1,0:T(8,128)(2,1)S(1)} %get-tuple-element.99), channel_id=1, source_target_pairs={{0,2},{1,3},{2,0},{3,1},{4,6},{5,7},{6,4},{7,5},{8,10},{9,11},{10,... | collective-permute-start | bytes 442376 | tf_op jit(solution)/shard_map/ppermute | solution.py:25
  40.1 7.4 %collective-permute-start.14 = (bf16[288,256]{1,0:T(8,128)(2,1)S(1)}, bf16[288,256]{1,0:T(8,128)(2,1)S(1)}, u32[]{:S(2)}, u32[]{:S(2)}) collective-permute-start(bf16[288,256]{1,0:T(8,128)(2,1)S(1)} %get-tuple-element.100), channel_id=1, source_target_pairs={{0,3},{1,2},{2,1},{3,0},{4,7},{5,6},{6,5},{7,4},{8,11},{9,10},{10,... | collective-permute-start | bytes 442376 | tf_op jit(solution)/shard_map/ppermute | solution.py:25
  47.6 9.6 %collective-permute-start.15 = (bf16[256,256]{1,0:T(8,128)(2,1)S(1)}, bf16[256,256]{1,0:T(8,128)(2,1)S(1)}, u32[]{:S(2)}, u32[]{:S(2)}) collective-permute-start(bf16[256,256]{1,0:T(8,128)(2,1)S(1)} %add_convert_fusion.7.refs_0_.refs_7_.refs_8_), channel_id=1, source_target_pairs={{16,0},{17,1},{18,2},{19,3},{20,4},{21,5},{22,6},{23,7},{24,8},{25... | collective-permute-start | bytes 393224 | tf_op jit(solution)/shard_map/ppermute | solution.py:71
  50.1 7.6 %collective-permute-start.16 = (bf16[256,256]{1,0:T(8,128)(2,1)S(1)}, bf16[256,256]{1,0:T(8,128)(2,1)S(1)}, u32[]{:S(2)}, u32[]{:S(2)}) collective-permute-start(bf16[256,256]{1,0:T(8,128)(2,1)S(1)} %add_convert_fusion.7.refs_0_.refs_7_.refs_8_), channel_id=1, source_target_pairs={{8,0},{9,1},{10,2},{11,3},{12,4},{13,5},{14,6},{15,7},{0,8},{1,9},... | collective-permute-start | bytes 393224 | tf_op jit(solution)/shard_map/ppermute | solution.py:71
  51.4 6.3 %collective-permute-start.17 = (bf16[256,256]{1,0:T(8,128)(2,1)S(1)}, bf16[256,256]{1,0:T(8,128)(2,1)S(1)}, u32[]{:S(2)}, u32[]{:S(2)}) collective-permute-start(bf16[256,256]{1,0:T(8,128)(2,1)S(1)} %add_convert_fusion.7.refs_0_.refs_7_.refs_8_), channel_id=1, source_target_pairs={{2,0},{5,1},{0,2},{7,3},{6,4},{1,5},{4,6},{3,7},{10,8},{13,9},{8,1... | collective-permute-start | bytes 393224 | tf_op jit(solution)/shard_map/ppermute | solution.py:71
  58.7 6.3 %collective-permute-start.20 = (bf16[256,256]{1,0:T(8,128)(2,1)S(1)}, bf16[256,256]{1,0:T(8,128)(2,1)S(1)}, u32[]{:S(2)}, u32[]{:S(2)}) collective-permute-start(bf16[256,256]{1,0:T(8,128)(2,1)S(1)} %collective-permute-done.16.refs_4_.refs_11_.refs_12_), channel_id=1, source_target_pairs={{2,0},{5,1},{0,2},{7,3},{6,4},{1,5},{4,6},{3,7},{10,8},{13,9},{8,1... | collective-permute-start | bytes 393224 | tf_op jit(solution)/shard_map/ppermute | solution.py:71
  61.6 6.4 %collective-permute-start.22 = (bf16[256,256]{1,0:T(8,128)(2,1)S(1)}, bf16[256,256]{1,0:T(8,128)(2,1)S(1)}, u32[]{:S(2)}, u32[]{:S(2)}) collective-permute-start(bf16[256,256]{1,0:T(8,128)(2,1)S(1)} %collective-permute-done.15.refs_0_.refs_15_.refs_16_), channel_id=1, source_target_pairs={{2,0},{5,1},{0,2},{7,3},{6,4},{1,5},{4,6},{3,7},{10,8},{13,9},{8,1... | collective-permute-start | bytes 393224 | tf_op jit(solution)/shard_map/ppermute | solution.py:71
  62.2 5.9 %collective-permute-start.23 = (bf16[256,256]{1,0:T(8,128)(2,1)S(1)}, bf16[256,256]{1,0:T(8,128)(2,1)S(1)}, u32[]{:S(2)}, u32[]{:S(2)}) collective-permute-start(bf16[256,256]{1,0:T(8,128)(2,1)S(1)} %collective-permute-done.15.refs_0_.refs_15_.refs_16_), channel_id=1, source_target_pairs={{4,0},{3,1},{6,2},{1,3},{0,4},{7,5},{2,6},{5,7},{12,8},{11,9},{14,... | collective-permute-start | bytes 393224 | tf_op jit(solution)/shard_map/ppermute | solution.py:71
  62.9 10.0 %collective-permute-start.25 = (bf16[256,256]{1,0:T(8,128)(2,1)S(1)}, bf16[256,256]{1,0:T(8,128)(2,1)S(1)}, u32[]{:S(2)}, u32[]{:S(2)}) collective-permute-start(bf16[256,256]{1,0:T(8,128)(2,1)S(1)} %collective-permute-done.17.refs_1_.refs_10_), channel_id=1, source_target_pairs={{4,0},{3,1},{6,2},{1,3},{0,4},{7,5},{2,6},{5,7},{12,8},{11,9},{14,... | collective-permute-start | bytes 393224 | tf_op jit(solution)/shard_map/ppermute | solution.py:71
  71.3 7.2 %collective-permute-start.24 = (bf16[256,256]{1,0:T(8,128)(2,1)S(1)}, bf16[256,256]{1,0:T(8,128)(2,1)S(1)}, u32[]{:S(2)}, u32[]{:S(2)}) collective-permute-start(bf16[256,256]{1,0:T(8,128)(2,1)S(1)} %collective-permute-done.22.refs_1_.refs_18_), channel_id=1, source_target_pairs={{4,0},{3,1},{6,2},{1,3},{0,4},{7,5},{2,6},{5,7},{12,8},{11,9},{14,... | collective-permute-start | bytes 393224 | tf_op jit(solution)/shard_map/ppermute | solution.py:71
  83.4 6.9 %collective-permute-start.33 = (bf16[256,1664]{1,0:T(8,128)(2,1)S(1)}, bf16[256,1664]{1,0:T(8,128)(2,1)S(1)}, u32[]{:S(2)}, u32[]{:S(2)}) collective-permute-start(bf16[256,1664]{1,0:T(8,128)(2,1)S(1)} %experts_in_second.3.refs_6_.act_ref), channel_id=1, source_target_pairs={{0,1},{1,0},{2,3},{3,2},{4,5},{5,4},{6,7},{7,6},{8,9},{9,8},{10,11... | collective-permute-start | bytes 2555912 | tf_op jit(solution)/shard_map/ppermute | solution.py:25
  86.1 5.9 %collective-permute-start.31 = (bf16[32,2048]{1,0:T(8,128)(2,1)S(1)}, bf16[32,2048]{1,0:T(8,128)(2,1)S(1)}, u32[]{:S(2)}, u32[]{:S(2)}) collective-permute-start(bf16[32,2048]{1,0:T(8,128)(2,1)S(1)} %get-tuple-element.120), channel_id=1, source_target_pairs={{4,0},{3,1},{6,2},{1,3},{0,4},{7,5},{2,6},{5,7},{12,8},{11,9},{14,... | collective-permute-start | bytes 393224 | tf_op jit(solution)/shard_map/ppermute | solution.py:71
  88.2 7.3 %collective-permute-start.37 = (bf16[32,2048]{1,0:T(8,128)(2,1)S(1)}, bf16[32,2048]{1,0:T(8,128)(2,1)S(1)}, u32[]{:S(2)}, u32[]{:S(2)}) collective-permute-start(bf16[32,2048]{1,0:T(8,128)(2,1)S(1)} %get-tuple-element.137), channel_id=1, source_target_pairs={{4,0},{3,1},{6,2},{1,3},{0,4},{7,5},{2,6},{5,7},{12,8},{11,9},{14,... | collective-permute-start | bytes 393224 | tf_op jit(solution)/shard_map/ppermute | solution.py:71
  88.9 14.6 %collective-permute-start.42 = (bf16[32,2048]{1,0:T(8,128)(2,1)S(1)}, bf16[32,2048]{1,0:T(8,128)(2,1)S(1)}, u32[]{:S(2)}, u32[]{:S(2)}) collective-permute-start(bf16[32,2048]{1,0:T(8,128)(2,1)S(1)} %get-tuple-element.145), channel_id=1, source_target_pairs={{4,0},{3,1},{6,2},{1,3},{0,4},{7,5},{2,6},{5,7},{12,8},{11,9},{14,... | collective-permute-start | bytes 393224 | tf_op jit(solution)/shard_map/ppermute | solution.py:71
  92.6 6.5 %collective-permute-start.36 = (bf16[32,2048]{1,0:T(8,128)(2,1)S(1)}, bf16[32,2048]{1,0:T(8,128)(2,1)S(1)}, u32[]{:S(2)}, u32[]{:S(2)}) collective-permute-start(bf16[32,2048]{1,0:T(8,128)(2,1)S(1)} %add_convert_fusion.6), channel_id=1, source_target_pairs={{2,0},{5,1},{0,2},{7,3},{6,4},{1,5},{4,6},{3,7},{10,8},{13,9},{8,1... | collective-permute-start | bytes 393224 | tf_op jit(solution)/shard_map/ppermute | solution.py:71
  93.4 6.3 %collective-permute-start.34 = (bf16[32,2048]{1,0:T(8,128)(2,1)S(1)}, bf16[32,2048]{1,0:T(8,128)(2,1)S(1)}, u32[]{:S(2)}, u32[]{:S(2)}) collective-permute-start(bf16[32,2048]{1,0:T(8,128)(2,1)S(1)} %get-tuple-element.133), channel_id=1, source_target_pairs={{4,0},{3,1},{6,2},{1,3},{0,4},{7,5},{2,6},{5,7},{12,8},{11,9},{14,... | collective-permute-start | bytes 393224 | tf_op jit(solution)/shard_map/ppermute | solution.py:71
  94.1 6.9 %collective-permute-start.35 = (bf16[32,2048]{1,0:T(8,128)(2,1)S(1)}, bf16[32,2048]{1,0:T(8,128)(2,1)S(1)}, u32[]{:S(2)}, u32[]{:S(2)}) collective-permute-start(bf16[32,2048]{1,0:T(8,128)(2,1)S(1)} %get-tuple-element.134), channel_id=1, source_target_pairs={{4,0},{3,1},{6,2},{1,3},{0,4},{7,5},{2,6},{5,7},{12,8},{11,9},{14,... | collective-permute-start | bytes 393224 | tf_op jit(solution)/shard_map/ppermute | solution.py:71
  95.5 9.1 %collective-permute-start.41 = (bf16[32,2048]{1,0:T(8,128)(2,1)S(1)}, bf16[32,2048]{1,0:T(8,128)(2,1)S(1)}, u32[]{:S(2)}, u32[]{:S(2)}) collective-permute-start(bf16[32,2048]{1,0:T(8,128)(2,1)S(1)} %add_convert_fusion.3), channel_id=1, source_target_pairs={{2,0},{5,1},{0,2},{7,3},{6,4},{1,5},{4,6},{3,7},{10,8},{13,9},{8,1... | collective-permute-start | bytes 393224 | tf_op jit(solution)/shard_map/ppermute | solution.py:71
  99.1 6.5 %collective-permute-start.40 = (bf16[32,2048]{1,0:T(8,128)(2,1)S(1)}, bf16[32,2048]{1,0:T(8,128)(2,1)S(1)}, u32[]{:S(2)}, u32[]{:S(2)}) collective-permute-start(bf16[32,2048]{1,0:T(8,128)(2,1)S(1)} %get-tuple-element.142), channel_id=1, source_target_pairs={{4,0},{3,1},{6,2},{1,3},{0,4},{7,5},{2,6},{5,7},{12,8},{11,9},{14,... | collective-permute-start | bytes 393224 | tf_op jit(solution)/shard_map/ppermute | solution.py:71
  101.0 6.3 %collective-permute-start.39 = (bf16[32,2048]{1,0:T(8,128)(2,1)S(1)}, bf16[32,2048]{1,0:T(8,128)(2,1)S(1)}, u32[]{:S(2)}, u32[]{:S(2)}) collective-permute-start(bf16[32,2048]{1,0:T(8,128)(2,1)S(1)} %add_convert_fusion.4), channel_id=1, source_target_pairs={{2,0},{5,1},{0,2},{7,3},{6,4},{1,5},{4,6},{3,7},{10,8},{13,9},{8,1... | collective-permute-start | bytes 393224 | tf_op jit(solution)/shard_map/ppermute | solution.py:71
  103.5 6.4 %collective-permute-start.46 = (bf16[32,2048]{1,0:T(8,128)(2,1)S(1)}, bf16[32,2048]{1,0:T(8,128)(2,1)S(1)}, u32[]{:S(2)}, u32[]{:S(2)}) collective-permute-start(bf16[32,2048]{1,0:T(8,128)(2,1)S(1)} %get-tuple-element.154), channel_id=1, source_target_pairs={{4,0},{3,1},{6,2},{1,3},{0,4},{7,5},{2,6},{5,7},{12,8},{11,9},{14,... | collective-permute-start | bytes 393224 | tf_op jit(solution)/shard_map/ppermute | solution.py:71
  107.4 7.4 %collective-permute-start.43 = (bf16[32,2048]{1,0:T(8,128)(2,1)S(1)}, bf16[32,2048]{1,0:T(8,128)(2,1)S(1)}, u32[]{:S(2)}, u32[]{:S(2)}) collective-permute-start(bf16[32,2048]{1,0:T(8,128)(2,1)S(1)} %add_convert_fusion.2), channel_id=1, source_target_pairs={{16,0},{17,1},{18,2},{19,3},{20,4},{21,5},{22,6},{23,7},{24,8},{25... | collective-permute-start | bytes 393224 | tf_op jit(solution)/shard_map/ppermute | solution.py:71
  (19 other events, 167.5 us)

commit v4 on v3

--- a/solution.py
+++ b/solution.py
@@ -56,7 +56,7 @@
     for number, first in enumerate(sorted(arrival)):
         held = [first]
         for moves in pairs:
-            tuned = (ctx_count, x_count) == (8, 2) and not rows_only and number in (0, 2)
+            tuned = (ctx_count, x_count) == (8, 2) and not rows_only and number == 0
             held = held + [go(source, moves, 1 if tuned and source != first else 0) for source in held]
     return sorted(transfers, key=lambda transfer: transfer[0]), places
 
@@ -77,7 +77,39 @@
 
 
 def stages_of(route):
-    return [[t for t in route if t[0] == stage] for stage in sorted({t[0] for t in route})]
+    stages, arrays = [], [((0, 0),)]
+    for stage in sorted({transfer[0] for transfer in route}):
+        sends = []
+        for moves in sorted({t[3] for t in route if t[0] == stage}):
+            left = {source: target for number, source, target, way in route if (number, way) == (stage, moves)}
+            groups = [group for group in arrays if len(group) > 1 and all(key in left for key in group)]
+            rest = tuple(sorted(key for key in left if not any(key in group for group in groups)))
+            for group in groups + [rest] * bool(rest):
+                sends.append((moves, group, tuple(left[key] for key in group)))
+        arrays = arrays + [send[2] for send in sends]
+        stages.append(sends)
+    return stages
+
+
+def spread(block, stages, beside=None):
+    arrays, at, joined = [block], {(0, 0): (0, 0)}, {}
+    rows = block.shape[0]
+    for number, sends in enumerate(stages):
+        came = []
+        for moves, group, _ in sends:
+            first, row = at[group[0]]
+            whole = row == 0 and arrays[first].shape[0] == len(group) * rows
+            if whole and all(at[key] == (first, place * rows) for place, key in enumerate(group)):
+                joined[group] = arrays[first]
+            elif group not in joined:
+                parts = [arrays[at[key][0]][at[key][1] : at[key][1] + rows] for key in group]
+                joined[group] = jnp.concatenate(parts, axis=0)
+            came.append(follow(joined[group], moves))
+        came = beside(number, came) if beside else (together(*came) if number < len(stages) - 1 else came)
+        for (_, _, targets), array in zip(sends, came):
+            at.update({key: (len(arrays), place * rows) for place, key in enumerate(targets)})
+            arrays.append(array)
+    return arrays, at
 
 
 def together(*values):
@@ -103,7 +135,7 @@
 def pack_kernel(plan, ctx_ref, exp_ref, key_scale_hbm, value_scale_hbm, query_hbm, key_hbm, value_hbm, ids_hbm,
                 route_hbm, residual_hbm, packed_ref, near_ref, far_ref, key_scale_ref, value_scale_ref,
                 key_ref, value_ref, ids_ref, route_ref, sems):
-    heads, group = plan
+    heads, group, piece_places = plan
     span, width = query_hbm.shape
     half, tok, cols = near_ref.shape
     my_ctx, my_exp = ctx_ref[0], exp_ref[0]
@@ -118,11 +150,11 @@
         (route_hbm, route_ref),
         (query_hbm, packed_ref.at[:, 2 * HEAD_SIZE : 2 * HEAD_SIZE + width]),
     ]
-    for offset in range(2 * half):
-        col = pl.multiple_of(lax.bitwise_xor(my_ctx, offset) * cols, cols)
-        pairs.append(
-            (residual_hbm.at[:, pl.ds(col, cols)], (near_ref if offset < half else far_ref).at[offset % half])
-        )
+    core = lax.bitwise_and(my_exp, 1)
+    for ref, places in zip((near_ref, far_ref), piece_places):
+        for number, place in enumerate(places):
+            col = pl.multiple_of(lax.bitwise_xor(my_ctx, by_core(core, place, 0)) * cols, cols)
+            pairs.append((residual_hbm.at[:, pl.ds(col, cols)], ref.at[number]))
     copies = copy_all(sems, pairs)
     for copy in copies[:6]:
         copy.wait()
@@ -255,15 +287,19 @@
 
 
 def attend_kernel(plan, ctx_ref, exp_ref, order_ref, *refs):
-    ctx_count, exp_count, tok, heads, piece_places, places_of = plan
-    packed, refs = refs[:ctx_count], refs[ctx_count:]
+    ctx_count, exp_count, tok, heads, piece_places, attend_at = plan
+    packed_at, places_of = [at for at, _ in attend_at], [place for _, place in attend_at]
+    array_count = 1 + max(array for array, _ in packed_at)
+    span = exp_count * tok
+    packed_refs, refs = refs[:array_count], refs[array_count:]
+    packed = []
+    for array, row in packed_at:
+        packed.append(packed_refs[array].at[pl.ds(row, span)])
     piece_refs, refs = refs[: 1 + bits_of(ctx_count)], refs[1 + bits_of(ctx_count) :]
     weight_ref, rest = refs[0], refs[2:]
-    keep_ref, own_route_ref = rest[0:2]
-    give_refs = rest[2 : 1 + exp_count]
-    key_scr, value_scr, place_scr, att_scr = rest[1 + exp_count :]
     x_count = exp_count // 2
-    span = packed[0].shape[0]
+    keep_refs, (give_ref, own_route_ref) = rest[:x_count], rest[x_count : x_count + 2]
+    key_scr, value_scr, place_scr, att_scr = rest[x_count + 2 :]
     positions = ctx_count * span
     my_ctx, my_exp = ctx_ref[0], exp_ref[0]
     my_x, my_core = lax.shift_right_logical(my_exp, 1), lax.bitwise_and(my_exp, 1)
@@ -308,21 +344,23 @@
     per_x = 2 * ctx_count * tok
     first = (heads + 2) * HEAD_SIZE
     route_lane = lax.broadcasted_iota(jnp.int32, (tok, HEAD_SIZE), 1)
-    for which in range(exp_count - 1, -1, -1):
-        side = lax.bitwise_xor(my_core, which % 2)
-        weight = weight_ref[:, pl.ds(pl.multiple_of(side * cols, cols), cols)]
-        part = jnp.dot(
-            att_scr[pl.ds(which // 2 * per_x, per_x), :], weight, preferred_element_type=jnp.float32
-        )
-        out_ref = give_refs[which - 1] if which else keep_ref
-        out_ref[0:per_x, :] = part.astype(out_ref.dtype)
-        if which < 2:
-            for offset, (array, place) in enumerate(piece_places):
-                row = (lax.bitwise_xor(my_ctx, offset) * 2 + my_core) * tok
-                at = pl.ds(pl.multiple_of(row, tok), tok)
-                piece = piece_refs[array][place, :, pl.ds(pl.multiple_of(side * cols, cols), cols)].astype(jnp.float32)
-                out_ref[at, :] = (out_ref[at, :].astype(jnp.float32) + piece).astype(out_ref.dtype)
-        expert = my_ctx * x_count + lax.bitwise_xor(my_x, which // 2)
+    route_base = x_count * per_x
+    for x_off in range(x_count):
+        rows = pl.ds(x_off * per_x, per_x)
+        for which in (1, 0):
+            side = lax.bitwise_xor(my_core, which)
+            weight = weight_ref[:, pl.ds(pl.multiple_of(side * cols, cols), cols)]
+            part = jnp.dot(att_scr[rows, :], weight, preferred_element_type=jnp.float32)
+            out_ref = give_ref if which else keep_refs[x_off]
+            out_ref[pl.ds(x_off * per_x if which else 0, per_x), :] = part.astype(out_ref.dtype)
+            if x_off == 0:
+                for (array, place), place_of in zip(piece_places, places_of):
+                    source = lax.bitwise_xor(my_ctx, by_core(my_core, place_of, 0))
+                    at = pl.ds(pl.multiple_of((source * 2 + my_core) * tok, tok), tok)
+                    piece = piece_refs[array][place, :, pl.ds(pl.multiple_of(side * cols, cols), cols)]
+                    value = out_ref[at, :].astype(jnp.float32) + piece.astype(jnp.float32)
+                    out_ref[at, :] = value.astype(out_ref.dtype)
+        expert = my_ctx * x_count + lax.bitwise_xor(my_x, x_off)
         sides = [jnp.zeros((tok, HEAD_SIZE), jnp.float32)] * 2
         for offset, ref in enumerate(packed):
             source = lax.bitwise_xor(my_ctx, by_core(my_core, places_of[offset], 0))
@@ -330,24 +368,25 @@
                 block = ref[part_of * tok : (part_of + 1) * tok, first:].astype(jnp.float32)
                 column = jnp.sum(jnp.where(route_lane == expert, block, 0.0), axis=1, keepdims=True)
                 sides[part_of] = sides[part_of] + jnp.where(route_lane == source, column, 0.0)
-        route_out, row = (give_refs[which - 1], per_x) if which else (own_route_ref, 0)
         for part_of, side in enumerate(sides):
-            at = pl.ds(row + part_of * tok, tok)
-            route_out[at, 0:HEAD_SIZE] = side.astype(jnp.bfloat16)
-            if route_out.shape[1] > HEAD_SIZE:
-                rest_shape = (tok, route_out.shape[1] - HEAD_SIZE)
-                route_out[at, HEAD_SIZE:] = jnp.zeros(rest_shape, jnp.bfloat16)
+            row = (2 * x_off + part_of) * tok
+            for ref, base in ((give_ref, route_base), (own_route_ref, 0)):
+                at = pl.ds(base + row, tok)
+                ref[at, 0:HEAD_SIZE] = side.astype(jnp.bfloat16)
+                if cols > HEAD_SIZE:
+                    ref[at, HEAD_SIZE:] = jnp.zeros((tok, cols - HEAD_SIZE), jnp.bfloat16)
 
 
 def fill_rows(plan, ctx_ref, exp_ref, gain_ref, chunk_refs, places, rows_scr, square_ref, groups):
-    ctx_count, x_count = plan
+    ctx_count, x_count, tok = plan
     half = ctx_count // 2
     my_ctx = ctx_ref[0]
     my_core = lax.bitwise_and(exp_ref[0], 1)
     mine = lax.shift_right_logical(my_ctx, bits_of(half))
-    rows, cols = chunk_refs[0].shape
-    rows = rows // 2
-    for ref, place_of in zip(chunk_refs, places):
+    cols = chunk_refs[0].shape[1]
+    rows = ctx_count * tok
+    for (array, first_row), place_of in places:
+        ref = chunk_refs[array]
         source = lax.bitwise_xor(my_ctx, by_core(my_core, place_of, 0))
         x_off = by_core(my_core, place_of, 1)
         gain_at = pl.multiple_of((source * 2 + my_core) * cols, cols)
@@ -355,7 +394,8 @@
         col = pl.multiple_of(lax.bitwise_and(source, half - 1) * cols, cols)
         for place, group in enumerate(groups):
             side = mine if group == 1 else 1 - mine
-            chunk = ref[pl.ds(pl.multiple_of(side * rows, rows), rows), :].astype(jnp.float32)
+            chunk_at = pl.ds(pl.multiple_of(first_row + side * rows, rows), rows)
+            chunk = ref[chunk_at, :].astype(jnp.float32)
             at = pl.ds(pl.multiple_of((place * x_count + x_off) * rows, rows), rows)
             rows_scr[at, pl.ds(col, cols)] = (chunk * gain).astype(jnp.bfloat16)
             square_ref[at, :] = square_ref[at, :] + jnp.sum(chunk * chunk, axis=-1, keepdims=True)
@@ -397,13 +437,12 @@
         act_ref[:, cols] = act.astype(jnp.bfloat16)
 
 
-def experts_out_kernel(plan, group, places, state_at, model_width, ctx_ref, exp_ref, act_ref, came_ref, *refs):
+def experts_out_kernel(plan, group, places, state_at, route_at, model_width, ctx_ref, exp_ref, act_ref, came_ref, *refs):
     ctx_count, exp_count, tok = plan
     x_count, half = exp_count // 2, ctx_count // 2
-    route_refs = refs[:exp_count]
-    own_ref, other_ref, _ = refs[exp_count : exp_count + 3]
-    rest = refs[exp_count + 3 :]
-    state_count = 1 + max((max(pair) for pair in state_at), default=-1)
+    route_refs, refs = refs[: x_count + 1], refs[x_count + 1 :]
+    (own_ref, other_ref, _), rest = refs[:3], refs[3:]
+    state_count = 1 + max((array for pair in state_at for array, _ in pair), default=-1)
     state_refs, rest = rest[:state_count], rest[state_count:]
     out_refs, hidden_scr = rest[:-1], rest[-1]
     my_ctx = ctx_ref[0]
@@ -414,9 +453,8 @@
     hidden = width // 2
     lane = lax.broadcasted_iota(jnp.int32, (tok, HEAD_SIZE), 1)
     blocks = []
-    for ref in route_refs:
-        row = ref.shape[0] - 2 * tok
-        both = ref[row : row + 2 * tok, 0:HEAD_SIZE].astype(jnp.float32)
+    for array, row in route_at:
+        both = route_refs[array][row : row + 2 * tok, 0:HEAD_SIZE].astype(jnp.float32)
         blocks.append(both[:tok] + both[tok:])
     columns = []
     for x_off in range(x_count):
@@ -454,14 +492,14 @@
             ref[:, at] = out[place * 2 * tok : (place + 1) * 2 * tok, :].astype(ref.dtype)
     for place, ref in zip(places, out_refs):
         if place[0] == (0, 0):
-            own_rows = pl.ds(pl.multiple_of(my_ctx * (2 * tok), 2 * tok), 2 * tok)
-            for c_off, (first, second) in enumerate(state_at):
-                cols = state_refs[first].shape[1]
+            for c_off, pair in enumerate(state_at):
+                states = []
+                for array, first_row in pair:
+                    own_row = pl.multiple_of(first_row + my_ctx * (2 * tok), 2 * tok)
+                    states.append(state_refs[array][pl.ds(own_row, 2 * tok), :].astype(jnp.float32))
+                state = states[0] if pair[0] == pair[1] else jnp.where(my_core == 0, *states)
+                cols = state.shape[1]
                 at = pl.ds(pl.multiple_of(lax.bitwise_xor(my_ctx, c_off) * cols, cols), cols)
-                state = state_refs[first][own_rows, :].astype(jnp.float32)
-                if second != first:
-                    other = state_refs[second][own_rows, :].astype(jnp.float32)
-                    state = jnp.where(my_core == 0, state, other)
                 ref[:, at] = ref[:, at] + state
 
 
@@ -504,8 +542,12 @@
 
     hbm = pl.BlockSpec(memory_space=pltpu.HBM)
     piece_shape = jax.ShapeDtypeStruct((ctx_count // 2, tok, 2 * cols), bf16)
+    row_route, row_places = gather_route(ctx_count, x_count, rows_only=True)
+    names = sorted(row_places)
+    piece_names = [[key for key in names if bool(key[0] & 2) == sent] for sent in (False, True)]
+    piece_places = tuple(tuple(row_places[key] for key in keys) for keys in piece_names)
     packed, near, far = pl.pallas_call(
-        functools.partial(pack_kernel, (heads, group)),
+        functools.partial(pack_kernel, (heads, group, piece_places)),
         in_specs=[smem] * 2 + [hbm] * 8,
         out_specs=[vmem] * 3,
         out_shape=[
@@ -538,52 +580,54 @@
             residual,
         ),
     )
-    held = {(0, 0): packed}
     piece_arrays = [near]
-    piece_at = {(0, offset): (0, offset) for offset in range(ctx_count // 2)}
-    sending, send_keys = far, [(0, offset) for offset in range(ctx_count // 2, ctx_count)]
-    row_route, row_places = gather_route(ctx_count, x_count, rows_only=True)
-    stages = stages_of(row_route)
-    for number, stage in enumerate(stages):
-        came = [follow(held[source], moves) for _, source, _, moves in stage]
-        piece_bit = bits_of(ctx_count) - 1 - number
-        came.append(from_ctx(sending, 1 << piece_bit))
+    piece_at = {(0, key[0]): (0, place) for place, key in enumerate(piece_names[0])}
+    piece_bits = [1, *range(bits_of(ctx_count) - 1, 1, -1), 0]
+    sending, weights = far, {}
+
+    def beside(number, came):
+        nonlocal sending
+        bit = 1 << piece_bits[number]
+        moves = {1: ((2, 0), (1, 0)), 0: ((1, 0), (2, 0))}.get(piece_bits[number], ((bit, 0),) * 2)
         if number == 0:
-            in_own, in_give = deq_in(
-                my_exp, gate_weight, gate_scale, up_weight, up_scale, ctx_count, packed
+            keys = [(0, key[0]) for key in piece_names[1]]
+        else:
+            keys = sorted(key for key in piece_at if key[1] & bit)
+            sending = jnp.stack([piece_arrays[array][place] for array, place in map(piece_at.pop, keys)])
+        pieces = follow(sending, moves)
+        if number == 0:
+            own, give = deq_in(my_exp, gate_weight, gate_scale, up_weight, up_scale, ctx_count, packed)
+            *came, pieces, weights["in_own"], weights["in_give"] = together(*came, pieces, own, give)
+        elif number == 1:
+            other = from_offset(weights["in_give"], 1)
+            own, give = deq_down(my_exp, down_weight, down_scale, ctx_count, piece_arrays[-1])
+            *came, pieces, weights["in_other"], weights["down_own"], weights["down_give"] = together(
+                *came, pieces, other, own, give
             )
-            *came, in_own, in_give = together(*came, in_own, in_give)
-        elif number == 1:
-            in_other = from_offset(in_give, 1)
-            down_own, down_give = deq_down(my_exp, down_weight, down_scale, ctx_count, came_first)
-            *came, in_other, down_own, down_give = together(*came, in_other, down_own, down_give)
-        elif number < len(stages) - 1:
-            came = together(*came)
-        came_first = came[0]
-        held.update({target: array for (_, _, target, _), array in zip(stage, came)})
-        piece_arrays.append(came[-1])
-        for place, (source, target) in enumerate(send_keys):
-            piece_at[source ^ 1 << piece_bit, target ^ 1 << piece_bit] = (number + 1, place)
-        if piece_bit:
-            below = 1 << piece_bit
-            send_keys = sorted(key for key in piece_at if below // 2 <= key[1] < below)
-            sending = jnp.stack([piece_arrays[array][place] for array, place in map(piece_at.get, send_keys)])
-    packed = [held[offset, 0] for offset in range(ctx_count)]
-    attend_places = tuple(row_places[offset, 0] for offset in range(ctx_count))
-    piece_places = tuple(piece_at[offset, 0] for offset in range(ctx_count))
-    down_other = from_offset(down_give, 1)
+        elif number < len(piece_bits) - 1:
+            *came, pieces = together(*came, pieces)
+        for place, (source, target) in enumerate(keys):
+            piece_at[source ^ bit, target ^ bit] = (len(piece_arrays), place)
+        piece_arrays.append(pieces)
+        return came
+
+    packed, packed_at = spread(packed, stages_of(row_route), beside)
+    attend_at = tuple((packed_at[key], row_places[key]) for key in names)
+    attend_pieces = tuple(piece_at[key[0], 0] for key in names)
+    in_own, in_other, down_own = weights["in_own"], weights["in_other"], weights["down_own"]
+    down_other = from_offset(weights["down_give"], 1)
 
     positions = ctx_count * span
     per_x = 2 * ctx_count * tok
-    keep, own_route, *gives = pl.pallas_call(
-        functools.partial(attend_kernel, (ctx_count, exp_count, tok, heads, piece_places, attend_places)),
-        in_specs=[smem] * 3 + [vmem] * (ctx_count + len(piece_arrays) + 1) + [anywhere],
-        out_specs=[vmem] * (1 + exp_count),
-        out_shape=[
-            jax.ShapeDtypeStruct((per_x, cols), f32),
-            jax.ShapeDtypeStruct((2 * tok, HEAD_SIZE), bf16),
-        ]
-        + [jax.ShapeDtypeStruct((per_x + 2 * tok, cols), bf16)] * (exp_count - 1),
+    *keeps, give, own_route = pl.pallas_call(
+        functools.partial(attend_kernel, (ctx_count, exp_count, tok, heads, attend_pieces, attend_at)),
+        in_specs=[smem] * 3 + [vmem] * (len(packed) + len(piece_arrays) + 1) + [anywhere],
+        out_specs=[vmem] * (2 + x_count),
+        out_shape=[jax.ShapeDtypeStruct((per_x, cols), f32)] * x_count
+        + [
+            jax.ShapeDtypeStruct((x_count * (per_x + 2 * tok), cols), bf16),
+            jax.ShapeDtypeStruct((x_count * 2 * tok, cols), bf16),
+        ],
         scratch_shapes=[
             pltpu.VMEM((positions, HEAD_SIZE), bf16),
             pltpu.VMEM((positions, HEAD_SIZE), bf16),
@@ -599,28 +643,38 @@
         name="attend",
     )(my_ctx, my_exp, block_order, *packed, *piece_arrays, out_weight, down_other)
 
-    gives = {offset: from_offset(gives[offset - 1], offset) for offset in reversed(range(1, exp_count))}
-    gives = [gives[offset] for offset in range(1, exp_count)]
-    state = keep
-    for give in gives:
-        state = state + give[:per_x].astype(f32)
+    given = from_offset(give, 1)
+    routes, route_at, state = [own_route, given], [(0, 0), (1, x_count * per_x)], keeps[0]
+    state = state + given[:per_x].astype(f32)
+    for x_off in range(1, x_count):
+        part = keeps[x_off] + given[x_off * per_x : (x_off + 1) * per_x].astype(f32)
+        row = x_count * per_x + x_off * 2 * tok
+        own = own_route[x_off * 2 * tok : (x_off + 1) * 2 * tok]
+        sent = jnp.concatenate([part.astype(bf16), own, given[row : row + 2 * tok]], axis=0)
+        came = from_offset(sent, 2 * x_off)
+        state = state + came[:per_x].astype(f32)
+        route_at += [(len(routes), per_x), (len(routes), per_x + 2 * tok)]
+        routes.append(came)
     state = state.astype(bf16)
 
-    chunks = {(0, 0): state}
-    for stage in stages_of(route):
-        came = [follow(chunks[source], moves) for _, source, _, moves in stage]
-        if stage[-1] != route[-1]:
-            came = together(*came)
-        chunks.update({target: array for (_, _, target, _), array in zip(stage, came)})
+    stages = stages_of(route)
+    chunks, chunk_at = spread(state, stages)
     gain = norm_gain.reshape(1, model_width)
     rows = x_count * per_x
     in_width = in_own.shape[1]
-    near = tuple(sorted(key for key in chunks if key[0] < ctx_count // 2))
-    far = tuple(sorted(key for key in chunks if key[0] >= ctx_count // 2))
-    near_places, far_places = (tuple(places[key] for key in keys) for keys in (near, far))
+    near = tuple(sorted(key for key in places if key[0] < ctx_count // 2))
+    far = tuple(sorted(key for key in places if key[0] >= ctx_count // 2))
+
+    def picked(keys):
+        arrays = sorted({chunk_at[key][0] for key in keys})
+        at = tuple(((arrays.index(chunk_at[key][0]), chunk_at[key][1]), places[key]) for key in keys)
+        return [chunks[array] for array in arrays], at
+
+    near_chunks, near_places = picked(near)
+    far_chunks, far_places = picked(far)
     first_act, first_square = pl.pallas_call(
-        functools.partial(experts_in_first, (ctx_count, x_count), near_places),
-        in_specs=[smem] * 2 + [vmem] * (len(near) + 3) + [anywhere],
+        functools.partial(experts_in_first, (ctx_count, x_count, tok), near_places),
+        in_specs=[smem] * 2 + [vmem] * (len(near_chunks) + 3) + [anywhere],
         out_specs=[vmem] * 2,
         out_shape=[
             jax.ShapeDtypeStruct((rows, 2 * in_width), f32),
@@ -632,13 +686,13 @@
             flops=2 * rows * half_width * in_width, bytes_accessed=8 * MIB, transcendentals=0
         ),
         name="experts_in_first",
-    )(my_ctx, my_exp, *[chunks[key] for key in near], gain, in_own, in_other, down_give)
+    )(my_ctx, my_exp, *near_chunks, gain, in_own, in_other, down_other)
     acts = []
     for part in range(2):
         acts.append(
             pl.pallas_call(
-                functools.partial(experts_in_second, (ctx_count, x_count), far_places, part),
-                in_specs=[smem] * 2 + [vmem] * (len(far) + 5) + [anywhere],
+                functools.partial(experts_in_second, (ctx_count, x_count, tok), far_places, part),
+                in_specs=[smem] * 2 + [vmem] * (len(far_chunks) + 5) + [anywhere],
                 out_specs=vmem,
                 out_shape=jax.ShapeDtypeStruct((rows // 2, 2 * in_width + HEAD_SIZE), bf16),
                 scratch_shapes=[
@@ -653,7 +707,7 @@
             )(
                 my_ctx,
                 my_exp,
-                *[chunks[key] for key in far],
+                *far_chunks,
                 gain,
                 in_own,
                 in_other,
@@ -662,26 +716,28 @@
                 acts[0] if part else first_square,
             )
         )
-    leaves = set(chunks) - {source for _, source, _, _ in route}
+    leaves = set(places) - {source for _, source, _, _ in route}
     sums = {}
     for part in range(2):
         slots = near if part == 1 else far
-        state_keys, state_at = [], []
-        for offset in range(ctx_count) if part == 1 else ():
-            pair = [next(key for key in chunks if places[key][core] == (offset, 0)) for core in range(2)]
-            state_keys += [key for key in pair if key not in state_keys]
-            state_at.append(tuple(state_keys.index(key) for key in pair))
-        states = [chunks[key] for key in state_keys]
+        state_keys = [
+            next(key for key in places if places[key][core] == (offset, 0))
+            for offset in (range(ctx_count) if part == 1 else ())
+            for core in range(2)
+        ]
+        states, state_at = picked(state_keys)
+        state_at = tuple((state_at[i][0], state_at[i + 1][0]) for i in range(0, len(state_at), 2))
         outs = pl.pallas_call(
             functools.partial(
                 experts_out_kernel,
                 (ctx_count, exp_count, tok),
                 part,
                 tuple(places[key] for key in slots),
-                tuple(state_at),
+                state_at,
+                tuple(route_at),
                 model_width,
             ),
-            in_specs=[smem] * 2 + [vmem] * (4 + exp_count) + [anywhere] + [vmem] * len(states),
+            in_specs=[smem] * 2 + [vmem] * (5 + x_count) + [anywhere] + [vmem] * len(states),
             out_specs=[vmem] * len(slots),
             out_shape=[
                 jax.ShapeDtypeStruct((2 * tok, half_width), bf16 if slot in leaves else f32)
@@ -700,8 +756,7 @@
             my_exp,
             acts[part],
             from_offset(acts[part], 1),
-            own_route,
-            *gives,
+            *routes,
             down_own,
             down_other,
             sums[slots_done[0]] if part else acts[1],
@@ -710,16 +765,20 @@
         slots_done = slots
         sums.update(zip(slots, outs))
 
-    backward = stages_of(route)[::-1]
-    for number, stage in enumerate(backward):
-        came = [follow(sums[target].astype(bf16), moves) for _, _, target, moves in stage]
-        if number < len(backward) - 1:
-            waiting = [key for key in near if key in sums] if number == 0 else []
+    for number, sends in enumerate(reversed(stages)):
+        came = []
+        for moves, _, targets in sends:
+            sent = [sums[key].astype(bf16) for key in targets]
+            came.append(follow(sent[0] if len(sent) == 1 else jnp.concatenate(sent, axis=0), moves))
+        if number < len(stages) - 1:
+            waiting = list(near) if number == 0 else []
             values = together(*came, *[sums[key] for key in waiting])
             came = values[: len(came)]
             sums.update(zip(waiting, values[len(came) :]))
-        for (_, source, target, _), array in zip(stage, came):
-            sums[source] = sums[source] + array.astype(f32)
+        for (_, sources, _), array in zip(sends, came):
+            for place, key in enumerate(sources):
+                part = array[place * 2 * tok : (place + 1) * 2 * tok]
+                sums[key] = sums[key] + part.astype(f32)
     total = sums[0, 0]
     core = lax.bitwise_and(my_exp[0], 1)
     mine = jnp.where(core == 0, total[:tok], total[tok:]).astype(bf16)

time: 117 us -> 120 us (1.026)
  waiting for transfers between devices: 44.5 us -> 65.8 us
  starting transfers between devices: 52.3 us -> 33.6 us
    ppermute x37 -> x31, waiting for transfers between devices: 24.4 us -> 57.7 us  [follow(): return lax.ppermute(array, ('ctx', 'exp'), pairs)]
    ppermute x37 -> x31, starting transfers between devices: 45.1 us -> 30.5 us  [follow(): return lax.ppermute(array, ('ctx', 'exp'), pairs)]
    ppermute x3 -> x0, waiting for transfers between devices: 11.3 us -> none  [from_ctx(): lax.ppermute(array, 'ctx', [(i, i ^ offset) for i in range(lax.axis_size(...]
    ppermute x3 -> x0, starting transfers between devices: 2.68 us -> none  [from_ctx(): lax.ppermute(array, 'ctx', [(i, i ^ offset) for i in range(lax.axis_size(...]
    ppermute x8 -> x7, starting transfers between devices: 4.54 us -> 3.05 us  [from_offset(): lax.ppermute(array, 'exp', [(i, i ^ offset) for i in range(lax.axis_size(...]
    ppermute x8 -> x7, waiting for transfers between devices: 8.76 us -> 8.15 us  [from_offset(): lax.ppermute(array, 'exp', [(i, i ^ offset) for i in range(lax.axis_size(...]
  transfers between devices with their start and end apart: 48 -> 38, of which waited for: 25 -> 26; matrix products, arithmetic and copies ran while one was open for 0% -> 0% of each run, Pallas kernels for 10% -> 10%
where the time goes in v4:
time: 120 us
  waiting for transfers between devices  65.8 us (55%)
  starting transfers between devices  33.6 us (28%)
  Pallas kernels  18.8 us (16%)
    ppermute x31, waiting for transfers between devices, follow(): return lax.ppermute(array, ('ctx', 'exp'), pairs)  57.7 us
    ppermute x31, starting transfers between devices, follow(): return lax.ppermute(array, ('ctx', 'exp'), pairs)  30.5 us
    ppermute x7, waiting for transfers between devices, from_offset(): lax.ppermute(array, 'exp', [(i, i ^ offset) for i in range(lax.axis_size(...  8.15 us
    pallas_call x1, Pallas kernels, shards(): pl.pallas_call(functools.partial(attend_kernel, (ctx_count, exp_count, to...  4.49 us
    pallas_call x2, Pallas kernels, shards(): pl.pallas_call(functools.partial(experts_out_kernel, (ctx_count, exp_coun...  3.72 us
    ppermute x7, starting transfers between devices, from_offset(): lax.ppermute(array, 'exp', [(i, i ^ offset) for i in range(lax.axis_size(...  3.05 us
    pallas_call x1, Pallas kernels, deq_in(): pl.pallas_call(functools.partial(deq_in_kernel, ctx_count), in_specs=[pl....  3 us
  transfers between devices with their start and end apart: 38, of which 26 were waited for; matrix products, arithmetic and copies ran while one was open for 0% of the time, Pallas kernels for 10%

profile of v4, /device:TPU:0, one launch (start us, length us, event | category | flops | bytes accessed | tf_op | source)
XLA Modules:
  0.0 120.0 jit_solution(11281145548721289169)
XLA Ops:
  1.2 3.0 %collective-permute-start = (bf16[64,1408]{1,0:T(8,128)(2,1)S(1)}, bf16[64,1408]{1,0:T(8,128)(2,1)S(1)}, u32[]{:S(2)}, u32[]{:S(2)}) collective-permute-start(bf16[64,1408]{1,0:T(8,128)(2,1)S(1)} %get-tuple-element.71._.refs_0_), channel_id=1, source_target_pairs={{4,0},{9,1},{6,2},{11,3},{0,4},{13,5},{2,6},{15,7},{12,8},{1,9},{1... | collective-permute-start | bytes 540680 | tf_op jit(solution)/shard_map/ppermute | solution.py:71
  4.2 1.6 %collective-permute-start.1 = (bf16[64,1408]{1,0:T(8,128)(2,1)S(1)}, bf16[64,1408]{1,0:T(8,128)(2,1)S(1)}, u32[]{:S(2)}, u32[]{:S(2)}) collective-permute-start(bf16[64,1408]{1,0:T(8,128)(2,1)S(1)} %get-tuple-element.71._.refs_0_), channel_id=1, source_target_pairs={{8,0},{5,1},{10,2},{7,3},{12,4},{1,5},{14,6},{3,7},{0,8},{13,9},{2... | collective-permute-start | bytes 540680 | tf_op jit(solution)/shard_map/ppermute | solution.py:71
  5.8 2.6 %collective-permute-start.2 = (bf16[64,1408]{1,0:T(8,128)(2,1)S(1)}, bf16[64,1408]{1,0:T(8,128)(2,1)S(1)}, u32[]{:S(2)}, u32[]{:S(2)}) collective-permute-start(bf16[64,1408]{1,0:T(8,128)(2,1)S(1)} %get-tuple-element.71._.refs_0_), channel_id=1, source_target_pairs={{16,0},{17,1},{18,2},{19,3},{20,4},{21,5},{22,6},{23,7},{24,8},{25... | collective-permute-start | bytes 540680 | tf_op jit(solution)/shard_map/ppermute | solution.py:71
  8.8 3.0 %dequant_in.1 = (bf16[2048,768]{1,0:T(8,128)(2,1)S(1)}, bf16[2048,768]{1,0:T(8,128)(2,1)S(1)}) custom-call(s32[1]{0:T(128)} %bitcast.1.exp_ref, s32[3,1,32]{2,1,0:T(1,128)} %bitcast.25, s32[3,1,32]{2,1,0:T(1,128)} %bitcast.26, bf16[1,4096,384]{2,1,0:T(8,128)(2,1)} %gate_hbm.1, bf16[1,4096,384]{2,1,0:T(8,128)(2,1)} %up_hbm.1, ...), custom_call_target="tpu_custom_call" | custom-call | flops 3145728 | bytes 12582912 | tf_op jit(solution)/shard_map/dequant_in/pallas_call | solution.py:220
  11.8 1.8 %collective-permute-done.3._.refs_8_ = bf16[4,16,512]{2,1,0:T(8,128)(2,1)S(1)} collective-permute-done((bf16[4,16,512]{2,1,0:T(8,128)(2,1)S(1)}, bf16[4,16,512]{2,1,0:T(8,128)(2,1)S(1)}, u32[]{:S(2)}, u32[]{:S(2)}) %collective-permute-start.3) | collective-permute-done | bytes 65568 | tf_op jit(solution)/shard_map/ppermute | solution.py:71
  13.6 2.6 %collective-permute-done.2.refs_3_ = bf16[64,1408]{1,0:T(8,128)(2,1)S(1)} collective-permute-done((bf16[64,1408]{1,0:T(8,128)(2,1)S(1)}, bf16[64,1408]{1,0:T(8,128)(2,1)S(1)}, u32[]{:S(2)}, u32[]{:S(2)}) %collective-permute-start.2) | collective-permute-done | bytes 180256 | tf_op jit(solution)/shard_map/ppermute | solution.py:71
  17.2 2.9 %collective-permute-start.6 = (bf16[4,16,512]{2,1,0:T(8,128)(2,1)S(1)}, bf16[4,16,512]{2,1,0:T(8,128)(2,1)S(1)}, u32[]{:S(2)}, u32[]{:S(2)}) collective-permute-start(bf16[4,16,512]{2,1,0:T(8,128)(2,1)S(1)} %pad_maximum_fusion.7), channel_id=1, source_target_pairs={{16,0},{17,1},{18,2},{19,3},{20,4},{21,5},{22,6},{23,7},{24,8},{25... | collective-permute-start | bytes 196616 | tf_op jit(solution)/shard_map/ppermute | solution.py:71
  20.0 2.0 %dequant_down.1 = (bf16[384,2048]{1,0:T(8,128)(2,1)S(1)}, bf16[384,2048]{1,0:T(8,128)(2,1)S(1)}) custom-call(s32[1]{0:T(128)} %bitcast.1.exp_ref, s32[3,1,32]{2,1,0:T(1,128)} %bitcast.27, bf16[1,384,4096]{2,1,0:T(8,128)(2,1)} %down_hbm.1, bf16[4,16,512]{2,1,0:T(8,128)(2,1)S(1)} %collective-permute-done.3._.refs_8_), custom_call_target="tpu_custom_call" | custom-call | flops 1572864 | bytes 6291456 | tf_op jit(solution)/shard_map/dequant_down/pallas_call | solution.py:269
  23.5 2.3 %collective-permute-done.5.refs_5_ = bf16[64,1408]{1,0:T(8,128)(2,1)S(1)} collective-permute-done((bf16[64,1408]{1,0:T(8,128)(2,1)S(1)}, bf16[64,1408]{1,0:T(8,128)(2,1)S(1)}, u32[]{:S(2)}, u32[]{:S(2)}) %collective-permute-start.5) | collective-permute-done | bytes 180256 | tf_op jit(solution)/shard_map/ppermute | solution.py:71
  28.6 4.1 %collective-permute-done.9.refs_10_ = bf16[4,16,512]{2,1,0:T(8,128)(2,1)S(1)} collective-permute-done((bf16[4,16,512]{2,1,0:T(8,128)(2,1)S(1)}, bf16[4,16,512]{2,1,0:T(8,128)(2,1)S(1)}, u32[]{:S(2)}, u32[]{:S(2)}) %collective-permute-start.9) | collective-permute-done | bytes 65568 | tf_op jit(solution)/shard_map/ppermute | solution.py:71
  32.7 4.5 %attend.1 = (f32[256,256]{1,0:T(8,128)S(1)}, f32[256,256]{1,0:T(8,128)S(1)}, bf16[576,256]{1,0:T(8,128)(2,1)S(1)}, bf16[64,256]{1,0:T(8,128)(2,1)S(1)}) custom-call(s32[1]{0:T(128)} %bitcast.ctx_ref, s32[1]{0:T(128)} %bitcast.1.exp_ref, s32[8]{0:T(128)S(1)} %copy-done.2, bf16[64,1408]{1,0:T(8,128)(2,1)S(1)} %get-tuple-element.71._.refs_0_, ...), custom_call_target="tpu_custom_call" | custom-call | flops 1610612736 | bytes 8388608 | tf_op jit(solution)/shard_map/attend/pallas_call | solution.py:622
  37.3 1.6 %collective-permute-done.11.refs_1_ = bf16[576,256]{1,0:T(8,128)(2,1)S(1)} collective-permute-done((bf16[576,256]{1,0:T(8,128)(2,1)S(1)}, bf16[576,256]{1,0:T(8,128)(2,1)S(1)}, u32[]{:S(2)}, u32[]{:S(2)}) %collective-permute-start.11) | collective-permute-done | bytes 294944 | tf_op jit(solution)/shard_map/ppermute | solution.py:25
  38.9 1.6 %collective-permute-start.12 = (bf16[320,256]{1,0:T(8,128)(2,1)S(1)}, bf16[320,256]{1,0:T(8,128)(2,1)S(1)}, u32[]{:S(2)}, u32[]{:S(2)}) collective-permute-start(bf16[320,256]{1,0:T(8,128)(2,1)S(1)} %pad_maximum_fusion.6), channel_id=1, source_target_pairs={{0,2},{1,3},{2,0},{3,1},{4,6},{5,7},{6,4},{7,5},{8,10},{9,11},{10,... | collective-permute-start | bytes 491528 | tf_op jit(solution)/shard_map/ppermute | solution.py:25
  40.5 4.7 %collective-permute-done.12.refs_2_ = bf16[320,256]{1,0:T(8,128)(2,1)S(1)} collective-permute-done((bf16[320,256]{1,0:T(8,128)(2,1)S(1)}, bf16[320,256]{1,0:T(8,128)(2,1)S(1)}, u32[]{:S(2)}, u32[]{:S(2)}) %collective-permute-start.12) | collective-permute-done | bytes 163872 | tf_op jit(solution)/shard_map/ppermute | solution.py:25
  45.3 1.6 %collective-permute-start.13 = (bf16[256,256]{1,0:T(8,128)(2,1)S(1)}, bf16[256,256]{1,0:T(8,128)(2,1)S(1)}, u32[]{:S(2)}, u32[]{:S(2)}) collective-permute-start(bf16[256,256]{1,0:T(8,128)(2,1)S(1)} %add_convert_fusion.7.refs_0_.refs_6_), channel_id=1, source_target_pairs={{2,0},{5,1},{0,2},{7,3},{6,4},{1,5},{4,6},{3,7},{10,8},{13,9},{8,1... | collective-permute-start | bytes 393224 | tf_op jit(solution)/shard_map/ppermute | solution.py:71
  48.8 1.9 %collective-permute-start.16 = (bf16[256,256]{1,0:T(8,128)(2,1)S(1)}, bf16[256,256]{1,0:T(8,128)(2,1)S(1)}, u32[]{:S(2)}, u32[]{:S(2)}) collective-permute-start(bf16[256,256]{1,0:T(8,128)(2,1)S(1)} %add_convert_fusion.7.refs_0_.refs_6_), channel_id=1, source_target_pairs={{16,0},{17,1},{18,2},{19,3},{20,4},{21,5},{22,6},{23,7},{24,8},{25... | collective-permute-start | bytes 393224 | tf_op jit(solution)/shard_map/ppermute | solution.py:71
  53.3 3.1 %collective-permute-done.16.refs_0_.refs_10_ = bf16[256,256]{1,0:T(8,128)(2,1)S(1)} collective-permute-done((bf16[256,256]{1,0:T(8,128)(2,1)S(1)}, bf16[256,256]{1,0:T(8,128)(2,1)S(1)}, u32[]{:S(2)}, u32[]{:S(2)}) %collective-permute-start.16) | collective-permute-done | bytes 131104 | tf_op jit(solution)/shard_map/ppermute | solution.py:71
  58.5 5.0 %collective-permute-done.19.refs_3_.refs_13_ = bf16[256,256]{1,0:T(8,128)(2,1)S(1)} collective-permute-done((bf16[256,256]{1,0:T(8,128)(2,1)S(1)}, bf16[256,256]{1,0:T(8,128)(2,1)S(1)}, u32[]{:S(2)}, u32[]{:S(2)}) %collective-permute-start.19) | collective-permute-done | bytes 131104 | tf_op jit(solution)/shard_map/ppermute | solution.py:71
  65.3 1.7 %collective-permute-start.21 = (bf16[512,256]{1,0:T(8,128)(2,1)S(1)}, bf16[512,256]{1,0:T(8,128)(2,1)S(1)}, u32[]{:S(2)}, u32[]{:S(2)}) collective-permute-start(bf16[512,256]{1,0:T(8,128)(2,1)S(1)} %collective-permute-done.17.refs_4_.refs_1_.refs_11_), channel_id=1, source_target_pairs={{4,0},{3,1},{6,2},{1,3},{0,4},{7,5},{2,6},{5,7},{12,8},{11,9},{14,... | collective-permute-start | bytes 786440 | tf_op jit(solution)/shard_map/ppermute | solution.py:71
  67.5 5.9 %collective-permute-done.20.refs_4_.refs_14_ = bf16[256,256]{1,0:T(8,128)(2,1)S(1)} collective-permute-done((bf16[256,256]{1,0:T(8,128)(2,1)S(1)}, bf16[256,256]{1,0:T(8,128)(2,1)S(1)}, u32[]{:S(2)}, u32[]{:S(2)}) %collective-permute-start.20) | collective-permute-done | bytes 131104 | tf_op jit(solution)/shard_map/ppermute | solution.py:71
  73.4 1.9 %collective-permute-done.21.refs_6_.refs_5_ = bf16[512,256]{1,0:T(8,128)(2,1)S(1)} collective-permute-done((bf16[512,256]{1,0:T(8,128)(2,1)S(1)}, bf16[512,256]{1,0:T(8,128)(2,1)S(1)}, u32[]{:S(2)}, u32[]{:S(2)}) %collective-permute-start.21) | collective-permute-done | bytes 262176 | tf_op jit(solution)/shard_map/ppermute | solution.py:71
  75.5 2.0 %experts_in_first.1 = (f32[512,1536]{1,0:T(8,128)S(1)}, f32[512,1]{1,0:T(8,128)S(1)}) custom-call(s32[1]{0:T(128)} %bitcast.ctx_ref, s32[1]{0:T(128)} %bitcast.1.exp_ref, bf16[256,256]{1,0:T(8,128)(2,1)S(1)} %add_convert_fusion.7.refs_0_.refs_6_, bf16[256,256]{1,0:T(8,128)(2,1)S(1)} %collective-permute-done.13.refs_1_.refs_7_, ...), custom_call_target="tpu_custom_call" | custom-call | flops 1610612736 | bytes 8388608 | tf_op jit(solution)/shard_map/experts_in_first/pallas_call | solution.py:675
  77.5 2.7 %collective-permute-done.23.refs_7_ = bf16[256,256]{1,0:T(8,128)(2,1)S(1)} collective-permute-done((bf16[256,256]{1,0:T(8,128)(2,1)S(1)}, bf16[256,256]{1,0:T(8,128)(2,1)S(1)}, u32[]{:S(2)}, u32[]{:S(2)}) %collective-permute-start.23) | collective-permute-done | bytes 131104 | tf_op jit(solution)/shard_map/ppermute | solution.py:71
  83.8 1.9 %experts_out.2 = (f32[32,2048]{1,0:T(8,128)S(1)}, f32[32,2048]{1,0:T(8,128)S(1)}, bf16[32,2048]{1,0:T(8,128)(2,1)S(1)}, bf16[32,2048]{1,0:T(8,128)(2,1)S(1)}, f3...) custom-call(s32[1]{0:T(128)} %bitcast.ctx_ref, ...), custom_call_target="tpu_custom_call" | custom-call | flops 805306368 | bytes 8388608 | tf_op jit(solution)/shard_map/experts_out/pallas_call | solution.py:730
  86.1 1.8 %experts_out.3 = (f32[32,2048]{1,0:T(8,128)S(1)}, f32[32,2048]{1,0:T(8,128)S(1)}, bf16[32,2048]{1,0:T(8,128)(2,1)S(1)}, bf16[32,2048]{1,0:T(8,128)(2,1)S(1)}, f3...) custom-call(s32[1]{0:T(128)} %bitcast.ctx_ref, ...), custom_call_target="tpu_custom_call" | custom-call | flops 805306368 | bytes 8388608 | tf_op jit(solution)/shard_map/experts_out/pallas_call | solution.py:730
  87.9 2.9 %collective-permute-done.25 = bf16[32,2048]{1,0:T(8,128)(2,1)S(1)} collective-permute-done((bf16[32,2048]{1,0:T(8,128)(2,1)S(1)}, bf16[32,2048]{1,0:T(8,128)(2,1)S(1)}, u32[]{:S(2)}, u32[]{:S(2)}) %collective-permute-start.25) | collective-permute-done | bytes 131104 | tf_op jit(solution)/shard_map/ppermute | solution.py:71
  91.2 1.8 %collective-permute-start.28 = (bf16[64,2048]{1,0:T(8,128)(2,1)S(1)}, bf16[64,2048]{1,0:T(8,128)(2,1)S(1)}, u32[]{:S(2)}, u32[]{:S(2)}) collective-permute-start(bf16[64,2048]{1,0:T(8,128)(2,1)S(1)} %pad_maximum_fusion.2), channel_id=1, source_target_pairs={{4,0},{3,1},{6,2},{1,3},{0,4},{7,5},{2,6},{5,7},{12,8},{11,9},{14,... | collective-permute-start | bytes 786440 | tf_op jit(solution)/shard_map/ppermute | solution.py:71
  94.0 5.5 %collective-permute-done.27 = bf16[32,2048]{1,0:T(8,128)(2,1)S(1)} collective-permute-done((bf16[32,2048]{1,0:T(8,128)(2,1)S(1)}, bf16[32,2048]{1,0:T(8,128)(2,1)S(1)}, u32[]{:S(2)}, u32[]{:S(2)}) %collective-permute-start.27) | collective-permute-done | bytes 131104 | tf_op jit(solution)/shard_map/ppermute | solution.py:71
  99.6 1.9 %collective-permute-done.28 = bf16[64,2048]{1,0:T(8,128)(2,1)S(1)} collective-permute-done((bf16[64,2048]{1,0:T(8,128)(2,1)S(1)}, bf16[64,2048]{1,0:T(8,128)(2,1)S(1)}, u32[]{:S(2)}, u32[]{:S(2)}) %collective-permute-start.28) | collective-permute-done | bytes 262176 | tf_op jit(solution)/shard_map/ppermute | solution.py:71
  104.1 1.7 %collective-permute-done.33 = bf16[64,2048]{1,0:T(8,128)(2,1)S(1)} collective-permute-done((bf16[64,2048]{1,0:T(8,128)(2,1)S(1)}, bf16[64,2048]{1,0:T(8,128)(2,1)S(1)}, u32[]{:S(2)}, u32[]{:S(2)}) %collective-permute-start.33) | collective-permute-done | bytes 262176 | tf_op jit(solution)/shard_map/ppermute | solution.py:71
  109.4 5.6 %collective-permute-done.35 = bf16[32,2048]{1,0:T(8,128)(2,1)S(1)} collective-permute-done((bf16[32,2048]{1,0:T(8,128)(2,1)S(1)}, bf16[32,2048]{1,0:T(8,128)(2,1)S(1)}, u32[]{:S(2)}, u32[]{:S(2)}) %collective-permute-start.35) | collective-permute-done | bytes 131104 | tf_op jit(solution)/shard_map/ppermute | solution.py:71
  115.0 2.7 %collective-permute-done.36 = bf16[32,2048]{1,0:T(8,128)(2,1)S(1)} collective-permute-done((bf16[32,2048]{1,0:T(8,128)(2,1)S(1)}, bf16[32,2048]{1,0:T(8,128)(2,1)S(1)}, u32[]{:S(2)}, u32[]{:S(2)}) %collective-permute-start.36) | collective-permute-done | bytes 131104 | tf_op jit(solution)/shard_map/ppermute | solution.py:71
  (90 shorter events, 30.1 us)
Async XLA Ops:
  1.2 12.5 %collective-permute-start = (bf16[64,1408]{1,0:T(8,128)(2,1)S(1)}, bf16[64,1408]{1,0:T(8,128)(2,1)S(1)}, u32[]{:S(2)}, u32[]{:S(2)}) collective-permute-start(bf16[64,1408]{1,0:T(8,128)(2,1)S(1)} %get-tuple-element.71._.refs_0_), channel_id=1, source_target_pairs={{4,0},{9,1},{6,2},{11,3},{0,4},{13,5},{2,6},{15,7},{12,8},{1,9},{1... | collective-permute-start | bytes 540680 | tf_op jit(solution)/shard_map/ppermute | solution.py:71
  4.2 9.4 %collective-permute-start.1 = (bf16[64,1408]{1,0:T(8,128)(2,1)S(1)}, bf16[64,1408]{1,0:T(8,128)(2,1)S(1)}, u32[]{:S(2)}, u32[]{:S(2)}) collective-permute-start(bf16[64,1408]{1,0:T(8,128)(2,1)S(1)} %get-tuple-element.71._.refs_0_), channel_id=1, source_target_pairs={{8,0},{5,1},{10,2},{7,3},{12,4},{1,5},{14,6},{3,7},{0,8},{13,9},{2... | collective-permute-start | bytes 540680 | tf_op jit(solution)/shard_map/ppermute | solution.py:71
  5.8 10.5 %collective-permute-start.2 = (bf16[64,1408]{1,0:T(8,128)(2,1)S(1)}, bf16[64,1408]{1,0:T(8,128)(2,1)S(1)}, u32[]{:S(2)}, u32[]{:S(2)}) collective-permute-start(bf16[64,1408]{1,0:T(8,128)(2,1)S(1)} %get-tuple-element.71._.refs_0_), channel_id=1, source_target_pairs={{16,0},{17,1},{18,2},{19,3},{20,4},{21,5},{22,6},{23,7},{24,8},{25... | collective-permute-start | bytes 540680 | tf_op jit(solution)/shard_map/ppermute | solution.py:71
  8.4 5.3 %collective-permute-start.3 = (bf16[4,16,512]{2,1,0:T(8,128)(2,1)S(1)}, bf16[4,16,512]{2,1,0:T(8,128)(2,1)S(1)}, u32[]{:S(2)}, u32[]{:S(2)}) collective-permute-start(bf16[4,16,512]{2,1,0:T(8,128)(2,1)S(1)} %get-tuple-element.72), channel_id=1, source_target_pairs={{8,0},{5,1},{10,2},{7,3},{12,4},{1,5},{14,6},{3,7},{0,8},{13,9},{2... | collective-permute-start | bytes 196616 | tf_op jit(solution)/shard_map/ppermute | solution.py:71
  16.3 9.5 %collective-permute-start.7 = (bf16[2048,768]{1,0:T(8,128)(2,1)S(1)}, bf16[2048,768]{1,0:T(8,128)(2,1)S(1)}, u32[]{:S(2)}, u32[]{:S(2)}) collective-permute-start(bf16[2048,768]{1,0:T(8,128)(2,1)S(1)} %get-tuple-element.80), channel_id=1, source_target_pairs={{0,1},{1,0},{2,3},{3,2},{4,5},{5,4},{6,7},{7,6},{8,9},{9,8},{10,11... | collective-permute-start | bytes 9437192 | tf_op jit(solution)/shard_map/ppermute | solution.py:25
  16.3 9.4 %collective-permute-start.4 = (bf16[128,1408]{1,0:T(8,128)(2,1)S(1)}, bf16[128,1408]{1,0:T(8,128)(2,1)S(1)}, u32[]{:S(2)}, u32[]{:S(2)}) collective-permute-start(bf16[128,1408]{1,0:T(8,128)(2,1)S(1)} %pad_maximum_fusion), channel_id=1, source_target_pairs={{4,0},{9,1},{6,2},{11,3},{0,4},{13,5},{2,6},{15,7},{12,8},{1,9},{1... | collective-permute-start | bytes 1081352 | tf_op jit(solution)/shard_map/ppermute | solution.py:71
  16.9 8.8 %collective-permute-start.5 = (bf16[64,1408]{1,0:T(8,128)(2,1)S(1)}, bf16[64,1408]{1,0:T(8,128)(2,1)S(1)}, u32[]{:S(2)}, u32[]{:S(2)}) collective-permute-start(bf16[64,1408]{1,0:T(8,128)(2,1)S(1)} %collective-permute-done.2.refs_3_), channel_id=1, source_target_pairs={{8,0},{5,1},{10,2},{7,3},{12,4},{1,5},{14,6},{3,7},{0,8},{13,9},{2... | collective-permute-start | bytes 540680 | tf_op jit(solution)/shard_map/ppermute | solution.py:71
  17.2 6.3 %collective-permute-start.6 = (bf16[4,16,512]{2,1,0:T(8,128)(2,1)S(1)}, bf16[4,16,512]{2,1,0:T(8,128)(2,1)S(1)}, u32[]{:S(2)}, u32[]{:S(2)}) collective-permute-start(bf16[4,16,512]{2,1,0:T(8,128)(2,1)S(1)} %pad_maximum_fusion.7), channel_id=1, source_target_pairs={{16,0},{17,1},{18,2},{19,3},{20,4},{21,5},{22,6},{23,7},{24,8},{25... | collective-permute-start | bytes 196616 | tf_op jit(solution)/shard_map/ppermute | solution.py:71
  25.7 6.9 %collective-permute-start.10 = (bf16[384,2048]{1,0:T(8,128)(2,1)S(1)}, bf16[384,2048]{1,0:T(8,128)(2,1)S(1)}, u32[]{:S(2)}, u32[]{:S(2)}) collective-permute-start(bf16[384,2048]{1,0:T(8,128)(2,1)S(1)} %get-tuple-element.86), channel_id=1, source_target_pairs={{0,1},{1,0},{2,3},{3,2},{4,5},{5,4},{6,7},{7,6},{8,9},{9,8},{10,11... | collective-permute-start | bytes 4718600 | tf_op jit(solution)/shard_map/ppermute | solution.py:25
  26.5 6.2 %collective-permute-start.8 = (bf16[64,1408]{1,0:T(8,128)(2,1)S(1)}, bf16[64,1408]{1,0:T(8,128)(2,1)S(1)}, u32[]{:S(2)}, u32[]{:S(2)}) collective-permute-start(bf16[64,1408]{1,0:T(8,128)(2,1)S(1)} %collective-permute-done.5.refs_5_), channel_id=1, source_target_pairs={{4,0},{9,1},{6,2},{11,3},{0,4},{13,5},{2,6},{15,7},{12,8},{1,9},{1... | collective-permute-start | bytes 540680 | tf_op jit(solution)/shard_map/ppermute | solution.py:71
  27.3 5.3 %collective-permute-start.9 = (bf16[4,16,512]{2,1,0:T(8,128)(2,1)S(1)}, bf16[4,16,512]{2,1,0:T(8,128)(2,1)S(1)}, u32[]{:S(2)}, u32[]{:S(2)}) collective-permute-start(bf16[4,16,512]{2,1,0:T(8,128)(2,1)S(1)} %pad_maximum_fusion.8), channel_id=1, source_target_pairs={{4,0},{9,1},{6,2},{11,3},{0,4},{13,5},{2,6},{15,7},{12,8},{1,9},{1... | collective-permute-start | bytes 196616 | tf_op jit(solution)/shard_map/ppermute | solution.py:71
  38.9 6.3 %collective-permute-start.12 = (bf16[320,256]{1,0:T(8,128)(2,1)S(1)}, bf16[320,256]{1,0:T(8,128)(2,1)S(1)}, u32[]{:S(2)}, u32[]{:S(2)}) collective-permute-start(bf16[320,256]{1,0:T(8,128)(2,1)S(1)} %pad_maximum_fusion.6), channel_id=1, source_target_pairs={{0,2},{1,3},{2,0},{3,1},{4,6},{5,7},{6,4},{7,5},{8,10},{9,11},{10,... | collective-permute-start | bytes 491528 | tf_op jit(solution)/shard_map/ppermute | solution.py:25
  45.3 5.4 %collective-permute-start.13 = (bf16[256,256]{1,0:T(8,128)(2,1)S(1)}, bf16[256,256]{1,0:T(8,128)(2,1)S(1)}, u32[]{:S(2)}, u32[]{:S(2)}) collective-permute-start(bf16[256,256]{1,0:T(8,128)(2,1)S(1)} %add_convert_fusion.7.refs_0_.refs_6_), channel_id=1, source_target_pairs={{2,0},{5,1},{0,2},{7,3},{6,4},{1,5},{4,6},{3,7},{10,8},{13,9},{8,1... | collective-permute-start | bytes 393224 | tf_op jit(solution)/shard_map/ppermute | solution.py:71
  46.8 5.0 %collective-permute-start.14 = (bf16[256,256]{1,0:T(8,128)(2,1)S(1)}, bf16[256,256]{1,0:T(8,128)(2,1)S(1)}, u32[]{:S(2)}, u32[]{:S(2)}) collective-permute-start(bf16[256,256]{1,0:T(8,128)(2,1)S(1)} %add_convert_fusion.7.refs_0_.refs_6_), channel_id=1, source_target_pairs={{4,0},{3,1},{6,2},{1,3},{0,4},{7,5},{2,6},{5,7},{12,8},{11,9},{14,... | collective-permute-start | bytes 393224 | tf_op jit(solution)/shard_map/ppermute | solution.py:71
  47.7 5.7 %collective-permute-start.15 = (bf16[256,256]{1,0:T(8,128)(2,1)S(1)}, bf16[256,256]{1,0:T(8,128)(2,1)S(1)}, u32[]{:S(2)}, u32[]{:S(2)}) collective-permute-start(bf16[256,256]{1,0:T(8,128)(2,1)S(1)} %add_convert_fusion.7.refs_0_.refs_6_), channel_id=1, source_target_pairs={{8,0},{9,1},{10,2},{11,3},{12,4},{13,5},{14,6},{15,7},{0,8},{1,9},... | collective-permute-start | bytes 393224 | tf_op jit(solution)/shard_map/ppermute | solution.py:71
  48.8 7.6 %collective-permute-start.16 = (bf16[256,256]{1,0:T(8,128)(2,1)S(1)}, bf16[256,256]{1,0:T(8,128)(2,1)S(1)}, u32[]{:S(2)}, u32[]{:S(2)}) collective-permute-start(bf16[256,256]{1,0:T(8,128)(2,1)S(1)} %add_convert_fusion.7.refs_0_.refs_6_), channel_id=1, source_target_pairs={{16,0},{17,1},{18,2},{19,3},{20,4},{21,5},{22,6},{23,7},{24,8},{25... | collective-permute-start | bytes 393224 | tf_op jit(solution)/shard_map/ppermute | solution.py:71
  56.4 8.4 %collective-permute-start.17 = (bf16[512,256]{1,0:T(8,128)(2,1)S(1)}, bf16[512,256]{1,0:T(8,128)(2,1)S(1)}, u32[]{:S(2)}, u32[]{:S(2)}) collective-permute-start(bf16[512,256]{1,0:T(8,128)(2,1)S(1)} %constant_dynamic-update-slice_fusion), channel_id=1, source_target_pairs={{2,0},{5,1},{0,2},{7,3},{6,4},{1,5},{4,6},{3,7},{10,8},{13,9},{8,1... | collective-permute-start | bytes 786440 | tf_op jit(solution)/shard_map/ppermute | solution.py:71
  57.0 7.8 %collective-permute-start.18 = (bf16[512,256]{1,0:T(8,128)(2,1)S(1)}, bf16[512,256]{1,0:T(8,128)(2,1)S(1)}, u32[]{:S(2)}, u32[]{:S(2)}) collective-permute-start(bf16[512,256]{1,0:T(8,128)(2,1)S(1)} %constant_dynamic-update-slice_fusion), channel_id=1, source_target_pairs={{4,0},{3,1},{6,2},{1,3},{0,4},{7,5},{2,6},{5,7},{12,8},{11,9},{14,... | collective-permute-start | bytes 786440 | tf_op jit(solution)/shard_map/ppermute | solution.py:71
  64.8 8.5 %collective-permute-start.22 = (bf16[512,256]{1,0:T(8,128)(2,1)S(1)}, bf16[512,256]{1,0:T(8,128)(2,1)S(1)}, u32[]{:S(2)}, u32[]{:S(2)}) collective-permute-start(bf16[512,256]{1,0:T(8,128)(2,1)S(1)} %pad_maximum_fusion.1), channel_id=1, source_target_pairs={{4,0},{3,1},{6,2},{1,3},{0,4},{7,5},{2,6},{5,7},{12,8},{11,9},{14,... | collective-permute-start | bytes 786440 | tf_op jit(solution)/shard_map/ppermute | solution.py:71
  65.3 10.0 %collective-permute-start.21 = (bf16[512,256]{1,0:T(8,128)(2,1)S(1)}, bf16[512,256]{1,0:T(8,128)(2,1)S(1)}, u32[]{:S(2)}, u32[]{:S(2)}) collective-permute-start(bf16[512,256]{1,0:T(8,128)(2,1)S(1)} %collective-permute-done.17.refs_4_.refs_1_.refs_11_), channel_id=1, source_target_pairs={{4,0},{3,1},{6,2},{1,3},{0,4},{7,5},{2,6},{5,7},{12,8},{11,9},{14,... | collective-permute-start | bytes 786440 | tf_op jit(solution)/shard_map/ppermute | solution.py:71
  66.9 6.4 %collective-permute-start.20 = (bf16[256,256]{1,0:T(8,128)(2,1)S(1)}, bf16[256,256]{1,0:T(8,128)(2,1)S(1)}, u32[]{:S(2)}, u32[]{:S(2)}) collective-permute-start(bf16[256,256]{1,0:T(8,128)(2,1)S(1)} %collective-permute-done.19.refs_3_.refs_13_), channel_id=1, source_target_pairs={{2,0},{5,1},{0,2},{7,3},{6,4},{1,5},{4,6},{3,7},{10,8},{13,9},{8,1... | collective-permute-start | bytes 393224 | tf_op jit(solution)/shard_map/ppermute | solution.py:71
  85.8 5.0 %collective-permute-start.25 = (bf16[32,2048]{1,0:T(8,128)(2,1)S(1)}, bf16[32,2048]{1,0:T(8,128)(2,1)S(1)}, u32[]{:S(2)}, u32[]{:S(2)}) collective-permute-start(bf16[32,2048]{1,0:T(8,128)(2,1)S(1)} %get-tuple-element.106), channel_id=1, source_target_pairs={{4,0},{3,1},{6,2},{1,3},{0,4},{7,5},{2,6},{5,7},{12,8},{11,9},{14,... | collective-permute-start | bytes 393224 | tf_op jit(solution)/shard_map/ppermute | solution.py:71
  90.8 8.7 %collective-permute-start.29 = (bf16[64,2048]{1,0:T(8,128)(2,1)S(1)}, bf16[64,2048]{1,0:T(8,128)(2,1)S(1)}, u32[]{:S(2)}, u32[]{:S(2)}) collective-permute-start(bf16[64,2048]{1,0:T(8,128)(2,1)S(1)} %pad_maximum_fusion.3), channel_id=1, source_target_pairs={{4,0},{3,1},{6,2},{1,3},{0,4},{7,5},{2,6},{5,7},{12,8},{11,9},{14,... | collective-permute-start | bytes 786440 | tf_op jit(solution)/shard_map/ppermute | solution.py:71
  91.2 10.2 %collective-permute-start.28 = (bf16[64,2048]{1,0:T(8,128)(2,1)S(1)}, bf16[64,2048]{1,0:T(8,128)(2,1)S(1)}, u32[]{:S(2)}, u32[]{:S(2)}) collective-permute-start(bf16[64,2048]{1,0:T(8,128)(2,1)S(1)} %pad_maximum_fusion.2), channel_id=1, source_target_pairs={{4,0},{3,1},{6,2},{1,3},{0,4},{7,5},{2,6},{5,7},{12,8},{11,9},{14,... | collective-permute-start | bytes 786440 | tf_op jit(solution)/shard_map/ppermute | solution.py:71
  93.0 6.5 %collective-permute-start.27 = (bf16[32,2048]{1,0:T(8,128)(2,1)S(1)}, bf16[32,2048]{1,0:T(8,128)(2,1)S(1)}, u32[]{:S(2)}, u32[]{:S(2)}) collective-permute-start(bf16[32,2048]{1,0:T(8,128)(2,1)S(1)} %add_convert_fusion.6), channel_id=1, source_target_pairs={{2,0},{5,1},{0,2},{7,3},{6,4},{1,5},{4,6},{3,7},{10,8},{13,9},{8,1... | collective-permute-start | bytes 393224 | tf_op jit(solution)/shard_map/ppermute | solution.py:71
  93.7 12.1 %collective-permute-start.33 = (bf16[64,2048]{1,0:T(8,128)(2,1)S(1)}, bf16[64,2048]{1,0:T(8,128)(2,1)S(1)}, u32[]{:S(2)}, u32[]{:S(2)}) collective-permute-start(bf16[64,2048]{1,0:T(8,128)(2,1)S(1)} %pad_maximum_fusion.5), channel_id=1, source_target_pairs={{4,0},{3,1},{6,2},{1,3},{0,4},{7,5},{2,6},{5,7},{12,8},{11,9},{14,... | collective-permute-start | bytes 786440 | tf_op jit(solution)/shard_map/ppermute | solution.py:71
  101.5 6.4 %collective-permute-start.32 = (bf16[64,2048]{1,0:T(8,128)(2,1)S(1)}, bf16[64,2048]{1,0:T(8,128)(2,1)S(1)}, u32[]{:S(2)}, u32[]{:S(2)}) collective-permute-start(bf16[64,2048]{1,0:T(8,128)(2,1)S(1)} %pad_maximum_fusion.4), channel_id=1, source_target_pairs={{2,0},{5,1},{0,2},{7,3},{6,4},{1,5},{4,6},{3,7},{10,8},{13,9},{8,1... | collective-permute-start | bytes 786440 | tf_op jit(solution)/shard_map/ppermute | solution.py:71
  102.2 5.0 %collective-permute-start.34 = (bf16[32,2048]{1,0:T(8,128)(2,1)S(1)}, bf16[32,2048]{1,0:T(8,128)(2,1)S(1)}, u32[]{:S(2)}, u32[]{:S(2)}) collective-permute-start(bf16[32,2048]{1,0:T(8,128)(2,1)S(1)} %get-tuple-element.140), channel_id=1, source_target_pairs={{8,0},{9,1},{10,2},{11,3},{12,4},{13,5},{14,6},{15,7},{0,8},{1,9},... | collective-permute-start | bytes 393224 | tf_op jit(solution)/shard_map/ppermute | solution.py:71
  102.3 6.6 %collective-permute-start.31 = (bf16[32,2048]{1,0:T(8,128)(2,1)S(1)}, bf16[32,2048]{1,0:T(8,128)(2,1)S(1)}, u32[]{:S(2)}, u32[]{:S(2)}) collective-permute-start(bf16[32,2048]{1,0:T(8,128)(2,1)S(1)} %get-tuple-element.125), channel_id=1, source_target_pairs={{4,0},{3,1},{6,2},{1,3},{0,4},{7,5},{2,6},{5,7},{12,8},{11,9},{14,... | collective-permute-start | bytes 393224 | tf_op jit(solution)/shard_map/ppermute | solution.py:71
  102.6 6.7 %collective-permute-start.30 = (bf16[32,2048]{1,0:T(8,128)(2,1)S(1)}, bf16[32,2048]{1,0:T(8,128)(2,1)S(1)}, u32[]{:S(2)}, u32[]{:S(2)}) collective-permute-start(bf16[32,2048]{1,0:T(8,128)(2,1)S(1)} %get-tuple-element.139), channel_id=1, source_target_pairs={{2,0},{5,1},{0,2},{7,3},{6,4},{1,5},{4,6},{3,7},{10,8},{13,9},{8,1... | collective-permute-start | bytes 393224 | tf_op jit(solution)/shard_map/ppermute | solution.py:71
  108.1 6.9 %collective-permute-start.35 = (bf16[32,2048]{1,0:T(8,128)(2,1)S(1)}, bf16[32,2048]{1,0:T(8,128)(2,1)S(1)}, u32[]{:S(2)}, u32[]{:S(2)}) collective-permute-start(bf16[32,2048]{1,0:T(8,128)(2,1)S(1)} %get-tuple-element.137), channel_id=1, source_target_pairs={{8,0},{9,1},{10,2},{11,3},{12,4},{13,5},{14,6},{15,7},{0,8},{1,9},... | collective-permute-start | bytes 393224 | tf_op jit(solution)/shard_map/ppermute | solution.py:71
  108.1 9.5 %collective-permute-start.36 = (bf16[32,2048]{1,0:T(8,128)(2,1)S(1)}, bf16[32,2048]{1,0:T(8,128)(2,1)S(1)}, u32[]{:S(2)}, u32[]{:S(2)}) collective-permute-start(bf16[32,2048]{1,0:T(8,128)(2,1)S(1)} %get-tuple-element.138), channel_id=1, source_target_pairs={{16,0},{17,1},{18,2},{19,3},{20,4},{21,5},{22,6},{23,7},{24,8},{25... | collective-permute-start | bytes 393224 | tf_op jit(solution)/shard_map/ppermute | solution.py:71
  (9 other events, 108.8 us)

commit v5 on v4

--- a/solution.py
+++ b/solution.py
@@ -78,6 +78,7 @@
 
 def stages_of(route):
     stages, arrays = [], [((0, 0),)]
+    top = max(moves[0][0] for _, _, _, moves in route)
     for stage in sorted({transfer[0] for transfer in route}):
         sends = []
         for moves in sorted({t[3] for t in route if t[0] == stage}):
@@ -86,6 +87,7 @@
             rest = tuple(sorted(key for key in left if not any(key in group for group in groups)))
             for group in groups + [rest] * bool(rest):
                 sends.append((moves, group, tuple(left[key] for key in group)))
+        sends.sort(key=lambda send: -len(send[1]) * (2 if send[0][0][0] == top > 2 else 1))
         arrays = arrays + [send[2] for send in sends]
         stages.append(sends)
     return stages

time: 120 us -> 117 us (0.975)
  waiting for transfers between devices: 65.8 us -> 59.7 us
  starting transfers between devices: 33.6 us -> 36.2 us
    ppermute x31, waiting for transfers between devices: 57.7 us -> 51.6 us  [follow(): return lax.ppermute(array, ('ctx', 'exp'), pairs)]
    ppermute x31, starting transfers between devices: 30.5 us -> 33.3 us  [follow(): return lax.ppermute(array, ('ctx', 'exp'), pairs)]
  transfers between devices with their start and end apart: 38 -> 38, of which waited for: 26 -> 23; matrix products, arithmetic and copies ran while one was open for 0% -> 0% of each run, Pallas kernels for 10% -> 10%
where the time goes in v5:
time: 117 us
  waiting for transfers between devices  59.7 us (51%)
  starting transfers between devices  36.2 us (31%)
  Pallas kernels  18.8 us (16%)
    ppermute x31, waiting for transfers between devices, follow(): return lax.ppermute(array, ('ctx', 'exp'), pairs)  51.6 us
    ppermute x31, starting transfers between devices, follow(): return lax.ppermute(array, ('ctx', 'exp'), pairs)  33.3 us
    ppermute x7, waiting for transfers between devices, from_offset(): lax.ppermute(array, 'exp', [(i, i ^ offset) for i in range(lax.axis_size(...  8.1 us
    pallas_call x1, Pallas kernels, shards(): pl.pallas_call(functools.partial(attend_kernel, (ctx_count, exp_count, to...  4.49 us
    pallas_call x2, Pallas kernels, shards(): pl.pallas_call(functools.partial(experts_out_kernel, (ctx_count, exp_coun...  3.72 us
    pallas_call x1, Pallas kernels, deq_in(): pl.pallas_call(functools.partial(deq_in_kernel, ctx_count), in_specs=[pl....  3 us
    ppermute x7, starting transfers between devices, from_offset(): lax.ppermute(array, 'exp', [(i, i ^ offset) for i in range(lax.axis_size(...  2.9 us
    pallas_call x2, Pallas kernels, shards(): pl.pallas_call(functools.partial(experts_in_second, (ctx_count, x_count,...  2.38 us
  transfers between devices with their start and end apart: 38, of which 23 were waited for; matrix products, arithmetic and copies ran while one was open for 0% of the time, Pallas kernels for 10%

profile of v5, /device:TPU:0, one launch (start us, length us, event | category | flops | bytes accessed | tf_op | source)
XLA Modules:
  0.0 116.6 jit_solution(17849898057917478477)
XLA Ops:
  1.2 4.1 %collective-permute-start = (bf16[64,1408]{1,0:T(8,128)(2,1)S(1)}, bf16[64,1408]{1,0:T(8,128)(2,1)S(1)}, u32[]{:S(2)}, u32[]{:S(2)}) collective-permute-start(bf16[64,1408]{1,0:T(8,128)(2,1)S(1)} %get-tuple-element.71._.refs_0_), channel_id=1, source_target_pairs={{16,0},{17,1},{18,2},{19,3},{20,4},{21,5},{22,6},{23,7},{24,8},{25... | collective-permute-start | bytes 540680 | tf_op jit(solution)/shard_map/ppermute | solution.py:71
  5.3 1.5 %collective-permute-start.1 = (bf16[64,1408]{1,0:T(8,128)(2,1)S(1)}, bf16[64,1408]{1,0:T(8,128)(2,1)S(1)}, u32[]{:S(2)}, u32[]{:S(2)}) collective-permute-start(bf16[64,1408]{1,0:T(8,128)(2,1)S(1)} %get-tuple-element.71._.refs_0_), channel_id=1, source_target_pairs={{4,0},{9,1},{6,2},{11,3},{0,4},{13,5},{2,6},{15,7},{12,8},{1,9},{1... | collective-permute-start | bytes 540680 | tf_op jit(solution)/shard_map/ppermute | solution.py:71
  6.8 1.6 %collective-permute-start.2 = (bf16[64,1408]{1,0:T(8,128)(2,1)S(1)}, bf16[64,1408]{1,0:T(8,128)(2,1)S(1)}, u32[]{:S(2)}, u32[]{:S(2)}) collective-permute-start(bf16[64,1408]{1,0:T(8,128)(2,1)S(1)} %get-tuple-element.71._.refs_0_), channel_id=1, source_target_pairs={{8,0},{5,1},{10,2},{7,3},{12,4},{1,5},{14,6},{3,7},{0,8},{13,9},{2... | collective-permute-start | bytes 540680 | tf_op jit(solution)/shard_map/ppermute | solution.py:71
  8.8 3.0 %dequant_in.1 = (bf16[2048,768]{1,0:T(8,128)(2,1)S(1)}, bf16[2048,768]{1,0:T(8,128)(2,1)S(1)}) custom-call(s32[1]{0:T(128)} %bitcast.1.exp_ref, s32[3,1,32]{2,1,0:T(1,128)} %bitcast.25, s32[3,1,32]{2,1,0:T(1,128)} %bitcast.26, bf16[1,4096,384]{2,1,0:T(8,128)(2,1)} %gate_hbm.1, bf16[1,4096,384]{2,1,0:T(8,128)(2,1)} %up_hbm.1, ...), custom_call_target="tpu_custom_call" | custom-call | flops 3145728 | bytes 12582912 | tf_op jit(solution)/shard_map/dequant_in/pallas_call | solution.py:222
  11.8 3.6 %collective-permute-done.3._.refs_8_ = bf16[4,16,512]{2,1,0:T(8,128)(2,1)S(1)} collective-permute-done((bf16[4,16,512]{2,1,0:T(8,128)(2,1)S(1)}, bf16[4,16,512]{2,1,0:T(8,128)(2,1)S(1)}, u32[]{:S(2)}, u32[]{:S(2)}) %collective-permute-start.3) | collective-permute-done | bytes 65568 | tf_op jit(solution)/shard_map/ppermute | solution.py:71
  16.4 1.4 %collective-permute-start.5 = (bf16[64,1408]{1,0:T(8,128)(2,1)S(1)}, bf16[64,1408]{1,0:T(8,128)(2,1)S(1)}, u32[]{:S(2)}, u32[]{:S(2)}) collective-permute-start(bf16[64,1408]{1,0:T(8,128)(2,1)S(1)} %collective-permute-done.refs_1_), channel_id=1, source_target_pairs={{8,0},{5,1},{10,2},{7,3},{12,4},{1,5},{14,6},{3,7},{0,8},{13,9},{2... | collective-permute-start | bytes 540680 | tf_op jit(solution)/shard_map/ppermute | solution.py:71
  17.9 1.6 %collective-permute-start.6 = (bf16[4,16,512]{2,1,0:T(8,128)(2,1)S(1)}, bf16[4,16,512]{2,1,0:T(8,128)(2,1)S(1)}, u32[]{:S(2)}, u32[]{:S(2)}) collective-permute-start(bf16[4,16,512]{2,1,0:T(8,128)(2,1)S(1)} %pad_maximum_fusion.7), channel_id=1, source_target_pairs={{16,0},{17,1},{18,2},{19,3},{20,4},{21,5},{22,6},{23,7},{24,8},{25... | collective-permute-start | bytes 196616 | tf_op jit(solution)/shard_map/ppermute | solution.py:71
  19.5 2.1 %dequant_down.1 = (bf16[384,2048]{1,0:T(8,128)(2,1)S(1)}, bf16[384,2048]{1,0:T(8,128)(2,1)S(1)}) custom-call(s32[1]{0:T(128)} %bitcast.1.exp_ref, s32[3,1,32]{2,1,0:T(1,128)} %bitcast.27, bf16[1,384,4096]{2,1,0:T(8,128)(2,1)} %down_hbm.1, bf16[4,16,512]{2,1,0:T(8,128)(2,1)S(1)} %collective-permute-done.3._.refs_8_), custom_call_target="tpu_custom_call" | custom-call | flops 1572864 | bytes 6291456 | tf_op jit(solution)/shard_map/dequant_down/pallas_call | solution.py:271
  21.6 2.6 %collective-permute-done.6.refs_9_ = bf16[4,16,512]{2,1,0:T(8,128)(2,1)S(1)} collective-permute-done((bf16[4,16,512]{2,1,0:T(8,128)(2,1)S(1)}, bf16[4,16,512]{2,1,0:T(8,128)(2,1)S(1)}, u32[]{:S(2)}, u32[]{:S(2)}) %collective-permute-start.6) | collective-permute-done | bytes 65568 | tf_op jit(solution)/shard_map/ppermute | solution.py:71
  27.9 4.1 %collective-permute-done.9.refs_10_ = bf16[4,16,512]{2,1,0:T(8,128)(2,1)S(1)} collective-permute-done((bf16[4,16,512]{2,1,0:T(8,128)(2,1)S(1)}, bf16[4,16,512]{2,1,0:T(8,128)(2,1)S(1)}, u32[]{:S(2)}, u32[]{:S(2)}) %collective-permute-start.9) | collective-permute-done | bytes 65568 | tf_op jit(solution)/shard_map/ppermute | solution.py:71
  32.0 4.5 %attend.1 = (f32[256,256]{1,0:T(8,128)S(1)}, f32[256,256]{1,0:T(8,128)S(1)}, bf16[576,256]{1,0:T(8,128)(2,1)S(1)}, bf16[64,256]{1,0:T(8,128)(2,1)S(1)}) custom-call(s32[1]{0:T(128)} %bitcast.ctx_ref, s32[1]{0:T(128)} %bitcast.1.exp_ref, s32[8]{0:T(128)S(1)} %copy-done.2, bf16[64,1408]{1,0:T(8,128)(2,1)S(1)} %get-tuple-element.71._.refs_0_, ...), custom_call_target="tpu_custom_call" | custom-call | flops 1610612736 | bytes 8388608 | tf_op jit(solution)/shard_map/attend/pallas_call | solution.py:624
  36.6 1.6 %collective-permute-done.11.refs_1_ = bf16[576,256]{1,0:T(8,128)(2,1)S(1)} collective-permute-done((bf16[576,256]{1,0:T(8,128)(2,1)S(1)}, bf16[576,256]{1,0:T(8,128)(2,1)S(1)}, u32[]{:S(2)}, u32[]{:S(2)}) %collective-permute-start.11) | collective-permute-done | bytes 294944 | tf_op jit(solution)/shard_map/ppermute | solution.py:25
  38.2 1.6 %collective-permute-start.12 = (bf16[320,256]{1,0:T(8,128)(2,1)S(1)}, bf16[320,256]{1,0:T(8,128)(2,1)S(1)}, u32[]{:S(2)}, u32[]{:S(2)}) collective-permute-start(bf16[320,256]{1,0:T(8,128)(2,1)S(1)} %pad_maximum_fusion.6), channel_id=1, source_target_pairs={{0,2},{1,3},{2,0},{3,1},{4,6},{5,7},{6,4},{7,5},{8,10},{9,11},{10,... | collective-permute-start | bytes 491528 | tf_op jit(solution)/shard_map/ppermute | solution.py:25
  39.8 4.7 %collective-permute-done.12.refs_2_ = bf16[320,256]{1,0:T(8,128)(2,1)S(1)} collective-permute-done((bf16[320,256]{1,0:T(8,128)(2,1)S(1)}, bf16[320,256]{1,0:T(8,128)(2,1)S(1)}, u32[]{:S(2)}, u32[]{:S(2)}) %collective-permute-start.12) | collective-permute-done | bytes 163872 | tf_op jit(solution)/shard_map/ppermute | solution.py:25
  44.6 2.0 %collective-permute-start.13 = (bf16[256,256]{1,0:T(8,128)(2,1)S(1)}, bf16[256,256]{1,0:T(8,128)(2,1)S(1)}, u32[]{:S(2)}, u32[]{:S(2)}) collective-permute-start(bf16[256,256]{1,0:T(8,128)(2,1)S(1)} %add_convert_fusion.7.refs_0_.refs_6_), channel_id=1, source_target_pairs={{16,0},{17,1},{18,2},{19,3},{20,4},{21,5},{22,6},{23,7},{24,8},{25... | collective-permute-start | bytes 393224 | tf_op jit(solution)/shard_map/ppermute | solution.py:71
  46.6 1.5 %collective-permute-start.14 = (bf16[256,256]{1,0:T(8,128)(2,1)S(1)}, bf16[256,256]{1,0:T(8,128)(2,1)S(1)}, u32[]{:S(2)}, u32[]{:S(2)}) collective-permute-start(bf16[256,256]{1,0:T(8,128)(2,1)S(1)} %add_convert_fusion.7.refs_0_.refs_6_), channel_id=1, source_target_pairs={{2,0},{5,1},{0,2},{7,3},{6,4},{1,5},{4,6},{3,7},{10,8},{13,9},{8,1... | collective-permute-start | bytes 393224 | tf_op jit(solution)/shard_map/ppermute | solution.py:71
  50.1 2.9 %collective-permute-done.13.refs_0_.refs_7_ = bf16[256,256]{1,0:T(8,128)(2,1)S(1)} collective-permute-done((bf16[256,256]{1,0:T(8,128)(2,1)S(1)}, bf16[256,256]{1,0:T(8,128)(2,1)S(1)}, u32[]{:S(2)}, u32[]{:S(2)}) %collective-permute-start.13) | collective-permute-done | bytes 131104 | tf_op jit(solution)/shard_map/ppermute | solution.py:71
  53.1 1.7 %collective-permute-done.16.refs_3_.refs_10_ = bf16[256,256]{1,0:T(8,128)(2,1)S(1)} collective-permute-done((bf16[256,256]{1,0:T(8,128)(2,1)S(1)}, bf16[256,256]{1,0:T(8,128)(2,1)S(1)}, u32[]{:S(2)}, u32[]{:S(2)}) %collective-permute-start.16) | collective-permute-done | bytes 131104 | tf_op jit(solution)/shard_map/ppermute | solution.py:71
  57.2 4.5 %collective-permute-done.19.refs_3_.refs_13_ = bf16[256,256]{1,0:T(8,128)(2,1)S(1)} collective-permute-done((bf16[256,256]{1,0:T(8,128)(2,1)S(1)}, bf16[256,256]{1,0:T(8,128)(2,1)S(1)}, u32[]{:S(2)}, u32[]{:S(2)}) %collective-permute-start.19) | collective-permute-done | bytes 131104 | tf_op jit(solution)/shard_map/ppermute | solution.py:71
  65.4 6.1 %collective-permute-done.22.refs_6_.refs_15_ = bf16[256,256]{1,0:T(8,128)(2,1)S(1)} collective-permute-done((bf16[256,256]{1,0:T(8,128)(2,1)S(1)}, bf16[256,256]{1,0:T(8,128)(2,1)S(1)}, u32[]{:S(2)}, u32[]{:S(2)}) %collective-permute-start.22) | collective-permute-done | bytes 131104 | tf_op jit(solution)/shard_map/ppermute | solution.py:71
  71.5 1.6 %collective-permute-done.20.refs_6_.refs_4_ = bf16[512,256]{1,0:T(8,128)(2,1)S(1)} collective-permute-done((bf16[512,256]{1,0:T(8,128)(2,1)S(1)}, bf16[512,256]{1,0:T(8,128)(2,1)S(1)}, u32[]{:S(2)}, u32[]{:S(2)}) %collective-permute-start.20) | collective-permute-done | bytes 262176 | tf_op jit(solution)/shard_map/ppermute | solution.py:71
  73.6 2.0 %experts_in_first.1 = (f32[512,1536]{1,0:T(8,128)S(1)}, f32[512,1]{1,0:T(8,128)S(1)}) custom-call(s32[1]{0:T(128)} %bitcast.ctx_ref, s32[1]{0:T(128)} %bitcast.1.exp_ref, bf16[256,256]{1,0:T(8,128)(2,1)S(1)} %add_convert_fusion.7.refs_0_.refs_6_, bf16[256,256]{1,0:T(8,128)(2,1)S(1)} %collective-permute-done.14.refs_1_.refs_8_, ...), custom_call_target="tpu_custom_call" | custom-call | flops 1610612736 | bytes 8388608 | tf_op jit(solution)/shard_map/experts_in_first/pallas_call | solution.py:677
  75.6 2.4 %collective-permute-done.23.refs_7_ = bf16[256,256]{1,0:T(8,128)(2,1)S(1)} collective-permute-done((bf16[256,256]{1,0:T(8,128)(2,1)S(1)}, bf16[256,256]{1,0:T(8,128)(2,1)S(1)}, u32[]{:S(2)}, u32[]{:S(2)}) %collective-permute-start.23) | collective-permute-done | bytes 131104 | tf_op jit(solution)/shard_map/ppermute | solution.py:71
  81.6 1.9 %experts_out.2 = (f32[32,2048]{1,0:T(8,128)S(1)}, f32[32,2048]{1,0:T(8,128)S(1)}, bf16[32,2048]{1,0:T(8,128)(2,1)S(1)}, bf16[32,2048]{1,0:T(8,128)(2,1)S(1)}, f3...) custom-call(s32[1]{0:T(128)} %bitcast.ctx_ref, ...), custom_call_target="tpu_custom_call" | custom-call | flops 805306368 | bytes 8388608 | tf_op jit(solution)/shard_map/experts_out/pallas_call | solution.py:732
  84.2 1.8 %experts_out.3 = (f32[32,2048]{1,0:T(8,128)S(1)}, f32[32,2048]{1,0:T(8,128)S(1)}, bf16[32,2048]{1,0:T(8,128)(2,1)S(1)}, bf16[32,2048]{1,0:T(8,128)(2,1)S(1)}, f3...) custom-call(s32[1]{0:T(128)} %bitcast.ctx_ref, ...), custom_call_target="tpu_custom_call" | custom-call | flops 805306368 | bytes 8388608 | tf_op jit(solution)/shard_map/experts_out/pallas_call | solution.py:732
  86.0 2.6 %collective-permute-done.25 = bf16[32,2048]{1,0:T(8,128)(2,1)S(1)} collective-permute-done((bf16[32,2048]{1,0:T(8,128)(2,1)S(1)}, bf16[32,2048]{1,0:T(8,128)(2,1)S(1)}, u32[]{:S(2)}, u32[]{:S(2)}) %collective-permute-start.25) | collective-permute-done | bytes 131104 | tf_op jit(solution)/shard_map/ppermute | solution.py:71
  89.3 1.5 %collective-permute-start.27 = (bf16[64,2048]{1,0:T(8,128)(2,1)S(1)}, bf16[64,2048]{1,0:T(8,128)(2,1)S(1)}, u32[]{:S(2)}, u32[]{:S(2)}) collective-permute-start(bf16[64,2048]{1,0:T(8,128)(2,1)S(1)} %pad_maximum_fusion.2), channel_id=1, source_target_pairs={{4,0},{3,1},{6,2},{1,3},{0,4},{7,5},{2,6},{5,7},{12,8},{11,9},{14,... | collective-permute-start | bytes 786440 | tf_op jit(solution)/shard_map/ppermute | solution.py:71
  91.9 5.4 %collective-permute-done.29 = bf16[32,2048]{1,0:T(8,128)(2,1)S(1)} collective-permute-done((bf16[32,2048]{1,0:T(8,128)(2,1)S(1)}, bf16[32,2048]{1,0:T(8,128)(2,1)S(1)}, u32[]{:S(2)}, u32[]{:S(2)}) %collective-permute-start.29) | collective-permute-done | bytes 131104 | tf_op jit(solution)/shard_map/ppermute | solution.py:71
  97.3 1.9 %collective-permute-done.27 = bf16[64,2048]{1,0:T(8,128)(2,1)S(1)} collective-permute-done((bf16[64,2048]{1,0:T(8,128)(2,1)S(1)}, bf16[64,2048]{1,0:T(8,128)(2,1)S(1)}, u32[]{:S(2)}, u32[]{:S(2)}) %collective-permute-start.27) | collective-permute-done | bytes 262176 | tf_op jit(solution)/shard_map/ppermute | solution.py:71
  100.8 1.4 %collective-permute-start.34 = (bf16[32,2048]{1,0:T(8,128)(2,1)S(1)}, bf16[32,2048]{1,0:T(8,128)(2,1)S(1)}, u32[]{:S(2)}, u32[]{:S(2)}) collective-permute-start(bf16[32,2048]{1,0:T(8,128)(2,1)S(1)} %get-tuple-element.139), channel_id=1, source_target_pairs={{2,0},{5,1},{0,2},{7,3},{6,4},{1,5},{4,6},{3,7},{10,8},{13,9},{8,1... | collective-permute-start | bytes 393224 | tf_op jit(solution)/shard_map/ppermute | solution.py:71
  106.1 1.9 %collective-permute-start.36 = (bf16[32,2048]{1,0:T(8,128)(2,1)S(1)}, bf16[32,2048]{1,0:T(8,128)(2,1)S(1)}, u32[]{:S(2)}, u32[]{:S(2)}) collective-permute-start(bf16[32,2048]{1,0:T(8,128)(2,1)S(1)} %get-tuple-element.138), channel_id=1, source_target_pairs={{8,0},{9,1},{10,2},{11,3},{12,4},{13,5},{14,6},{15,7},{0,8},{1,9},... | collective-permute-start | bytes 393224 | tf_op jit(solution)/shard_map/ppermute | solution.py:71
  107.9 5.8 %collective-permute-done.33 = bf16[32,2048]{1,0:T(8,128)(2,1)S(1)} collective-permute-done((bf16[32,2048]{1,0:T(8,128)(2,1)S(1)}, bf16[32,2048]{1,0:T(8,128)(2,1)S(1)}, u32[]{:S(2)}, u32[]{:S(2)}) %collective-permute-start.33) | collective-permute-done | bytes 131104 | tf_op jit(solution)/shard_map/ppermute | solution.py:71
  (90 shorter events, 29.5 us)
Async XLA Ops:
  1.2 14.3 %collective-permute-start = (bf16[64,1408]{1,0:T(8,128)(2,1)S(1)}, bf16[64,1408]{1,0:T(8,128)(2,1)S(1)}, u32[]{:S(2)}, u32[]{:S(2)}) collective-permute-start(bf16[64,1408]{1,0:T(8,128)(2,1)S(1)} %get-tuple-element.71._.refs_0_), channel_id=1, source_target_pairs={{16,0},{17,1},{18,2},{19,3},{20,4},{21,5},{22,6},{23,7},{24,8},{25... | collective-permute-start | bytes 540680 | tf_op jit(solution)/shard_map/ppermute | solution.py:71
  5.3 10.2 %collective-permute-start.1 = (bf16[64,1408]{1,0:T(8,128)(2,1)S(1)}, bf16[64,1408]{1,0:T(8,128)(2,1)S(1)}, u32[]{:S(2)}, u32[]{:S(2)}) collective-permute-start(bf16[64,1408]{1,0:T(8,128)(2,1)S(1)} %get-tuple-element.71._.refs_0_), channel_id=1, source_target_pairs={{4,0},{9,1},{6,2},{11,3},{0,4},{13,5},{2,6},{15,7},{12,8},{1,9},{1... | collective-permute-start | bytes 540680 | tf_op jit(solution)/shard_map/ppermute | solution.py:71
  6.8 8.7 %collective-permute-start.2 = (bf16[64,1408]{1,0:T(8,128)(2,1)S(1)}, bf16[64,1408]{1,0:T(8,128)(2,1)S(1)}, u32[]{:S(2)}, u32[]{:S(2)}) collective-permute-start(bf16[64,1408]{1,0:T(8,128)(2,1)S(1)} %get-tuple-element.71._.refs_0_), channel_id=1, source_target_pairs={{8,0},{5,1},{10,2},{7,3},{12,4},{1,5},{14,6},{3,7},{0,8},{13,9},{2... | collective-permute-start | bytes 540680 | tf_op jit(solution)/shard_map/ppermute | solution.py:71
  8.4 7.1 %collective-permute-start.3 = (bf16[4,16,512]{2,1,0:T(8,128)(2,1)S(1)}, bf16[4,16,512]{2,1,0:T(8,128)(2,1)S(1)}, u32[]{:S(2)}, u32[]{:S(2)}) collective-permute-start(bf16[4,16,512]{2,1,0:T(8,128)(2,1)S(1)} %get-tuple-element.72), channel_id=1, source_target_pairs={{8,0},{5,1},{10,2},{7,3},{12,4},{1,5},{14,6},{3,7},{0,8},{13,9},{2... | collective-permute-start | bytes 196616 | tf_op jit(solution)/shard_map/ppermute | solution.py:71
  15.5 9.8 %collective-permute-start.7 = (bf16[2048,768]{1,0:T(8,128)(2,1)S(1)}, bf16[2048,768]{1,0:T(8,128)(2,1)S(1)}, u32[]{:S(2)}, u32[]{:S(2)}) collective-permute-start(bf16[2048,768]{1,0:T(8,128)(2,1)S(1)} %get-tuple-element.80), channel_id=1, source_target_pairs={{0,1},{1,0},{2,3},{3,2},{4,5},{5,4},{6,7},{7,6},{8,9},{9,8},{10,11... | collective-permute-start | bytes 9437192 | tf_op jit(solution)/shard_map/ppermute | solution.py:25
  15.6 9.7 %collective-permute-start.4 = (bf16[128,1408]{1,0:T(8,128)(2,1)S(1)}, bf16[128,1408]{1,0:T(8,128)(2,1)S(1)}, u32[]{:S(2)}, u32[]{:S(2)}) collective-permute-start(bf16[128,1408]{1,0:T(8,128)(2,1)S(1)} %pad_maximum_fusion), channel_id=1, source_target_pairs={{4,0},{9,1},{6,2},{11,3},{0,4},{13,5},{2,6},{15,7},{12,8},{1,9},{1... | collective-permute-start | bytes 1081352 | tf_op jit(solution)/shard_map/ppermute | solution.py:71
  16.4 8.9 %collective-permute-start.5 = (bf16[64,1408]{1,0:T(8,128)(2,1)S(1)}, bf16[64,1408]{1,0:T(8,128)(2,1)S(1)}, u32[]{:S(2)}, u32[]{:S(2)}) collective-permute-start(bf16[64,1408]{1,0:T(8,128)(2,1)S(1)} %collective-permute-done.refs_1_), channel_id=1, source_target_pairs={{8,0},{5,1},{10,2},{7,3},{12,4},{1,5},{14,6},{3,7},{0,8},{13,9},{2... | collective-permute-start | bytes 540680 | tf_op jit(solution)/shard_map/ppermute | solution.py:71
  17.9 6.3 %collective-permute-start.6 = (bf16[4,16,512]{2,1,0:T(8,128)(2,1)S(1)}, bf16[4,16,512]{2,1,0:T(8,128)(2,1)S(1)}, u32[]{:S(2)}, u32[]{:S(2)}) collective-permute-start(bf16[4,16,512]{2,1,0:T(8,128)(2,1)S(1)} %pad_maximum_fusion.7), channel_id=1, source_target_pairs={{16,0},{17,1},{18,2},{19,3},{20,4},{21,5},{22,6},{23,7},{24,8},{25... | collective-permute-start | bytes 196616 | tf_op jit(solution)/shard_map/ppermute | solution.py:71
  25.3 6.7 %collective-permute-start.10 = (bf16[384,2048]{1,0:T(8,128)(2,1)S(1)}, bf16[384,2048]{1,0:T(8,128)(2,1)S(1)}, u32[]{:S(2)}, u32[]{:S(2)}) collective-permute-start(bf16[384,2048]{1,0:T(8,128)(2,1)S(1)} %get-tuple-element.86), channel_id=1, source_target_pairs={{0,1},{1,0},{2,3},{3,2},{4,5},{5,4},{6,7},{7,6},{8,9},{9,8},{10,11... | collective-permute-start | bytes 4718600 | tf_op jit(solution)/shard_map/ppermute | solution.py:25
  25.8 6.2 %collective-permute-start.8 = (bf16[64,1408]{1,0:T(8,128)(2,1)S(1)}, bf16[64,1408]{1,0:T(8,128)(2,1)S(1)}, u32[]{:S(2)}, u32[]{:S(2)}) collective-permute-start(bf16[64,1408]{1,0:T(8,128)(2,1)S(1)} %collective-permute-done.5.refs_5_), channel_id=1, source_target_pairs={{4,0},{9,1},{6,2},{11,3},{0,4},{13,5},{2,6},{15,7},{12,8},{1,9},{1... | collective-permute-start | bytes 540680 | tf_op jit(solution)/shard_map/ppermute | solution.py:71
  26.7 5.2 %collective-permute-start.9 = (bf16[4,16,512]{2,1,0:T(8,128)(2,1)S(1)}, bf16[4,16,512]{2,1,0:T(8,128)(2,1)S(1)}, u32[]{:S(2)}, u32[]{:S(2)}) collective-permute-start(bf16[4,16,512]{2,1,0:T(8,128)(2,1)S(1)} %pad_maximum_fusion.8), channel_id=1, source_target_pairs={{4,0},{9,1},{6,2},{11,3},{0,4},{13,5},{2,6},{15,7},{12,8},{1,9},{1... | collective-permute-start | bytes 196616 | tf_op jit(solution)/shard_map/ppermute | solution.py:71
  38.2 6.3 %collective-permute-start.12 = (bf16[320,256]{1,0:T(8,128)(2,1)S(1)}, bf16[320,256]{1,0:T(8,128)(2,1)S(1)}, u32[]{:S(2)}, u32[]{:S(2)}) collective-permute-start(bf16[320,256]{1,0:T(8,128)(2,1)S(1)} %pad_maximum_fusion.6), channel_id=1, source_target_pairs={{0,2},{1,3},{2,0},{3,1},{4,6},{5,7},{6,4},{7,5},{8,10},{9,11},{10,... | collective-permute-start | bytes 491528 | tf_op jit(solution)/shard_map/ppermute | solution.py:25
  44.6 8.5 %collective-permute-start.13 = (bf16[256,256]{1,0:T(8,128)(2,1)S(1)}, bf16[256,256]{1,0:T(8,128)(2,1)S(1)}, u32[]{:S(2)}, u32[]{:S(2)}) collective-permute-start(bf16[256,256]{1,0:T(8,128)(2,1)S(1)} %add_convert_fusion.7.refs_0_.refs_6_), channel_id=1, source_target_pairs={{16,0},{17,1},{18,2},{19,3},{20,4},{21,5},{22,6},{23,7},{24,8},{25... | collective-permute-start | bytes 393224 | tf_op jit(solution)/shard_map/ppermute | solution.py:71
  46.6 6.5 %collective-permute-start.14 = (bf16[256,256]{1,0:T(8,128)(2,1)S(1)}, bf16[256,256]{1,0:T(8,128)(2,1)S(1)}, u32[]{:S(2)}, u32[]{:S(2)}) collective-permute-start(bf16[256,256]{1,0:T(8,128)(2,1)S(1)} %add_convert_fusion.7.refs_0_.refs_6_), channel_id=1, source_target_pairs={{2,0},{5,1},{0,2},{7,3},{6,4},{1,5},{4,6},{3,7},{10,8},{13,9},{8,1... | collective-permute-start | bytes 393224 | tf_op jit(solution)/shard_map/ppermute | solution.py:71
  48.1 5.0 %collective-permute-start.15 = (bf16[256,256]{1,0:T(8,128)(2,1)S(1)}, bf16[256,256]{1,0:T(8,128)(2,1)S(1)}, u32[]{:S(2)}, u32[]{:S(2)}) collective-permute-start(bf16[256,256]{1,0:T(8,128)(2,1)S(1)} %add_convert_fusion.7.refs_0_.refs_6_), channel_id=1, source_target_pairs={{4,0},{3,1},{6,2},{1,3},{0,4},{7,5},{2,6},{5,7},{12,8},{11,9},{14,... | collective-permute-start | bytes 393224 | tf_op jit(solution)/shard_map/ppermute | solution.py:71
  49.3 5.5 %collective-permute-start.16 = (bf16[256,256]{1,0:T(8,128)(2,1)S(1)}, bf16[256,256]{1,0:T(8,128)(2,1)S(1)}, u32[]{:S(2)}, u32[]{:S(2)}) collective-permute-start(bf16[256,256]{1,0:T(8,128)(2,1)S(1)} %add_convert_fusion.7.refs_0_.refs_6_), channel_id=1, source_target_pairs={{8,0},{9,1},{10,2},{11,3},{12,4},{13,5},{14,6},{15,7},{0,8},{1,9},... | collective-permute-start | bytes 393224 | tf_op jit(solution)/shard_map/ppermute | solution.py:71
  54.8 8.1 %collective-permute-start.17 = (bf16[512,256]{1,0:T(8,128)(2,1)S(1)}, bf16[512,256]{1,0:T(8,128)(2,1)S(1)}, u32[]{:S(2)}, u32[]{:S(2)}) collective-permute-start(bf16[512,256]{1,0:T(8,128)(2,1)S(1)} %constant_dynamic-update-slice_fusion), channel_id=1, source_target_pairs={{2,0},{5,1},{0,2},{7,3},{6,4},{1,5},{4,6},{3,7},{10,8},{13,9},{8,1... | collective-permute-start | bytes 786440 | tf_op jit(solution)/shard_map/ppermute | solution.py:71
  55.6 7.3 %collective-permute-start.18 = (bf16[512,256]{1,0:T(8,128)(2,1)S(1)}, bf16[512,256]{1,0:T(8,128)(2,1)S(1)}, u32[]{:S(2)}, u32[]{:S(2)}) collective-permute-start(bf16[512,256]{1,0:T(8,128)(2,1)S(1)} %constant_dynamic-update-slice_fusion), channel_id=1, source_target_pairs={{4,0},{3,1},{6,2},{1,3},{0,4},{7,5},{2,6},{5,7},{12,8},{11,9},{14,... | collective-permute-start | bytes 786440 | tf_op jit(solution)/shard_map/ppermute | solution.py:71
  62.9 8.5 %collective-permute-start.21 = (bf16[512,256]{1,0:T(8,128)(2,1)S(1)}, bf16[512,256]{1,0:T(8,128)(2,1)S(1)}, u32[]{:S(2)}, u32[]{:S(2)}) collective-permute-start(bf16[512,256]{1,0:T(8,128)(2,1)S(1)} %pad_maximum_fusion.1), channel_id=1, source_target_pairs={{4,0},{3,1},{6,2},{1,3},{0,4},{7,5},{2,6},{5,7},{12,8},{11,9},{14,... | collective-permute-start | bytes 786440 | tf_op jit(solution)/shard_map/ppermute | solution.py:71
  63.8 9.2 %collective-permute-start.20 = (bf16[512,256]{1,0:T(8,128)(2,1)S(1)}, bf16[512,256]{1,0:T(8,128)(2,1)S(1)}, u32[]{:S(2)}, u32[]{:S(2)}) collective-permute-start(bf16[512,256]{1,0:T(8,128)(2,1)S(1)} %collective-permute-done.17.refs_4_.refs_1_.refs_11_), channel_id=1, source_target_pairs={{4,0},{3,1},{6,2},{1,3},{0,4},{7,5},{2,6},{5,7},{12,8},{11,9},{14,... | collective-permute-start | bytes 786440 | tf_op jit(solution)/shard_map/ppermute | solution.py:71
  65.0 6.4 %collective-permute-start.22 = (bf16[256,256]{1,0:T(8,128)(2,1)S(1)}, bf16[256,256]{1,0:T(8,128)(2,1)S(1)}, u32[]{:S(2)}, u32[]{:S(2)}) collective-permute-start(bf16[256,256]{1,0:T(8,128)(2,1)S(1)} %collective-permute-done.19.refs_3_.refs_13_), channel_id=1, source_target_pairs={{2,0},{5,1},{0,2},{7,3},{6,4},{1,5},{4,6},{3,7},{10,8},{13,9},{8,1... | collective-permute-start | bytes 393224 | tf_op jit(solution)/shard_map/ppermute | solution.py:71
  83.6 5.0 %collective-permute-start.25 = (bf16[32,2048]{1,0:T(8,128)(2,1)S(1)}, bf16[32,2048]{1,0:T(8,128)(2,1)S(1)}, u32[]{:S(2)}, u32[]{:S(2)}) collective-permute-start(bf16[32,2048]{1,0:T(8,128)(2,1)S(1)} %get-tuple-element.106), channel_id=1, source_target_pairs={{4,0},{3,1},{6,2},{1,3},{0,4},{7,5},{2,6},{5,7},{12,8},{11,9},{14,... | collective-permute-start | bytes 393224 | tf_op jit(solution)/shard_map/ppermute | solution.py:71
  88.6 8.7 %collective-permute-start.28 = (bf16[64,2048]{1,0:T(8,128)(2,1)S(1)}, bf16[64,2048]{1,0:T(8,128)(2,1)S(1)}, u32[]{:S(2)}, u32[]{:S(2)}) collective-permute-start(bf16[64,2048]{1,0:T(8,128)(2,1)S(1)} %pad_maximum_fusion.3), channel_id=1, source_target_pairs={{4,0},{3,1},{6,2},{1,3},{0,4},{7,5},{2,6},{5,7},{12,8},{11,9},{14,... | collective-permute-start | bytes 786440 | tf_op jit(solution)/shard_map/ppermute | solution.py:71
  89.3 10.0 %collective-permute-start.27 = (bf16[64,2048]{1,0:T(8,128)(2,1)S(1)}, bf16[64,2048]{1,0:T(8,128)(2,1)S(1)}, u32[]{:S(2)}, u32[]{:S(2)}) collective-permute-start(bf16[64,2048]{1,0:T(8,128)(2,1)S(1)} %pad_maximum_fusion.2), channel_id=1, source_target_pairs={{4,0},{3,1},{6,2},{1,3},{0,4},{7,5},{2,6},{5,7},{12,8},{11,9},{14,... | collective-permute-start | bytes 786440 | tf_op jit(solution)/shard_map/ppermute | solution.py:71
  90.8 6.5 %collective-permute-start.29 = (bf16[32,2048]{1,0:T(8,128)(2,1)S(1)}, bf16[32,2048]{1,0:T(8,128)(2,1)S(1)}, u32[]{:S(2)}, u32[]{:S(2)}) collective-permute-start(bf16[32,2048]{1,0:T(8,128)(2,1)S(1)} %add_convert_fusion.6), channel_id=1, source_target_pairs={{2,0},{5,1},{0,2},{7,3},{6,4},{1,5},{4,6},{3,7},{10,8},{13,9},{8,1... | collective-permute-start | bytes 393224 | tf_op jit(solution)/shard_map/ppermute | solution.py:71
  91.3 12.3 %collective-permute-start.31 = (bf16[64,2048]{1,0:T(8,128)(2,1)S(1)}, bf16[64,2048]{1,0:T(8,128)(2,1)S(1)}, u32[]{:S(2)}, u32[]{:S(2)}) collective-permute-start(bf16[64,2048]{1,0:T(8,128)(2,1)S(1)} %pad_maximum_fusion.5), channel_id=1, source_target_pairs={{4,0},{3,1},{6,2},{1,3},{0,4},{7,5},{2,6},{5,7},{12,8},{11,9},{14,... | collective-permute-start | bytes 786440 | tf_op jit(solution)/shard_map/ppermute | solution.py:71
  99.3 6.4 %collective-permute-start.30 = (bf16[64,2048]{1,0:T(8,128)(2,1)S(1)}, bf16[64,2048]{1,0:T(8,128)(2,1)S(1)}, u32[]{:S(2)}, u32[]{:S(2)}) collective-permute-start(bf16[64,2048]{1,0:T(8,128)(2,1)S(1)} %pad_maximum_fusion.4), channel_id=1, source_target_pairs={{2,0},{5,1},{0,2},{7,3},{6,4},{1,5},{4,6},{3,7},{10,8},{13,9},{8,1... | collective-permute-start | bytes 786440 | tf_op jit(solution)/shard_map/ppermute | solution.py:71
  99.8 5.0 %collective-permute-start.32 = (bf16[32,2048]{1,0:T(8,128)(2,1)S(1)}, bf16[32,2048]{1,0:T(8,128)(2,1)S(1)}, u32[]{:S(2)}, u32[]{:S(2)}) collective-permute-start(bf16[32,2048]{1,0:T(8,128)(2,1)S(1)} %get-tuple-element.140), channel_id=1, source_target_pairs={{8,0},{9,1},{10,2},{11,3},{12,4},{13,5},{14,6},{15,7},{0,8},{1,9},... | collective-permute-start | bytes 393224 | tf_op jit(solution)/shard_map/ppermute | solution.py:71
  100.4 7.5 %collective-permute-start.35 = (bf16[32,2048]{1,0:T(8,128)(2,1)S(1)}, bf16[32,2048]{1,0:T(8,128)(2,1)S(1)}, u32[]{:S(2)}, u32[]{:S(2)}) collective-permute-start(bf16[32,2048]{1,0:T(8,128)(2,1)S(1)} %get-tuple-element.135), channel_id=1, source_target_pairs={{4,0},{3,1},{6,2},{1,3},{0,4},{7,5},{2,6},{5,7},{12,8},{11,9},{14,... | collective-permute-start | bytes 393224 | tf_op jit(solution)/shard_map/ppermute | solution.py:71
  100.8 7.1 %collective-permute-start.34 = (bf16[32,2048]{1,0:T(8,128)(2,1)S(1)}, bf16[32,2048]{1,0:T(8,128)(2,1)S(1)}, u32[]{:S(2)}, u32[]{:S(2)}) collective-permute-start(bf16[32,2048]{1,0:T(8,128)(2,1)S(1)} %get-tuple-element.139), channel_id=1, source_target_pairs={{2,0},{5,1},{0,2},{7,3},{6,4},{1,5},{4,6},{3,7},{10,8},{13,9},{8,1... | collective-permute-start | bytes 393224 | tf_op jit(solution)/shard_map/ppermute | solution.py:71
  105.9 7.9 %collective-permute-start.33 = (bf16[32,2048]{1,0:T(8,128)(2,1)S(1)}, bf16[32,2048]{1,0:T(8,128)(2,1)S(1)}, u32[]{:S(2)}, u32[]{:S(2)}) collective-permute-start(bf16[32,2048]{1,0:T(8,128)(2,1)S(1)} %get-tuple-element.137), channel_id=1, source_target_pairs={{16,0},{17,1},{18,2},{19,3},{20,4},{21,5},{22,6},{23,7},{24,8},{25... | collective-permute-start | bytes 393224 | tf_op jit(solution)/shard_map/ppermute | solution.py:71
  106.1 8.2 %collective-permute-start.36 = (bf16[32,2048]{1,0:T(8,128)(2,1)S(1)}, bf16[32,2048]{1,0:T(8,128)(2,1)S(1)}, u32[]{:S(2)}, u32[]{:S(2)}) collective-permute-start(bf16[32,2048]{1,0:T(8,128)(2,1)S(1)} %get-tuple-element.138), channel_id=1, source_target_pairs={{8,0},{9,1},{10,2},{11,3},{12,4},{13,5},{14,6},{15,7},{0,8},{1,9},... | collective-permute-start | bytes 393224 | tf_op jit(solution)/shard_map/ppermute | solution.py:71
  (9 other events, 106.3 us)

commit v6 on v5

--- a/solution.py
+++ b/solution.py
@@ -45,6 +45,26 @@
 
     bits = bits_of(ctx_count)
     y_move = (1, 0)
+    if (ctx_count, x_count) == (8, 2) and not rows_only:
+        z_far, z_near = ((4, 0),) * 2, ((2, 0),) * 2
+        first, second = ((0, 2), y_move), (y_move, (0, 2))
+        at = {"0": (0, 0)}
+        for stage, moves, hops in (
+            (1, z_far, "0>4"),
+            (1, z_near, "0>2"),
+            (1, first, "0>0a"),
+            (1, second, "0>0b"),
+            (2, z_near, "4>6 0b>2b"),
+            (2, first, "2>2a 4>4a"),
+            (2, second, "4>4b 0a>0ab"),
+            (3, z_near, "4a>6a"),
+            (3, second, "2a>2ab 4a>4ab 6>6b"),
+            (4, second, "6a>6ab"),
+        ):
+            for hop in hops.split():
+                source, target = hop.split(">")
+                at[target] = go(at[source], moves, stage - 1 - arrival[at[source]])
+        return sorted(transfers, key=lambda transfer: transfer[0]), places
     if rows_only:
         shared, steps = range(bits - 1, 1, -1), [(2, 0), y_move]
     else:
@@ -53,11 +73,10 @@
     for bit in shared:
         for source in list(arrival):
             go(source, ((1 << bit, 0),) * 2)
-    for number, first in enumerate(sorted(arrival)):
+    for first in sorted(arrival):
         held = [first]
         for moves in pairs:
-            tuned = (ctx_count, x_count) == (8, 2) and not rows_only and number == 0
-            held = held + [go(source, moves, 1 if tuned and source != first else 0) for source in held]
+            held = held + [go(source, moves) for source in held]
     return sorted(transfers, key=lambda transfer: transfer[0]), places
 
 
@@ -363,20 +382,18 @@
                     value = out_ref[at, :].astype(jnp.float32) + piece.astype(jnp.float32)
                     out_ref[at, :] = value.astype(out_ref.dtype)
         expert = my_ctx * x_count + lax.bitwise_xor(my_x, x_off)
-        sides = [jnp.zeros((tok, HEAD_SIZE), jnp.float32)] * 2
+        block_out = jnp.zeros((tok, HEAD_SIZE), jnp.float32)
         for offset, ref in enumerate(packed):
             source = lax.bitwise_xor(my_ctx, by_core(my_core, places_of[offset], 0))
             for part_of in range(2):
                 block = ref[part_of * tok : (part_of + 1) * tok, first:].astype(jnp.float32)
                 column = jnp.sum(jnp.where(route_lane == expert, block, 0.0), axis=1, keepdims=True)
-                sides[part_of] = sides[part_of] + jnp.where(route_lane == source, column, 0.0)
-        for part_of, side in enumerate(sides):
-            row = (2 * x_off + part_of) * tok
-            for ref, base in ((give_ref, route_base), (own_route_ref, 0)):
-                at = pl.ds(base + row, tok)
-                ref[at, 0:HEAD_SIZE] = side.astype(jnp.bfloat16)
-                if cols > HEAD_SIZE:
-                    ref[at, HEAD_SIZE:] = jnp.zeros((tok, cols - HEAD_SIZE), jnp.bfloat16)
+                block_out = jnp.where(route_lane == source + part_of * ctx_count, column, block_out)
+        for ref, base in ((give_ref, route_base), (own_route_ref, 0)):
+            at = pl.ds(base + x_off * tok, tok)
+            ref[at, 0:HEAD_SIZE] = block_out.astype(jnp.bfloat16)
+            if cols > HEAD_SIZE:
+                ref[at, HEAD_SIZE:] = jnp.zeros((tok, cols - HEAD_SIZE), jnp.bfloat16)
 
 
 def fill_rows(plan, ctx_ref, exp_ref, gain_ref, chunk_refs, places, rows_scr, square_ref, groups):
@@ -456,15 +473,14 @@
     lane = lax.broadcasted_iota(jnp.int32, (tok, HEAD_SIZE), 1)
     blocks = []
     for array, row in route_at:
-        both = route_refs[array][row : row + 2 * tok, 0:HEAD_SIZE].astype(jnp.float32)
-        blocks.append(both[:tok] + both[tok:])
+        blocks.append(route_refs[array][row : row + tok, 0:HEAD_SIZE].astype(jnp.float32))
     columns = []
     for x_off in range(x_count):
         for low in range(half):
             for core in range(2):
                 same, swapped = blocks[2 * x_off + core], blocks[2 * x_off + 1 - core]
                 block = jnp.where(my_core == 0, same, swapped)
-                picked = jnp.where(lane == first_ctx + low, block, 0.0)
+                picked = jnp.where(lane % ctx_count == first_ctx + low, block, 0.0)
                 columns.append(jnp.sum(picked, axis=1, keepdims=True))
     route = jnp.concatenate(columns, axis=0)
     squares = act_ref[:, 2 * width :].astype(jnp.float32) + came_ref[:, 2 * width :].astype(jnp.float32)
@@ -627,8 +643,8 @@
         out_specs=[vmem] * (2 + x_count),
         out_shape=[jax.ShapeDtypeStruct((per_x, cols), f32)] * x_count
         + [
-            jax.ShapeDtypeStruct((x_count * (per_x + 2 * tok), cols), bf16),
-            jax.ShapeDtypeStruct((x_count * 2 * tok, cols), bf16),
+            jax.ShapeDtypeStruct((x_count * (per_x + tok), cols), bf16),
+            jax.ShapeDtypeStruct((x_count * tok, cols), bf16),
         ],
         scratch_shapes=[
             pltpu.VMEM((positions, HEAD_SIZE), bf16),
@@ -650,12 +666,12 @@
     state = state + given[:per_x].astype(f32)
     for x_off in range(1, x_count):
         part = keeps[x_off] + given[x_off * per_x : (x_off + 1) * per_x].astype(f32)
-        row = x_count * per_x + x_off * 2 * tok
-        own = own_route[x_off * 2 * tok : (x_off + 1) * 2 * tok]
-        sent = jnp.concatenate([part.astype(bf16), own, given[row : row + 2 * tok]], axis=0)
+        row = x_count * per_x + x_off * tok
+        own = own_route[x_off * tok : (x_off + 1) * tok]
+        sent = jnp.concatenate([part.astype(bf16), own, given[row : row + tok]], axis=0)
         came = from_offset(sent, 2 * x_off)
         state = state + came[:per_x].astype(f32)
-        route_at += [(len(routes), per_x), (len(routes), per_x + 2 * tok)]
+        route_at += [(len(routes), per_x), (len(routes), per_x + tok)]
         routes.append(came)
     state = state.astype(bf16)
 

time: 117 us -> 112 us (0.957)
  waiting for transfers between devices: 59.7 us -> 51.4 us
  starting transfers between devices: 36.2 us -> 39.7 us
    ppermute x31, waiting for transfers between devices: 51.6 us -> 43.7 us  [follow(): return lax.ppermute(array, ('ctx', 'exp'), pairs)]
    ppermute x31, starting transfers between devices: 33.3 us -> 36.8 us  [follow(): return lax.ppermute(array, ('ctx', 'exp'), pairs)]
  transfers between devices with their start and end apart: 38 -> 38, of which waited for: 23 -> 24; matrix products, arithmetic and copies ran while one was open for 0% -> 0% of each run, Pallas kernels for 10% -> 11%
where the time goes in v6:
time: 112 us
  waiting for transfers between devices  51.4 us (46%)
  starting transfers between devices  39.7 us (35%)
  Pallas kernels  18.8 us (17%)
    ppermute x31, waiting for transfers between devices, follow(): return lax.ppermute(array, ('ctx', 'exp'), pairs)  43.7 us
    ppermute x31, starting transfers between devices, follow(): return lax.ppermute(array, ('ctx', 'exp'), pairs)  36.8 us
    ppermute x7, waiting for transfers between devices, from_offset(): lax.ppermute(array, 'exp', [(i, i ^ offset) for i in range(lax.axis_size(...  7.72 us
    pallas_call x1, Pallas kernels, shards(): pl.pallas_call(functools.partial(attend_kernel, (ctx_count, exp_count, to...  4.49 us
    pallas_call x2, Pallas kernels, shards(): pl.pallas_call(functools.partial(experts_out_kernel, (ctx_count, exp_coun...  3.73 us
    pallas_call x1, Pallas kernels, deq_in(): pl.pallas_call(functools.partial(deq_in_kernel, ctx_count), in_specs=[pl....  3 us
    ppermute x7, starting transfers between devices, from_offset(): lax.ppermute(array, 'exp', [(i, i ^ offset) for i in range(lax.axis_size(...  2.91 us
    pallas_call x2, Pallas kernels, shards(): pl.pallas_call(functools.partial(experts_in_second, (ctx_count, x_count,...  2.38 us
  transfers between devices with their start and end apart: 38, of which 24 were waited for; matrix products, arithmetic and copies ran while one was open for 0% of the time, Pallas kernels for 11%

profile of v6, /device:TPU:0, one launch (start us, length us, event | category | flops | bytes accessed | tf_op | source)
XLA Modules:
  0.0 111.8 jit_solution(7431022096177934420)
XLA Ops:
  1.2 4.1 %collective-permute-start = (bf16[64,1408]{1,0:T(8,128)(2,1)S(1)}, bf16[64,1408]{1,0:T(8,128)(2,1)S(1)}, u32[]{:S(2)}, u32[]{:S(2)}) collective-permute-start(bf16[64,1408]{1,0:T(8,128)(2,1)S(1)} %get-tuple-element.71._.refs_0_), channel_id=1, source_target_pairs={{16,0},{17,1},{18,2},{19,3},{20,4},{21,5},{22,6},{23,7},{24,8},{25... | collective-permute-start | bytes 540680 | tf_op jit(solution)/shard_map/ppermute | solution.py:90
  5.3 1.5 %collective-permute-start.1 = (bf16[64,1408]{1,0:T(8,128)(2,1)S(1)}, bf16[64,1408]{1,0:T(8,128)(2,1)S(1)}, u32[]{:S(2)}, u32[]{:S(2)}) collective-permute-start(bf16[64,1408]{1,0:T(8,128)(2,1)S(1)} %get-tuple-element.71._.refs_0_), channel_id=1, source_target_pairs={{4,0},{9,1},{6,2},{11,3},{0,4},{13,5},{2,6},{15,7},{12,8},{1,9},{1... | collective-permute-start | bytes 540680 | tf_op jit(solution)/shard_map/ppermute | solution.py:90
  6.8 1.6 %collective-permute-start.2 = (bf16[64,1408]{1,0:T(8,128)(2,1)S(1)}, bf16[64,1408]{1,0:T(8,128)(2,1)S(1)}, u32[]{:S(2)}, u32[]{:S(2)}) collective-permute-start(bf16[64,1408]{1,0:T(8,128)(2,1)S(1)} %get-tuple-element.71._.refs_0_), channel_id=1, source_target_pairs={{8,0},{5,1},{10,2},{7,3},{12,4},{1,5},{14,6},{3,7},{0,8},{13,9},{2... | collective-permute-start | bytes 540680 | tf_op jit(solution)/shard_map/ppermute | solution.py:90
  8.8 3.0 %dequant_in.1 = (bf16[2048,768]{1,0:T(8,128)(2,1)S(1)}, bf16[2048,768]{1,0:T(8,128)(2,1)S(1)}) custom-call(s32[1]{0:T(128)} %bitcast.1.exp_ref, s32[3,1,32]{2,1,0:T(1,128)} %bitcast.25, s32[3,1,32]{2,1,0:T(1,128)} %bitcast.26, bf16[1,4096,384]{2,1,0:T(8,128)(2,1)} %gate_hbm.1, bf16[1,4096,384]{2,1,0:T(8,128)(2,1)} %up_hbm.1, ...), custom_call_target="tpu_custom_call" | custom-call | flops 3145728 | bytes 12582912 | tf_op jit(solution)/shard_map/dequant_in/pallas_call | solution.py:241
  11.8 3.6 %collective-permute-done.3._.refs_8_ = bf16[4,16,512]{2,1,0:T(8,128)(2,1)S(1)} collective-permute-done((bf16[4,16,512]{2,1,0:T(8,128)(2,1)S(1)}, bf16[4,16,512]{2,1,0:T(8,128)(2,1)S(1)}, u32[]{:S(2)}, u32[]{:S(2)}) %collective-permute-start.3) | collective-permute-done | bytes 65568 | tf_op jit(solution)/shard_map/ppermute | solution.py:90
  16.4 1.4 %collective-permute-start.5 = (bf16[64,1408]{1,0:T(8,128)(2,1)S(1)}, bf16[64,1408]{1,0:T(8,128)(2,1)S(1)}, u32[]{:S(2)}, u32[]{:S(2)}) collective-permute-start(bf16[64,1408]{1,0:T(8,128)(2,1)S(1)} %collective-permute-done.refs_1_), channel_id=1, source_target_pairs={{8,0},{5,1},{10,2},{7,3},{12,4},{1,5},{14,6},{3,7},{0,8},{13,9},{2... | collective-permute-start | bytes 540680 | tf_op jit(solution)/shard_map/ppermute | solution.py:90
  17.9 1.6 %collective-permute-start.6 = (bf16[4,16,512]{2,1,0:T(8,128)(2,1)S(1)}, bf16[4,16,512]{2,1,0:T(8,128)(2,1)S(1)}, u32[]{:S(2)}, u32[]{:S(2)}) collective-permute-start(bf16[4,16,512]{2,1,0:T(8,128)(2,1)S(1)} %pad_maximum_fusion.9), channel_id=1, source_target_pairs={{16,0},{17,1},{18,2},{19,3},{20,4},{21,5},{22,6},{23,7},{24,8},{25... | collective-permute-start | bytes 196616 | tf_op jit(solution)/shard_map/ppermute | solution.py:90
  19.5 2.1 %dequant_down.1 = (bf16[384,2048]{1,0:T(8,128)(2,1)S(1)}, bf16[384,2048]{1,0:T(8,128)(2,1)S(1)}) custom-call(s32[1]{0:T(128)} %bitcast.1.exp_ref, s32[3,1,32]{2,1,0:T(1,128)} %bitcast.27, bf16[1,384,4096]{2,1,0:T(8,128)(2,1)} %down_hbm.1, bf16[4,16,512]{2,1,0:T(8,128)(2,1)S(1)} %collective-permute-done.3._.refs_8_), custom_call_target="tpu_custom_call" | custom-call | flops 1572864 | bytes 6291456 | tf_op jit(solution)/shard_map/dequant_down/pallas_call | solution.py:290
  21.6 2.6 %collective-permute-done.6.refs_9_ = bf16[4,16,512]{2,1,0:T(8,128)(2,1)S(1)} collective-permute-done((bf16[4,16,512]{2,1,0:T(8,128)(2,1)S(1)}, bf16[4,16,512]{2,1,0:T(8,128)(2,1)S(1)}, u32[]{:S(2)}, u32[]{:S(2)}) %collective-permute-start.6) | collective-permute-done | bytes 65568 | tf_op jit(solution)/shard_map/ppermute | solution.py:90
  27.9 4.1 %collective-permute-done.9.refs_10_ = bf16[4,16,512]{2,1,0:T(8,128)(2,1)S(1)} collective-permute-done((bf16[4,16,512]{2,1,0:T(8,128)(2,1)S(1)}, bf16[4,16,512]{2,1,0:T(8,128)(2,1)S(1)}, u32[]{:S(2)}, u32[]{:S(2)}) %collective-permute-start.9) | collective-permute-done | bytes 65568 | tf_op jit(solution)/shard_map/ppermute | solution.py:90
  32.0 4.5 %attend.1 = (f32[256,256]{1,0:T(8,128)S(1)}, f32[256,256]{1,0:T(8,128)S(1)}, bf16[544,256]{1,0:T(8,128)(2,1)S(1)}, bf16[32,256]{1,0:T(8,128)(2,1)S(1)}) custom-call(s32[1]{0:T(128)} %bitcast.ctx_ref, s32[1]{0:T(128)} %bitcast.1.exp_ref, s32[8]{0:T(128)S(1)} %copy-done.2, bf16[64,1408]{1,0:T(8,128)(2,1)S(1)} %get-tuple-element.71._.refs_0_, ...), custom_call_target="tpu_custom_call" | custom-call | flops 1610612736 | bytes 8388608 | tf_op jit(solution)/shard_map/attend/pallas_call | solution.py:640
  36.6 1.5 %collective-permute-done.11.refs_1_ = bf16[544,256]{1,0:T(8,128)(2,1)S(1)} collective-permute-done((bf16[544,256]{1,0:T(8,128)(2,1)S(1)}, bf16[544,256]{1,0:T(8,128)(2,1)S(1)}, u32[]{:S(2)}, u32[]{:S(2)}) %collective-permute-start.11) | collective-permute-done | bytes 278560 | tf_op jit(solution)/shard_map/ppermute | solution.py:25
  38.2 1.6 %collective-permute-start.12 = (bf16[288,256]{1,0:T(8,128)(2,1)S(1)}, bf16[288,256]{1,0:T(8,128)(2,1)S(1)}, u32[]{:S(2)}, u32[]{:S(2)}) collective-permute-start(bf16[288,256]{1,0:T(8,128)(2,1)S(1)} %pad_maximum_fusion.8), channel_id=1, source_target_pairs={{0,2},{1,3},{2,0},{3,1},{4,6},{5,7},{6,4},{7,5},{8,10},{9,11},{10,... | collective-permute-start | bytes 442376 | tf_op jit(solution)/shard_map/ppermute | solution.py:25
  39.8 4.3 %collective-permute-done.12.refs_2_ = bf16[288,256]{1,0:T(8,128)(2,1)S(1)} collective-permute-done((bf16[288,256]{1,0:T(8,128)(2,1)S(1)}, bf16[288,256]{1,0:T(8,128)(2,1)S(1)}, u32[]{:S(2)}, u32[]{:S(2)}) %collective-permute-start.12) | collective-permute-done | bytes 147488 | tf_op jit(solution)/shard_map/ppermute | solution.py:25
  44.2 2.0 %collective-permute-start.13 = (bf16[256,256]{1,0:T(8,128)(2,1)S(1)}, bf16[256,256]{1,0:T(8,128)(2,1)S(1)}, u32[]{:S(2)}, u32[]{:S(2)}) collective-permute-start(bf16[256,256]{1,0:T(8,128)(2,1)S(1)} %add_convert_fusion.8.refs_0_.refs_6_), channel_id=1, source_target_pairs={{16,0},{17,1},{18,2},{19,3},{20,4},{21,5},{22,6},{23,7},{24,8},{25... | collective-permute-start | bytes 393224 | tf_op jit(solution)/shard_map/ppermute | solution.py:90
  46.2 1.5 %collective-permute-start.14 = (bf16[256,256]{1,0:T(8,128)(2,1)S(1)}, bf16[256,256]{1,0:T(8,128)(2,1)S(1)}, u32[]{:S(2)}, u32[]{:S(2)}) collective-permute-start(bf16[256,256]{1,0:T(8,128)(2,1)S(1)} %add_convert_fusion.8.refs_0_.refs_6_), channel_id=1, source_target_pairs={{2,0},{5,1},{0,2},{7,3},{6,4},{1,5},{4,6},{3,7},{10,8},{13,9},{8,1... | collective-permute-start | bytes 393224 | tf_op jit(solution)/shard_map/ppermute | solution.py:90
  47.7 1.2 %collective-permute-start.15 = (bf16[256,256]{1,0:T(8,128)(2,1)S(1)}, bf16[256,256]{1,0:T(8,128)(2,1)S(1)}, u32[]{:S(2)}, u32[]{:S(2)}) collective-permute-start(bf16[256,256]{1,0:T(8,128)(2,1)S(1)} %add_convert_fusion.8.refs_0_.refs_6_), channel_id=1, source_target_pairs={{4,0},{3,1},{6,2},{1,3},{0,4},{7,5},{2,6},{5,7},{12,8},{11,9},{14,... | collective-permute-start | bytes 393224 | tf_op jit(solution)/shard_map/ppermute | solution.py:90
  49.8 3.0 %collective-permute-done.13.refs_0_.refs_7_ = bf16[256,256]{1,0:T(8,128)(2,1)S(1)} collective-permute-done((bf16[256,256]{1,0:T(8,128)(2,1)S(1)}, bf16[256,256]{1,0:T(8,128)(2,1)S(1)}, u32[]{:S(2)}, u32[]{:S(2)}) %collective-permute-start.13) | collective-permute-done | bytes 131104 | tf_op jit(solution)/shard_map/ppermute | solution.py:90
  52.7 1.7 %collective-permute-done.16.refs_3_.refs_10_ = bf16[256,256]{1,0:T(8,128)(2,1)S(1)} collective-permute-done((bf16[256,256]{1,0:T(8,128)(2,1)S(1)}, bf16[256,256]{1,0:T(8,128)(2,1)S(1)}, u32[]{:S(2)}, u32[]{:S(2)}) %collective-permute-start.16) | collective-permute-done | bytes 131104 | tf_op jit(solution)/shard_map/ppermute | solution.py:90
  56.8 5.7 %collective-permute-done.17.refs_4_.refs_1_.refs_11_ = bf16[512,256]{1,0:T(8,128)(2,1)S(1)} collective-permute-done((bf16[512,256]{1,0:T(8,128)(2,1)S(1)}, bf16[512,256]{1,0:T(8,128)(2,1)S(1)}, u32[]{:S(2)}, u32[]{:S(2)}) %collective-permute-start.17) | collective-permute-done | bytes 262176 | tf_op jit(solution)/shard_map/ppermute | solution.py:90
  65.4 5.1 %collective-permute-done.21.refs_5_.refs_14_ = bf16[256,256]{1,0:T(8,128)(2,1)S(1)} collective-permute-done((bf16[256,256]{1,0:T(8,128)(2,1)S(1)}, bf16[256,256]{1,0:T(8,128)(2,1)S(1)}, u32[]{:S(2)}, u32[]{:S(2)}) %collective-permute-start.21) | collective-permute-done | bytes 131104 | tf_op jit(solution)/shard_map/ppermute | solution.py:90
  71.4 2.0 %experts_in_first.1 = (f32[512,1536]{1,0:T(8,128)S(1)}, f32[512,1]{1,0:T(8,128)S(1)}) custom-call(s32[1]{0:T(128)} %bitcast.ctx_ref, s32[1]{0:T(128)} %bitcast.1.exp_ref, bf16[256,256]{1,0:T(8,128)(2,1)S(1)} %add_convert_fusion.8.refs_0_.refs_6_, bf16[256,256]{1,0:T(8,128)(2,1)S(1)} %collective-permute-done.14.refs_1_.refs_8_, ...), custom_call_target="tpu_custom_call" | custom-call | flops 1610612736 | bytes 8388608 | tf_op jit(solution)/shard_map/experts_in_first/pallas_call | solution.py:693
  73.5 2.0 %collective-permute-done.23.refs_7_ = bf16[256,256]{1,0:T(8,128)(2,1)S(1)} collective-permute-done((bf16[256,256]{1,0:T(8,128)(2,1)S(1)}, bf16[256,256]{1,0:T(8,128)(2,1)S(1)}, u32[]{:S(2)}, u32[]{:S(2)}) %collective-permute-start.23) | collective-permute-done | bytes 131104 | tf_op jit(solution)/shard_map/ppermute | solution.py:90
  79.1 1.9 %experts_out.2 = (f32[32,2048]{1,0:T(8,128)S(1)}, f32[32,2048]{1,0:T(8,128)S(1)}, bf16[32,2048]{1,0:T(8,128)(2,1)S(1)}, bf16[32,2048]{1,0:T(8,128)(2,1)S(1)}, f3...) custom-call(s32[1]{0:T(128)} %bitcast.ctx_ref, ...), custom_call_target="tpu_custom_call" | custom-call | flops 805306368 | bytes 8388608 | tf_op jit(solution)/shard_map/experts_out/pallas_call | solution.py:748
  83.1 1.8 %experts_out.3 = (f32[32,2048]{1,0:T(8,128)S(1)}, f32[32,2048]{1,0:T(8,128)S(1)}, f32[32,2048]{1,0:T(8,128)S(1)}, bf16[32,2048]{1,0:T(8,128)(2,1)S(1)}, f32[32,2...) custom-call(s32[1]{0:T(128)} %bitcast.ctx_ref, ...), custom_call_target="tpu_custom_call" | custom-call | flops 805306368 | bytes 8388608 | tf_op jit(solution)/shard_map/experts_out/pallas_call | solution.py:748
  87.7 1.2 %collective-permute-start.31 = (bf16[64,2048]{1,0:T(8,128)(2,1)S(1)}, bf16[64,2048]{1,0:T(8,128)(2,1)S(1)}, u32[]{:S(2)}, u32[]{:S(2)}) collective-permute-start(bf16[64,2048]{1,0:T(8,128)(2,1)S(1)} %pad_maximum_fusion.6), channel_id=1, source_target_pairs={{4,0},{3,1},{6,2},{1,3},{0,4},{7,5},{2,6},{5,7},{12,8},{11,9},{14,... | collective-permute-start | bytes 786440 | tf_op jit(solution)/shard_map/ppermute | solution.py:90
  88.9 3.3 %collective-permute-done.29 = bf16[32,2048]{1,0:T(8,128)(2,1)S(1)} collective-permute-done((bf16[32,2048]{1,0:T(8,128)(2,1)S(1)}, bf16[32,2048]{1,0:T(8,128)(2,1)S(1)}, u32[]{:S(2)}, u32[]{:S(2)}) %collective-permute-start.29) | collective-permute-done | bytes 131104 | tf_op jit(solution)/shard_map/ppermute | solution.py:90
  93.3 1.4 %collective-permute-start.30 = (bf16[64,2048]{1,0:T(8,128)(2,1)S(1)}, bf16[64,2048]{1,0:T(8,128)(2,1)S(1)}, u32[]{:S(2)}, u32[]{:S(2)}) collective-permute-start(bf16[64,2048]{1,0:T(8,128)(2,1)S(1)} %pad_maximum_fusion.5), channel_id=1, source_target_pairs={{2,0},{5,1},{0,2},{7,3},{6,4},{1,5},{4,6},{3,7},{10,8},{13,9},{8,1... | collective-permute-start | bytes 786440 | tf_op jit(solution)/shard_map/ppermute | solution.py:90
  94.7 1.8 %collective-permute-done.31 = bf16[64,2048]{1,0:T(8,128)(2,1)S(1)} collective-permute-done((bf16[64,2048]{1,0:T(8,128)(2,1)S(1)}, bf16[64,2048]{1,0:T(8,128)(2,1)S(1)}, u32[]{:S(2)}, u32[]{:S(2)}) %collective-permute-start.31) | collective-permute-done | bytes 262176 | tf_op jit(solution)/shard_map/ppermute | solution.py:90
  96.5 2.8 %collective-permute-done.32 = bf16[64,2048]{1,0:T(8,128)(2,1)S(1)} collective-permute-done((bf16[64,2048]{1,0:T(8,128)(2,1)S(1)}, bf16[64,2048]{1,0:T(8,128)(2,1)S(1)}, u32[]{:S(2)}, u32[]{:S(2)}) %collective-permute-start.32) | collective-permute-done | bytes 262176 | tf_op jit(solution)/shard_map/ppermute | solution.py:90
  99.9 2.5 %collective-permute-start.33 = (bf16[32,2048]{1,0:T(8,128)(2,1)S(1)}, bf16[32,2048]{1,0:T(8,128)(2,1)S(1)}, u32[]{:S(2)}, u32[]{:S(2)}) collective-permute-start(bf16[32,2048]{1,0:T(8,128)(2,1)S(1)} %get-tuple-element.137), channel_id=1, source_target_pairs={{16,0},{17,1},{18,2},{19,3},{20,4},{21,5},{22,6},{23,7},{24,8},{25... | collective-permute-start | bytes 393224 | tf_op jit(solution)/shard_map/ppermute | solution.py:90
  104.6 2.4 %collective-permute-done.33 = bf16[32,2048]{1,0:T(8,128)(2,1)S(1)} collective-permute-done((bf16[32,2048]{1,0:T(8,128)(2,1)S(1)}, bf16[32,2048]{1,0:T(8,128)(2,1)S(1)}, u32[]{:S(2)}, u32[]{:S(2)}) %collective-permute-start.33) | collective-permute-done | bytes 131104 | tf_op jit(solution)/shard_map/ppermute | solution.py:90
  (90 shorter events, 30.6 us)
Async XLA Ops:
  1.2 14.3 %collective-permute-start = (bf16[64,1408]{1,0:T(8,128)(2,1)S(1)}, bf16[64,1408]{1,0:T(8,128)(2,1)S(1)}, u32[]{:S(2)}, u32[]{:S(2)}) collective-permute-start(bf16[64,1408]{1,0:T(8,128)(2,1)S(1)} %get-tuple-element.71._.refs_0_), channel_id=1, source_target_pairs={{16,0},{17,1},{18,2},{19,3},{20,4},{21,5},{22,6},{23,7},{24,8},{25... | collective-permute-start | bytes 540680 | tf_op jit(solution)/shard_map/ppermute | solution.py:90
  5.3 10.2 %collective-permute-start.1 = (bf16[64,1408]{1,0:T(8,128)(2,1)S(1)}, bf16[64,1408]{1,0:T(8,128)(2,1)S(1)}, u32[]{:S(2)}, u32[]{:S(2)}) collective-permute-start(bf16[64,1408]{1,0:T(8,128)(2,1)S(1)} %get-tuple-element.71._.refs_0_), channel_id=1, source_target_pairs={{4,0},{9,1},{6,2},{11,3},{0,4},{13,5},{2,6},{15,7},{12,8},{1,9},{1... | collective-permute-start | bytes 540680 | tf_op jit(solution)/shard_map/ppermute | solution.py:90
  6.8 8.7 %collective-permute-start.2 = (bf16[64,1408]{1,0:T(8,128)(2,1)S(1)}, bf16[64,1408]{1,0:T(8,128)(2,1)S(1)}, u32[]{:S(2)}, u32[]{:S(2)}) collective-permute-start(bf16[64,1408]{1,0:T(8,128)(2,1)S(1)} %get-tuple-element.71._.refs_0_), channel_id=1, source_target_pairs={{8,0},{5,1},{10,2},{7,3},{12,4},{1,5},{14,6},{3,7},{0,8},{13,9},{2... | collective-permute-start | bytes 540680 | tf_op jit(solution)/shard_map/ppermute | solution.py:90
  8.4 7.1 %collective-permute-start.3 = (bf16[4,16,512]{2,1,0:T(8,128)(2,1)S(1)}, bf16[4,16,512]{2,1,0:T(8,128)(2,1)S(1)}, u32[]{:S(2)}, u32[]{:S(2)}) collective-permute-start(bf16[4,16,512]{2,1,0:T(8,128)(2,1)S(1)} %get-tuple-element.72), channel_id=1, source_target_pairs={{8,0},{5,1},{10,2},{7,3},{12,4},{1,5},{14,6},{3,7},{0,8},{13,9},{2... | collective-permute-start | bytes 196616 | tf_op jit(solution)/shard_map/ppermute | solution.py:90
  15.5 9.8 %collective-permute-start.7 = (bf16[2048,768]{1,0:T(8,128)(2,1)S(1)}, bf16[2048,768]{1,0:T(8,128)(2,1)S(1)}, u32[]{:S(2)}, u32[]{:S(2)}) collective-permute-start(bf16[2048,768]{1,0:T(8,128)(2,1)S(1)} %get-tuple-element.80), channel_id=1, source_target_pairs={{0,1},{1,0},{2,3},{3,2},{4,5},{5,4},{6,7},{7,6},{8,9},{9,8},{10,11... | collective-permute-start | bytes 9437192 | tf_op jit(solution)/shard_map/ppermute | solution.py:25
  15.6 9.7 %collective-permute-start.4 = (bf16[128,1408]{1,0:T(8,128)(2,1)S(1)}, bf16[128,1408]{1,0:T(8,128)(2,1)S(1)}, u32[]{:S(2)}, u32[]{:S(2)}) collective-permute-start(bf16[128,1408]{1,0:T(8,128)(2,1)S(1)} %pad_maximum_fusion), channel_id=1, source_target_pairs={{4,0},{9,1},{6,2},{11,3},{0,4},{13,5},{2,6},{15,7},{12,8},{1,9},{1... | collective-permute-start | bytes 1081352 | tf_op jit(solution)/shard_map/ppermute | solution.py:90
  16.4 8.9 %collective-permute-start.5 = (bf16[64,1408]{1,0:T(8,128)(2,1)S(1)}, bf16[64,1408]{1,0:T(8,128)(2,1)S(1)}, u32[]{:S(2)}, u32[]{:S(2)}) collective-permute-start(bf16[64,1408]{1,0:T(8,128)(2,1)S(1)} %collective-permute-done.refs_1_), channel_id=1, source_target_pairs={{8,0},{5,1},{10,2},{7,3},{12,4},{1,5},{14,6},{3,7},{0,8},{13,9},{2... | collective-permute-start | bytes 540680 | tf_op jit(solution)/shard_map/ppermute | solution.py:90
  17.9 6.3 %collective-permute-start.6 = (bf16[4,16,512]{2,1,0:T(8,128)(2,1)S(1)}, bf16[4,16,512]{2,1,0:T(8,128)(2,1)S(1)}, u32[]{:S(2)}, u32[]{:S(2)}) collective-permute-start(bf16[4,16,512]{2,1,0:T(8,128)(2,1)S(1)} %pad_maximum_fusion.9), channel_id=1, source_target_pairs={{16,0},{17,1},{18,2},{19,3},{20,4},{21,5},{22,6},{23,7},{24,8},{25... | collective-permute-start | bytes 196616 | tf_op jit(solution)/shard_map/ppermute | solution.py:90
  25.3 6.7 %collective-permute-start.10 = (bf16[384,2048]{1,0:T(8,128)(2,1)S(1)}, bf16[384,2048]{1,0:T(8,128)(2,1)S(1)}, u32[]{:S(2)}, u32[]{:S(2)}) collective-permute-start(bf16[384,2048]{1,0:T(8,128)(2,1)S(1)} %get-tuple-element.86), channel_id=1, source_target_pairs={{0,1},{1,0},{2,3},{3,2},{4,5},{5,4},{6,7},{7,6},{8,9},{9,8},{10,11... | collective-permute-start | bytes 4718600 | tf_op jit(solution)/shard_map/ppermute | solution.py:25
  25.8 6.2 %collective-permute-start.8 = (bf16[64,1408]{1,0:T(8,128)(2,1)S(1)}, bf16[64,1408]{1,0:T(8,128)(2,1)S(1)}, u32[]{:S(2)}, u32[]{:S(2)}) collective-permute-start(bf16[64,1408]{1,0:T(8,128)(2,1)S(1)} %collective-permute-done.5.refs_5_), channel_id=1, source_target_pairs={{4,0},{9,1},{6,2},{11,3},{0,4},{13,5},{2,6},{15,7},{12,8},{1,9},{1... | collective-permute-start | bytes 540680 | tf_op jit(solution)/shard_map/ppermute | solution.py:90
  26.7 5.2 %collective-permute-start.9 = (bf16[4,16,512]{2,1,0:T(8,128)(2,1)S(1)}, bf16[4,16,512]{2,1,0:T(8,128)(2,1)S(1)}, u32[]{:S(2)}, u32[]{:S(2)}) collective-permute-start(bf16[4,16,512]{2,1,0:T(8,128)(2,1)S(1)} %pad_maximum_fusion.10), channel_id=1, source_target_pairs={{4,0},{9,1},{6,2},{11,3},{0,4},{13,5},{2,6},{15,7},{12,8},{1,9},{1... | collective-permute-start | bytes 196616 | tf_op jit(solution)/shard_map/ppermute | solution.py:90
  38.2 6.0 %collective-permute-start.12 = (bf16[288,256]{1,0:T(8,128)(2,1)S(1)}, bf16[288,256]{1,0:T(8,128)(2,1)S(1)}, u32[]{:S(2)}, u32[]{:S(2)}) collective-permute-start(bf16[288,256]{1,0:T(8,128)(2,1)S(1)} %pad_maximum_fusion.8), channel_id=1, source_target_pairs={{0,2},{1,3},{2,0},{3,1},{4,6},{5,7},{6,4},{7,5},{8,10},{9,11},{10,... | collective-permute-start | bytes 442376 | tf_op jit(solution)/shard_map/ppermute | solution.py:25
  44.2 8.5 %collective-permute-start.13 = (bf16[256,256]{1,0:T(8,128)(2,1)S(1)}, bf16[256,256]{1,0:T(8,128)(2,1)S(1)}, u32[]{:S(2)}, u32[]{:S(2)}) collective-permute-start(bf16[256,256]{1,0:T(8,128)(2,1)S(1)} %add_convert_fusion.8.refs_0_.refs_6_), channel_id=1, source_target_pairs={{16,0},{17,1},{18,2},{19,3},{20,4},{21,5},{22,6},{23,7},{24,8},{25... | collective-permute-start | bytes 393224 | tf_op jit(solution)/shard_map/ppermute | solution.py:90
  46.2 6.5 %collective-permute-start.14 = (bf16[256,256]{1,0:T(8,128)(2,1)S(1)}, bf16[256,256]{1,0:T(8,128)(2,1)S(1)}, u32[]{:S(2)}, u32[]{:S(2)}) collective-permute-start(bf16[256,256]{1,0:T(8,128)(2,1)S(1)} %add_convert_fusion.8.refs_0_.refs_6_), channel_id=1, source_target_pairs={{2,0},{5,1},{0,2},{7,3},{6,4},{1,5},{4,6},{3,7},{10,8},{13,9},{8,1... | collective-permute-start | bytes 393224 | tf_op jit(solution)/shard_map/ppermute | solution.py:90
  47.7 5.1 %collective-permute-start.15 = (bf16[256,256]{1,0:T(8,128)(2,1)S(1)}, bf16[256,256]{1,0:T(8,128)(2,1)S(1)}, u32[]{:S(2)}, u32[]{:S(2)}) collective-permute-start(bf16[256,256]{1,0:T(8,128)(2,1)S(1)} %add_convert_fusion.8.refs_0_.refs_6_), channel_id=1, source_target_pairs={{4,0},{3,1},{6,2},{1,3},{0,4},{7,5},{2,6},{5,7},{12,8},{11,9},{14,... | collective-permute-start | bytes 393224 | tf_op jit(solution)/shard_map/ppermute | solution.py:90
  48.9 5.5 %collective-permute-start.16 = (bf16[256,256]{1,0:T(8,128)(2,1)S(1)}, bf16[256,256]{1,0:T(8,128)(2,1)S(1)}, u32[]{:S(2)}, u32[]{:S(2)}) collective-permute-start(bf16[256,256]{1,0:T(8,128)(2,1)S(1)} %add_convert_fusion.8.refs_0_.refs_6_), channel_id=1, source_target_pairs={{8,0},{9,1},{10,2},{11,3},{12,4},{13,5},{14,6},{15,7},{0,8},{1,9},... | collective-permute-start | bytes 393224 | tf_op jit(solution)/shard_map/ppermute | solution.py:90
  54.5 8.1 %collective-permute-start.17 = (bf16[512,256]{1,0:T(8,128)(2,1)S(1)}, bf16[512,256]{1,0:T(8,128)(2,1)S(1)}, u32[]{:S(2)}, u32[]{:S(2)}) collective-permute-start(bf16[512,256]{1,0:T(8,128)(2,1)S(1)} %get-tuple-element.147), channel_id=1, source_target_pairs={{2,0},{5,1},{0,2},{7,3},{6,4},{1,5},{4,6},{3,7},{10,8},{13,9},{8,1... | collective-permute-start | bytes 786440 | tf_op jit(solution)/shard_map/ppermute | solution.py:90
  55.3 7.3 %collective-permute-start.18 = (bf16[512,256]{1,0:T(8,128)(2,1)S(1)}, bf16[512,256]{1,0:T(8,128)(2,1)S(1)}, u32[]{:S(2)}, u32[]{:S(2)}) collective-permute-start(bf16[512,256]{1,0:T(8,128)(2,1)S(1)} %get-tuple-element.146), channel_id=1, source_target_pairs={{4,0},{3,1},{6,2},{1,3},{0,4},{7,5},{2,6},{5,7},{12,8},{11,9},{14,... | collective-permute-start | bytes 786440 | tf_op jit(solution)/shard_map/ppermute | solution.py:90
  56.3 6.4 %collective-permute-start.19 = (bf16[512,256]{1,0:T(8,128)(2,1)S(1)}, bf16[512,256]{1,0:T(8,128)(2,1)S(1)}, u32[]{:S(2)}, u32[]{:S(2)}) collective-permute-start(bf16[512,256]{1,0:T(8,128)(2,1)S(1)} %get-tuple-element.145), channel_id=1, source_target_pairs={{8,0},{9,1},{10,2},{11,3},{12,4},{13,5},{14,6},{15,7},{0,8},{1,9},... | collective-permute-start | bytes 786440 | tf_op jit(solution)/shard_map/ppermute | solution.py:90
  62.7 7.8 %collective-permute-start.20 = (bf16[512,256]{1,0:T(8,128)(2,1)S(1)}, bf16[512,256]{1,0:T(8,128)(2,1)S(1)}, u32[]{:S(2)}, u32[]{:S(2)}) collective-permute-start(bf16[512,256]{1,0:T(8,128)(2,1)S(1)} %collective-permute-done.17.refs_4_.refs_1_.refs_11_), channel_id=1, source_target_pairs={{4,0},{3,1},{6,2},{1,3},{0,4},{7,5},{2,6},{5,7},{12,8},{11,9},{14,... | collective-permute-start | bytes 786440 | tf_op jit(solution)/shard_map/ppermute | solution.py:90
  63.7 6.8 %collective-permute-start.21 = (bf16[256,256]{1,0:T(8,128)(2,1)S(1)}, bf16[256,256]{1,0:T(8,128)(2,1)S(1)}, u32[]{:S(2)}, u32[]{:S(2)}) collective-permute-start(bf16[256,256]{1,0:T(8,128)(2,1)S(1)} %slice.86), channel_id=1, source_target_pairs={{4,0},{3,1},{6,2},{1,3},{0,4},{7,5},{2,6},{5,7},{12,8},{11,9},{14,... | collective-permute-start | bytes 393224 | tf_op jit(solution)/shard_map/ppermute | solution.py:90
  64.8 5.7 %collective-permute-start.22 = (bf16[256,256]{1,0:T(8,128)(2,1)S(1)}, bf16[256,256]{1,0:T(8,128)(2,1)S(1)}, u32[]{:S(2)}, u32[]{:S(2)}) collective-permute-start(bf16[256,256]{1,0:T(8,128)(2,1)S(1)} %slice.87), channel_id=1, source_target_pairs={{8,0},{9,1},{10,2},{11,3},{12,4},{13,5},{14,6},{15,7},{0,8},{1,9},... | collective-permute-start | bytes 393224 | tf_op jit(solution)/shard_map/ppermute | solution.py:90
  70.5 5.0 %collective-permute-start.23 = (bf16[256,256]{1,0:T(8,128)(2,1)S(1)}, bf16[256,256]{1,0:T(8,128)(2,1)S(1)}, u32[]{:S(2)}, u32[]{:S(2)}) collective-permute-start(bf16[256,256]{1,0:T(8,128)(2,1)S(1)} %collective-permute-done.22.refs_6_.refs_15_), channel_id=1, source_target_pairs={{4,0},{3,1},{6,2},{1,3},{0,4},{7,5},{2,6},{5,7},{12,8},{11,9},{14,... | collective-permute-start | bytes 393224 | tf_op jit(solution)/shard_map/ppermute | solution.py:90
  77.9 5.2 %collective-permute-start.26 = (bf16[256,1664]{1,0:T(8,128)(2,1)S(1)}, bf16[256,1664]{1,0:T(8,128)(2,1)S(1)}, u32[]{:S(2)}, u32[]{:S(2)}) collective-permute-start(bf16[256,1664]{1,0:T(8,128)(2,1)S(1)} %experts_in_second.3.refs_5_.act_ref), channel_id=1, source_target_pairs={{0,1},{1,0},{2,3},{3,2},{4,5},{5,4},{6,7},{7,6},{8,9},{9,8},{10,11... | collective-permute-start | bytes 2555912 | tf_op jit(solution)/shard_map/ppermute | solution.py:25
  81.0 5.0 %collective-permute-start.25 = (bf16[32,2048]{1,0:T(8,128)(2,1)S(1)}, bf16[32,2048]{1,0:T(8,128)(2,1)S(1)}, u32[]{:S(2)}, u32[]{:S(2)}) collective-permute-start(bf16[32,2048]{1,0:T(8,128)(2,1)S(1)} %get-tuple-element.106), channel_id=1, source_target_pairs={{4,0},{3,1},{6,2},{1,3},{0,4},{7,5},{2,6},{5,7},{12,8},{11,9},{14,... | collective-permute-start | bytes 393224 | tf_op jit(solution)/shard_map/ppermute | solution.py:90
  82.1 6.9 %collective-permute-start.28 = (bf16[32,2048]{1,0:T(8,128)(2,1)S(1)}, bf16[32,2048]{1,0:T(8,128)(2,1)S(1)}, u32[]{:S(2)}, u32[]{:S(2)}) collective-permute-start(bf16[32,2048]{1,0:T(8,128)(2,1)S(1)} %get-tuple-element.120), channel_id=1, source_target_pairs={{4,0},{3,1},{6,2},{1,3},{0,4},{7,5},{2,6},{5,7},{12,8},{11,9},{14,... | collective-permute-start | bytes 393224 | tf_op jit(solution)/shard_map/ppermute | solution.py:90
  86.1 6.4 %collective-permute-start.27 = (bf16[64,2048]{1,0:T(8,128)(2,1)S(1)}, bf16[64,2048]{1,0:T(8,128)(2,1)S(1)}, u32[]{:S(2)}, u32[]{:S(2)}) collective-permute-start(bf16[64,2048]{1,0:T(8,128)(2,1)S(1)} %pad_maximum_fusion.4), channel_id=1, source_target_pairs={{4,0},{3,1},{6,2},{1,3},{0,4},{7,5},{2,6},{5,7},{12,8},{11,9},{14,... | collective-permute-start | bytes 786440 | tf_op jit(solution)/shard_map/ppermute | solution.py:90
  87.2 5.1 %collective-permute-start.29 = (bf16[32,2048]{1,0:T(8,128)(2,1)S(1)}, bf16[32,2048]{1,0:T(8,128)(2,1)S(1)}, u32[]{:S(2)}, u32[]{:S(2)}) collective-permute-start(bf16[32,2048]{1,0:T(8,128)(2,1)S(1)} %add_convert_fusion.7), channel_id=1, source_target_pairs={{8,0},{9,1},{10,2},{11,3},{12,4},{13,5},{14,6},{15,7},{0,8},{1,9},... | collective-permute-start | bytes 393224 | tf_op jit(solution)/shard_map/ppermute | solution.py:90
  87.7 8.8 %collective-permute-start.31 = (bf16[64,2048]{1,0:T(8,128)(2,1)S(1)}, bf16[64,2048]{1,0:T(8,128)(2,1)S(1)}, u32[]{:S(2)}, u32[]{:S(2)}) collective-permute-start(bf16[64,2048]{1,0:T(8,128)(2,1)S(1)} %pad_maximum_fusion.6), channel_id=1, source_target_pairs={{4,0},{3,1},{6,2},{1,3},{0,4},{7,5},{2,6},{5,7},{12,8},{11,9},{14,... | collective-permute-start | bytes 786440 | tf_op jit(solution)/shard_map/ppermute | solution.py:90
  92.6 6.7 %collective-permute-start.32 = (bf16[64,2048]{1,0:T(8,128)(2,1)S(1)}, bf16[64,2048]{1,0:T(8,128)(2,1)S(1)}, u32[]{:S(2)}, u32[]{:S(2)}) collective-permute-start(bf16[64,2048]{1,0:T(8,128)(2,1)S(1)} %pad_maximum_fusion.7), channel_id=1, source_target_pairs={{8,0},{9,1},{10,2},{11,3},{12,4},{13,5},{14,6},{15,7},{0,8},{1,9},... | collective-permute-start | bytes 786440 | tf_op jit(solution)/shard_map/ppermute | solution.py:90
  93.3 6.4 %collective-permute-start.30 = (bf16[64,2048]{1,0:T(8,128)(2,1)S(1)}, bf16[64,2048]{1,0:T(8,128)(2,1)S(1)}, u32[]{:S(2)}, u32[]{:S(2)}) collective-permute-start(bf16[64,2048]{1,0:T(8,128)(2,1)S(1)} %pad_maximum_fusion.5), channel_id=1, source_target_pairs={{2,0},{5,1},{0,2},{7,3},{6,4},{1,5},{4,6},{3,7},{10,8},{13,9},{8,1... | collective-permute-start | bytes 786440 | tf_op jit(solution)/shard_map/ppermute | solution.py:90
  99.9 7.2 %collective-permute-start.33 = (bf16[32,2048]{1,0:T(8,128)(2,1)S(1)}, bf16[32,2048]{1,0:T(8,128)(2,1)S(1)}, u32[]{:S(2)}, u32[]{:S(2)}) collective-permute-start(bf16[32,2048]{1,0:T(8,128)(2,1)S(1)} %get-tuple-element.137), channel_id=1, source_target_pairs={{16,0},{17,1},{18,2},{19,3},{20,4},{21,5},{22,6},{23,7},{24,8},{25... | collective-permute-start | bytes 393224 | tf_op jit(solution)/shard_map/ppermute | solution.py:90
  (9 other events, 95.6 us)

commit v7 on v6

--- a/solution.py
+++ b/solution.py
@@ -106,7 +106,11 @@
             rest = tuple(sorted(key for key in left if not any(key in group for group in groups)))
             for group in groups + [rest] * bool(rest):
                 sends.append((moves, group, tuple(left[key] for key in group)))
-        sends.sort(key=lambda send: -len(send[1]) * (2 if send[0][0][0] == top > 2 else 1))
+        def load(send):
+            share = 1 if send[0][0] == send[0][1] else 0.5
+            return len(send[1]) * (2 if send[0][0][0] == top > 2 else share)
+
+        sends.sort(key=lambda send: (-load(send), send[0][0] != send[0][1]))
         arrays = arrays + [send[2] for send in sends]
         stages.append(sends)
     return stages
@@ -156,9 +160,10 @@
 def pack_kernel(plan, ctx_ref, exp_ref, key_scale_hbm, value_scale_hbm, query_hbm, key_hbm, value_hbm, ids_hbm,
                 route_hbm, residual_hbm, packed_ref, near_ref, far_ref, key_scale_ref, value_scale_ref,
                 key_ref, value_ref, ids_ref, route_ref, sems):
-    heads, group, piece_places = plan
+    heads, group, x_count, piece_places = plan
     span, width = query_hbm.shape
     half, tok, cols = near_ref.shape
+    cols = cols - HEAD_SIZE
     my_ctx, my_exp = ctx_ref[0], exp_ref[0]
     kv_head = my_exp * heads // group
     at = pl.ds(pl.multiple_of(kv_head * HEAD_SIZE, HEAD_SIZE), HEAD_SIZE)
@@ -175,7 +180,7 @@
     for ref, places in zip((near_ref, far_ref), piece_places):
         for number, place in enumerate(places):
             col = pl.multiple_of(lax.bitwise_xor(my_ctx, by_core(core, place, 0)) * cols, cols)
-            pairs.append((residual_hbm.at[:, pl.ds(col, cols)], ref.at[number]))
+            pairs.append((residual_hbm.at[:, pl.ds(col, cols)], ref.at[number, :, 0:cols]))
     copies = copy_all(sems, pairs)
     for copy in copies[:6]:
         copy.wait()
@@ -197,12 +202,16 @@
         dense = dense + jnp.where(ids_ref[k : k + 1, :] == number, route_ref[k : k + 1, :], 0.0)
     dense = jnp.concatenate([dense, jnp.zeros((128, 128 - tok), jnp.float32)], axis=1)
     dense = jnp.transpose(dense)[:tok, :]
-    high = dense.astype(jnp.bfloat16)
-    packed_ref[0:tok, 2 * HEAD_SIZE + width :] = high
-    packed_ref[tok : 2 * tok, 2 * HEAD_SIZE + width :] = (dense - high.astype(jnp.float32)).astype(
-        jnp.bfloat16
-    )
-    packed_ref[2 * tok :, 2 * HEAD_SIZE + width :] = jnp.zeros((span - 2 * tok, 128), jnp.bfloat16)
+    lane = lax.broadcasted_iota(jnp.int32, (tok, HEAD_SIZE), 1)
+    for ref, places in zip((near_ref, far_ref), piece_places):
+        for number, place in enumerate(places):
+            expert = lax.bitwise_xor(my_ctx, by_core(core, place, 0)) * x_count
+            block = jnp.zeros((tok, HEAD_SIZE), jnp.float32)
+            for x in range(x_count):
+                column = jnp.sum(jnp.where(lane == expert + x, dense, 0.0), axis=1, keepdims=True)
+                high = column.astype(jnp.bfloat16).astype(jnp.float32)
+                block = jnp.where(lane == x, high, jnp.where(lane == x_count + x, column - high, block))
+            ref[number, :, cols:] = block.astype(jnp.bfloat16)
     for copy in copies[6:]:
         copy.wait()
 
@@ -328,11 +337,12 @@
     places = lane % span
     for offset, ref in enumerate(packed):
         key_scr[pl.ds(offset * span, span), :] = ref[:, 0:HEAD_SIZE]
-        value_scr[pl.ds(offset * span, span), :] = ref[:, HEAD_SIZE : 2 * HEAD_SIZE]
+        value_scr[pl.ds(offset * span, span), 0:HEAD_SIZE] = ref[:, HEAD_SIZE : 2 * HEAD_SIZE]
         base = order_ref[lax.bitwise_xor(my_ctx, by_core(my_core, places_of[offset], 0))] * span
         places = places + jnp.where(lane // span == offset, base, 0)
     place_scr[...] = places
-    scale = 1.0 / math.sqrt(HEAD_SIZE)
+    scale = math.log2(math.e) / math.sqrt(HEAD_SIZE)
+    value_scr[:, HEAD_SIZE:] = jnp.ones((positions, HEAD_SIZE), jnp.bfloat16)
     for offset, ref in enumerate(packed):
         source = lax.bitwise_xor(my_ctx, by_core(my_core, places_of[offset], 0))
         queries = jnp.concatenate(
@@ -344,15 +354,14 @@
         own_place = order_ref[source] * span + lax.broadcasted_iota(jnp.int32, (span, positions), 0)
         bias = jnp.where(place_scr[0:1, :] <= own_place, 0.0, -1e30)
         scores = scores.reshape(heads, span, positions) * scale + bias[None]
-        largest = jnp.max(scores, axis=-1, keepdims=True)
-        exps = jnp.exp(scores - largest)
-        total = jnp.sum(exps, axis=-1, keepdims=True)
+        exps = jnp.exp2(scores - jnp.max(scores, axis=-1, keepdims=True))
         mixed = jnp.dot(
             exps.astype(jnp.bfloat16).reshape(heads * span, positions),
             value_scr[...],
             preferred_element_type=jnp.float32,
-        ).reshape(heads, span, HEAD_SIZE)
-        mixed = (mixed / total).astype(jnp.bfloat16)
+        )
+        mixed = mixed[:, :HEAD_SIZE] * (1.0 / mixed[:, HEAD_SIZE : HEAD_SIZE + 1])
+        mixed = mixed.astype(jnp.bfloat16).reshape(heads, span, HEAD_SIZE)
         for owner in range(exp_count):
             x_off = lax.bitwise_xor(my_x, owner // 2)
             row = pl.multiple_of(((x_off * ctx_count + source) * 2 + owner % 2) * tok, tok)
@@ -363,7 +372,6 @@
 
     cols = weight_ref.shape[1] // 2
     per_x = 2 * ctx_count * tok
-    first = (heads + 2) * HEAD_SIZE
     route_lane = lax.broadcasted_iota(jnp.int32, (tok, HEAD_SIZE), 1)
     route_base = x_count * per_x
     for x_off in range(x_count):
@@ -381,13 +389,13 @@
                     piece = piece_refs[array][place, :, pl.ds(pl.multiple_of(side * cols, cols), cols)]
                     value = out_ref[at, :].astype(jnp.float32) + piece.astype(jnp.float32)
                     out_ref[at, :] = value.astype(out_ref.dtype)
-        expert = my_ctx * x_count + lax.bitwise_xor(my_x, x_off)
         block_out = jnp.zeros((tok, HEAD_SIZE), jnp.float32)
-        for offset, ref in enumerate(packed):
-            source = lax.bitwise_xor(my_ctx, by_core(my_core, places_of[offset], 0))
+        for (array, place), place_of in zip(piece_places, places_of):
+            source = lax.bitwise_xor(my_ctx, by_core(my_core, place_of, 0))
+            block = piece_refs[array][place, :, 2 * cols :].astype(jnp.float32)
             for part_of in range(2):
-                block = ref[part_of * tok : (part_of + 1) * tok, first:].astype(jnp.float32)
-                column = jnp.sum(jnp.where(route_lane == expert, block, 0.0), axis=1, keepdims=True)
+                wanted = lax.bitwise_xor(my_x, x_off) + part_of * x_count
+                column = jnp.sum(jnp.where(route_lane == wanted, block, 0.0), axis=1, keepdims=True)
                 block_out = jnp.where(route_lane == source + part_of * ctx_count, column, block_out)
         for ref, base in ((give_ref, route_base), (own_route_ref, 0)):
             at = pl.ds(base + x_off * tok, tok)
@@ -559,17 +567,17 @@
     route, places = gather_route(ctx_count, x_count)
 
     hbm = pl.BlockSpec(memory_space=pltpu.HBM)
-    piece_shape = jax.ShapeDtypeStruct((ctx_count // 2, tok, 2 * cols), bf16)
+    piece_shape = jax.ShapeDtypeStruct((ctx_count // 2, tok, 2 * cols + HEAD_SIZE), bf16)
     row_route, row_places = gather_route(ctx_count, x_count, rows_only=True)
     names = sorted(row_places)
     piece_names = [[key for key in names if bool(key[0] & 2) == sent] for sent in (False, True)]
     piece_places = tuple(tuple(row_places[key] for key in keys) for keys in piece_names)
     packed, near, far = pl.pallas_call(
-        functools.partial(pack_kernel, (heads, group, piece_places)),
+        functools.partial(pack_kernel, (heads, group, x_count, piece_places)),
         in_specs=[smem] * 2 + [hbm] * 8,
         out_specs=[vmem] * 3,
         out_shape=[
-            jax.ShapeDtypeStruct((span, query_width + 3 * HEAD_SIZE), bf16),
+            jax.ShapeDtypeStruct((span, query_width + 2 * HEAD_SIZE), bf16),
             piece_shape,
             piece_shape,
         ],
@@ -600,7 +608,7 @@
     )
     piece_arrays = [near]
     piece_at = {(0, key[0]): (0, place) for place, key in enumerate(piece_names[0])}
-    piece_bits = [1, *range(bits_of(ctx_count) - 1, 1, -1), 0]
+    piece_bits = [1, 0, *range(bits_of(ctx_count) - 1, 1, -1)]
     sending, weights = far, {}
 
     def beside(number, came):
@@ -648,7 +656,7 @@
         ],
         scratch_shapes=[
             pltpu.VMEM((positions, HEAD_SIZE), bf16),
-            pltpu.VMEM((positions, HEAD_SIZE), bf16),
+            pltpu.VMEM((positions, 2 * HEAD_SIZE), bf16),
             pltpu.VMEM((8, positions), jnp.int32),
             pltpu.VMEM((positions, query_width), bf16),
         ],

time: 112 us -> 111 us (level)
  waiting for transfers between devices: 51.4 us -> 50.2 us
    ppermute x31, waiting for transfers between devices: 43.7 us -> 42.4 us  [follow(): return lax.ppermute(array, ('ctx', 'exp'), pairs)]
  transfers between devices with their start and end apart: 38 -> 38, of which waited for: 24 -> 23; matrix products, arithmetic and copies ran while one was open for 0% -> 0% of each run, Pallas kernels for 11% -> 11%
where the time goes in v7:
time: 111 us
  waiting for transfers between devices  50.2 us (45%)
  starting transfers between devices  39.8 us (36%)
  Pallas kernels  18.7 us (17%)
    ppermute x31, waiting for transfers between devices, follow(): return lax.ppermute(array, ('ctx', 'exp'), pairs)  42.4 us
    ppermute x31, starting transfers between devices, follow(): return lax.ppermute(array, ('ctx', 'exp'), pairs)  37 us
    ppermute x7, waiting for transfers between devices, from_offset(): lax.ppermute(array, 'exp', [(i, i ^ offset) for i in range(lax.axis_size(...  7.77 us
    pallas_call x1, Pallas kernels, shards(): pl.pallas_call(functools.partial(attend_kernel, (ctx_count, exp_count, to...  4.37 us
    pallas_call x2, Pallas kernels, shards(): pl.pallas_call(functools.partial(experts_out_kernel, (ctx_count, exp_coun...  3.72 us
    pallas_call x1, Pallas kernels, deq_in(): pl.pallas_call(functools.partial(deq_in_kernel, ctx_count), in_specs=[pl....  3 us
    ppermute x7, starting transfers between devices, from_offset(): lax.ppermute(array, 'exp', [(i, i ^ offset) for i in range(lax.axis_size(...  2.82 us
    pallas_call x2, Pallas kernels, shards(): pl.pallas_call(functools.partial(experts_in_second, (ctx_count, x_count,...  2.38 us
  transfers between devices with their start and end apart: 38, of which 23 were waited for; matrix products, arithmetic and copies ran while one was open for 0% of the time, Pallas kernels for 11%

profile of v7, /device:TPU:0, one launch (start us, length us, event | category | flops | bytes accessed | tf_op | source)
XLA Modules:
  0.0 110.7 jit_solution(12466221002462009633)
XLA Ops:
  1.2 4.1 %collective-permute-start = (bf16[64,1280]{1,0:T(8,128)(2,1)S(1)}, bf16[64,1280]{1,0:T(8,128)(2,1)S(1)}, u32[]{:S(2)}, u32[]{:S(2)}) collective-permute-start(bf16[64,1280]{1,0:T(8,128)(2,1)S(1)} %get-tuple-element.71._.refs_0_), channel_id=1, source_target_pairs={{16,0},{17,1},{18,2},{19,3},{20,4},{21,5},{22,6},{23,7},{24,8},{25... | collective-permute-start | bytes 491528 | tf_op jit(solution)/shard_map/ppermute | solution.py:90
  5.3 1.5 %collective-permute-start.1 = (bf16[64,1280]{1,0:T(8,128)(2,1)S(1)}, bf16[64,1280]{1,0:T(8,128)(2,1)S(1)}, u32[]{:S(2)}, u32[]{:S(2)}) collective-permute-start(bf16[64,1280]{1,0:T(8,128)(2,1)S(1)} %get-tuple-element.71._.refs_0_), channel_id=1, source_target_pairs={{4,0},{9,1},{6,2},{11,3},{0,4},{13,5},{2,6},{15,7},{12,8},{1,9},{1... | collective-permute-start | bytes 491528 | tf_op jit(solution)/shard_map/ppermute | solution.py:90
  6.8 1.6 %collective-permute-start.2 = (bf16[64,1280]{1,0:T(8,128)(2,1)S(1)}, bf16[64,1280]{1,0:T(8,128)(2,1)S(1)}, u32[]{:S(2)}, u32[]{:S(2)}) collective-permute-start(bf16[64,1280]{1,0:T(8,128)(2,1)S(1)} %get-tuple-element.71._.refs_0_), channel_id=1, source_target_pairs={{8,0},{5,1},{10,2},{7,3},{12,4},{1,5},{14,6},{3,7},{0,8},{13,9},{2... | collective-permute-start | bytes 491528 | tf_op jit(solution)/shard_map/ppermute | solution.py:90
  8.8 3.0 %dequant_in.1 = (bf16[2048,768]{1,0:T(8,128)(2,1)S(1)}, bf16[2048,768]{1,0:T(8,128)(2,1)S(1)}) custom-call(s32[1]{0:T(128)} %bitcast.1.exp_ref, s32[3,1,32]{2,1,0:T(1,128)} %bitcast.25, s32[3,1,32]{2,1,0:T(1,128)} %bitcast.26, bf16[1,4096,384]{2,1,0:T(8,128)(2,1)} %gate_hbm.1, bf16[1,4096,384]{2,1,0:T(8,128)(2,1)} %up_hbm.1, ...), custom_call_target="tpu_custom_call" | custom-call | flops 3145728 | bytes 12582912 | tf_op jit(solution)/shard_map/dequant_in/pallas_call | solution.py:250
  11.8 3.1 %collective-permute-done.3._.refs_8_ = bf16[4,16,640]{2,1,0:T(8,128)(2,1)S(1)} collective-permute-done((bf16[4,16,640]{2,1,0:T(8,128)(2,1)S(1)}, bf16[4,16,640]{2,1,0:T(8,128)(2,1)S(1)}, u32[]{:S(2)}, u32[]{:S(2)}) %collective-permute-start.3) | collective-permute-done | bytes 81952 | tf_op jit(solution)/shard_map/ppermute | solution.py:90
  15.8 1.6 %collective-permute-start.4 = (bf16[128,1280]{1,0:T(8,128)(2,1)S(1)}, bf16[128,1280]{1,0:T(8,128)(2,1)S(1)}, u32[]{:S(2)}, u32[]{:S(2)}) collective-permute-start(bf16[128,1280]{1,0:T(8,128)(2,1)S(1)} %pad_maximum_fusion.3), channel_id=1, source_target_pairs={{4,0},{9,1},{6,2},{11,3},{0,4},{13,5},{2,6},{15,7},{12,8},{1,9},{1... | collective-permute-start | bytes 983048 | tf_op jit(solution)/shard_map/ppermute | solution.py:90
  18.0 2.1 %dequant_down.1 = (bf16[384,2048]{1,0:T(8,128)(2,1)S(1)}, bf16[384,2048]{1,0:T(8,128)(2,1)S(1)}) custom-call(s32[1]{0:T(128)} %bitcast.1.exp_ref, s32[3,1,32]{2,1,0:T(1,128)} %bitcast.27, bf16[1,384,4096]{2,1,0:T(8,128)(2,1)} %down_hbm.1, bf16[4,16,640]{2,1,0:T(8,128)(2,1)S(1)} %collective-permute-done.3._.refs_8_), custom_call_target="tpu_custom_call" | custom-call | flops 1572864 | bytes 6291456 | tf_op jit(solution)/shard_map/dequant_down/pallas_call | solution.py:299
  20.1 4.2 %collective-permute-done.6.refs_9_ = bf16[4,16,640]{2,1,0:T(8,128)(2,1)S(1)} collective-permute-done((bf16[4,16,640]{2,1,0:T(8,128)(2,1)S(1)}, bf16[4,16,640]{2,1,0:T(8,128)(2,1)S(1)}, u32[]{:S(2)}, u32[]{:S(2)}) %collective-permute-start.6) | collective-permute-done | bytes 81952 | tf_op jit(solution)/shard_map/ppermute | solution.py:90
  25.7 1.6 %collective-permute-start.9 = (bf16[4,16,640]{2,1,0:T(8,128)(2,1)S(1)}, bf16[4,16,640]{2,1,0:T(8,128)(2,1)S(1)}, u32[]{:S(2)}, u32[]{:S(2)}) collective-permute-start(bf16[4,16,640]{2,1,0:T(8,128)(2,1)S(1)} %pad_maximum_fusion.10), channel_id=1, source_target_pairs={{16,0},{17,1},{18,2},{19,3},{20,4},{21,5},{22,6},{23,7},{24,8},{25... | collective-permute-start | bytes 245768 | tf_op jit(solution)/shard_map/ppermute | solution.py:90
  27.3 5.6 %collective-permute-done.9.refs_10_ = bf16[4,16,640]{2,1,0:T(8,128)(2,1)S(1)} collective-permute-done((bf16[4,16,640]{2,1,0:T(8,128)(2,1)S(1)}, bf16[4,16,640]{2,1,0:T(8,128)(2,1)S(1)}, u32[]{:S(2)}, u32[]{:S(2)}) %collective-permute-start.9) | collective-permute-done | bytes 81952 | tf_op jit(solution)/shard_map/ppermute | solution.py:90
  32.9 4.4 %attend.1 = (f32[256,256]{1,0:T(8,128)S(1)}, f32[256,256]{1,0:T(8,128)S(1)}, bf16[544,256]{1,0:T(8,128)(2,1)S(1)}, bf16[32,256]{1,0:T(8,128)(2,1)S(1)}) custom-call(s32[1]{0:T(128)} %bitcast.ctx_ref, s32[1]{0:T(128)} %bitcast.1.exp_ref, s32[8]{0:T(128)S(1)} %copy-done.2, bf16[64,1280]{1,0:T(8,128)(2,1)S(1)} %get-tuple-element.71._.refs_0_, ...), custom_call_target="tpu_custom_call" | custom-call | flops 1610612736 | bytes 8388608 | tf_op jit(solution)/shard_map/attend/pallas_call | solution.py:648
  37.4 1.5 %collective-permute-done.11.refs_1_ = bf16[544,256]{1,0:T(8,128)(2,1)S(1)} collective-permute-done((bf16[544,256]{1,0:T(8,128)(2,1)S(1)}, bf16[544,256]{1,0:T(8,128)(2,1)S(1)}, u32[]{:S(2)}, u32[]{:S(2)}) %collective-permute-start.11) | collective-permute-done | bytes 278560 | tf_op jit(solution)/shard_map/ppermute | solution.py:25
  38.9 1.6 %collective-permute-start.12 = (bf16[288,256]{1,0:T(8,128)(2,1)S(1)}, bf16[288,256]{1,0:T(8,128)(2,1)S(1)}, u32[]{:S(2)}, u32[]{:S(2)}) collective-permute-start(bf16[288,256]{1,0:T(8,128)(2,1)S(1)} %pad_maximum_fusion.8), channel_id=1, source_target_pairs={{0,2},{1,3},{2,0},{3,1},{4,6},{5,7},{6,4},{7,5},{8,10},{9,11},{10,... | collective-permute-start | bytes 442376 | tf_op jit(solution)/shard_map/ppermute | solution.py:25
  40.5 4.4 %collective-permute-done.12.refs_2_ = bf16[288,256]{1,0:T(8,128)(2,1)S(1)} collective-permute-done((bf16[288,256]{1,0:T(8,128)(2,1)S(1)}, bf16[288,256]{1,0:T(8,128)(2,1)S(1)}, u32[]{:S(2)}, u32[]{:S(2)}) %collective-permute-start.12) | collective-permute-done | bytes 147488 | tf_op jit(solution)/shard_map/ppermute | solution.py:25
  45.6 2.6 %collective-permute-start.14 = (bf16[256,256]{1,0:T(8,128)(2,1)S(1)}, bf16[256,256]{1,0:T(8,128)(2,1)S(1)}, u32[]{:S(2)}, u32[]{:S(2)}) collective-permute-start(bf16[256,256]{1,0:T(8,128)(2,1)S(1)} %add_convert_fusion.8.refs_0_.refs_6_), channel_id=1, source_target_pairs={{8,0},{9,1},{10,2},{11,3},{12,4},{13,5},{14,6},{15,7},{0,8},{1,9},... | collective-permute-start | bytes 393224 | tf_op jit(solution)/shard_map/ppermute | solution.py:90
  48.1 1.5 %collective-permute-start.15 = (bf16[256,256]{1,0:T(8,128)(2,1)S(1)}, bf16[256,256]{1,0:T(8,128)(2,1)S(1)}, u32[]{:S(2)}, u32[]{:S(2)}) collective-permute-start(bf16[256,256]{1,0:T(8,128)(2,1)S(1)} %add_convert_fusion.8.refs_0_.refs_6_), channel_id=1, source_target_pairs={{2,0},{5,1},{0,2},{7,3},{6,4},{1,5},{4,6},{3,7},{10,8},{13,9},{8,1... | collective-permute-start | bytes 393224 | tf_op jit(solution)/shard_map/ppermute | solution.py:90
  50.1 3.3 %collective-permute-done.13.refs_0_.refs_7_ = bf16[256,256]{1,0:T(8,128)(2,1)S(1)} collective-permute-done((bf16[256,256]{1,0:T(8,128)(2,1)S(1)}, bf16[256,256]{1,0:T(8,128)(2,1)S(1)}, u32[]{:S(2)}, u32[]{:S(2)}) %collective-permute-start.13) | collective-permute-done | bytes 131104 | tf_op jit(solution)/shard_map/ppermute | solution.py:90
  55.9 5.6 %collective-permute-done.17.refs_4_.refs_1_.refs_11_ = bf16[512,256]{1,0:T(8,128)(2,1)S(1)} collective-permute-done((bf16[512,256]{1,0:T(8,128)(2,1)S(1)}, bf16[512,256]{1,0:T(8,128)(2,1)S(1)}, u32[]{:S(2)}, u32[]{:S(2)}) %collective-permute-start.17) | collective-permute-done | bytes 262176 | tf_op jit(solution)/shard_map/ppermute | solution.py:90
  61.7 1.7 %collective-permute-start.21 = (bf16[512,256]{1,0:T(8,128)(2,1)S(1)}, bf16[512,256]{1,0:T(8,128)(2,1)S(1)}, u32[]{:S(2)}, u32[]{:S(2)}) collective-permute-start(bf16[512,256]{1,0:T(8,128)(2,1)S(1)} %collective-permute-done.18.refs_5_.refs_2_.refs_12_), channel_id=1, source_target_pairs={{4,0},{3,1},{6,2},{1,3},{0,4},{7,5},{2,6},{5,7},{12,8},{11,9},{14,... | collective-permute-start | bytes 786440 | tf_op jit(solution)/shard_map/ppermute | solution.py:90
  63.4 1.7 %collective-permute-start.20 = (bf16[256,256]{1,0:T(8,128)(2,1)S(1)}, bf16[256,256]{1,0:T(8,128)(2,1)S(1)}, u32[]{:S(2)}, u32[]{:S(2)}) collective-permute-start(bf16[256,256]{1,0:T(8,128)(2,1)S(1)} %slice.90), channel_id=1, source_target_pairs={{8,0},{9,1},{10,2},{11,3},{12,4},{13,5},{14,6},{15,7},{0,8},{1,9},... | collective-permute-start | bytes 393224 | tf_op jit(solution)/shard_map/ppermute | solution.py:90
  65.8 2.6 %collective-permute-done.20.refs_4_.refs_14_ = bf16[256,256]{1,0:T(8,128)(2,1)S(1)} collective-permute-done((bf16[256,256]{1,0:T(8,128)(2,1)S(1)}, bf16[256,256]{1,0:T(8,128)(2,1)S(1)}, u32[]{:S(2)}, u32[]{:S(2)}) %collective-permute-start.20) | collective-permute-done | bytes 131104 | tf_op jit(solution)/shard_map/ppermute | solution.py:90
  68.4 1.7 %collective-permute-done.22.refs_6_.refs_15_ = bf16[256,256]{1,0:T(8,128)(2,1)S(1)} collective-permute-done((bf16[256,256]{1,0:T(8,128)(2,1)S(1)}, bf16[256,256]{1,0:T(8,128)(2,1)S(1)}, u32[]{:S(2)}, u32[]{:S(2)}) %collective-permute-start.22) | collective-permute-done | bytes 131104 | tf_op jit(solution)/shard_map/ppermute | solution.py:90
  71.1 2.0 %experts_in_first.1 = (f32[512,1536]{1,0:T(8,128)S(1)}, f32[512,1]{1,0:T(8,128)S(1)}) custom-call(s32[1]{0:T(128)} %bitcast.ctx_ref, s32[1]{0:T(128)} %bitcast.1.exp_ref, bf16[256,256]{1,0:T(8,128)(2,1)S(1)} %add_convert_fusion.8.refs_0_.refs_6_, bf16[256,256]{1,0:T(8,128)(2,1)S(1)} %collective-permute-done.14.refs_1_.refs_8_, ...), custom_call_target="tpu_custom_call" | custom-call | flops 1610612736 | bytes 8388608 | tf_op jit(solution)/shard_map/experts_in_first/pallas_call | solution.py:701
  73.2 2.0 %collective-permute-done.23.refs_7_ = bf16[256,256]{1,0:T(8,128)(2,1)S(1)} collective-permute-done((bf16[256,256]{1,0:T(8,128)(2,1)S(1)}, bf16[256,256]{1,0:T(8,128)(2,1)S(1)}, u32[]{:S(2)}, u32[]{:S(2)}) %collective-permute-start.23) | collective-permute-done | bytes 131104 | tf_op jit(solution)/shard_map/ppermute | solution.py:90
  78.8 1.9 %experts_out.2 = (f32[32,2048]{1,0:T(8,128)S(1)}, f32[32,2048]{1,0:T(8,128)S(1)}, bf16[32,2048]{1,0:T(8,128)(2,1)S(1)}, bf16[32,2048]{1,0:T(8,128)(2,1)S(1)}, f3...) custom-call(s32[1]{0:T(128)} %bitcast.ctx_ref, ...), custom_call_target="tpu_custom_call" | custom-call | flops 805306368 | bytes 8388608 | tf_op jit(solution)/shard_map/experts_out/pallas_call | solution.py:756
  82.8 1.8 %experts_out.3 = (f32[32,2048]{1,0:T(8,128)S(1)}, f32[32,2048]{1,0:T(8,128)S(1)}, f32[32,2048]{1,0:T(8,128)S(1)}, bf16[32,2048]{1,0:T(8,128)(2,1)S(1)}, f32[32,2...) custom-call(s32[1]{0:T(128)} %bitcast.ctx_ref, ...), custom_call_target="tpu_custom_call" | custom-call | flops 805306368 | bytes 8388608 | tf_op jit(solution)/shard_map/experts_out/pallas_call | solution.py:756
  86.9 1.7 %collective-permute-start.27 = (bf16[32,2048]{1,0:T(8,128)(2,1)S(1)}, bf16[32,2048]{1,0:T(8,128)(2,1)S(1)}, u32[]{:S(2)}, u32[]{:S(2)}) collective-permute-start(bf16[32,2048]{1,0:T(8,128)(2,1)S(1)} %add_convert_fusion.7), channel_id=1, source_target_pairs={{8,0},{9,1},{10,2},{11,3},{12,4},{13,5},{14,6},{15,7},{0,8},{1,9},... | collective-permute-start | bytes 393224 | tf_op jit(solution)/shard_map/ppermute | solution.py:90
  89.3 2.6 %collective-permute-done.27 = bf16[32,2048]{1,0:T(8,128)(2,1)S(1)} collective-permute-done((bf16[32,2048]{1,0:T(8,128)(2,1)S(1)}, bf16[32,2048]{1,0:T(8,128)(2,1)S(1)}, u32[]{:S(2)}, u32[]{:S(2)}) %collective-permute-start.27) | collective-permute-done | bytes 131104 | tf_op jit(solution)/shard_map/ppermute | solution.py:90
  92.3 1.6 %collective-permute-start.31 = (bf16[64,2048]{1,0:T(8,128)(2,1)S(1)}, bf16[64,2048]{1,0:T(8,128)(2,1)S(1)}, u32[]{:S(2)}, u32[]{:S(2)}) collective-permute-start(bf16[64,2048]{1,0:T(8,128)(2,1)S(1)} %pad_maximum_fusion.6), channel_id=1, source_target_pairs={{2,0},{5,1},{0,2},{7,3},{6,4},{1,5},{4,6},{3,7},{10,8},{13,9},{8,1... | collective-permute-start | bytes 786440 | tf_op jit(solution)/shard_map/ppermute | solution.py:90
  96.7 2.1 %collective-permute-done.31 = bf16[64,2048]{1,0:T(8,128)(2,1)S(1)} collective-permute-done((bf16[64,2048]{1,0:T(8,128)(2,1)S(1)}, bf16[64,2048]{1,0:T(8,128)(2,1)S(1)}, u32[]{:S(2)}, u32[]{:S(2)}) %collective-permute-start.31) | collective-permute-done | bytes 262176 | tf_op jit(solution)/shard_map/ppermute | solution.py:90
  98.7 1.6 %collective-permute-done.30 = bf16[64,2048]{1,0:T(8,128)(2,1)S(1)} collective-permute-done((bf16[64,2048]{1,0:T(8,128)(2,1)S(1)}, bf16[64,2048]{1,0:T(8,128)(2,1)S(1)}, u32[]{:S(2)}, u32[]{:S(2)}) %collective-permute-start.30) | collective-permute-done | bytes 262176 | tf_op jit(solution)/shard_map/ppermute | solution.py:90
  104.4 3.5 %collective-permute-done.33 = bf16[32,2048]{1,0:T(8,128)(2,1)S(1)} collective-permute-done((bf16[32,2048]{1,0:T(8,128)(2,1)S(1)}, bf16[32,2048]{1,0:T(8,128)(2,1)S(1)}, u32[]{:S(2)}, u32[]{:S(2)}) %collective-permute-start.33) | collective-permute-done | bytes 131104 | tf_op jit(solution)/shard_map/ppermute | solution.py:90
  (88 shorter events, 28.8 us)
Async XLA Ops:
  1.2 13.8 %collective-permute-start = (bf16[64,1280]{1,0:T(8,128)(2,1)S(1)}, bf16[64,1280]{1,0:T(8,128)(2,1)S(1)}, u32[]{:S(2)}, u32[]{:S(2)}) collective-permute-start(bf16[64,1280]{1,0:T(8,128)(2,1)S(1)} %get-tuple-element.71._.refs_0_), channel_id=1, source_target_pairs={{16,0},{17,1},{18,2},{19,3},{20,4},{21,5},{22,6},{23,7},{24,8},{25... | collective-permute-start | bytes 491528 | tf_op jit(solution)/shard_map/ppermute | solution.py:90
  5.3 9.7 %collective-permute-start.1 = (bf16[64,1280]{1,0:T(8,128)(2,1)S(1)}, bf16[64,1280]{1,0:T(8,128)(2,1)S(1)}, u32[]{:S(2)}, u32[]{:S(2)}) collective-permute-start(bf16[64,1280]{1,0:T(8,128)(2,1)S(1)} %get-tuple-element.71._.refs_0_), channel_id=1, source_target_pairs={{4,0},{9,1},{6,2},{11,3},{0,4},{13,5},{2,6},{15,7},{12,8},{1,9},{1... | collective-permute-start | bytes 491528 | tf_op jit(solution)/shard_map/ppermute | solution.py:90
  6.8 8.2 %collective-permute-start.2 = (bf16[64,1280]{1,0:T(8,128)(2,1)S(1)}, bf16[64,1280]{1,0:T(8,128)(2,1)S(1)}, u32[]{:S(2)}, u32[]{:S(2)}) collective-permute-start(bf16[64,1280]{1,0:T(8,128)(2,1)S(1)} %get-tuple-element.71._.refs_0_), channel_id=1, source_target_pairs={{8,0},{5,1},{10,2},{7,3},{12,4},{1,5},{14,6},{3,7},{0,8},{13,9},{2... | collective-permute-start | bytes 491528 | tf_op jit(solution)/shard_map/ppermute | solution.py:90
  8.4 6.6 %collective-permute-start.3 = (bf16[4,16,640]{2,1,0:T(8,128)(2,1)S(1)}, bf16[4,16,640]{2,1,0:T(8,128)(2,1)S(1)}, u32[]{:S(2)}, u32[]{:S(2)}) collective-permute-start(bf16[4,16,640]{2,1,0:T(8,128)(2,1)S(1)} %get-tuple-element.72), channel_id=1, source_target_pairs={{8,0},{5,1},{10,2},{7,3},{12,4},{1,5},{14,6},{3,7},{0,8},{13,9},{2... | collective-permute-start | bytes 245768 | tf_op jit(solution)/shard_map/ppermute | solution.py:90
  15.0 9.3 %collective-permute-start.7 = (bf16[2048,768]{1,0:T(8,128)(2,1)S(1)}, bf16[2048,768]{1,0:T(8,128)(2,1)S(1)}, u32[]{:S(2)}, u32[]{:S(2)}) collective-permute-start(bf16[2048,768]{1,0:T(8,128)(2,1)S(1)} %get-tuple-element.80), channel_id=1, source_target_pairs={{0,1},{1,0},{2,3},{3,2},{4,5},{5,4},{6,7},{7,6},{8,9},{9,8},{10,11... | collective-permute-start | bytes 9437192 | tf_op jit(solution)/shard_map/ppermute | solution.py:25
  15.0 9.2 %collective-permute-start.5 = (bf16[64,1280]{1,0:T(8,128)(2,1)S(1)}, bf16[64,1280]{1,0:T(8,128)(2,1)S(1)}, u32[]{:S(2)}, u32[]{:S(2)}) collective-permute-start(bf16[64,1280]{1,0:T(8,128)(2,1)S(1)} %collective-permute-done.refs_1_), channel_id=1, source_target_pairs={{8,0},{5,1},{10,2},{7,3},{12,4},{1,5},{14,6},{3,7},{0,8},{13,9},{2... | collective-permute-start | bytes 491528 | tf_op jit(solution)/shard_map/ppermute | solution.py:90
  15.8 8.4 %collective-permute-start.4 = (bf16[128,1280]{1,0:T(8,128)(2,1)S(1)}, bf16[128,1280]{1,0:T(8,128)(2,1)S(1)}, u32[]{:S(2)}, u32[]{:S(2)}) collective-permute-start(bf16[128,1280]{1,0:T(8,128)(2,1)S(1)} %pad_maximum_fusion.3), channel_id=1, source_target_pairs={{4,0},{9,1},{6,2},{11,3},{0,4},{13,5},{2,6},{15,7},{12,8},{1,9},{1... | collective-permute-start | bytes 983048 | tf_op jit(solution)/shard_map/ppermute | solution.py:90
  17.4 6.8 %collective-permute-start.6 = (bf16[4,16,640]{2,1,0:T(8,128)(2,1)S(1)}, bf16[4,16,640]{2,1,0:T(8,128)(2,1)S(1)}, u32[]{:S(2)}, u32[]{:S(2)}) collective-permute-start(bf16[4,16,640]{2,1,0:T(8,128)(2,1)S(1)} %pad_maximum_fusion.9), channel_id=1, source_target_pairs={{4,0},{9,1},{6,2},{11,3},{0,4},{13,5},{2,6},{15,7},{12,8},{1,9},{1... | collective-permute-start | bytes 245768 | tf_op jit(solution)/shard_map/ppermute | solution.py:90
  24.3 8.6 %collective-permute-start.10 = (bf16[384,2048]{1,0:T(8,128)(2,1)S(1)}, bf16[384,2048]{1,0:T(8,128)(2,1)S(1)}, u32[]{:S(2)}, u32[]{:S(2)}) collective-permute-start(bf16[384,2048]{1,0:T(8,128)(2,1)S(1)} %get-tuple-element.86), channel_id=1, source_target_pairs={{0,1},{1,0},{2,3},{3,2},{4,5},{5,4},{6,7},{7,6},{8,9},{9,8},{10,11... | collective-permute-start | bytes 4718600 | tf_op jit(solution)/shard_map/ppermute | solution.py:25
  24.7 8.1 %collective-permute-start.8 = (bf16[64,1280]{1,0:T(8,128)(2,1)S(1)}, bf16[64,1280]{1,0:T(8,128)(2,1)S(1)}, u32[]{:S(2)}, u32[]{:S(2)}) collective-permute-start(bf16[64,1280]{1,0:T(8,128)(2,1)S(1)} %collective-permute-done.5.refs_5_), channel_id=1, source_target_pairs={{4,0},{9,1},{6,2},{11,3},{0,4},{13,5},{2,6},{15,7},{12,8},{1,9},{1... | collective-permute-start | bytes 491528 | tf_op jit(solution)/shard_map/ppermute | solution.py:90
  25.7 7.2 %collective-permute-start.9 = (bf16[4,16,640]{2,1,0:T(8,128)(2,1)S(1)}, bf16[4,16,640]{2,1,0:T(8,128)(2,1)S(1)}, u32[]{:S(2)}, u32[]{:S(2)}) collective-permute-start(bf16[4,16,640]{2,1,0:T(8,128)(2,1)S(1)} %pad_maximum_fusion.10), channel_id=1, source_target_pairs={{16,0},{17,1},{18,2},{19,3},{20,4},{21,5},{22,6},{23,7},{24,8},{25... | collective-permute-start | bytes 245768 | tf_op jit(solution)/shard_map/ppermute | solution.py:90
  38.9 6.0 %collective-permute-start.12 = (bf16[288,256]{1,0:T(8,128)(2,1)S(1)}, bf16[288,256]{1,0:T(8,128)(2,1)S(1)}, u32[]{:S(2)}, u32[]{:S(2)}) collective-permute-start(bf16[288,256]{1,0:T(8,128)(2,1)S(1)} %pad_maximum_fusion.8), channel_id=1, source_target_pairs={{0,2},{1,3},{2,0},{3,1},{4,6},{5,7},{6,4},{7,5},{8,10},{9,11},{10,... | collective-permute-start | bytes 442376 | tf_op jit(solution)/shard_map/ppermute | solution.py:25
  45.0 8.4 %collective-permute-start.13 = (bf16[256,256]{1,0:T(8,128)(2,1)S(1)}, bf16[256,256]{1,0:T(8,128)(2,1)S(1)}, u32[]{:S(2)}, u32[]{:S(2)}) collective-permute-start(bf16[256,256]{1,0:T(8,128)(2,1)S(1)} %add_convert_fusion.8.refs_0_.refs_6_), channel_id=1, source_target_pairs={{16,0},{17,1},{18,2},{19,3},{20,4},{21,5},{22,6},{23,7},{24,8},{25... | collective-permute-start | bytes 393224 | tf_op jit(solution)/shard_map/ppermute | solution.py:90
  45.6 8.0 %collective-permute-start.14 = (bf16[256,256]{1,0:T(8,128)(2,1)S(1)}, bf16[256,256]{1,0:T(8,128)(2,1)S(1)}, u32[]{:S(2)}, u32[]{:S(2)}) collective-permute-start(bf16[256,256]{1,0:T(8,128)(2,1)S(1)} %add_convert_fusion.8.refs_0_.refs_6_), channel_id=1, source_target_pairs={{8,0},{9,1},{10,2},{11,3},{12,4},{13,5},{14,6},{15,7},{0,8},{1,9},... | collective-permute-start | bytes 393224 | tf_op jit(solution)/shard_map/ppermute | solution.py:90
  48.1 5.5 %collective-permute-start.15 = (bf16[256,256]{1,0:T(8,128)(2,1)S(1)}, bf16[256,256]{1,0:T(8,128)(2,1)S(1)}, u32[]{:S(2)}, u32[]{:S(2)}) collective-permute-start(bf16[256,256]{1,0:T(8,128)(2,1)S(1)} %add_convert_fusion.8.refs_0_.refs_6_), channel_id=1, source_target_pairs={{2,0},{5,1},{0,2},{7,3},{6,4},{1,5},{4,6},{3,7},{10,8},{13,9},{8,1... | collective-permute-start | bytes 393224 | tf_op jit(solution)/shard_map/ppermute | solution.py:90
  54.6 6.9 %collective-permute-start.17 = (bf16[512,256]{1,0:T(8,128)(2,1)S(1)}, bf16[512,256]{1,0:T(8,128)(2,1)S(1)}, u32[]{:S(2)}, u32[]{:S(2)}) collective-permute-start(bf16[512,256]{1,0:T(8,128)(2,1)S(1)} %get-tuple-element.147), channel_id=1, source_target_pairs={{8,0},{9,1},{10,2},{11,3},{12,4},{13,5},{14,6},{15,7},{0,8},{1,9},... | collective-permute-start | bytes 786440 | tf_op jit(solution)/shard_map/ppermute | solution.py:90
  54.7 7.0 %collective-permute-start.18 = (bf16[512,256]{1,0:T(8,128)(2,1)S(1)}, bf16[512,256]{1,0:T(8,128)(2,1)S(1)}, u32[]{:S(2)}, u32[]{:S(2)}) collective-permute-start(bf16[512,256]{1,0:T(8,128)(2,1)S(1)} %get-tuple-element.146), channel_id=1, source_target_pairs={{2,0},{5,1},{0,2},{7,3},{6,4},{1,5},{4,6},{3,7},{10,8},{13,9},{8,1... | collective-permute-start | bytes 786440 | tf_op jit(solution)/shard_map/ppermute | solution.py:90
  55.3 6.4 %collective-permute-start.19 = (bf16[512,256]{1,0:T(8,128)(2,1)S(1)}, bf16[512,256]{1,0:T(8,128)(2,1)S(1)}, u32[]{:S(2)}, u32[]{:S(2)}) collective-permute-start(bf16[512,256]{1,0:T(8,128)(2,1)S(1)} %get-tuple-element.145), channel_id=1, source_target_pairs={{4,0},{3,1},{6,2},{1,3},{0,4},{7,5},{2,6},{5,7},{12,8},{11,9},{14,... | collective-permute-start | bytes 786440 | tf_op jit(solution)/shard_map/ppermute | solution.py:90
  61.7 8.5 %collective-permute-start.21 = (bf16[512,256]{1,0:T(8,128)(2,1)S(1)}, bf16[512,256]{1,0:T(8,128)(2,1)S(1)}, u32[]{:S(2)}, u32[]{:S(2)}) collective-permute-start(bf16[512,256]{1,0:T(8,128)(2,1)S(1)} %collective-permute-done.18.refs_5_.refs_2_.refs_12_), channel_id=1, source_target_pairs={{4,0},{3,1},{6,2},{1,3},{0,4},{7,5},{2,6},{5,7},{12,8},{11,9},{14,... | collective-permute-start | bytes 786440 | tf_op jit(solution)/shard_map/ppermute | solution.py:90
  63.4 5.0 %collective-permute-start.20 = (bf16[256,256]{1,0:T(8,128)(2,1)S(1)}, bf16[256,256]{1,0:T(8,128)(2,1)S(1)}, u32[]{:S(2)}, u32[]{:S(2)}) collective-permute-start(bf16[256,256]{1,0:T(8,128)(2,1)S(1)} %slice.90), channel_id=1, source_target_pairs={{8,0},{9,1},{10,2},{11,3},{12,4},{13,5},{14,6},{15,7},{0,8},{1,9},... | collective-permute-start | bytes 393224 | tf_op jit(solution)/shard_map/ppermute | solution.py:90
  65.1 5.0 %collective-permute-start.22 = (bf16[256,256]{1,0:T(8,128)(2,1)S(1)}, bf16[256,256]{1,0:T(8,128)(2,1)S(1)}, u32[]{:S(2)}, u32[]{:S(2)}) collective-permute-start(bf16[256,256]{1,0:T(8,128)(2,1)S(1)} %slice.91), channel_id=1, source_target_pairs={{4,0},{3,1},{6,2},{1,3},{0,4},{7,5},{2,6},{5,7},{12,8},{11,9},{14,... | collective-permute-start | bytes 393224 | tf_op jit(solution)/shard_map/ppermute | solution.py:90
  77.6 5.2 %collective-permute-start.26 = (bf16[256,1664]{1,0:T(8,128)(2,1)S(1)}, bf16[256,1664]{1,0:T(8,128)(2,1)S(1)}, u32[]{:S(2)}, u32[]{:S(2)}) collective-permute-start(bf16[256,1664]{1,0:T(8,128)(2,1)S(1)} %experts_in_second.3.refs_5_.act_ref), channel_id=1, source_target_pairs={{0,1},{1,0},{2,3},{3,2},{4,5},{5,4},{6,7},{7,6},{8,9},{9,8},{10,11... | collective-permute-start | bytes 2555912 | tf_op jit(solution)/shard_map/ppermute | solution.py:25
  80.7 5.0 %collective-permute-start.25 = (bf16[32,2048]{1,0:T(8,128)(2,1)S(1)}, bf16[32,2048]{1,0:T(8,128)(2,1)S(1)}, u32[]{:S(2)}, u32[]{:S(2)}) collective-permute-start(bf16[32,2048]{1,0:T(8,128)(2,1)S(1)} %get-tuple-element.106), channel_id=1, source_target_pairs={{4,0},{3,1},{6,2},{1,3},{0,4},{7,5},{2,6},{5,7},{12,8},{11,9},{14,... | collective-permute-start | bytes 393224 | tf_op jit(solution)/shard_map/ppermute | solution.py:90
  81.8 7.5 %collective-permute-start.29 = (bf16[32,2048]{1,0:T(8,128)(2,1)S(1)}, bf16[32,2048]{1,0:T(8,128)(2,1)S(1)}, u32[]{:S(2)}, u32[]{:S(2)}) collective-permute-start(bf16[32,2048]{1,0:T(8,128)(2,1)S(1)} %get-tuple-element.123), channel_id=1, source_target_pairs={{4,0},{3,1},{6,2},{1,3},{0,4},{7,5},{2,6},{5,7},{12,8},{11,9},{14,... | collective-permute-start | bytes 393224 | tf_op jit(solution)/shard_map/ppermute | solution.py:90
  85.8 6.4 %collective-permute-start.28 = (bf16[64,2048]{1,0:T(8,128)(2,1)S(1)}, bf16[64,2048]{1,0:T(8,128)(2,1)S(1)}, u32[]{:S(2)}, u32[]{:S(2)}) collective-permute-start(bf16[64,2048]{1,0:T(8,128)(2,1)S(1)} %pad_maximum_fusion.4), channel_id=1, source_target_pairs={{4,0},{3,1},{6,2},{1,3},{0,4},{7,5},{2,6},{5,7},{12,8},{11,9},{14,... | collective-permute-start | bytes 786440 | tf_op jit(solution)/shard_map/ppermute | solution.py:90
  86.9 5.0 %collective-permute-start.27 = (bf16[32,2048]{1,0:T(8,128)(2,1)S(1)}, bf16[32,2048]{1,0:T(8,128)(2,1)S(1)}, u32[]{:S(2)}, u32[]{:S(2)}) collective-permute-start(bf16[32,2048]{1,0:T(8,128)(2,1)S(1)} %add_convert_fusion.7), channel_id=1, source_target_pairs={{8,0},{9,1},{10,2},{11,3},{12,4},{13,5},{14,6},{15,7},{0,8},{1,9},... | collective-permute-start | bytes 393224 | tf_op jit(solution)/shard_map/ppermute | solution.py:90
  88.6 8.1 %collective-permute-start.32 = (bf16[64,2048]{1,0:T(8,128)(2,1)S(1)}, bf16[64,2048]{1,0:T(8,128)(2,1)S(1)}, u32[]{:S(2)}, u32[]{:S(2)}) collective-permute-start(bf16[64,2048]{1,0:T(8,128)(2,1)S(1)} %pad_maximum_fusion.7), channel_id=1, source_target_pairs={{4,0},{3,1},{6,2},{1,3},{0,4},{7,5},{2,6},{5,7},{12,8},{11,9},{14,... | collective-permute-start | bytes 786440 | tf_op jit(solution)/shard_map/ppermute | solution.py:90
  92.3 6.4 %collective-permute-start.31 = (bf16[64,2048]{1,0:T(8,128)(2,1)S(1)}, bf16[64,2048]{1,0:T(8,128)(2,1)S(1)}, u32[]{:S(2)}, u32[]{:S(2)}) collective-permute-start(bf16[64,2048]{1,0:T(8,128)(2,1)S(1)} %pad_maximum_fusion.6), channel_id=1, source_target_pairs={{2,0},{5,1},{0,2},{7,3},{6,4},{1,5},{4,6},{3,7},{10,8},{13,9},{8,1... | collective-permute-start | bytes 786440 | tf_op jit(solution)/shard_map/ppermute | solution.py:90
  93.9 6.4 %collective-permute-start.30 = (bf16[64,2048]{1,0:T(8,128)(2,1)S(1)}, bf16[64,2048]{1,0:T(8,128)(2,1)S(1)}, u32[]{:S(2)}, u32[]{:S(2)}) collective-permute-start(bf16[64,2048]{1,0:T(8,128)(2,1)S(1)} %pad_maximum_fusion.5), channel_id=1, source_target_pairs={{8,0},{9,1},{10,2},{11,3},{12,4},{13,5},{14,6},{15,7},{0,8},{1,9},... | collective-permute-start | bytes 786440 | tf_op jit(solution)/shard_map/ppermute | solution.py:90
  100.5 7.3 %collective-permute-start.33 = (bf16[32,2048]{1,0:T(8,128)(2,1)S(1)}, bf16[32,2048]{1,0:T(8,128)(2,1)S(1)}, u32[]{:S(2)}, u32[]{:S(2)}) collective-permute-start(bf16[32,2048]{1,0:T(8,128)(2,1)S(1)} %get-tuple-element.137), channel_id=1, source_target_pairs={{16,0},{17,1},{18,2},{19,3},{20,4},{21,5},{22,6},{23,7},{24,8},{25... | collective-permute-start | bytes 393224 | tf_op jit(solution)/shard_map/ppermute | solution.py:90
  102.0 5.9 %collective-permute-start.34 = (bf16[32,2048]{1,0:T(8,128)(2,1)S(1)}, bf16[32,2048]{1,0:T(8,128)(2,1)S(1)}, u32[]{:S(2)}, u32[]{:S(2)}) collective-permute-start(bf16[32,2048]{1,0:T(8,128)(2,1)S(1)} %get-tuple-element.139), channel_id=1, source_target_pairs={{8,0},{9,1},{10,2},{11,3},{12,4},{13,5},{14,6},{15,7},{0,8},{1,9},... | collective-permute-start | bytes 393224 | tf_op jit(solution)/shard_map/ppermute | solution.py:90
  102.4 5.5 %collective-permute-start.35 = (bf16[32,2048]{1,0:T(8,128)(2,1)S(1)}, bf16[32,2048]{1,0:T(8,128)(2,1)S(1)}, u32[]{:S(2)}, u32[]{:S(2)}) collective-permute-start(bf16[32,2048]{1,0:T(8,128)(2,1)S(1)} %get-tuple-element.140), channel_id=1, source_target_pairs={{2,0},{5,1},{0,2},{7,3},{6,4},{1,5},{4,6},{3,7},{10,8},{13,9},{8,1... | collective-permute-start | bytes 393224 | tf_op jit(solution)/shard_map/ppermute | solution.py:90
  (9 other events, 96.3 us)

commit v8 on v7

--- a/solution.py
+++ b/solution.py
@@ -106,11 +106,13 @@
             rest = tuple(sorted(key for key in left if not any(key in group for group in groups)))
             for group in groups + [rest] * bool(rest):
                 sends.append((moves, group, tuple(left[key] for key in group)))
-        def load(send):
-            share = 1 if send[0][0] == send[0][1] else 0.5
-            return len(send[1]) * (2 if send[0][0][0] == top > 2 else share)
-
-        sends.sort(key=lambda send: (-load(send), send[0][0] != send[0][1]))
+        def order(send):
+            moves, group, _ = send
+            shared, load = moves[0] == moves[1], len(group) * (2 if moves[0][0] == top > 2 else 1)
+            rank = (0 if shared else 1) if len(group) == 1 else (1 if shared else 2 * moves[0][0])
+            return -load, rank
+
+        sends.sort(key=order)
         arrays = arrays + [send[2] for send in sends]
         stages.append(sends)
     return stages
@@ -317,7 +319,7 @@
 
 
 def attend_kernel(plan, ctx_ref, exp_ref, order_ref, *refs):
-    ctx_count, exp_count, tok, heads, piece_places, attend_at = plan
+    ctx_count, exp_count, tok, heads, attend_at = plan
     packed_at, places_of = [at for at, _ in attend_at], [place for _, place in attend_at]
     array_count = 1 + max(array for array, _ in packed_at)
     span = exp_count * tok
@@ -325,11 +327,10 @@
     packed = []
     for array, row in packed_at:
         packed.append(packed_refs[array].at[pl.ds(row, span)])
-    piece_refs, refs = refs[: 1 + bits_of(ctx_count)], refs[1 + bits_of(ctx_count) :]
     weight_ref, rest = refs[0], refs[2:]
     x_count = exp_count // 2
-    keep_refs, (give_ref, own_route_ref) = rest[:x_count], rest[x_count : x_count + 2]
-    key_scr, value_scr, place_scr, att_scr = rest[x_count + 2 :]
+    keep_refs, give_ref = rest[:x_count], rest[x_count]
+    key_scr, value_scr, place_scr, att_scr = rest[x_count + 1 :]
     positions = ctx_count * span
     my_ctx, my_exp = ctx_ref[0], exp_ref[0]
     my_x, my_core = lax.shift_right_logical(my_exp, 1), lax.bitwise_and(my_exp, 1)
@@ -372,8 +373,6 @@
 
     cols = weight_ref.shape[1] // 2
     per_x = 2 * ctx_count * tok
-    route_lane = lax.broadcasted_iota(jnp.int32, (tok, HEAD_SIZE), 1)
-    route_base = x_count * per_x
     for x_off in range(x_count):
         rows = pl.ds(x_off * per_x, per_x)
         for which in (1, 0):
@@ -382,24 +381,37 @@
             part = jnp.dot(att_scr[rows, :], weight, preferred_element_type=jnp.float32)
             out_ref = give_ref if which else keep_refs[x_off]
             out_ref[pl.ds(x_off * per_x if which else 0, per_x), :] = part.astype(out_ref.dtype)
-            if x_off == 0:
-                for (array, place), place_of in zip(piece_places, places_of):
-                    source = lax.bitwise_xor(my_ctx, by_core(my_core, place_of, 0))
-                    at = pl.ds(pl.multiple_of((source * 2 + my_core) * tok, tok), tok)
-                    piece = piece_refs[array][place, :, pl.ds(pl.multiple_of(side * cols, cols), cols)]
-                    value = out_ref[at, :].astype(jnp.float32) + piece.astype(jnp.float32)
-                    out_ref[at, :] = value.astype(out_ref.dtype)
-        block_out = jnp.zeros((tok, HEAD_SIZE), jnp.float32)
-        for (array, place), place_of in zip(piece_places, places_of):
-            source = lax.bitwise_xor(my_ctx, by_core(my_core, place_of, 0))
-            block = piece_refs[array][place, :, 2 * cols :].astype(jnp.float32)
-            for part_of in range(2):
-                wanted = lax.bitwise_xor(my_x, x_off) + part_of * x_count
-                column = jnp.sum(jnp.where(route_lane == wanted, block, 0.0), axis=1, keepdims=True)
-                block_out = jnp.where(route_lane == source + part_of * ctx_count, column, block_out)
+
+
+def finish_kernel(plan, ctx_ref, exp_ref, keep_in, give_in, *refs):
+    ctx_count, x_count, tok, piece_places, places_of = plan
+    piece_refs, (keep_ref, give_ref, own_route_ref) = refs[:-3], refs[-3:]
+    my_ctx, my_exp = ctx_ref[0], exp_ref[0]
+    my_x, my_core = lax.shift_right_logical(my_exp, 1), lax.bitwise_and(my_exp, 1)
+    cols = keep_ref.shape[1]
+    route_base = give_in.shape[0]
+    keep_ref[...] = keep_in[...]
+    give_ref[0:route_base, :] = give_in[...]
+    blocks = [jnp.zeros((tok, HEAD_SIZE), jnp.float32)] * x_count
+    lane = lax.broadcasted_iota(jnp.int32, (tok, HEAD_SIZE), 1)
+    for (array, place), place_of in zip(piece_places, places_of):
+        source = lax.bitwise_xor(my_ctx, by_core(my_core, place_of, 0))
+        at = pl.ds(pl.multiple_of((source * 2 + my_core) * tok, tok), tok)
+        for which, ref in enumerate((keep_ref, give_ref)):
+            side = lax.bitwise_xor(my_core, which)
+            piece = piece_refs[array][place, :, pl.ds(pl.multiple_of(side * cols, cols), cols)]
+            value = ref[at, :].astype(jnp.float32) + piece.astype(jnp.float32)
+            ref[at, :] = value.astype(ref.dtype)
+        block = piece_refs[array][place, :, 2 * cols :].astype(jnp.float32)
+        for x_off in range(x_count):
+            for part in range(2):
+                wanted = lax.bitwise_xor(my_x, x_off) + part * x_count
+                column = jnp.sum(jnp.where(lane == wanted, block, 0.0), axis=1, keepdims=True)
+                blocks[x_off] = jnp.where(lane == source + part * ctx_count, column, blocks[x_off])
+    for x_off, block in enumerate(blocks):
         for ref, base in ((give_ref, route_base), (own_route_ref, 0)):
             at = pl.ds(base + x_off * tok, tok)
-            ref[at, 0:HEAD_SIZE] = block_out.astype(jnp.bfloat16)
+            ref[at, 0:HEAD_SIZE] = block.astype(jnp.bfloat16)
             if cols > HEAD_SIZE:
                 ref[at, HEAD_SIZE:] = jnp.zeros((tok, cols - HEAD_SIZE), jnp.bfloat16)
 
@@ -645,15 +657,12 @@
 
     positions = ctx_count * span
     per_x = 2 * ctx_count * tok
-    *keeps, give, own_route = pl.pallas_call(
-        functools.partial(attend_kernel, (ctx_count, exp_count, tok, heads, attend_pieces, attend_at)),
-        in_specs=[smem] * 3 + [vmem] * (len(packed) + len(piece_arrays) + 1) + [anywhere],
-        out_specs=[vmem] * (2 + x_count),
+    *keeps, give = pl.pallas_call(
+        functools.partial(attend_kernel, (ctx_count, exp_count, tok, heads, attend_at)),
+        in_specs=[smem] * 3 + [vmem] * (len(packed) + 1) + [anywhere],
+        out_specs=[vmem] * (1 + x_count),
         out_shape=[jax.ShapeDtypeStruct((per_x, cols), f32)] * x_count
-        + [
-            jax.ShapeDtypeStruct((x_count * (per_x + tok), cols), bf16),
-            jax.ShapeDtypeStruct((x_count * tok, cols), bf16),
-        ],
+        + [jax.ShapeDtypeStruct((x_count * per_x, cols), bf16)],
         scratch_shapes=[
             pltpu.VMEM((positions, HEAD_SIZE), bf16),
             pltpu.VMEM((positions, 2 * HEAD_SIZE), bf16),
@@ -667,7 +676,22 @@
             transcendentals=heads * positions * positions,
         ),
         name="attend",
-    )(my_ctx, my_exp, block_order, *packed, *piece_arrays, out_weight, down_other)
+    )(my_ctx, my_exp, block_order, *packed, out_weight, down_other)
+    keeps[0], give, own_route = pl.pallas_call(
+        functools.partial(
+            finish_kernel,
+            (ctx_count, x_count, tok, attend_pieces, tuple(place for _, place in attend_at)),
+        ),
+        in_specs=[smem] * 2 + [vmem] * (2 + len(piece_arrays)),
+        out_specs=[vmem] * 3,
+        out_shape=[
+            jax.ShapeDtypeStruct((per_x, cols), f32),
+            jax.ShapeDtypeStruct((x_count * (per_x + tok), cols), bf16),
+            jax.ShapeDtypeStruct((x_count * tok, cols), bf16),
+        ],
+        compiler_params=pltpu.CompilerParams(vmem_limit_bytes=8 * MIB),
+        name="finish",
+    )(my_ctx, my_exp, keeps[0], give, *piece_arrays)
 
     given = from_offset(give, 1)
     routes, route_at, state = [own_route, given], [(0, 0), (1, x_count * per_x)], keeps[0]

time: 111 us -> 109 us (0.982)
  waiting for transfers between devices: 50.2 us -> 47 us
    ppermute x31, waiting for transfers between devices: 42.4 us -> 39.4 us  [follow(): return lax.ppermute(array, ('ctx', 'exp'), pairs)]
  transfers between devices with their start and end apart: 38 -> 38, of which waited for: 23 -> 25; matrix products, arithmetic and copies ran while one was open for 0% -> 0% of each run, Pallas kernels for 11% -> 15%
where the time goes in v8:
time: 109 us
  waiting for transfers between devices  47 us (43%)
  starting transfers between devices  40.8 us (37%)
  Pallas kernels  18.8 us (17%)
    ppermute x31, waiting for transfers between devices, follow(): return lax.ppermute(array, ('ctx', 'exp'), pairs)  39.4 us
    ppermute x31, starting transfers between devices, follow(): return lax.ppermute(array, ('ctx', 'exp'), pairs)  37.8 us
    ppermute x7, waiting for transfers between devices, from_offset(): lax.ppermute(array, 'exp', [(i, i ^ offset) for i in range(lax.axis_size(...  7.62 us
    pallas_call x1, Pallas kernels, shards(): pl.pallas_call(functools.partial(attend_kernel, (ctx_count, exp_count, to...  4.33 us
    pallas_call x2, Pallas kernels, shards(): pl.pallas_call(functools.partial(experts_out_kernel, (ctx_count, exp_coun...  3.73 us
    pallas_call x1, Pallas kernels, deq_in(): pl.pallas_call(functools.partial(deq_in_kernel, ctx_count), in_specs=[pl....  3 us
    ppermute x7, starting transfers between devices, from_offset(): lax.ppermute(array, 'exp', [(i, i ^ offset) for i in range(lax.axis_size(...  2.99 us
    pallas_call x2, Pallas kernels, shards(): pl.pallas_call(functools.partial(experts_in_second, (ctx_count, x_count,...  2.38 us
  transfers between devices with their start and end apart: 38, of which 25 were waited for; matrix products, arithmetic and copies ran while one was open for 0% of the time, Pallas kernels for 15%

profile of v8, /device:TPU:0, one launch (start us, length us, event | category | flops | bytes accessed | tf_op | source)
XLA Modules:
  0.0 108.6 jit_solution(15078130206097060390)
XLA Ops:
  1.2 4.1 %collective-permute-start = (bf16[64,1280]{1,0:T(8,128)(2,1)S(1)}, bf16[64,1280]{1,0:T(8,128)(2,1)S(1)}, u32[]{:S(2)}, u32[]{:S(2)}) collective-permute-start(bf16[64,1280]{1,0:T(8,128)(2,1)S(1)} %get-tuple-element.73._.refs_0_), channel_id=1, source_target_pairs={{16,0},{17,1},{18,2},{19,3},{20,4},{21,5},{22,6},{23,7},{24,8},{25... | collective-permute-start | bytes 491528 | tf_op jit(solution)/shard_map/ppermute | solution.py:90
  5.3 1.5 %collective-permute-start.1 = (bf16[64,1280]{1,0:T(8,128)(2,1)S(1)}, bf16[64,1280]{1,0:T(8,128)(2,1)S(1)}, u32[]{:S(2)}, u32[]{:S(2)}) collective-permute-start(bf16[64,1280]{1,0:T(8,128)(2,1)S(1)} %get-tuple-element.73._.refs_0_), channel_id=1, source_target_pairs={{4,0},{9,1},{6,2},{11,3},{0,4},{13,5},{2,6},{15,7},{12,8},{1,9},{1... | collective-permute-start | bytes 491528 | tf_op jit(solution)/shard_map/ppermute | solution.py:90
  6.8 1.6 %collective-permute-start.2 = (bf16[64,1280]{1,0:T(8,128)(2,1)S(1)}, bf16[64,1280]{1,0:T(8,128)(2,1)S(1)}, u32[]{:S(2)}, u32[]{:S(2)}) collective-permute-start(bf16[64,1280]{1,0:T(8,128)(2,1)S(1)} %get-tuple-element.73._.refs_0_), channel_id=1, source_target_pairs={{8,0},{5,1},{10,2},{7,3},{12,4},{1,5},{14,6},{3,7},{0,8},{13,9},{2... | collective-permute-start | bytes 491528 | tf_op jit(solution)/shard_map/ppermute | solution.py:90
  8.8 3.0 %dequant_in.1 = (bf16[2048,768]{1,0:T(8,128)(2,1)S(1)}, bf16[2048,768]{1,0:T(8,128)(2,1)S(1)}) custom-call(s32[1]{0:T(128)} %bitcast.1.exp_ref, s32[3,1,32]{2,1,0:T(1,128)} %bitcast.25, s32[3,1,32]{2,1,0:T(1,128)} %bitcast.26, bf16[1,4096,384]{2,1,0:T(8,128)(2,1)} %gate_hbm.1, bf16[1,4096,384]{2,1,0:T(8,128)(2,1)} %up_hbm.1, ...), custom_call_target="tpu_custom_call" | custom-call | flops 3145728 | bytes 12582912 | tf_op jit(solution)/shard_map/dequant_in/pallas_call | solution.py:252
  11.8 3.1 %collective-permute-done.3._.refs_1_ = bf16[4,16,640]{2,1,0:T(8,128)(2,1)S(1)} collective-permute-done((bf16[4,16,640]{2,1,0:T(8,128)(2,1)S(1)}, bf16[4,16,640]{2,1,0:T(8,128)(2,1)S(1)}, u32[]{:S(2)}, u32[]{:S(2)}) %collective-permute-start.3) | collective-permute-done | bytes 81952 | tf_op jit(solution)/shard_map/ppermute | solution.py:90
  15.8 1.6 %collective-permute-start.4 = (bf16[128,1280]{1,0:T(8,128)(2,1)S(1)}, bf16[128,1280]{1,0:T(8,128)(2,1)S(1)}, u32[]{:S(2)}, u32[]{:S(2)}) collective-permute-start(bf16[128,1280]{1,0:T(8,128)(2,1)S(1)} %pad_maximum_fusion.3), channel_id=1, source_target_pairs={{4,0},{9,1},{6,2},{11,3},{0,4},{13,5},{2,6},{15,7},{12,8},{1,9},{1... | collective-permute-start | bytes 983048 | tf_op jit(solution)/shard_map/ppermute | solution.py:90
  18.0 2.1 %dequant_down.1 = (bf16[384,2048]{1,0:T(8,128)(2,1)S(1)}, bf16[384,2048]{1,0:T(8,128)(2,1)S(1)}) custom-call(s32[1]{0:T(128)} %bitcast.1.exp_ref, s32[3,1,32]{2,1,0:T(1,128)} %bitcast.27, bf16[1,384,4096]{2,1,0:T(8,128)(2,1)} %down_hbm.1, bf16[4,16,640]{2,1,0:T(8,128)(2,1)S(1)} %collective-permute-done.3._.refs_1_), custom_call_target="tpu_custom_call" | custom-call | flops 1572864 | bytes 6291456 | tf_op jit(solution)/shard_map/dequant_down/pallas_call | solution.py:301
  20.1 4.2 %collective-permute-done.6.refs_2_ = bf16[4,16,640]{2,1,0:T(8,128)(2,1)S(1)} collective-permute-done((bf16[4,16,640]{2,1,0:T(8,128)(2,1)S(1)}, bf16[4,16,640]{2,1,0:T(8,128)(2,1)S(1)}, u32[]{:S(2)}, u32[]{:S(2)}) %collective-permute-start.6) | collective-permute-done | bytes 81952 | tf_op jit(solution)/shard_map/ppermute | solution.py:90
  25.7 1.6 %collective-permute-start.10 = (bf16[4,16,640]{2,1,0:T(8,128)(2,1)S(1)}, bf16[4,16,640]{2,1,0:T(8,128)(2,1)S(1)}, u32[]{:S(2)}, u32[]{:S(2)}) collective-permute-start(bf16[4,16,640]{2,1,0:T(8,128)(2,1)S(1)} %pad_maximum_fusion.10), channel_id=1, source_target_pairs={{16,0},{17,1},{18,2},{19,3},{20,4},{21,5},{22,6},{23,7},{24,8},{25... | collective-permute-start | bytes 245768 | tf_op jit(solution)/shard_map/ppermute | solution.py:90
  27.3 2.8 %collective-permute-done.8.refs_6_ = bf16[64,1280]{1,0:T(8,128)(2,1)S(1)} collective-permute-done((bf16[64,1280]{1,0:T(8,128)(2,1)S(1)}, bf16[64,1280]{1,0:T(8,128)(2,1)S(1)}, u32[]{:S(2)}, u32[]{:S(2)}) %collective-permute-start.8) | collective-permute-done | bytes 163872 | tf_op jit(solution)/shard_map/ppermute | solution.py:90
  30.0 4.3 %attend.1 = (f32[256,256]{1,0:T(8,128)S(1)}, f32[256,256]{1,0:T(8,128)S(1)}, bf16[512,256]{1,0:T(8,128)(2,1)S(1)}) custom-call(s32[1]{0:T(128)} %bitcast.ctx_ref, s32[1]{0:T(128)} %bitcast.1.exp_ref, s32[8]{0:T(128)S(1)} %copy-done.2, bf16[64,1280]{1,0:T(8,128)(2,1)S(1)} %get-tuple-element.73._.refs_0_, bf16[64,1280]{1,0:T(8,128)(2,1)S(1)} %collective-permute-done.refs_1_, ...), custom_call_target="tpu_custom_call" | custom-call | flops 1610612736 | bytes 8388608 | tf_op jit(solution)/shard_map/attend/pallas_call | solution.py:660
  34.8 1.4 %collective-permute-done.11.refs_1_ = bf16[544,256]{1,0:T(8,128)(2,1)S(1)} collective-permute-done((bf16[544,256]{1,0:T(8,128)(2,1)S(1)}, bf16[544,256]{1,0:T(8,128)(2,1)S(1)}, u32[]{:S(2)}, u32[]{:S(2)}) %collective-permute-start.11) | collective-permute-done | bytes 278560 | tf_op jit(solution)/shard_map/ppermute | solution.py:25
  36.3 1.6 %collective-permute-start.12 = (bf16[288,256]{1,0:T(8,128)(2,1)S(1)}, bf16[288,256]{1,0:T(8,128)(2,1)S(1)}, u32[]{:S(2)}, u32[]{:S(2)}) collective-permute-start(bf16[288,256]{1,0:T(8,128)(2,1)S(1)} %pad_maximum_fusion.8), channel_id=1, source_target_pairs={{0,2},{1,3},{2,0},{3,1},{4,6},{5,7},{6,4},{7,5},{8,10},{9,11},{10,... | collective-permute-start | bytes 442376 | tf_op jit(solution)/shard_map/ppermute | solution.py:25
  37.9 4.3 %collective-permute-done.12.refs_2_ = bf16[288,256]{1,0:T(8,128)(2,1)S(1)} collective-permute-done((bf16[288,256]{1,0:T(8,128)(2,1)S(1)}, bf16[288,256]{1,0:T(8,128)(2,1)S(1)}, u32[]{:S(2)}, u32[]{:S(2)}) %collective-permute-start.12) | collective-permute-done | bytes 147488 | tf_op jit(solution)/shard_map/ppermute | solution.py:25
  42.3 2.0 %collective-permute-start.13 = (bf16[256,256]{1,0:T(8,128)(2,1)S(1)}, bf16[256,256]{1,0:T(8,128)(2,1)S(1)}, u32[]{:S(2)}, u32[]{:S(2)}) collective-permute-start(bf16[256,256]{1,0:T(8,128)(2,1)S(1)} %add_convert_fusion.8.refs_0_.refs_6_), channel_id=1, source_target_pairs={{16,0},{17,1},{18,2},{19,3},{20,4},{21,5},{22,6},{23,7},{24,8},{25... | collective-permute-start | bytes 393224 | tf_op jit(solution)/shard_map/ppermute | solution.py:90
  45.5 1.5 %collective-permute-start.15 = (bf16[256,256]{1,0:T(8,128)(2,1)S(1)}, bf16[256,256]{1,0:T(8,128)(2,1)S(1)}, u32[]{:S(2)}, u32[]{:S(2)}) collective-permute-start(bf16[256,256]{1,0:T(8,128)(2,1)S(1)} %add_convert_fusion.8.refs_0_.refs_6_), channel_id=1, source_target_pairs={{2,0},{5,1},{0,2},{7,3},{6,4},{1,5},{4,6},{3,7},{10,8},{13,9},{8,1... | collective-permute-start | bytes 393224 | tf_op jit(solution)/shard_map/ppermute | solution.py:90
  47.7 3.1 %collective-permute-done.13.refs_0_.refs_7_ = bf16[256,256]{1,0:T(8,128)(2,1)S(1)} collective-permute-done((bf16[256,256]{1,0:T(8,128)(2,1)S(1)}, bf16[256,256]{1,0:T(8,128)(2,1)S(1)}, u32[]{:S(2)}, u32[]{:S(2)}) %collective-permute-start.13) | collective-permute-done | bytes 131104 | tf_op jit(solution)/shard_map/ppermute | solution.py:90
  54.0 5.3 %collective-permute-done.17.refs_4_.refs_1_.refs_11_ = bf16[512,256]{1,0:T(8,128)(2,1)S(1)} collective-permute-done((bf16[512,256]{1,0:T(8,128)(2,1)S(1)}, bf16[512,256]{1,0:T(8,128)(2,1)S(1)}, u32[]{:S(2)}, u32[]{:S(2)}) %collective-permute-start.17) | collective-permute-done | bytes 262176 | tf_op jit(solution)/shard_map/ppermute | solution.py:90
  60.8 1.8 %collective-permute-start.21 = (bf16[256,256]{1,0:T(8,128)(2,1)S(1)}, bf16[256,256]{1,0:T(8,128)(2,1)S(1)}, u32[]{:S(2)}, u32[]{:S(2)}) collective-permute-start(bf16[256,256]{1,0:T(8,128)(2,1)S(1)} %slice.90), channel_id=1, source_target_pairs={{8,0},{9,1},{10,2},{11,3},{12,4},{13,5},{14,6},{15,7},{0,8},{1,9},... | collective-permute-start | bytes 393224 | tf_op jit(solution)/shard_map/ppermute | solution.py:90
  63.6 2.3 %collective-permute-done.21.refs_5_.refs_14_ = bf16[256,256]{1,0:T(8,128)(2,1)S(1)} collective-permute-done((bf16[256,256]{1,0:T(8,128)(2,1)S(1)}, bf16[256,256]{1,0:T(8,128)(2,1)S(1)}, u32[]{:S(2)}, u32[]{:S(2)}) %collective-permute-start.21) | collective-permute-done | bytes 131104 | tf_op jit(solution)/shard_map/ppermute | solution.py:90
  65.9 1.8 %collective-permute-done.22.refs_6_.refs_15_ = bf16[256,256]{1,0:T(8,128)(2,1)S(1)} collective-permute-done((bf16[256,256]{1,0:T(8,128)(2,1)S(1)}, bf16[256,256]{1,0:T(8,128)(2,1)S(1)}, u32[]{:S(2)}, u32[]{:S(2)}) %collective-permute-start.22) | collective-permute-done | bytes 131104 | tf_op jit(solution)/shard_map/ppermute | solution.py:90
  68.5 2.0 %experts_in_first.1 = (f32[512,1536]{1,0:T(8,128)S(1)}, f32[512,1]{1,0:T(8,128)S(1)}) custom-call(s32[1]{0:T(128)} %bitcast.ctx_ref, s32[1]{0:T(128)} %bitcast.1.exp_ref, bf16[256,256]{1,0:T(8,128)(2,1)S(1)} %add_convert_fusion.8.refs_0_.refs_6_, bf16[256,256]{1,0:T(8,128)(2,1)S(1)} %collective-permute-done.14.refs_1_.refs_8_, ...), custom_call_target="tpu_custom_call" | custom-call | flops 1610612736 | bytes 8388608 | tf_op jit(solution)/shard_map/experts_in_first/pallas_call | solution.py:725
  70.6 2.1 %collective-permute-done.23.refs_7_ = bf16[256,256]{1,0:T(8,128)(2,1)S(1)} collective-permute-done((bf16[256,256]{1,0:T(8,128)(2,1)S(1)}, bf16[256,256]{1,0:T(8,128)(2,1)S(1)}, u32[]{:S(2)}, u32[]{:S(2)}) %collective-permute-start.23) | collective-permute-done | bytes 131104 | tf_op jit(solution)/shard_map/ppermute | solution.py:90
  76.3 1.9 %experts_out.2 = (f32[32,2048]{1,0:T(8,128)S(1)}, f32[32,2048]{1,0:T(8,128)S(1)}, bf16[32,2048]{1,0:T(8,128)(2,1)S(1)}, bf16[32,2048]{1,0:T(8,128)(2,1)S(1)}, f3...) custom-call(s32[1]{0:T(128)} %bitcast.ctx_ref, ...), custom_call_target="tpu_custom_call" | custom-call | flops 805306368 | bytes 8388608 | tf_op jit(solution)/shard_map/experts_out/pallas_call | solution.py:780
  80.3 1.8 %experts_out.3 = (f32[32,2048]{1,0:T(8,128)S(1)}, f32[32,2048]{1,0:T(8,128)S(1)}, f32[32,2048]{1,0:T(8,128)S(1)}, bf16[32,2048]{1,0:T(8,128)(2,1)S(1)}, f32[32,2...) custom-call(s32[1]{0:T(128)} %bitcast.ctx_ref, ...), custom_call_target="tpu_custom_call" | custom-call | flops 805306368 | bytes 8388608 | tf_op jit(solution)/shard_map/experts_out/pallas_call | solution.py:780
  84.2 1.8 %collective-permute-start.28 = (bf16[32,2048]{1,0:T(8,128)(2,1)S(1)}, bf16[32,2048]{1,0:T(8,128)(2,1)S(1)}, u32[]{:S(2)}, u32[]{:S(2)}) collective-permute-start(bf16[32,2048]{1,0:T(8,128)(2,1)S(1)} %add_convert_fusion.7), channel_id=1, source_target_pairs={{8,0},{9,1},{10,2},{11,3},{12,4},{13,5},{14,6},{15,7},{0,8},{1,9},... | collective-permute-start | bytes 393224 | tf_op jit(solution)/shard_map/ppermute | solution.py:90
  87.1 2.2 %collective-permute-done.28 = bf16[32,2048]{1,0:T(8,128)(2,1)S(1)} collective-permute-done((bf16[32,2048]{1,0:T(8,128)(2,1)S(1)}, bf16[32,2048]{1,0:T(8,128)(2,1)S(1)}, u32[]{:S(2)}, u32[]{:S(2)}) %collective-permute-start.28) | collective-permute-done | bytes 131104 | tf_op jit(solution)/shard_map/ppermute | solution.py:90
  89.8 1.6 %collective-permute-start.31 = (bf16[64,2048]{1,0:T(8,128)(2,1)S(1)}, bf16[64,2048]{1,0:T(8,128)(2,1)S(1)}, u32[]{:S(2)}, u32[]{:S(2)}) collective-permute-start(bf16[64,2048]{1,0:T(8,128)(2,1)S(1)} %pad_maximum_fusion.6), channel_id=1, source_target_pairs={{8,0},{9,1},{10,2},{11,3},{12,4},{13,5},{14,6},{15,7},{0,8},{1,9},... | collective-permute-start | bytes 786440 | tf_op jit(solution)/shard_map/ppermute | solution.py:90
  92.7 3.7 %collective-permute-done.31 = bf16[64,2048]{1,0:T(8,128)(2,1)S(1)} collective-permute-done((bf16[64,2048]{1,0:T(8,128)(2,1)S(1)}, bf16[64,2048]{1,0:T(8,128)(2,1)S(1)}, u32[]{:S(2)}, u32[]{:S(2)}) %collective-permute-start.31) | collective-permute-done | bytes 262176 | tf_op jit(solution)/shard_map/ppermute | solution.py:90
  96.5 1.4 %collective-permute-done.30 = bf16[64,2048]{1,0:T(8,128)(2,1)S(1)} collective-permute-done((bf16[64,2048]{1,0:T(8,128)(2,1)S(1)}, bf16[64,2048]{1,0:T(8,128)(2,1)S(1)}, u32[]{:S(2)}, u32[]{:S(2)}) %collective-permute-start.30) | collective-permute-done | bytes 262176 | tf_op jit(solution)/shard_map/ppermute | solution.py:90
  99.3 1.4 %collective-permute-start.34 = (bf16[32,2048]{1,0:T(8,128)(2,1)S(1)}, bf16[32,2048]{1,0:T(8,128)(2,1)S(1)}, u32[]{:S(2)}, u32[]{:S(2)}) collective-permute-start(bf16[32,2048]{1,0:T(8,128)(2,1)S(1)} %get-tuple-element.142), channel_id=1, source_target_pairs={{8,0},{9,1},{10,2},{11,3},{12,4},{13,5},{14,6},{15,7},{0,8},{1,9},... | collective-permute-start | bytes 393224 | tf_op jit(solution)/shard_map/ppermute | solution.py:90
  102.2 3.3 %collective-permute-done.33 = bf16[32,2048]{1,0:T(8,128)(2,1)S(1)} collective-permute-done((bf16[32,2048]{1,0:T(8,128)(2,1)S(1)}, bf16[32,2048]{1,0:T(8,128)(2,1)S(1)}, u32[]{:S(2)}, u32[]{:S(2)}) %collective-permute-start.33) | collective-permute-done | bytes 131104 | tf_op jit(solution)/shard_map/ppermute | solution.py:90
  (89 shorter events, 30.1 us)
Async XLA Ops:
  1.2 13.8 %collective-permute-start = (bf16[64,1280]{1,0:T(8,128)(2,1)S(1)}, bf16[64,1280]{1,0:T(8,128)(2,1)S(1)}, u32[]{:S(2)}, u32[]{:S(2)}) collective-permute-start(bf16[64,1280]{1,0:T(8,128)(2,1)S(1)} %get-tuple-element.73._.refs_0_), channel_id=1, source_target_pairs={{16,0},{17,1},{18,2},{19,3},{20,4},{21,5},{22,6},{23,7},{24,8},{25... | collective-permute-start | bytes 491528 | tf_op jit(solution)/shard_map/ppermute | solution.py:90
  5.3 9.7 %collective-permute-start.1 = (bf16[64,1280]{1,0:T(8,128)(2,1)S(1)}, bf16[64,1280]{1,0:T(8,128)(2,1)S(1)}, u32[]{:S(2)}, u32[]{:S(2)}) collective-permute-start(bf16[64,1280]{1,0:T(8,128)(2,1)S(1)} %get-tuple-element.73._.refs_0_), channel_id=1, source_target_pairs={{4,0},{9,1},{6,2},{11,3},{0,4},{13,5},{2,6},{15,7},{12,8},{1,9},{1... | collective-permute-start | bytes 491528 | tf_op jit(solution)/shard_map/ppermute | solution.py:90
  6.8 8.2 %collective-permute-start.2 = (bf16[64,1280]{1,0:T(8,128)(2,1)S(1)}, bf16[64,1280]{1,0:T(8,128)(2,1)S(1)}, u32[]{:S(2)}, u32[]{:S(2)}) collective-permute-start(bf16[64,1280]{1,0:T(8,128)(2,1)S(1)} %get-tuple-element.73._.refs_0_), channel_id=1, source_target_pairs={{8,0},{5,1},{10,2},{7,3},{12,4},{1,5},{14,6},{3,7},{0,8},{13,9},{2... | collective-permute-start | bytes 491528 | tf_op jit(solution)/shard_map/ppermute | solution.py:90
  8.4 6.6 %collective-permute-start.3 = (bf16[4,16,640]{2,1,0:T(8,128)(2,1)S(1)}, bf16[4,16,640]{2,1,0:T(8,128)(2,1)S(1)}, u32[]{:S(2)}, u32[]{:S(2)}) collective-permute-start(bf16[4,16,640]{2,1,0:T(8,128)(2,1)S(1)} %get-tuple-element.74), channel_id=1, source_target_pairs={{8,0},{5,1},{10,2},{7,3},{12,4},{1,5},{14,6},{3,7},{0,8},{13,9},{2... | collective-permute-start | bytes 245768 | tf_op jit(solution)/shard_map/ppermute | solution.py:90
  15.0 9.3 %collective-permute-start.7 = (bf16[2048,768]{1,0:T(8,128)(2,1)S(1)}, bf16[2048,768]{1,0:T(8,128)(2,1)S(1)}, u32[]{:S(2)}, u32[]{:S(2)}) collective-permute-start(bf16[2048,768]{1,0:T(8,128)(2,1)S(1)} %get-tuple-element.82), channel_id=1, source_target_pairs={{0,1},{1,0},{2,3},{3,2},{4,5},{5,4},{6,7},{7,6},{8,9},{9,8},{10,11... | collective-permute-start | bytes 9437192 | tf_op jit(solution)/shard_map/ppermute | solution.py:25
  15.0 9.2 %collective-permute-start.5 = (bf16[64,1280]{1,0:T(8,128)(2,1)S(1)}, bf16[64,1280]{1,0:T(8,128)(2,1)S(1)}, u32[]{:S(2)}, u32[]{:S(2)}) collective-permute-start(bf16[64,1280]{1,0:T(8,128)(2,1)S(1)} %collective-permute-done.refs_1_), channel_id=1, source_target_pairs={{8,0},{5,1},{10,2},{7,3},{12,4},{1,5},{14,6},{3,7},{0,8},{13,9},{2... | collective-permute-start | bytes 491528 | tf_op jit(solution)/shard_map/ppermute | solution.py:90
  15.8 8.4 %collective-permute-start.4 = (bf16[128,1280]{1,0:T(8,128)(2,1)S(1)}, bf16[128,1280]{1,0:T(8,128)(2,1)S(1)}, u32[]{:S(2)}, u32[]{:S(2)}) collective-permute-start(bf16[128,1280]{1,0:T(8,128)(2,1)S(1)} %pad_maximum_fusion.3), channel_id=1, source_target_pairs={{4,0},{9,1},{6,2},{11,3},{0,4},{13,5},{2,6},{15,7},{12,8},{1,9},{1... | collective-permute-start | bytes 983048 | tf_op jit(solution)/shard_map/ppermute | solution.py:90
  17.4 6.8 %collective-permute-start.6 = (bf16[4,16,640]{2,1,0:T(8,128)(2,1)S(1)}, bf16[4,16,640]{2,1,0:T(8,128)(2,1)S(1)}, u32[]{:S(2)}, u32[]{:S(2)}) collective-permute-start(bf16[4,16,640]{2,1,0:T(8,128)(2,1)S(1)} %pad_maximum_fusion.9), channel_id=1, source_target_pairs={{4,0},{9,1},{6,2},{11,3},{0,4},{13,5},{2,6},{15,7},{12,8},{1,9},{1... | collective-permute-start | bytes 245768 | tf_op jit(solution)/shard_map/ppermute | solution.py:90
  24.3 5.8 %collective-permute-start.9 = (bf16[384,2048]{1,0:T(8,128)(2,1)S(1)}, bf16[384,2048]{1,0:T(8,128)(2,1)S(1)}, u32[]{:S(2)}, u32[]{:S(2)}) collective-permute-start(bf16[384,2048]{1,0:T(8,128)(2,1)S(1)} %get-tuple-element.87), channel_id=1, source_target_pairs={{0,1},{1,0},{2,3},{3,2},{4,5},{5,4},{6,7},{7,6},{8,9},{9,8},{10,11... | collective-permute-start | bytes 4718600 | tf_op jit(solution)/shard_map/ppermute | solution.py:25
  24.7 5.3 %collective-permute-start.8 = (bf16[64,1280]{1,0:T(8,128)(2,1)S(1)}, bf16[64,1280]{1,0:T(8,128)(2,1)S(1)}, u32[]{:S(2)}, u32[]{:S(2)}) collective-permute-start(bf16[64,1280]{1,0:T(8,128)(2,1)S(1)} %collective-permute-done.5.refs_5_), channel_id=1, source_target_pairs={{4,0},{9,1},{6,2},{11,3},{0,4},{13,5},{2,6},{15,7},{12,8},{1,9},{1... | collective-permute-start | bytes 491528 | tf_op jit(solution)/shard_map/ppermute | solution.py:90
  25.7 8.7 %collective-permute-start.10 = (bf16[4,16,640]{2,1,0:T(8,128)(2,1)S(1)}, bf16[4,16,640]{2,1,0:T(8,128)(2,1)S(1)}, u32[]{:S(2)}, u32[]{:S(2)}) collective-permute-start(bf16[4,16,640]{2,1,0:T(8,128)(2,1)S(1)} %pad_maximum_fusion.10), channel_id=1, source_target_pairs={{16,0},{17,1},{18,2},{19,3},{20,4},{21,5},{22,6},{23,7},{24,8},{25... | collective-permute-start | bytes 245768 | tf_op jit(solution)/shard_map/ppermute | solution.py:90
  36.3 6.0 %collective-permute-start.12 = (bf16[288,256]{1,0:T(8,128)(2,1)S(1)}, bf16[288,256]{1,0:T(8,128)(2,1)S(1)}, u32[]{:S(2)}, u32[]{:S(2)}) collective-permute-start(bf16[288,256]{1,0:T(8,128)(2,1)S(1)} %pad_maximum_fusion.8), channel_id=1, source_target_pairs={{0,2},{1,3},{2,0},{3,1},{4,6},{5,7},{6,4},{7,5},{8,10},{9,11},{10,... | collective-permute-start | bytes 442376 | tf_op jit(solution)/shard_map/ppermute | solution.py:25
  42.3 8.5 %collective-permute-start.13 = (bf16[256,256]{1,0:T(8,128)(2,1)S(1)}, bf16[256,256]{1,0:T(8,128)(2,1)S(1)}, u32[]{:S(2)}, u32[]{:S(2)}) collective-permute-start(bf16[256,256]{1,0:T(8,128)(2,1)S(1)} %add_convert_fusion.8.refs_0_.refs_6_), channel_id=1, source_target_pairs={{16,0},{17,1},{18,2},{19,3},{20,4},{21,5},{22,6},{23,7},{24,8},{25... | collective-permute-start | bytes 393224 | tf_op jit(solution)/shard_map/ppermute | solution.py:90
  44.3 7.0 %collective-permute-start.14 = (bf16[256,256]{1,0:T(8,128)(2,1)S(1)}, bf16[256,256]{1,0:T(8,128)(2,1)S(1)}, u32[]{:S(2)}, u32[]{:S(2)}) collective-permute-start(bf16[256,256]{1,0:T(8,128)(2,1)S(1)} %add_convert_fusion.8.refs_0_.refs_6_), channel_id=1, source_target_pairs={{8,0},{9,1},{10,2},{11,3},{12,4},{13,5},{14,6},{15,7},{0,8},{1,9},... | collective-permute-start | bytes 393224 | tf_op jit(solution)/shard_map/ppermute | solution.py:90
  45.5 5.8 %collective-permute-start.15 = (bf16[256,256]{1,0:T(8,128)(2,1)S(1)}, bf16[256,256]{1,0:T(8,128)(2,1)S(1)}, u32[]{:S(2)}, u32[]{:S(2)}) collective-permute-start(bf16[256,256]{1,0:T(8,128)(2,1)S(1)} %add_convert_fusion.8.refs_0_.refs_6_), channel_id=1, source_target_pairs={{2,0},{5,1},{0,2},{7,3},{6,4},{1,5},{4,6},{3,7},{10,8},{13,9},{8,1... | collective-permute-start | bytes 393224 | tf_op jit(solution)/shard_map/ppermute | solution.py:90
  52.0 7.3 %collective-permute-start.17 = (bf16[512,256]{1,0:T(8,128)(2,1)S(1)}, bf16[512,256]{1,0:T(8,128)(2,1)S(1)}, u32[]{:S(2)}, u32[]{:S(2)}) collective-permute-start(bf16[512,256]{1,0:T(8,128)(2,1)S(1)} %get-tuple-element.151), channel_id=1, source_target_pairs={{2,0},{5,1},{0,2},{7,3},{6,4},{1,5},{4,6},{3,7},{10,8},{13,9},{8,1... | collective-permute-start | bytes 786440 | tf_op jit(solution)/shard_map/ppermute | solution.py:90
  53.0 6.4 %collective-permute-start.18 = (bf16[512,256]{1,0:T(8,128)(2,1)S(1)}, bf16[512,256]{1,0:T(8,128)(2,1)S(1)}, u32[]{:S(2)}, u32[]{:S(2)}) collective-permute-start(bf16[512,256]{1,0:T(8,128)(2,1)S(1)} %get-tuple-element.150), channel_id=1, source_target_pairs={{8,0},{9,1},{10,2},{11,3},{12,4},{13,5},{14,6},{15,7},{0,8},{1,9},... | collective-permute-start | bytes 786440 | tf_op jit(solution)/shard_map/ppermute | solution.py:90
  53.5 6.4 %collective-permute-start.19 = (bf16[512,256]{1,0:T(8,128)(2,1)S(1)}, bf16[512,256]{1,0:T(8,128)(2,1)S(1)}, u32[]{:S(2)}, u32[]{:S(2)}) collective-permute-start(bf16[512,256]{1,0:T(8,128)(2,1)S(1)} %get-tuple-element.149), channel_id=1, source_target_pairs={{4,0},{3,1},{6,2},{1,3},{0,4},{7,5},{2,6},{5,7},{12,8},{11,9},{14,... | collective-permute-start | bytes 786440 | tf_op jit(solution)/shard_map/ppermute | solution.py:90
  59.9 7.8 %collective-permute-start.20 = (bf16[512,256]{1,0:T(8,128)(2,1)S(1)}, bf16[512,256]{1,0:T(8,128)(2,1)S(1)}, u32[]{:S(2)}, u32[]{:S(2)}) collective-permute-start(bf16[512,256]{1,0:T(8,128)(2,1)S(1)} %collective-permute-done.17.refs_4_.refs_1_.refs_11_), channel_id=1, source_target_pairs={{4,0},{3,1},{6,2},{1,3},{0,4},{7,5},{2,6},{5,7},{12,8},{11,9},{14,... | collective-permute-start | bytes 786440 | tf_op jit(solution)/shard_map/ppermute | solution.py:90
  60.8 5.1 %collective-permute-start.21 = (bf16[256,256]{1,0:T(8,128)(2,1)S(1)}, bf16[256,256]{1,0:T(8,128)(2,1)S(1)}, u32[]{:S(2)}, u32[]{:S(2)}) collective-permute-start(bf16[256,256]{1,0:T(8,128)(2,1)S(1)} %slice.90), channel_id=1, source_target_pairs={{8,0},{9,1},{10,2},{11,3},{12,4},{13,5},{14,6},{15,7},{0,8},{1,9},... | collective-permute-start | bytes 393224 | tf_op jit(solution)/shard_map/ppermute | solution.py:90
  62.6 5.1 %collective-permute-start.22 = (bf16[256,256]{1,0:T(8,128)(2,1)S(1)}, bf16[256,256]{1,0:T(8,128)(2,1)S(1)}, u32[]{:S(2)}, u32[]{:S(2)}) collective-permute-start(bf16[256,256]{1,0:T(8,128)(2,1)S(1)} %slice.91), channel_id=1, source_target_pairs={{4,0},{3,1},{6,2},{1,3},{0,4},{7,5},{2,6},{5,7},{12,8},{11,9},{14,... | collective-permute-start | bytes 393224 | tf_op jit(solution)/shard_map/ppermute | solution.py:90
  67.7 5.0 %collective-permute-start.23 = (bf16[256,256]{1,0:T(8,128)(2,1)S(1)}, bf16[256,256]{1,0:T(8,128)(2,1)S(1)}, u32[]{:S(2)}, u32[]{:S(2)}) collective-permute-start(bf16[256,256]{1,0:T(8,128)(2,1)S(1)} %collective-permute-done.21.refs_5_.refs_14_), channel_id=1, source_target_pairs={{4,0},{3,1},{6,2},{1,3},{0,4},{7,5},{2,6},{5,7},{12,8},{11,9},{14,... | collective-permute-start | bytes 393224 | tf_op jit(solution)/shard_map/ppermute | solution.py:90
  75.1 5.2 %collective-permute-start.26 = (bf16[256,1664]{1,0:T(8,128)(2,1)S(1)}, bf16[256,1664]{1,0:T(8,128)(2,1)S(1)}, u32[]{:S(2)}, u32[]{:S(2)}) collective-permute-start(bf16[256,1664]{1,0:T(8,128)(2,1)S(1)} %experts_in_second.3.refs_5_.act_ref), channel_id=1, source_target_pairs={{0,1},{1,0},{2,3},{3,2},{4,5},{5,4},{6,7},{7,6},{8,9},{9,8},{10,11... | collective-permute-start | bytes 2555912 | tf_op jit(solution)/shard_map/ppermute | solution.py:25
  78.2 5.0 %collective-permute-start.25 = (bf16[32,2048]{1,0:T(8,128)(2,1)S(1)}, bf16[32,2048]{1,0:T(8,128)(2,1)S(1)}, u32[]{:S(2)}, u32[]{:S(2)}) collective-permute-start(bf16[32,2048]{1,0:T(8,128)(2,1)S(1)} %get-tuple-element.110), channel_id=1, source_target_pairs={{4,0},{3,1},{6,2},{1,3},{0,4},{7,5},{2,6},{5,7},{12,8},{11,9},{14,... | collective-permute-start | bytes 393224 | tf_op jit(solution)/shard_map/ppermute | solution.py:90
  79.2 7.9 %collective-permute-start.29 = (bf16[32,2048]{1,0:T(8,128)(2,1)S(1)}, bf16[32,2048]{1,0:T(8,128)(2,1)S(1)}, u32[]{:S(2)}, u32[]{:S(2)}) collective-permute-start(bf16[32,2048]{1,0:T(8,128)(2,1)S(1)} %get-tuple-element.126), channel_id=1, source_target_pairs={{4,0},{3,1},{6,2},{1,3},{0,4},{7,5},{2,6},{5,7},{12,8},{11,9},{14,... | collective-permute-start | bytes 393224 | tf_op jit(solution)/shard_map/ppermute | solution.py:90
  83.3 6.4 %collective-permute-start.27 = (bf16[64,2048]{1,0:T(8,128)(2,1)S(1)}, bf16[64,2048]{1,0:T(8,128)(2,1)S(1)}, u32[]{:S(2)}, u32[]{:S(2)}) collective-permute-start(bf16[64,2048]{1,0:T(8,128)(2,1)S(1)} %pad_maximum_fusion.4), channel_id=1, source_target_pairs={{4,0},{3,1},{6,2},{1,3},{0,4},{7,5},{2,6},{5,7},{12,8},{11,9},{14,... | collective-permute-start | bytes 786440 | tf_op jit(solution)/shard_map/ppermute | solution.py:90
  84.2 5.0 %collective-permute-start.28 = (bf16[32,2048]{1,0:T(8,128)(2,1)S(1)}, bf16[32,2048]{1,0:T(8,128)(2,1)S(1)}, u32[]{:S(2)}, u32[]{:S(2)}) collective-permute-start(bf16[32,2048]{1,0:T(8,128)(2,1)S(1)} %add_convert_fusion.7), channel_id=1, source_target_pairs={{8,0},{9,1},{10,2},{11,3},{12,4},{13,5},{14,6},{15,7},{0,8},{1,9},... | collective-permute-start | bytes 393224 | tf_op jit(solution)/shard_map/ppermute | solution.py:90
  86.1 6.7 %collective-permute-start.32 = (bf16[64,2048]{1,0:T(8,128)(2,1)S(1)}, bf16[64,2048]{1,0:T(8,128)(2,1)S(1)}, u32[]{:S(2)}, u32[]{:S(2)}) collective-permute-start(bf16[64,2048]{1,0:T(8,128)(2,1)S(1)} %pad_maximum_fusion.7), channel_id=1, source_target_pairs={{4,0},{3,1},{6,2},{1,3},{0,4},{7,5},{2,6},{5,7},{12,8},{11,9},{14,... | collective-permute-start | bytes 786440 | tf_op jit(solution)/shard_map/ppermute | solution.py:90
  89.8 6.7 %collective-permute-start.31 = (bf16[64,2048]{1,0:T(8,128)(2,1)S(1)}, bf16[64,2048]{1,0:T(8,128)(2,1)S(1)}, u32[]{:S(2)}, u32[]{:S(2)}) collective-permute-start(bf16[64,2048]{1,0:T(8,128)(2,1)S(1)} %pad_maximum_fusion.6), channel_id=1, source_target_pairs={{8,0},{9,1},{10,2},{11,3},{12,4},{13,5},{14,6},{15,7},{0,8},{1,9},... | collective-permute-start | bytes 786440 | tf_op jit(solution)/shard_map/ppermute | solution.py:90
  91.4 6.4 %collective-permute-start.30 = (bf16[64,2048]{1,0:T(8,128)(2,1)S(1)}, bf16[64,2048]{1,0:T(8,128)(2,1)S(1)}, u32[]{:S(2)}, u32[]{:S(2)}) collective-permute-start(bf16[64,2048]{1,0:T(8,128)(2,1)S(1)} %pad_maximum_fusion.5), channel_id=1, source_target_pairs={{2,0},{5,1},{0,2},{7,3},{6,4},{1,5},{4,6},{3,7},{10,8},{13,9},{8,1... | collective-permute-start | bytes 786440 | tf_op jit(solution)/shard_map/ppermute | solution.py:90
  98.0 7.4 %collective-permute-start.33 = (bf16[32,2048]{1,0:T(8,128)(2,1)S(1)}, bf16[32,2048]{1,0:T(8,128)(2,1)S(1)}, u32[]{:S(2)}, u32[]{:S(2)}) collective-permute-start(bf16[32,2048]{1,0:T(8,128)(2,1)S(1)} %get-tuple-element.141), channel_id=1, source_target_pairs={{16,0},{17,1},{18,2},{19,3},{20,4},{21,5},{22,6},{23,7},{24,8},{25... | collective-permute-start | bytes 393224 | tf_op jit(solution)/shard_map/ppermute | solution.py:90
  99.3 6.2 %collective-permute-start.34 = (bf16[32,2048]{1,0:T(8,128)(2,1)S(1)}, bf16[32,2048]{1,0:T(8,128)(2,1)S(1)}, u32[]{:S(2)}, u32[]{:S(2)}) collective-permute-start(bf16[32,2048]{1,0:T(8,128)(2,1)S(1)} %get-tuple-element.142), channel_id=1, source_target_pairs={{8,0},{9,1},{10,2},{11,3},{12,4},{13,5},{14,6},{15,7},{0,8},{1,9},... | collective-permute-start | bytes 393224 | tf_op jit(solution)/shard_map/ppermute | solution.py:90
  (9 other events, 90.9 us)

commit v9 on v8

--- a/solution.py
+++ b/solution.py
@@ -47,19 +47,21 @@
     y_move = (1, 0)
     if (ctx_count, x_count) == (8, 2) and not rows_only:
         z_far, z_near = ((4, 0),) * 2, ((2, 0),) * 2
-        first, second = ((0, 2), y_move), (y_move, (0, 2))
+        first, second, both = ((0, 2), y_move), (y_move, (0, 2)), ((1, 2),) * 2
         at = {"0": (0, 0)}
         for stage, moves, hops in (
             (1, z_far, "0>4"),
             (1, z_near, "0>2"),
             (1, first, "0>0a"),
             (1, second, "0>0b"),
-            (2, z_near, "4>6 0b>2b"),
+            (1, both, "0>0ab"),
+            (2, z_far, "0ab>4ab"),
+            (2, z_near, "4>6"),
             (2, first, "2>2a 4>4a"),
-            (2, second, "4>4b 0a>0ab"),
-            (3, z_near, "4a>6a"),
-            (3, second, "2a>2ab 4a>4ab 6>6b"),
-            (4, second, "6a>6ab"),
+            (2, second, "2>2b 4>4b"),
+            (3, z_near, "4ab>6ab"),
+            (3, first, "6>6a"),
+            (3, second, "6>6b 2a>2ab"),
         ):
             for hop in hops.split():
                 source, target = hop.split(">")
@@ -90,6 +92,21 @@
     return lax.ppermute(array, ("ctx", "exp"), pairs)
 
 
+def side_of(index, bit):
+    return (index >> bit) & 1
+
+
+def without(index, bit):
+    return (index & ((1 << bit) - 1)) | ((index >> bit + 1) << bit)
+
+
+def runs(ctx_count, bit, side, each):
+    length = each << bit
+    return [
+        (pl.multiple_of((2 * k + side) * length, length), k * length, length) for k in range(ctx_count >> bit + 1)
+    ]
+
+
 def by_core(core, place, part):
     first, second = place[0][part], place[1][part]
     return first if first == second else jnp.where(core == 0, first, second)
@@ -108,9 +125,9 @@
                 sends.append((moves, group, tuple(left[key] for key in group)))
         def order(send):
             moves, group, _ = send
-            shared, load = moves[0] == moves[1], len(group) * (2 if moves[0][0] == top > 2 else 1)
+            shared, far = moves[0] == moves[1], moves[0][0] == top > 2
             rank = (0 if shared else 1) if len(group) == 1 else (1 if shared else 2 * moves[0][0])
-            return -load, rank
+            return -len(group) * (2 if far else 1), -1 if far else rank
 
         sends.sort(key=order)
         arrays = arrays + [send[2] for send in sends]
@@ -417,11 +434,10 @@
 
 
 def fill_rows(plan, ctx_ref, exp_ref, gain_ref, chunk_refs, places, rows_scr, square_ref, groups):
-    ctx_count, x_count, tok = plan
-    half = ctx_count // 2
+    ctx_count, x_count, tok, bit = plan
     my_ctx = ctx_ref[0]
     my_core = lax.bitwise_and(exp_ref[0], 1)
-    mine = lax.shift_right_logical(my_ctx, bits_of(half))
+    mine = side_of(my_ctx, bit)
     cols = chunk_refs[0].shape[1]
     rows = ctx_count * tok
     for (array, first_row), place_of in places:
@@ -430,54 +446,61 @@
         x_off = by_core(my_core, place_of, 1)
         gain_at = pl.multiple_of((source * 2 + my_core) * cols, cols)
         gain = gain_ref[:, pl.ds(gain_at, cols)]
-        col = pl.multiple_of(lax.bitwise_and(source, half - 1) * cols, cols)
+        col = pl.multiple_of(without(source, bit) * cols, cols)
         for place, group in enumerate(groups):
-            side = mine if group == 1 else 1 - mine
-            chunk_at = pl.ds(pl.multiple_of(first_row + side * rows, rows), rows)
-            chunk = ref[chunk_at, :].astype(jnp.float32)
-            at = pl.ds(pl.multiple_of((place * x_count + x_off) * rows, rows), rows)
-            rows_scr[at, pl.ds(col, cols)] = (chunk * gain).astype(jnp.bfloat16)
-            square_ref[at, :] = square_ref[at, :] + jnp.sum(chunk * chunk, axis=-1, keepdims=True)
+            for start, low, length in runs(ctx_count, bit, mine if group == 1 else 1 - mine, 2 * tok):
+                chunk = ref[pl.ds(first_row + start, length), :].astype(jnp.float32)
+                row = (place * x_count + x_off) * rows + low
+                at = pl.ds(pl.multiple_of(row, 2 * tok), length)
+                rows_scr[at, pl.ds(col, cols)] = (chunk * gain).astype(jnp.bfloat16)
+                square_ref[at, :] = square_ref[at, :] + jnp.sum(chunk * chunk, axis=-1, keepdims=True)
+
+
+def product(plan, side, rows_scr, weight_ref, cols):
+    ctx_count, _, _, bit = plan
+    total = None
+    for start, low, length in runs(ctx_count, bit, side, cols):
+        part = jnp.dot(
+            rows_scr[:, low : low + length],
+            weight_ref[pl.ds(start, length), :],
+            preferred_element_type=jnp.float32,
+        )
+        total = part if total is None else total + part
+    return total
 
 
 def experts_in_first(plan, offsets, ctx_ref, exp_ref, *refs):
     chunk_refs, (gain_ref, own_ref, other_ref, _, act_ref, square_ref, rows_scr) = refs[:-7], refs[-7:]
-    half = plan[0] // 2
     square_ref[...] = jnp.zeros(square_ref.shape, jnp.float32)
     fill_rows(plan, ctx_ref, exp_ref, gain_ref, chunk_refs, offsets, rows_scr, square_ref, (0, 1))
-    depth, width = rows_scr.shape[1], own_ref.shape[1]
-    start = lax.shift_right_logical(ctx_ref[0], bits_of(half)) * depth
-    at = pl.ds(pl.multiple_of(start, depth), depth)
+    width, side = own_ref.shape[1], side_of(ctx_ref[0], plan[3])
     for place, ref in enumerate((own_ref, other_ref)):
-        act_ref[:, place * width : (place + 1) * width] = jnp.dot(
-            rows_scr[...], ref[at, :], preferred_element_type=jnp.float32
+        act_ref[:, place * width : (place + 1) * width] = product(
+            plan, side, rows_scr, ref, chunk_refs[0].shape[1]
         )
 
 
 def experts_in_second(plan, offsets, group, ctx_ref, exp_ref, *refs):
     chunk_refs, rest = refs[:-9], refs[-9:]
     gain_ref, own_ref, other_ref, first_ref, square_ref, _, act_ref, rows_scr, sum_scr = rest
-    half = plan[0] // 2
-    count, depth = rows_scr.shape
-    width = own_ref.shape[1]
+    count, width = rows_scr.shape[0], own_ref.shape[1]
     sum_scr[...] = square_ref[group * count : (group + 1) * count, :]
     fill_rows(plan, ctx_ref, exp_ref, gain_ref, chunk_refs, offsets, rows_scr, sum_scr, (group,))
     lane = lax.broadcasted_iota(jnp.int32, (1, HEAD_SIZE), 1)
     square = sum_scr[...]
     high = square.astype(jnp.bfloat16).astype(jnp.float32)
     act_ref[:, 2 * width :] = jnp.where(lane == 0, high, square - high).astype(jnp.bfloat16)
-    start = (1 - lax.shift_right_logical(ctx_ref[0], bits_of(half))) * depth
-    at = pl.ds(pl.multiple_of(start, depth), depth)
+    side = 1 - side_of(ctx_ref[0], plan[3])
     for place, ref in enumerate((own_ref, other_ref)):
         cols = slice(place * width, (place + 1) * width)
-        act = first_ref[group * count : (group + 1) * count, cols] + jnp.dot(
-            rows_scr[...], ref[at, :], preferred_element_type=jnp.float32
+        act = first_ref[group * count : (group + 1) * count, cols] + product(
+            plan, side, rows_scr, ref, chunk_refs[0].shape[1]
         )
         act_ref[:, cols] = act.astype(jnp.bfloat16)
 
 
 def experts_out_kernel(plan, group, places, state_at, route_at, model_width, ctx_ref, exp_ref, act_ref, came_ref, *refs):
-    ctx_count, exp_count, tok = plan
+    ctx_count, exp_count, tok, bit = plan
     x_count, half = exp_count // 2, ctx_count // 2
     route_refs, refs = refs[: x_count + 1], refs[x_count + 1 :]
     (own_ref, other_ref, _), rest = refs[:3], refs[3:]
@@ -486,8 +509,8 @@
     out_refs, hidden_scr = rest[:-1], rest[-1]
     my_ctx = ctx_ref[0]
     my_core = lax.bitwise_and(exp_ref[0], 1)
-    mine = lax.shift_right_logical(my_ctx, bits_of(half))
-    first_ctx = (mine if group == 1 else 1 - mine) * half
+    mine = side_of(my_ctx, bit)
+    side = mine if group == 1 else 1 - mine
     width = (act_ref.shape[1] - HEAD_SIZE) // 2
     hidden = width // 2
     lane = lax.broadcasted_iota(jnp.int32, (tok, HEAD_SIZE), 1)
@@ -500,23 +523,24 @@
             for core in range(2):
                 same, swapped = blocks[2 * x_off + core], blocks[2 * x_off + 1 - core]
                 block = jnp.where(my_core == 0, same, swapped)
-                picked = jnp.where(lane % ctx_count == first_ctx + low, block, 0.0)
+                number = (low >> bit << bit + 1) + (low & ((1 << bit) - 1)) + side * (1 << bit)
+                picked = jnp.where(lane % ctx_count == number, block, 0.0)
                 columns.append(jnp.sum(picked, axis=1, keepdims=True))
     route = jnp.concatenate(columns, axis=0)
     squares = act_ref[:, 2 * width :].astype(jnp.float32) + came_ref[:, 2 * width :].astype(jnp.float32)
     norm = lax.rsqrt((squares[:, 0:1] + squares[:, 1:2]) / model_width + 1e-06)
     scaled_route = norm * route
-    for side in range(2):
-        acts = act_ref[:, side * width : (side + 1) * width].astype(jnp.float32) + came_ref[
-            :, (1 - side) * width : (2 - side) * width
+    for part in range(2):
+        acts = act_ref[:, part * width : (part + 1) * width].astype(jnp.float32) + came_ref[
+            :, (1 - part) * width : (2 - part) * width
         ].astype(jnp.float32)
         gate = acts[:, :hidden] * norm
         value = gate / (1.0 + jnp.exp(-gate)) * (acts[:, hidden:] * scaled_route)
-        hidden_scr[:, side * hidden : (side + 1) * hidden] = value.astype(jnp.bfloat16)
+        hidden_scr[:, part * hidden : (part + 1) * hidden] = value.astype(jnp.bfloat16)
     picked = []
     for place in places:
         x_off = by_core(my_core, place, 1)
-        low = lax.bitwise_and(lax.bitwise_xor(my_ctx, by_core(my_core, place, 0)), half - 1)
+        low = without(lax.bitwise_xor(my_ctx, by_core(my_core, place, 0)), bit)
         row = pl.multiple_of((x_off * half + low) * (2 * tok), 2 * tok)
         picked.append(hidden_scr[pl.ds(row, 2 * tok), :])
     picked = jnp.concatenate(picked, axis=0)
@@ -712,8 +736,9 @@
     gain = norm_gain.reshape(1, model_width)
     rows = x_count * per_x
     in_width = in_own.shape[1]
-    near = tuple(sorted(key for key in places if key[0] < ctx_count // 2))
-    far = tuple(sorted(key for key in places if key[0] >= ctx_count // 2))
+    bit = 1 if (ctx_count, x_count) == (8, 2) else bits_of(ctx_count) - 1
+    near = tuple(sorted(key for key in places if not side_of(key[0], bit)))
+    far = tuple(sorted(key for key in places if side_of(key[0], bit)))
 
     def picked(keys):
         arrays = sorted({chunk_at[key][0] for key in keys})
@@ -723,7 +748,7 @@
     near_chunks, near_places = picked(near)
     far_chunks, far_places = picked(far)
     first_act, first_square = pl.pallas_call(
-        functools.partial(experts_in_first, (ctx_count, x_count, tok), near_places),
+        functools.partial(experts_in_first, (ctx_count, x_count, tok, bit), near_places),
         in_specs=[smem] * 2 + [vmem] * (len(near_chunks) + 3) + [anywhere],
         out_specs=[vmem] * 2,
         out_shape=[
@@ -741,7 +766,7 @@
     for part in range(2):
         acts.append(
             pl.pallas_call(
-                functools.partial(experts_in_second, (ctx_count, x_count, tok), far_places, part),
+                functools.partial(experts_in_second, (ctx_count, x_count, tok, bit), far_places, part),
                 in_specs=[smem] * 2 + [vmem] * (len(far_chunks) + 5) + [anywhere],
                 out_specs=vmem,
                 out_shape=jax.ShapeDtypeStruct((rows // 2, 2 * in_width + HEAD_SIZE), bf16),
@@ -780,7 +805,7 @@
         outs = pl.pallas_call(
             functools.partial(
                 experts_out_kernel,
-                (ctx_count, exp_count, tok),
+                (ctx_count, exp_count, tok, bit),
                 part,
                 tuple(places[key] for key in slots),
                 state_at,

time: 109 us -> 105 us (0.963)
  waiting for transfers between devices: 47 us -> 40.9 us
  starting transfers between devices: 40.8 us -> 43 us
    ppermute x31 -> x33, waiting for transfers between devices: 39.4 us -> 33.5 us  [follow(): return lax.ppermute(array, ('ctx', 'exp'), pairs)]
    ppermute x31 -> x33, starting transfers between devices: 37.8 us -> 40 us  [follow(): return lax.ppermute(array, ('ctx', 'exp'), pairs)]
  transfers between devices with their start and end apart: 38 -> 40, of which waited for: 25 -> 21; matrix products, arithmetic and copies ran while one was open for 0% -> 0% of each run, Pallas kernels for 15% -> 16%
where the time goes in v9:
time: 105 us
  starting transfers between devices  43 us (41%)
  waiting for transfers between devices  40.9 us (39%)
  Pallas kernels  19 us (18%)
    ppermute x33, starting transfers between devices, follow(): return lax.ppermute(array, ('ctx', 'exp'), pairs)  40 us
    ppermute x33, waiting for transfers between devices, follow(): return lax.ppermute(array, ('ctx', 'exp'), pairs)  33.5 us
    ppermute x7, waiting for transfers between devices, from_offset(): lax.ppermute(array, 'exp', [(i, i ^ offset) for i in range(lax.axis_size(...  7.44 us
    pallas_call x1, Pallas kernels, shards(): pl.pallas_call(functools.partial(attend_kernel, (ctx_count, exp_count, to...  4.33 us
    pallas_call x2, Pallas kernels, shards(): pl.pallas_call(functools.partial(experts_out_kernel, (ctx_count, exp_coun...  3.63 us
    pallas_call x1, Pallas kernels, deq_in(): pl.pallas_call(functools.partial(deq_in_kernel, ctx_count), in_specs=[pl....  3 us
    ppermute x7, starting transfers between devices, from_offset(): lax.ppermute(array, 'exp', [(i, i ^ offset) for i in range(lax.axis_size(...  2.98 us
    pallas_call x2, Pallas kernels, shards(): pl.pallas_call(functools.partial(experts_in_second, (ctx_count, x_count,...  2.58 us
  transfers between devices with their start and end apart: 40, of which 21 were waited for; matrix products, arithmetic and copies ran while one was open for 0% of the time, Pallas kernels for 16%

profile of v9, /device:TPU:0, one launch (start us, length us, event | category | flops | bytes accessed | tf_op | source)
XLA Modules:
  0.0 104.9 jit_solution(13599438170892403116)
XLA Ops:
  1.2 4.1 %collective-permute-start = (bf16[64,1280]{1,0:T(8,128)(2,1)S(1)}, bf16[64,1280]{1,0:T(8,128)(2,1)S(1)}, u32[]{:S(2)}, u32[]{:S(2)}) collective-permute-start(bf16[64,1280]{1,0:T(8,128)(2,1)S(1)} %get-tuple-element.72._.refs_0_), channel_id=1, source_target_pairs={{16,0},{17,1},{18,2},{19,3},{20,4},{21,5},{22,6},{23,7},{24,8},{25... | collective-permute-start | bytes 491528 | tf_op jit(solution)/shard_map/ppermute | solution.py:92
  5.3 1.5 %collective-permute-start.1 = (bf16[64,1280]{1,0:T(8,128)(2,1)S(1)}, bf16[64,1280]{1,0:T(8,128)(2,1)S(1)}, u32[]{:S(2)}, u32[]{:S(2)}) collective-permute-start(bf16[64,1280]{1,0:T(8,128)(2,1)S(1)} %get-tuple-element.72._.refs_0_), channel_id=1, source_target_pairs={{4,0},{9,1},{6,2},{11,3},{0,4},{13,5},{2,6},{15,7},{12,8},{1,9},{1... | collective-permute-start | bytes 491528 | tf_op jit(solution)/shard_map/ppermute | solution.py:92
  6.8 1.6 %collective-permute-start.2 = (bf16[64,1280]{1,0:T(8,128)(2,1)S(1)}, bf16[64,1280]{1,0:T(8,128)(2,1)S(1)}, u32[]{:S(2)}, u32[]{:S(2)}) collective-permute-start(bf16[64,1280]{1,0:T(8,128)(2,1)S(1)} %get-tuple-element.72._.refs_0_), channel_id=1, source_target_pairs={{8,0},{5,1},{10,2},{7,3},{12,4},{1,5},{14,6},{3,7},{0,8},{13,9},{2... | collective-permute-start | bytes 491528 | tf_op jit(solution)/shard_map/ppermute | solution.py:92
  8.8 3.0 %dequant_in.1 = (bf16[2048,768]{1,0:T(8,128)(2,1)S(1)}, bf16[2048,768]{1,0:T(8,128)(2,1)S(1)}) custom-call(s32[1]{0:T(128)} %bitcast.1.exp_ref, s32[3,1,32]{2,1,0:T(1,128)} %bitcast.25, s32[3,1,32]{2,1,0:T(1,128)} %bitcast.26, bf16[1,4096,384]{2,1,0:T(8,128)(2,1)} %gate_hbm.1, bf16[1,4096,384]{2,1,0:T(8,128)(2,1)} %up_hbm.1, ...), custom_call_target="tpu_custom_call" | custom-call | flops 3145728 | bytes 12582912 | tf_op jit(solution)/shard_map/dequant_in/pallas_call | solution.py:269
  11.8 3.1 %collective-permute-done.3._.refs_1_ = bf16[4,16,640]{2,1,0:T(8,128)(2,1)S(1)} collective-permute-done((bf16[4,16,640]{2,1,0:T(8,128)(2,1)S(1)}, bf16[4,16,640]{2,1,0:T(8,128)(2,1)S(1)}, u32[]{:S(2)}, u32[]{:S(2)}) %collective-permute-start.3) | collective-permute-done | bytes 81952 | tf_op jit(solution)/shard_map/ppermute | solution.py:92
  15.8 1.6 %collective-permute-start.4 = (bf16[128,1280]{1,0:T(8,128)(2,1)S(1)}, bf16[128,1280]{1,0:T(8,128)(2,1)S(1)}, u32[]{:S(2)}, u32[]{:S(2)}) collective-permute-start(bf16[128,1280]{1,0:T(8,128)(2,1)S(1)} %pad_maximum_fusion), channel_id=1, source_target_pairs={{4,0},{9,1},{6,2},{11,3},{0,4},{13,5},{2,6},{15,7},{12,8},{1,9},{1... | collective-permute-start | bytes 983048 | tf_op jit(solution)/shard_map/ppermute | solution.py:92
  18.0 2.1 %dequant_down.1 = (bf16[384,2048]{1,0:T(8,128)(2,1)S(1)}, bf16[384,2048]{1,0:T(8,128)(2,1)S(1)}) custom-call(s32[1]{0:T(128)} %bitcast.1.exp_ref, s32[3,1,32]{2,1,0:T(1,128)} %bitcast.27, bf16[1,384,4096]{2,1,0:T(8,128)(2,1)} %down_hbm.1, bf16[4,16,640]{2,1,0:T(8,128)(2,1)S(1)} %collective-permute-done.3._.refs_1_), custom_call_target="tpu_custom_call" | custom-call | flops 1572864 | bytes 6291456 | tf_op jit(solution)/shard_map/dequant_down/pallas_call | solution.py:318
  20.1 4.2 %collective-permute-done.6.refs_2_ = bf16[4,16,640]{2,1,0:T(8,128)(2,1)S(1)} collective-permute-done((bf16[4,16,640]{2,1,0:T(8,128)(2,1)S(1)}, bf16[4,16,640]{2,1,0:T(8,128)(2,1)S(1)}, u32[]{:S(2)}, u32[]{:S(2)}) %collective-permute-start.6) | collective-permute-done | bytes 81952 | tf_op jit(solution)/shard_map/ppermute | solution.py:92
  25.7 1.6 %collective-permute-start.10 = (bf16[4,16,640]{2,1,0:T(8,128)(2,1)S(1)}, bf16[4,16,640]{2,1,0:T(8,128)(2,1)S(1)}, u32[]{:S(2)}, u32[]{:S(2)}) collective-permute-start(bf16[4,16,640]{2,1,0:T(8,128)(2,1)S(1)} %pad_maximum_fusion.7), channel_id=1, source_target_pairs={{16,0},{17,1},{18,2},{19,3},{20,4},{21,5},{22,6},{23,7},{24,8},{25... | collective-permute-start | bytes 245768 | tf_op jit(solution)/shard_map/ppermute | solution.py:92
  27.3 2.8 %collective-permute-done.8.refs_6_ = bf16[64,1280]{1,0:T(8,128)(2,1)S(1)} collective-permute-done((bf16[64,1280]{1,0:T(8,128)(2,1)S(1)}, bf16[64,1280]{1,0:T(8,128)(2,1)S(1)}, u32[]{:S(2)}, u32[]{:S(2)}) %collective-permute-start.8) | collective-permute-done | bytes 163872 | tf_op jit(solution)/shard_map/ppermute | solution.py:92
  30.0 4.3 %attend.1 = (f32[256,256]{1,0:T(8,128)S(1)}, f32[256,256]{1,0:T(8,128)S(1)}, bf16[512,256]{1,0:T(8,128)(2,1)S(1)}) custom-call(s32[1]{0:T(128)} %bitcast.ctx_ref, s32[1]{0:T(128)} %bitcast.1.exp_ref, s32[8]{0:T(128)S(1)} %copy-done.2, bf16[64,1280]{1,0:T(8,128)(2,1)S(1)} %get-tuple-element.72._.refs_0_, bf16[64,1280]{1,0:T(8,128)(2,1)S(1)} %collective-permute-done.refs_1_, ...), custom_call_target="tpu_custom_call" | custom-call | flops 1610612736 | bytes 8388608 | tf_op jit(solution)/shard_map/attend/pallas_call | solution.py:684
  34.8 1.4 %collective-permute-done.11.refs_1_ = bf16[544,256]{1,0:T(8,128)(2,1)S(1)} collective-permute-done((bf16[544,256]{1,0:T(8,128)(2,1)S(1)}, bf16[544,256]{1,0:T(8,128)(2,1)S(1)}, u32[]{:S(2)}, u32[]{:S(2)}) %collective-permute-start.11) | collective-permute-done | bytes 278560 | tf_op jit(solution)/shard_map/ppermute | solution.py:25
  36.3 1.6 %collective-permute-start.12 = (bf16[288,256]{1,0:T(8,128)(2,1)S(1)}, bf16[288,256]{1,0:T(8,128)(2,1)S(1)}, u32[]{:S(2)}, u32[]{:S(2)}) collective-permute-start(bf16[288,256]{1,0:T(8,128)(2,1)S(1)} %pad_maximum_fusion.5), channel_id=1, source_target_pairs={{0,2},{1,3},{2,0},{3,1},{4,6},{5,7},{6,4},{7,5},{8,10},{9,11},{10,... | collective-permute-start | bytes 442376 | tf_op jit(solution)/shard_map/ppermute | solution.py:25
  37.9 4.3 %collective-permute-done.12.refs_2_ = bf16[288,256]{1,0:T(8,128)(2,1)S(1)} collective-permute-done((bf16[288,256]{1,0:T(8,128)(2,1)S(1)}, bf16[288,256]{1,0:T(8,128)(2,1)S(1)}, u32[]{:S(2)}, u32[]{:S(2)}) %collective-permute-start.12) | collective-permute-done | bytes 147488 | tf_op jit(solution)/shard_map/ppermute | solution.py:25
  42.3 2.0 %collective-permute-start.13 = (bf16[256,256]{1,0:T(8,128)(2,1)S(1)}, bf16[256,256]{1,0:T(8,128)(2,1)S(1)}, u32[]{:S(2)}, u32[]{:S(2)}) collective-permute-start(bf16[256,256]{1,0:T(8,128)(2,1)S(1)} %add_convert_fusion.6.refs_0_.refs_6_), channel_id=1, source_target_pairs={{16,0},{17,1},{18,2},{19,3},{20,4},{21,5},{22,6},{23,7},{24,8},{25... | collective-permute-start | bytes 393224 | tf_op jit(solution)/shard_map/ppermute | solution.py:92
  44.3 1.4 %collective-permute-start.14 = (bf16[256,256]{1,0:T(8,128)(2,1)S(1)}, bf16[256,256]{1,0:T(8,128)(2,1)S(1)}, u32[]{:S(2)}, u32[]{:S(2)}) collective-permute-start(bf16[256,256]{1,0:T(8,128)(2,1)S(1)} %add_convert_fusion.6.refs_0_.refs_6_), channel_id=1, source_target_pairs={{6,0},{7,1},{4,2},{5,3},{2,4},{3,5},{0,6},{1,7},{14,8},{15,9},{12,... | collective-permute-start | bytes 393224 | tf_op jit(solution)/shard_map/ppermute | solution.py:92
  45.7 1.4 %collective-permute-start.15 = (bf16[256,256]{1,0:T(8,128)(2,1)S(1)}, bf16[256,256]{1,0:T(8,128)(2,1)S(1)}, u32[]{:S(2)}, u32[]{:S(2)}) collective-permute-start(bf16[256,256]{1,0:T(8,128)(2,1)S(1)} %add_convert_fusion.6.refs_0_.refs_6_), channel_id=1, source_target_pairs={{8,0},{9,1},{10,2},{11,3},{12,4},{13,5},{14,6},{15,7},{0,8},{1,9},... | collective-permute-start | bytes 393224 | tf_op jit(solution)/shard_map/ppermute | solution.py:92
  49.0 1.9 %collective-permute-done.13.refs_1_.refs_7_ = bf16[256,256]{1,0:T(8,128)(2,1)S(1)} collective-permute-done((bf16[256,256]{1,0:T(8,128)(2,1)S(1)}, bf16[256,256]{1,0:T(8,128)(2,1)S(1)}, u32[]{:S(2)}, u32[]{:S(2)}) %collective-permute-start.13) | collective-permute-done | bytes 131104 | tf_op jit(solution)/shard_map/ppermute | solution.py:92
  52.7 1.6 %collective-permute-start.19 = (bf16[512,256]{1,0:T(8,128)(2,1)S(1)}, bf16[512,256]{1,0:T(8,128)(2,1)S(1)}, u32[]{:S(2)}, u32[]{:S(2)}) collective-permute-start(bf16[512,256]{1,0:T(8,128)(2,1)S(1)} %constant_dynamic-update-slice_fusion), channel_id=1, source_target_pairs={{2,0},{5,1},{0,2},{7,3},{6,4},{1,5},{4,6},{3,7},{10,8},{13,9},{8,1... | collective-permute-start | bytes 786440 | tf_op jit(solution)/shard_map/ppermute | solution.py:92
  57.4 5.4 %collective-permute-done.18.refs_5_ = bf16[256,256]{1,0:T(8,128)(2,1)S(1)} collective-permute-done((bf16[256,256]{1,0:T(8,128)(2,1)S(1)}, bf16[256,256]{1,0:T(8,128)(2,1)S(1)}, u32[]{:S(2)}, u32[]{:S(2)}) %collective-permute-start.18) | collective-permute-done | bytes 131104 | tf_op jit(solution)/shard_map/ppermute | solution.py:92
  64.4 2.1 %experts_in_first.1 = (f32[512,1536]{1,0:T(8,128)S(1)}, f32[512,1]{1,0:T(8,128)S(1)}) custom-call(s32[1]{0:T(128)} %bitcast.ctx_ref, s32[1]{0:T(128)} %bitcast.1.exp_ref, bf16[256,256]{1,0:T(8,128)(2,1)S(1)} %add_convert_fusion.6.refs_0_.refs_6_, bf16[256,256]{1,0:T(8,128)(2,1)S(1)} %collective-permute-done.13.refs_1_.refs_7_, ...), custom_call_target="tpu_custom_call" | custom-call | flops 1610612736 | bytes 8388608 | tf_op jit(solution)/shard_map/experts_in_first/pallas_call | solution.py:750
  66.5 2.7 %collective-permute-done.23.refs_5_ = bf16[256,256]{1,0:T(8,128)(2,1)S(1)} collective-permute-done((bf16[256,256]{1,0:T(8,128)(2,1)S(1)}, bf16[256,256]{1,0:T(8,128)(2,1)S(1)}, u32[]{:S(2)}, u32[]{:S(2)}) %collective-permute-start.23) | collective-permute-done | bytes 131104 | tf_op jit(solution)/shard_map/ppermute | solution.py:92
  70.6 1.4 %experts_in_second.3.refs_5_.act_ref = bf16[256,1664]{1,0:T(8,128)(2,1)S(1)} custom-call(s32[1]{0:T(128)} %bitcast.ctx_ref, s32[1]{0:T(128)} %bitcast.1.exp_ref, bf16[256,256]{1,0:T(8,128)(2,1)S(1)} %collective-permute-done.15.refs_0_.refs_8_, bf16[512,256]{1,0:T(8,128)(2,1)S(1)} %collective-permute-done.19.refs_6_.refs_1_.refs_11_, ...), custom_call_target="tpu_custom_call" | custom-call | flops 805306368 | bytes 8388608 | tf_op jit(solution)/shard_map/experts_in_second/pallas_call | solution.py:768
  72.9 1.8 %experts_out.2 = (f32[32,2048]{1,0:T(8,128)S(1)}, f32[32,2048]{1,0:T(8,128)S(1)}, bf16[32,2048]{1,0:T(8,128)(2,1)S(1)}, bf16[32,2048]{1,0:T(8,128)(2,1)S(1)}, f3...) custom-call(s32[1]{0:T(128)} %bitcast.ctx_ref, ...), custom_call_target="tpu_custom_call" | custom-call | flops 805306368 | bytes 8388608 | tf_op jit(solution)/shard_map/experts_out/pallas_call | solution.py:805
  77.5 1.8 %experts_out.3 = (f32[32,2048]{1,0:T(8,128)S(1)}, bf16[32,2048]{1,0:T(8,128)(2,1)S(1)}, bf16[32,2048]{1,0:T(8,128)(2,1)S(1)}, f32[32,2048]{1,0:T(8,128)S(1)}, f3...) custom-call(s32[1]{0:T(128)} %bitcast.ctx_ref, ...), custom_call_target="tpu_custom_call" | custom-call | flops 805306368 | bytes 8388608 | tf_op jit(solution)/shard_map/experts_out/pallas_call | solution.py:805
  79.3 2.1 %collective-permute-done.27 = bf16[32,2048]{1,0:T(8,128)(2,1)S(1)} collective-permute-done((bf16[32,2048]{1,0:T(8,128)(2,1)S(1)}, bf16[32,2048]{1,0:T(8,128)(2,1)S(1)}, u32[]{:S(2)}, u32[]{:S(2)}) %collective-permute-start.27) | collective-permute-done | bytes 131104 | tf_op jit(solution)/shard_map/ppermute | solution.py:92
  85.6 2.1 %collective-permute-start.30 = (bf16[32,2048]{1,0:T(8,128)(2,1)S(1)}, bf16[32,2048]{1,0:T(8,128)(2,1)S(1)}, u32[]{:S(2)}, u32[]{:S(2)}) collective-permute-start(bf16[32,2048]{1,0:T(8,128)(2,1)S(1)} %add_convert_fusion.5), channel_id=1, source_target_pairs={{16,0},{17,1},{18,2},{19,3},{20,4},{21,5},{22,6},{23,7},{24,8},{25... | collective-permute-start | bytes 393224 | tf_op jit(solution)/shard_map/ppermute | solution.py:92
  88.6 2.1 %collective-permute-done.33 = bf16[32,2048]{1,0:T(8,128)(2,1)S(1)} collective-permute-done((bf16[32,2048]{1,0:T(8,128)(2,1)S(1)}, bf16[32,2048]{1,0:T(8,128)(2,1)S(1)}, u32[]{:S(2)}, u32[]{:S(2)}) %collective-permute-start.33) | collective-permute-done | bytes 131104 | tf_op jit(solution)/shard_map/ppermute | solution.py:92
  92.0 1.8 %collective-permute-done.30 = bf16[32,2048]{1,0:T(8,128)(2,1)S(1)} collective-permute-done((bf16[32,2048]{1,0:T(8,128)(2,1)S(1)}, bf16[32,2048]{1,0:T(8,128)(2,1)S(1)}, u32[]{:S(2)}, u32[]{:S(2)}) %collective-permute-start.30) | collective-permute-done | bytes 131104 | tf_op jit(solution)/shard_map/ppermute | solution.py:92
  95.4 2.8 %collective-permute-start.36 = (bf16[32,2048]{1,0:T(8,128)(2,1)S(1)}, bf16[32,2048]{1,0:T(8,128)(2,1)S(1)}, u32[]{:S(2)}, u32[]{:S(2)}) collective-permute-start(bf16[32,2048]{1,0:T(8,128)(2,1)S(1)} %get-tuple-element.140), channel_id=1, source_target_pairs={{8,0},{9,1},{10,2},{11,3},{12,4},{13,5},{14,6},{15,7},{0,8},{1,9},... | collective-permute-start | bytes 393224 | tf_op jit(solution)/shard_map/ppermute | solution.py:92
  98.2 1.6 %collective-permute-done.35 = bf16[32,2048]{1,0:T(8,128)(2,1)S(1)} collective-permute-done((bf16[32,2048]{1,0:T(8,128)(2,1)S(1)}, bf16[32,2048]{1,0:T(8,128)(2,1)S(1)}, u32[]{:S(2)}, u32[]{:S(2)}) %collective-permute-start.35) | collective-permute-done | bytes 131104 | tf_op jit(solution)/shard_map/ppermute | solution.py:92
  99.8 2.7 %collective-permute-done.34 = bf16[32,2048]{1,0:T(8,128)(2,1)S(1)} collective-permute-done((bf16[32,2048]{1,0:T(8,128)(2,1)S(1)}, bf16[32,2048]{1,0:T(8,128)(2,1)S(1)}, u32[]{:S(2)}, u32[]{:S(2)}) %collective-permute-start.34) | collective-permute-done | bytes 131104 | tf_op jit(solution)/shard_map/ppermute | solution.py:92
  (93 shorter events, 28.5 us)
Async XLA Ops:
  1.2 13.8 %collective-permute-start = (bf16[64,1280]{1,0:T(8,128)(2,1)S(1)}, bf16[64,1280]{1,0:T(8,128)(2,1)S(1)}, u32[]{:S(2)}, u32[]{:S(2)}) collective-permute-start(bf16[64,1280]{1,0:T(8,128)(2,1)S(1)} %get-tuple-element.72._.refs_0_), channel_id=1, source_target_pairs={{16,0},{17,1},{18,2},{19,3},{20,4},{21,5},{22,6},{23,7},{24,8},{25... | collective-permute-start | bytes 491528 | tf_op jit(solution)/shard_map/ppermute | solution.py:92
  5.3 9.7 %collective-permute-start.1 = (bf16[64,1280]{1,0:T(8,128)(2,1)S(1)}, bf16[64,1280]{1,0:T(8,128)(2,1)S(1)}, u32[]{:S(2)}, u32[]{:S(2)}) collective-permute-start(bf16[64,1280]{1,0:T(8,128)(2,1)S(1)} %get-tuple-element.72._.refs_0_), channel_id=1, source_target_pairs={{4,0},{9,1},{6,2},{11,3},{0,4},{13,5},{2,6},{15,7},{12,8},{1,9},{1... | collective-permute-start | bytes 491528 | tf_op jit(solution)/shard_map/ppermute | solution.py:92
  6.8 8.2 %collective-permute-start.2 = (bf16[64,1280]{1,0:T(8,128)(2,1)S(1)}, bf16[64,1280]{1,0:T(8,128)(2,1)S(1)}, u32[]{:S(2)}, u32[]{:S(2)}) collective-permute-start(bf16[64,1280]{1,0:T(8,128)(2,1)S(1)} %get-tuple-element.72._.refs_0_), channel_id=1, source_target_pairs={{8,0},{5,1},{10,2},{7,3},{12,4},{1,5},{14,6},{3,7},{0,8},{13,9},{2... | collective-permute-start | bytes 491528 | tf_op jit(solution)/shard_map/ppermute | solution.py:92
  8.4 6.6 %collective-permute-start.3 = (bf16[4,16,640]{2,1,0:T(8,128)(2,1)S(1)}, bf16[4,16,640]{2,1,0:T(8,128)(2,1)S(1)}, u32[]{:S(2)}, u32[]{:S(2)}) collective-permute-start(bf16[4,16,640]{2,1,0:T(8,128)(2,1)S(1)} %get-tuple-element.73), channel_id=1, source_target_pairs={{8,0},{5,1},{10,2},{7,3},{12,4},{1,5},{14,6},{3,7},{0,8},{13,9},{2... | collective-permute-start | bytes 245768 | tf_op jit(solution)/shard_map/ppermute | solution.py:92
  15.0 9.3 %collective-permute-start.7 = (bf16[2048,768]{1,0:T(8,128)(2,1)S(1)}, bf16[2048,768]{1,0:T(8,128)(2,1)S(1)}, u32[]{:S(2)}, u32[]{:S(2)}) collective-permute-start(bf16[2048,768]{1,0:T(8,128)(2,1)S(1)} %get-tuple-element.81), channel_id=1, source_target_pairs={{0,1},{1,0},{2,3},{3,2},{4,5},{5,4},{6,7},{7,6},{8,9},{9,8},{10,11... | collective-permute-start | bytes 9437192 | tf_op jit(solution)/shard_map/ppermute | solution.py:25
  15.0 9.2 %collective-permute-start.5 = (bf16[64,1280]{1,0:T(8,128)(2,1)S(1)}, bf16[64,1280]{1,0:T(8,128)(2,1)S(1)}, u32[]{:S(2)}, u32[]{:S(2)}) collective-permute-start(bf16[64,1280]{1,0:T(8,128)(2,1)S(1)} %collective-permute-done.refs_1_), channel_id=1, source_target_pairs={{8,0},{5,1},{10,2},{7,3},{12,4},{1,5},{14,6},{3,7},{0,8},{13,9},{2... | collective-permute-start | bytes 491528 | tf_op jit(solution)/shard_map/ppermute | solution.py:92
  15.8 8.4 %collective-permute-start.4 = (bf16[128,1280]{1,0:T(8,128)(2,1)S(1)}, bf16[128,1280]{1,0:T(8,128)(2,1)S(1)}, u32[]{:S(2)}, u32[]{:S(2)}) collective-permute-start(bf16[128,1280]{1,0:T(8,128)(2,1)S(1)} %pad_maximum_fusion), channel_id=1, source_target_pairs={{4,0},{9,1},{6,2},{11,3},{0,4},{13,5},{2,6},{15,7},{12,8},{1,9},{1... | collective-permute-start | bytes 983048 | tf_op jit(solution)/shard_map/ppermute | solution.py:92
  17.4 6.8 %collective-permute-start.6 = (bf16[4,16,640]{2,1,0:T(8,128)(2,1)S(1)}, bf16[4,16,640]{2,1,0:T(8,128)(2,1)S(1)}, u32[]{:S(2)}, u32[]{:S(2)}) collective-permute-start(bf16[4,16,640]{2,1,0:T(8,128)(2,1)S(1)} %pad_maximum_fusion.6), channel_id=1, source_target_pairs={{4,0},{9,1},{6,2},{11,3},{0,4},{13,5},{2,6},{15,7},{12,8},{1,9},{1... | collective-permute-start | bytes 245768 | tf_op jit(solution)/shard_map/ppermute | solution.py:92
  24.3 5.8 %collective-permute-start.9 = (bf16[384,2048]{1,0:T(8,128)(2,1)S(1)}, bf16[384,2048]{1,0:T(8,128)(2,1)S(1)}, u32[]{:S(2)}, u32[]{:S(2)}) collective-permute-start(bf16[384,2048]{1,0:T(8,128)(2,1)S(1)} %get-tuple-element.86), channel_id=1, source_target_pairs={{0,1},{1,0},{2,3},{3,2},{4,5},{5,4},{6,7},{7,6},{8,9},{9,8},{10,11... | collective-permute-start | bytes 4718600 | tf_op jit(solution)/shard_map/ppermute | solution.py:25
  25.7 8.7 %collective-permute-start.10 = (bf16[4,16,640]{2,1,0:T(8,128)(2,1)S(1)}, bf16[4,16,640]{2,1,0:T(8,128)(2,1)S(1)}, u32[]{:S(2)}, u32[]{:S(2)}) collective-permute-start(bf16[4,16,640]{2,1,0:T(8,128)(2,1)S(1)} %pad_maximum_fusion.7), channel_id=1, source_target_pairs={{16,0},{17,1},{18,2},{19,3},{20,4},{21,5},{22,6},{23,7},{24,8},{25... | collective-permute-start | bytes 245768 | tf_op jit(solution)/shard_map/ppermute | solution.py:92
  36.3 6.0 %collective-permute-start.12 = (bf16[288,256]{1,0:T(8,128)(2,1)S(1)}, bf16[288,256]{1,0:T(8,128)(2,1)S(1)}, u32[]{:S(2)}, u32[]{:S(2)}) collective-permute-start(bf16[288,256]{1,0:T(8,128)(2,1)S(1)} %pad_maximum_fusion.5), channel_id=1, source_target_pairs={{0,2},{1,3},{2,0},{3,1},{4,6},{5,7},{6,4},{7,5},{8,10},{9,11},{10,... | collective-permute-start | bytes 442376 | tf_op jit(solution)/shard_map/ppermute | solution.py:25
  42.3 8.5 %collective-permute-start.13 = (bf16[256,256]{1,0:T(8,128)(2,1)S(1)}, bf16[256,256]{1,0:T(8,128)(2,1)S(1)}, u32[]{:S(2)}, u32[]{:S(2)}) collective-permute-start(bf16[256,256]{1,0:T(8,128)(2,1)S(1)} %add_convert_fusion.6.refs_0_.refs_6_), channel_id=1, source_target_pairs={{16,0},{17,1},{18,2},{19,3},{20,4},{21,5},{22,6},{23,7},{24,8},{25... | collective-permute-start | bytes 393224 | tf_op jit(solution)/shard_map/ppermute | solution.py:92
  44.3 6.7 %collective-permute-start.14 = (bf16[256,256]{1,0:T(8,128)(2,1)S(1)}, bf16[256,256]{1,0:T(8,128)(2,1)S(1)}, u32[]{:S(2)}, u32[]{:S(2)}) collective-permute-start(bf16[256,256]{1,0:T(8,128)(2,1)S(1)} %add_convert_fusion.6.refs_0_.refs_6_), channel_id=1, source_target_pairs={{6,0},{7,1},{4,2},{5,3},{2,4},{3,5},{0,6},{1,7},{14,8},{15,9},{12,... | collective-permute-start | bytes 393224 | tf_op jit(solution)/shard_map/ppermute | solution.py:92
  45.7 6.6 %collective-permute-start.15 = (bf16[256,256]{1,0:T(8,128)(2,1)S(1)}, bf16[256,256]{1,0:T(8,128)(2,1)S(1)}, u32[]{:S(2)}, u32[]{:S(2)}) collective-permute-start(bf16[256,256]{1,0:T(8,128)(2,1)S(1)} %add_convert_fusion.6.refs_0_.refs_6_), channel_id=1, source_target_pairs={{8,0},{9,1},{10,2},{11,3},{12,4},{13,5},{14,6},{15,7},{0,8},{1,9},... | collective-permute-start | bytes 393224 | tf_op jit(solution)/shard_map/ppermute | solution.py:92
  52.7 10.1 %collective-permute-start.19 = (bf16[512,256]{1,0:T(8,128)(2,1)S(1)}, bf16[512,256]{1,0:T(8,128)(2,1)S(1)}, u32[]{:S(2)}, u32[]{:S(2)}) collective-permute-start(bf16[512,256]{1,0:T(8,128)(2,1)S(1)} %constant_dynamic-update-slice_fusion), channel_id=1, source_target_pairs={{2,0},{5,1},{0,2},{7,3},{6,4},{1,5},{4,6},{3,7},{10,8},{13,9},{8,1... | collective-permute-start | bytes 786440 | tf_op jit(solution)/shard_map/ppermute | solution.py:92
  54.2 8.6 %collective-permute-start.20 = (bf16[512,256]{1,0:T(8,128)(2,1)S(1)}, bf16[512,256]{1,0:T(8,128)(2,1)S(1)}, u32[]{:S(2)}, u32[]{:S(2)}) collective-permute-start(bf16[512,256]{1,0:T(8,128)(2,1)S(1)} %constant_dynamic-update-slice_fusion), channel_id=1, source_target_pairs={{4,0},{3,1},{6,2},{1,3},{0,4},{7,5},{2,6},{5,7},{12,8},{11,9},{14,... | collective-permute-start | bytes 786440 | tf_op jit(solution)/shard_map/ppermute | solution.py:92
  55.5 7.3 %collective-permute-start.18 = (bf16[256,256]{1,0:T(8,128)(2,1)S(1)}, bf16[256,256]{1,0:T(8,128)(2,1)S(1)}, u32[]{:S(2)}, u32[]{:S(2)}) collective-permute-start(bf16[256,256]{1,0:T(8,128)(2,1)S(1)} %collective-permute-done.14.refs_2_), channel_id=1, source_target_pairs={{16,0},{17,1},{18,2},{19,3},{20,4},{21,5},{22,6},{23,7},{24,8},{25... | collective-permute-start | bytes 393224 | tf_op jit(solution)/shard_map/ppermute | solution.py:92
  56.0 6.8 %collective-permute-start.21 = (bf16[256,256]{1,0:T(8,128)(2,1)S(1)}, bf16[256,256]{1,0:T(8,128)(2,1)S(1)}, u32[]{:S(2)}, u32[]{:S(2)}) collective-permute-start(bf16[256,256]{1,0:T(8,128)(2,1)S(1)} %collective-permute-done.13.refs_1_.refs_7_), channel_id=1, source_target_pairs={{8,0},{9,1},{10,2},{11,3},{12,4},{13,5},{14,6},{15,7},{0,8},{1,9},... | collective-permute-start | bytes 393224 | tf_op jit(solution)/shard_map/ppermute | solution.py:92
  62.9 6.4 %collective-permute-start.22 = (bf16[512,256]{1,0:T(8,128)(2,1)S(1)}, bf16[512,256]{1,0:T(8,128)(2,1)S(1)}, u32[]{:S(2)}, u32[]{:S(2)}) collective-permute-start(bf16[512,256]{1,0:T(8,128)(2,1)S(1)} %pad_maximum_fusion.1), channel_id=1, source_target_pairs={{4,0},{3,1},{6,2},{1,3},{0,4},{7,5},{2,6},{5,7},{12,8},{11,9},{14,... | collective-permute-start | bytes 786440 | tf_op jit(solution)/shard_map/ppermute | solution.py:92
  63.7 5.5 %collective-permute-start.24 = (bf16[256,256]{1,0:T(8,128)(2,1)S(1)}, bf16[256,256]{1,0:T(8,128)(2,1)S(1)}, u32[]{:S(2)}, u32[]{:S(2)}) collective-permute-start(bf16[256,256]{1,0:T(8,128)(2,1)S(1)} %collective-permute-done.21.refs_3_.refs_13_), channel_id=1, source_target_pairs={{2,0},{5,1},{0,2},{7,3},{6,4},{1,5},{4,6},{3,7},{10,8},{13,9},{8,1... | collective-permute-start | bytes 393224 | tf_op jit(solution)/shard_map/ppermute | solution.py:92
  72.0 5.5 %collective-permute-start.29 = (bf16[256,1664]{1,0:T(8,128)(2,1)S(1)}, bf16[256,1664]{1,0:T(8,128)(2,1)S(1)}, u32[]{:S(2)}, u32[]{:S(2)}) collective-permute-start(bf16[256,1664]{1,0:T(8,128)(2,1)S(1)} %experts_in_second.3.refs_5_.act_ref), channel_id=1, source_target_pairs={{0,1},{1,0},{2,3},{3,2},{4,5},{5,4},{6,7},{7,6},{8,9},{9,8},{10,11... | collective-permute-start | bytes 2555912 | tf_op jit(solution)/shard_map/ppermute | solution.py:25
  74.8 7.8 %collective-permute-start.26 = (bf16[64,2048]{1,0:T(8,128)(2,1)S(1)}, bf16[64,2048]{1,0:T(8,128)(2,1)S(1)}, u32[]{:S(2)}, u32[]{:S(2)}) collective-permute-start(bf16[64,2048]{1,0:T(8,128)(2,1)S(1)} %pad_maximum_fusion.2), channel_id=1, source_target_pairs={{4,0},{3,1},{6,2},{1,3},{0,4},{7,5},{2,6},{5,7},{12,8},{11,9},{14,... | collective-permute-start | bytes 786440 | tf_op jit(solution)/shard_map/ppermute | solution.py:92
  76.3 5.5 %collective-permute-start.28 = (bf16[32,2048]{1,0:T(8,128)(2,1)S(1)}, bf16[32,2048]{1,0:T(8,128)(2,1)S(1)}, u32[]{:S(2)}, u32[]{:S(2)}) collective-permute-start(bf16[32,2048]{1,0:T(8,128)(2,1)S(1)} %get-tuple-element.111), channel_id=1, source_target_pairs={{2,0},{5,1},{0,2},{7,3},{6,4},{1,5},{4,6},{3,7},{10,8},{13,9},{8,1... | collective-permute-start | bytes 393224 | tf_op jit(solution)/shard_map/ppermute | solution.py:92
  82.7 11.2 %collective-permute-start.32 = (bf16[64,2048]{1,0:T(8,128)(2,1)S(1)}, bf16[64,2048]{1,0:T(8,128)(2,1)S(1)}, u32[]{:S(2)}, u32[]{:S(2)}) collective-permute-start(bf16[64,2048]{1,0:T(8,128)(2,1)S(1)} %pad_maximum_fusion.4), channel_id=1, source_target_pairs={{4,0},{3,1},{6,2},{1,3},{0,4},{7,5},{2,6},{5,7},{12,8},{11,9},{14,... | collective-permute-start | bytes 786440 | tf_op jit(solution)/shard_map/ppermute | solution.py:92
  84.0 9.8 %collective-permute-start.31 = (bf16[64,2048]{1,0:T(8,128)(2,1)S(1)}, bf16[64,2048]{1,0:T(8,128)(2,1)S(1)}, u32[]{:S(2)}, u32[]{:S(2)}) collective-permute-start(bf16[64,2048]{1,0:T(8,128)(2,1)S(1)} %pad_maximum_fusion.3), channel_id=1, source_target_pairs={{2,0},{5,1},{0,2},{7,3},{6,4},{1,5},{4,6},{3,7},{10,8},{13,9},{8,1... | collective-permute-start | bytes 786440 | tf_op jit(solution)/shard_map/ppermute | solution.py:92
  85.0 5.8 %collective-permute-start.33 = (bf16[32,2048]{1,0:T(8,128)(2,1)S(1)}, bf16[32,2048]{1,0:T(8,128)(2,1)S(1)}, u32[]{:S(2)}, u32[]{:S(2)}) collective-permute-start(bf16[32,2048]{1,0:T(8,128)(2,1)S(1)} %get-tuple-element.141), channel_id=1, source_target_pairs={{8,0},{9,1},{10,2},{11,3},{12,4},{13,5},{14,6},{15,7},{0,8},{1,9},... | collective-permute-start | bytes 393224 | tf_op jit(solution)/shard_map/ppermute | solution.py:92
  85.6 8.2 %collective-permute-start.30 = (bf16[32,2048]{1,0:T(8,128)(2,1)S(1)}, bf16[32,2048]{1,0:T(8,128)(2,1)S(1)}, u32[]{:S(2)}, u32[]{:S(2)}) collective-permute-start(bf16[32,2048]{1,0:T(8,128)(2,1)S(1)} %add_convert_fusion.5), channel_id=1, source_target_pairs={{16,0},{17,1},{18,2},{19,3},{20,4},{21,5},{22,6},{23,7},{24,8},{25... | collective-permute-start | bytes 393224 | tf_op jit(solution)/shard_map/ppermute | solution.py:92
  87.7 10.5 %collective-permute-start.37 = (bf16[32,2048]{1,0:T(8,128)(2,1)S(1)}, bf16[32,2048]{1,0:T(8,128)(2,1)S(1)}, u32[]{:S(2)}, u32[]{:S(2)}) collective-permute-start(bf16[32,2048]{1,0:T(8,128)(2,1)S(1)} %get-tuple-element.137), channel_id=1, source_target_pairs={{2,0},{5,1},{0,2},{7,3},{6,4},{1,5},{4,6},{3,7},{10,8},{13,9},{8,1... | collective-permute-start | bytes 393224 | tf_op jit(solution)/shard_map/ppermute | solution.py:92
  90.8 7.4 %collective-permute-start.38 = (bf16[32,2048]{1,0:T(8,128)(2,1)S(1)}, bf16[32,2048]{1,0:T(8,128)(2,1)S(1)}, u32[]{:S(2)}, u32[]{:S(2)}) collective-permute-start(bf16[32,2048]{1,0:T(8,128)(2,1)S(1)} %get-tuple-element.138), channel_id=1, source_target_pairs={{4,0},{3,1},{6,2},{1,3},{0,4},{7,5},{2,6},{5,7},{12,8},{11,9},{14,... | collective-permute-start | bytes 393224 | tf_op jit(solution)/shard_map/ppermute | solution.py:92
  93.9 5.9 %collective-permute-start.35 = (bf16[32,2048]{1,0:T(8,128)(2,1)S(1)}, bf16[32,2048]{1,0:T(8,128)(2,1)S(1)}, u32[]{:S(2)}, u32[]{:S(2)}) collective-permute-start(bf16[32,2048]{1,0:T(8,128)(2,1)S(1)} %add_convert_fusion.1), channel_id=1, source_target_pairs={{6,0},{7,1},{4,2},{5,3},{2,4},{3,5},{0,6},{1,7},{14,8},{15,9},{12,... | collective-permute-start | bytes 393224 | tf_op jit(solution)/shard_map/ppermute | solution.py:92
  95.1 7.4 %collective-permute-start.34 = (bf16[32,2048]{1,0:T(8,128)(2,1)S(1)}, bf16[32,2048]{1,0:T(8,128)(2,1)S(1)}, u32[]{:S(2)}, u32[]{:S(2)}) collective-permute-start(bf16[32,2048]{1,0:T(8,128)(2,1)S(1)} %get-tuple-element.139), channel_id=1, source_target_pairs={{16,0},{17,1},{18,2},{19,3},{20,4},{21,5},{22,6},{23,7},{24,8},{25... | collective-permute-start | bytes 393224 | tf_op jit(solution)/shard_map/ppermute | solution.py:92
  95.4 7.1 %collective-permute-start.36 = (bf16[32,2048]{1,0:T(8,128)(2,1)S(1)}, bf16[32,2048]{1,0:T(8,128)(2,1)S(1)}, u32[]{:S(2)}, u32[]{:S(2)}) collective-permute-start(bf16[32,2048]{1,0:T(8,128)(2,1)S(1)} %get-tuple-element.140), channel_id=1, source_target_pairs={{8,0},{9,1},{10,2},{11,3},{12,4},{13,5},{14,6},{15,7},{0,8},{1,9},... | collective-permute-start | bytes 393224 | tf_op jit(solution)/shard_map/ppermute | solution.py:92
  (11 other events, 97.7 us)

commit v10 on v9

--- a/solution.py
+++ b/solution.py
@@ -149,7 +149,7 @@
                 parts = [arrays[at[key][0]][at[key][1] : at[key][1] + rows] for key in group]
                 joined[group] = jnp.concatenate(parts, axis=0)
             came.append(follow(joined[group], moves))
-        came = beside(number, came) if beside else (together(*came) if number < len(stages) - 1 else came)
+        came = beside(number, came, arrays, at) if beside else (together(*came) if number < len(stages) - 1 else came)
         for (_, _, targets), array in zip(sends, came):
             at.update({key: (len(arrays), place * rows) for place, key in enumerate(targets)})
             arrays.append(array)
@@ -336,24 +336,30 @@
 
 
 def attend_kernel(plan, ctx_ref, exp_ref, order_ref, *refs):
-    ctx_count, exp_count, tok, heads, attend_at = plan
+    ctx_count, exp_count, tok, heads, attend_at, slots, kv_apart, more, final = plan
     packed_at, places_of = [at for at, _ in attend_at], [place for _, place in attend_at]
-    array_count = 1 + max(array for array, _ in packed_at)
+    array_count = 1 + max(at[0] for at in packed_at if at)
     span = exp_count * tok
     packed_refs, refs = refs[:array_count], refs[array_count:]
-    packed = []
-    for array, row in packed_at:
-        packed.append(packed_refs[array].at[pl.ds(row, span)])
-    weight_ref, rest = refs[0], refs[2:]
+    packed = [packed_refs[at[0]].at[pl.ds(at[1], span)] if at else None for at in packed_at]
+    kv_refs = list(packed)
+    if kv_apart:
+        kv_refs[packed_at.index(None)], refs = refs[0], refs[1:]
+    if more:
+        more_ref, refs = refs[0], refs[1:]
     x_count = exp_count // 2
-    keep_refs, give_ref = rest[:x_count], rest[x_count]
-    key_scr, value_scr, place_scr, att_scr = rest[x_count + 1 :]
+    if final:
+        weight_ref, rest = refs[0], refs[2:]
+        keep_refs, give_ref = rest[:x_count], rest[x_count]
+    key_scr, value_scr, place_scr, att_ref = refs[-4:] if final else (*refs[1:], refs[0])
+    if more:
+        att_ref[...] = more_ref[...]
     positions = ctx_count * span
     my_ctx, my_exp = ctx_ref[0], exp_ref[0]
     my_x, my_core = lax.shift_right_logical(my_exp, 1), lax.bitwise_and(my_exp, 1)
     lane = lax.broadcasted_iota(jnp.int32, (8, positions), 1)
     places = lane % span
-    for offset, ref in enumerate(packed):
+    for offset, ref in enumerate(kv_refs):
         key_scr[pl.ds(offset * span, span), :] = ref[:, 0:HEAD_SIZE]
         value_scr[pl.ds(offset * span, span), 0:HEAD_SIZE] = ref[:, HEAD_SIZE : 2 * HEAD_SIZE]
         base = order_ref[lax.bitwise_xor(my_ctx, by_core(my_core, places_of[offset], 0))] * span
@@ -361,7 +367,8 @@
     place_scr[...] = places
     scale = math.log2(math.e) / math.sqrt(HEAD_SIZE)
     value_scr[:, HEAD_SIZE:] = jnp.ones((positions, HEAD_SIZE), jnp.bfloat16)
-    for offset, ref in enumerate(packed):
+    for offset in slots:
+        ref = packed[offset]
         source = lax.bitwise_xor(my_ctx, by_core(my_core, places_of[offset], 0))
         queries = jnp.concatenate(
             [ref[:, (h + 2) * HEAD_SIZE : (h + 3) * HEAD_SIZE] for h in range(heads)], axis=0
@@ -384,10 +391,12 @@
             x_off = lax.bitwise_xor(my_x, owner // 2)
             row = pl.multiple_of(((x_off * ctx_count + source) * 2 + owner % 2) * tok, tok)
             for head in range(heads):
-                att_scr[pl.ds(row, tok), pl.ds(head * HEAD_SIZE, HEAD_SIZE)] = mixed[
+                att_ref[pl.ds(row, tok), pl.ds(head * HEAD_SIZE, HEAD_SIZE)] = mixed[
                     head, owner * tok : (owner + 1) * tok, :
                 ]
 
+    if not final:
+        return
     cols = weight_ref.shape[1] // 2
     per_x = 2 * ctx_count * tok
     for x_off in range(x_count):
@@ -395,7 +404,7 @@
         for which in (1, 0):
             side = lax.bitwise_xor(my_core, which)
             weight = weight_ref[:, pl.ds(pl.multiple_of(side * cols, cols), cols)]
-            part = jnp.dot(att_scr[rows, :], weight, preferred_element_type=jnp.float32)
+            part = jnp.dot(att_ref[rows, :], weight, preferred_element_type=jnp.float32)
             out_ref = give_ref if which else keep_refs[x_off]
             out_ref[pl.ds(x_off * per_x if which else 0, per_x), :] = part.astype(out_ref.dtype)
 
@@ -646,8 +655,9 @@
     piece_at = {(0, key[0]): (0, place) for place, key in enumerate(piece_names[0])}
     piece_bits = [1, 0, *range(bits_of(ctx_count) - 1, 1, -1)]
     sending, weights = far, {}
-
-    def beside(number, came):
+    early, last_kv = ctx_count == 8, []
+
+    def beside(number, came, arrays, at):
         nonlocal sending
         bit = 1 << piece_bits[number]
         moves = {1: ((2, 0), (1, 0)), 0: ((1, 0), (2, 0))}.get(piece_bits[number], ((bit, 0),) * 2)
@@ -663,9 +673,13 @@
         elif number == 1:
             other = from_offset(weights["in_give"], 1)
             own, give = deq_down(my_exp, down_weight, down_scale, ctx_count, piece_arrays[-1])
-            *came, pieces, weights["in_other"], weights["down_own"], weights["down_give"] = together(
-                *came, pieces, other, own, give
-            )
+            if early:
+                array, row = at[4, 0]
+                last_kv.append(follow(arrays[array][row : row + span, : 2 * HEAD_SIZE], ((3, 0),) * 2))
+            held = together(*came, pieces, other, own, give, *last_kv)
+            *came, pieces, other, own, give = held[: len(held) - len(last_kv)]
+            last_kv[:] = held[len(held) - len(last_kv) :]
+            weights.update(in_other=other, down_own=own, down_give=give)
         elif number < len(piece_bits) - 1:
             *came, pieces = together(*came, pieces)
         for place, (source, target) in enumerate(keys):
@@ -681,26 +695,46 @@
 
     positions = ctx_count * span
     per_x = 2 * ctx_count * tok
-    *keeps, give = pl.pallas_call(
-        functools.partial(attend_kernel, (ctx_count, exp_count, tok, heads, attend_at)),
-        in_specs=[smem] * 3 + [vmem] * (len(packed) + 1) + [anywhere],
-        out_specs=[vmem] * (1 + x_count),
-        out_shape=[jax.ShapeDtypeStruct((per_x, cols), f32)] * x_count
-        + [jax.ShapeDtypeStruct((x_count * per_x, cols), bf16)],
-        scratch_shapes=[
+    def attend(arrays, at, slots, kv, more, final):
+        scratch = [
             pltpu.VMEM((positions, HEAD_SIZE), bf16),
             pltpu.VMEM((positions, 2 * HEAD_SIZE), bf16),
             pltpu.VMEM((8, positions), jnp.int32),
-            pltpu.VMEM((positions, query_width), bf16),
-        ],
-        compiler_params=pltpu.CompilerParams(vmem_limit_bytes=3 * ctx_count * MIB),
-        cost_estimate=pl.CostEstimate(
-            flops=4 * positions * positions * query_width + 4 * positions * query_width * cols,
-            bytes_accessed=8 * MIB,
-            transcendentals=heads * positions * positions,
-        ),
-        name="attend",
-    )(my_ctx, my_exp, block_order, *packed, out_weight, down_other)
+        ]
+        rows_shape = (positions, query_width)
+        out_shape = [jax.ShapeDtypeStruct(rows_shape, bf16)]
+        if final:
+            out_shape = [jax.ShapeDtypeStruct((per_x, cols), f32)] * x_count
+            out_shape += [jax.ShapeDtypeStruct((x_count * per_x, cols), bf16)]
+            scratch.append(pltpu.VMEM(rows_shape, bf16))
+        operands = [*arrays, *kv, *more, *([out_weight] if final else [])]
+        return pl.pallas_call(
+            functools.partial(
+                attend_kernel,
+                (ctx_count, exp_count, tok, heads, at, slots, bool(kv), bool(more), final),
+            ),
+            in_specs=[smem] * 3 + [vmem] * len(operands) + [anywhere] * final,
+            out_specs=[vmem] * len(out_shape),
+            out_shape=out_shape,
+            scratch_shapes=scratch,
+            compiler_params=pltpu.CompilerParams(vmem_limit_bytes=3 * ctx_count * MIB),
+            cost_estimate=pl.CostEstimate(
+                flops=4 * positions * len(slots) * span * query_width
+                + 4 * positions * query_width * cols * final,
+                bytes_accessed=4 * MIB,
+                transcendentals=heads * positions * len(slots) * span,
+            ),
+            name="attend",
+        )(my_ctx, my_exp, block_order, *operands, *([down_other] if final else []))
+
+    more, slots = [], tuple(range(ctx_count))
+    if early:
+        late = max(packed_at[key][0] for key in names)
+        early_at = tuple((None if at[0] == late else at, place) for at, place in attend_at)
+        slots = tuple(i for i, (at, _) in enumerate(early_at) if at is None)
+        rest = tuple(i for i, (at, _) in enumerate(early_at) if at is not None)
+        more = attend(packed[:late], early_at, rest, last_kv, [], False)
+    *keeps, give = attend(packed, attend_at, slots, [], more, True)
     keeps[0], give, own_route = pl.pallas_call(
         functools.partial(
             finish_kernel,

time: 105 us -> 104 us (level)
  waiting for transfers between devices: 40.9 us -> 37 us
  starting transfers between devices: 43 us -> 45.2 us
  Pallas kernels: 19 us -> 20.2 us
    ppermute x33 -> x34, waiting for transfers between devices: 33.5 us -> 29.5 us  [follow(): return lax.ppermute(array, ('ctx', 'exp'), pairs)]
    ppermute x33 -> x34, starting transfers between devices: 40 us -> 41.6 us  [follow(): return lax.ppermute(array, ('ctx', 'exp'), pairs)]
    pallas_call x1 -> x2, Pallas kernels: 4.33 us -> 5.34 us  [attend(): pl.pallas_call(functools.partial(attend_kernel, (ctx_count, exp_count, to...]
  transfers between devices with their start and end apart: 40 -> 41, of which waited for: 21 -> 24; matrix products, arithmetic and copies ran while one was open for 0% -> 0% of each run, Pallas kernels for 16% -> 17%
where the time goes in v10:
time: 104 us
  starting transfers between devices  45.2 us (43%)
  waiting for transfers between devices  37 us (36%)
  Pallas kernels  20.2 us (19%)
    ppermute x34, starting transfers between devices, follow(): return lax.ppermute(array, ('ctx', 'exp'), pairs)  41.6 us
    ppermute x34, waiting for transfers between devices, follow(): return lax.ppermute(array, ('ctx', 'exp'), pairs)  29.5 us
    ppermute x7, waiting for transfers between devices, from_offset(): lax.ppermute(array, 'exp', [(i, i ^ offset) for i in range(lax.axis_size(...  7.52 us
    pallas_call x2, Pallas kernels, attend(): pl.pallas_call(functools.partial(attend_kernel, (ctx_count, exp_count, to...  5.34 us
    pallas_call x2, Pallas kernels, shards(): pl.pallas_call(functools.partial(experts_out_kernel, (ctx_count, exp_coun...  3.63 us
    ppermute x7, starting transfers between devices, from_offset(): lax.ppermute(array, 'exp', [(i, i ^ offset) for i in range(lax.axis_size(...  3.61 us
    pallas_call x1, Pallas kernels, deq_in(): pl.pallas_call(functools.partial(deq_in_kernel, ctx_count), in_specs=[pl....  3 us
    pallas_call x2, Pallas kernels, shards(): pl.pallas_call(functools.partial(experts_in_second, (ctx_count, x_count,...  2.59 us
  transfers between devices with their start and end apart: 41, of which 24 were waited for; matrix products, arithmetic and copies ran while one was open for 0% of the time, Pallas kernels for 17%

profile of v10, /device:TPU:0, one launch (start us, length us, event | category | flops | bytes accessed | tf_op | source)
XLA Modules:
  0.0 104.2 jit_solution(15561907490557073280)
XLA Ops:
  1.2 4.1 %collective-permute-start = (bf16[64,1280]{1,0:T(8,128)(2,1)S(1)}, bf16[64,1280]{1,0:T(8,128)(2,1)S(1)}, u32[]{:S(2)}, u32[]{:S(2)}) collective-permute-start(bf16[64,1280]{1,0:T(8,128)(2,1)S(1)} %get-tuple-element.73._.refs_0_), channel_id=1, source_target_pairs={{16,0},{17,1},{18,2},{19,3},{20,4},{21,5},{22,6},{23,7},{24,8},{25... | collective-permute-start | bytes 491528 | tf_op jit(solution)/shard_map/ppermute | solution.py:92
  5.3 1.5 %collective-permute-start.1 = (bf16[64,1280]{1,0:T(8,128)(2,1)S(1)}, bf16[64,1280]{1,0:T(8,128)(2,1)S(1)}, u32[]{:S(2)}, u32[]{:S(2)}) collective-permute-start(bf16[64,1280]{1,0:T(8,128)(2,1)S(1)} %get-tuple-element.73._.refs_0_), channel_id=1, source_target_pairs={{4,0},{9,1},{6,2},{11,3},{0,4},{13,5},{2,6},{15,7},{12,8},{1,9},{1... | collective-permute-start | bytes 491528 | tf_op jit(solution)/shard_map/ppermute | solution.py:92
  6.8 1.6 %collective-permute-start.2 = (bf16[64,1280]{1,0:T(8,128)(2,1)S(1)}, bf16[64,1280]{1,0:T(8,128)(2,1)S(1)}, u32[]{:S(2)}, u32[]{:S(2)}) collective-permute-start(bf16[64,1280]{1,0:T(8,128)(2,1)S(1)} %get-tuple-element.73._.refs_0_), channel_id=1, source_target_pairs={{8,0},{5,1},{10,2},{7,3},{12,4},{1,5},{14,6},{3,7},{0,8},{13,9},{2... | collective-permute-start | bytes 491528 | tf_op jit(solution)/shard_map/ppermute | solution.py:92
  8.8 3.0 %dequant_in.1 = (bf16[2048,768]{1,0:T(8,128)(2,1)S(1)}, bf16[2048,768]{1,0:T(8,128)(2,1)S(1)}) custom-call(s32[1]{0:T(128)} %bitcast.1.exp_ref, s32[3,1,32]{2,1,0:T(1,128)} %bitcast.25, s32[3,1,32]{2,1,0:T(1,128)} %bitcast.26, bf16[1,4096,384]{2,1,0:T(8,128)(2,1)} %gate_hbm.1, bf16[1,4096,384]{2,1,0:T(8,128)(2,1)} %up_hbm.1, ...), custom_call_target="tpu_custom_call" | custom-call | flops 3145728 | bytes 12582912 | tf_op jit(solution)/shard_map/dequant_in/pallas_call | solution.py:269
  11.8 3.1 %collective-permute-done.3._.refs_1_ = bf16[4,16,640]{2,1,0:T(8,128)(2,1)S(1)} collective-permute-done((bf16[4,16,640]{2,1,0:T(8,128)(2,1)S(1)}, bf16[4,16,640]{2,1,0:T(8,128)(2,1)S(1)}, u32[]{:S(2)}, u32[]{:S(2)}) %collective-permute-start.3) | collective-permute-done | bytes 81952 | tf_op jit(solution)/shard_map/ppermute | solution.py:92
  15.8 1.6 %collective-permute-start.4 = (bf16[128,1280]{1,0:T(8,128)(2,1)S(1)}, bf16[128,1280]{1,0:T(8,128)(2,1)S(1)}, u32[]{:S(2)}, u32[]{:S(2)}) collective-permute-start(bf16[128,1280]{1,0:T(8,128)(2,1)S(1)} %pad_maximum_fusion), channel_id=1, source_target_pairs={{4,0},{9,1},{6,2},{11,3},{0,4},{13,5},{2,6},{15,7},{12,8},{1,9},{1... | collective-permute-start | bytes 983048 | tf_op jit(solution)/shard_map/ppermute | solution.py:92
  18.0 1.7 %collective-permute-start.8 = (bf16[64,256]{1,0:T(8,128)(2,1)S(1)}, bf16[64,256]{1,0:T(8,128)(2,1)S(1)}, u32[]{:S(2)}, u32[]{:S(2)}) collective-permute-start(bf16[64,256]{1,0:T(8,128)(2,1)S(1)} %slice.75), channel_id=1, source_target_pairs={{12,0},{13,1},{14,2},{15,3},{8,4},{9,5},{10,6},{11,7},{4,8},{5,9},... | collective-permute-start | bytes 98312 | tf_op jit(solution)/shard_map/ppermute | solution.py:92
  19.7 2.1 %dequant_down.1 = (bf16[384,2048]{1,0:T(8,128)(2,1)S(1)}, bf16[384,2048]{1,0:T(8,128)(2,1)S(1)}) custom-call(s32[1]{0:T(128)} %bitcast.1.exp_ref, s32[3,1,32]{2,1,0:T(1,128)} %bitcast.27, bf16[1,384,4096]{2,1,0:T(8,128)(2,1)} %down_hbm.1, bf16[4,16,640]{2,1,0:T(8,128)(2,1)S(1)} %collective-permute-done.3._.refs_1_), custom_call_target="tpu_custom_call" | custom-call | flops 1572864 | bytes 6291456 | tf_op jit(solution)/shard_map/dequant_down/pallas_call | solution.py:318
  26.9 1.4 %collective-permute-start.11 = (bf16[4,16,640]{2,1,0:T(8,128)(2,1)S(1)}, bf16[4,16,640]{2,1,0:T(8,128)(2,1)S(1)}, u32[]{:S(2)}, u32[]{:S(2)}) collective-permute-start(bf16[4,16,640]{2,1,0:T(8,128)(2,1)S(1)} %pad_maximum_fusion.7), channel_id=1, source_target_pairs={{16,0},{17,1},{18,2},{19,3},{20,4},{21,5},{22,6},{23,7},{24,8},{25... | collective-permute-start | bytes 245768 | tf_op jit(solution)/shard_map/ppermute | solution.py:92
  28.3 3.2 %attend.2.refs_7_ = bf16[512,1024]{1,0:T(8,128)(2,1)S(1)} custom-call(s32[1]{0:T(128)} %bitcast.ctx_ref, s32[1]{0:T(128)} %bitcast.1.exp_ref, s32[8]{0:T(128)S(1)} %copy-done.2, bf16[64,1280]{1,0:T(8,128)(2,1)S(1)} %get-tuple-element.73._.refs_0_, bf16[64,1280]{1,0:T(8,128)(2,1)S(1)} %collective-permute-done.refs_1_, ...), custom_call_target="tpu_custom_call" | custom-call | flops 939524096 | bytes 4194304 | tf_op jit(solution)/shard_map/attend/pallas_call | solution.py:711
  31.6 2.1 %attend.3 = (f32[256,256]{1,0:T(8,128)S(1)}, f32[256,256]{1,0:T(8,128)S(1)}, bf16[512,256]{1,0:T(8,128)(2,1)S(1)}) custom-call(s32[1]{0:T(128)} %bitcast.ctx_ref, s32[1]{0:T(128)} %bitcast.1.exp_ref, s32[8]{0:T(128)S(1)} %copy-done.2, bf16[64,1280]{1,0:T(8,128)(2,1)S(1)} %get-tuple-element.73._.refs_0_, bf16[64,1280]{1,0:T(8,128)(2,1)S(1)} %collective-permute-done.refs_1_, ...), custom_call_target="tpu_custom_call" | custom-call | flops 671088640 | bytes 4194304 | tf_op jit(solution)/shard_map/attend/pallas_call | solution.py:711
  34.4 1.5 %collective-permute-done.12.refs_1_ = bf16[544,256]{1,0:T(8,128)(2,1)S(1)} collective-permute-done((bf16[544,256]{1,0:T(8,128)(2,1)S(1)}, bf16[544,256]{1,0:T(8,128)(2,1)S(1)}, u32[]{:S(2)}, u32[]{:S(2)}) %collective-permute-start.12) | collective-permute-done | bytes 278560 | tf_op jit(solution)/shard_map/ppermute | solution.py:25
  35.9 1.6 %collective-permute-start.13 = (bf16[288,256]{1,0:T(8,128)(2,1)S(1)}, bf16[288,256]{1,0:T(8,128)(2,1)S(1)}, u32[]{:S(2)}, u32[]{:S(2)}) collective-permute-start(bf16[288,256]{1,0:T(8,128)(2,1)S(1)} %pad_maximum_fusion.5), channel_id=1, source_target_pairs={{0,2},{1,3},{2,0},{3,1},{4,6},{5,7},{6,4},{7,5},{8,10},{9,11},{10,... | collective-permute-start | bytes 442376 | tf_op jit(solution)/shard_map/ppermute | solution.py:25
  37.6 4.3 %collective-permute-done.13.refs_2_ = bf16[288,256]{1,0:T(8,128)(2,1)S(1)} collective-permute-done((bf16[288,256]{1,0:T(8,128)(2,1)S(1)}, bf16[288,256]{1,0:T(8,128)(2,1)S(1)}, u32[]{:S(2)}, u32[]{:S(2)}) %collective-permute-start.13) | collective-permute-done | bytes 147488 | tf_op jit(solution)/shard_map/ppermute | solution.py:25
  43.3 1.9 %collective-permute-start.15 = (bf16[256,256]{1,0:T(8,128)(2,1)S(1)}, bf16[256,256]{1,0:T(8,128)(2,1)S(1)}, u32[]{:S(2)}, u32[]{:S(2)}) collective-permute-start(bf16[256,256]{1,0:T(8,128)(2,1)S(1)} %add_convert_fusion.6.refs_0_.refs_6_), channel_id=1, source_target_pairs={{6,0},{7,1},{4,2},{5,3},{2,4},{3,5},{0,6},{1,7},{14,8},{15,9},{12,... | collective-permute-start | bytes 393224 | tf_op jit(solution)/shard_map/ppermute | solution.py:92
  48.1 2.4 %collective-permute-done.14.refs_1_.refs_7_ = bf16[256,256]{1,0:T(8,128)(2,1)S(1)} collective-permute-done((bf16[256,256]{1,0:T(8,128)(2,1)S(1)}, bf16[256,256]{1,0:T(8,128)(2,1)S(1)}, u32[]{:S(2)}, u32[]{:S(2)}) %collective-permute-start.14) | collective-permute-done | bytes 131104 | tf_op jit(solution)/shard_map/ppermute | solution.py:92
  51.9 1.6 %collective-permute-start.20 = (bf16[512,256]{1,0:T(8,128)(2,1)S(1)}, bf16[512,256]{1,0:T(8,128)(2,1)S(1)}, u32[]{:S(2)}, u32[]{:S(2)}) collective-permute-start(bf16[512,256]{1,0:T(8,128)(2,1)S(1)} %constant_dynamic-update-slice_fusion), channel_id=1, source_target_pairs={{2,0},{5,1},{0,2},{7,3},{6,4},{1,5},{4,6},{3,7},{10,8},{13,9},{8,1... | collective-permute-start | bytes 786440 | tf_op jit(solution)/shard_map/ppermute | solution.py:92
  54.6 1.8 %collective-permute-start.19 = (bf16[256,256]{1,0:T(8,128)(2,1)S(1)}, bf16[256,256]{1,0:T(8,128)(2,1)S(1)}, u32[]{:S(2)}, u32[]{:S(2)}) collective-permute-start(bf16[256,256]{1,0:T(8,128)(2,1)S(1)} %collective-permute-done.15.refs_2_), channel_id=1, source_target_pairs={{16,0},{17,1},{18,2},{19,3},{20,4},{21,5},{22,6},{23,7},{24,8},{25... | collective-permute-start | bytes 393224 | tf_op jit(solution)/shard_map/ppermute | solution.py:92
  57.1 4.9 %collective-permute-done.19.refs_5_ = bf16[256,256]{1,0:T(8,128)(2,1)S(1)} collective-permute-done((bf16[256,256]{1,0:T(8,128)(2,1)S(1)}, bf16[256,256]{1,0:T(8,128)(2,1)S(1)}, u32[]{:S(2)}, u32[]{:S(2)}) %collective-permute-start.19) | collective-permute-done | bytes 131104 | tf_op jit(solution)/shard_map/ppermute | solution.py:92
  64.2 2.1 %experts_in_first.1 = (f32[512,1536]{1,0:T(8,128)S(1)}, f32[512,1]{1,0:T(8,128)S(1)}) custom-call(s32[1]{0:T(128)} %bitcast.ctx_ref, s32[1]{0:T(128)} %bitcast.1.exp_ref, bf16[256,256]{1,0:T(8,128)(2,1)S(1)} %add_convert_fusion.6.refs_0_.refs_6_, bf16[256,256]{1,0:T(8,128)(2,1)S(1)} %collective-permute-done.14.refs_1_.refs_7_, ...), custom_call_target="tpu_custom_call" | custom-call | flops 1610612736 | bytes 8388608 | tf_op jit(solution)/shard_map/experts_in_first/pallas_call | solution.py:784
  66.4 2.2 %collective-permute-done.24.refs_5_ = bf16[256,256]{1,0:T(8,128)(2,1)S(1)} collective-permute-done((bf16[256,256]{1,0:T(8,128)(2,1)S(1)}, bf16[256,256]{1,0:T(8,128)(2,1)S(1)}, u32[]{:S(2)}, u32[]{:S(2)}) %collective-permute-start.24) | collective-permute-done | bytes 131104 | tf_op jit(solution)/shard_map/ppermute | solution.py:92
  70.3 1.4 %experts_in_second.3.refs_5_.act_ref = bf16[256,1664]{1,0:T(8,128)(2,1)S(1)} custom-call(s32[1]{0:T(128)} %bitcast.ctx_ref, s32[1]{0:T(128)} %bitcast.1.exp_ref, bf16[256,256]{1,0:T(8,128)(2,1)S(1)} %collective-permute-done.16.refs_0_.refs_8_, bf16[512,256]{1,0:T(8,128)(2,1)S(1)} %collective-permute-done.20.refs_6_.refs_1_.refs_11_, ...), custom_call_target="tpu_custom_call" | custom-call | flops 805306368 | bytes 8388608 | tf_op jit(solution)/shard_map/experts_in_second/pallas_call | solution.py:802
  72.7 1.8 %experts_out.2 = (f32[32,2048]{1,0:T(8,128)S(1)}, f32[32,2048]{1,0:T(8,128)S(1)}, bf16[32,2048]{1,0:T(8,128)(2,1)S(1)}, bf16[32,2048]{1,0:T(8,128)(2,1)S(1)}, f3...) custom-call(s32[1]{0:T(128)} %bitcast.ctx_ref, ...), custom_call_target="tpu_custom_call" | custom-call | flops 805306368 | bytes 8388608 | tf_op jit(solution)/shard_map/experts_out/pallas_call | solution.py:839
  76.1 1.5 %collective-permute-start.29 = (bf16[32,2048]{1,0:T(8,128)(2,1)S(1)}, bf16[32,2048]{1,0:T(8,128)(2,1)S(1)}, u32[]{:S(2)}, u32[]{:S(2)}) collective-permute-start(bf16[32,2048]{1,0:T(8,128)(2,1)S(1)} %get-tuple-element.113), channel_id=1, source_target_pairs={{2,0},{5,1},{0,2},{7,3},{6,4},{1,5},{4,6},{3,7},{10,8},{13,9},{8,1... | collective-permute-start | bytes 393224 | tf_op jit(solution)/shard_map/ppermute | solution.py:92
  77.6 1.8 %experts_out.3 = (f32[32,2048]{1,0:T(8,128)S(1)}, bf16[32,2048]{1,0:T(8,128)(2,1)S(1)}, bf16[32,2048]{1,0:T(8,128)(2,1)S(1)}, f32[32,2048]{1,0:T(8,128)S(1)}, f3...) custom-call(s32[1]{0:T(128)} %bitcast.ctx_ref, ...), custom_call_target="tpu_custom_call" | custom-call | flops 805306368 | bytes 8388608 | tf_op jit(solution)/shard_map/experts_out/pallas_call | solution.py:839
  79.4 1.7 %collective-permute-done.28 = bf16[32,2048]{1,0:T(8,128)(2,1)S(1)} collective-permute-done((bf16[32,2048]{1,0:T(8,128)(2,1)S(1)}, bf16[32,2048]{1,0:T(8,128)(2,1)S(1)}, u32[]{:S(2)}, u32[]{:S(2)}) %collective-permute-start.28) | collective-permute-done | bytes 131104 | tf_op jit(solution)/shard_map/ppermute | solution.py:92
  85.6 1.4 %collective-permute-start.31 = (bf16[32,2048]{1,0:T(8,128)(2,1)S(1)}, bf16[32,2048]{1,0:T(8,128)(2,1)S(1)}, u32[]{:S(2)}, u32[]{:S(2)}) collective-permute-start(bf16[32,2048]{1,0:T(8,128)(2,1)S(1)} %add_convert_fusion.5), channel_id=1, source_target_pairs={{16,0},{17,1},{18,2},{19,3},{20,4},{21,5},{22,6},{23,7},{24,8},{25... | collective-permute-start | bytes 393224 | tf_op jit(solution)/shard_map/ppermute | solution.py:92
  88.2 2.6 %collective-permute-done.34 = bf16[32,2048]{1,0:T(8,128)(2,1)S(1)} collective-permute-done((bf16[32,2048]{1,0:T(8,128)(2,1)S(1)}, bf16[32,2048]{1,0:T(8,128)(2,1)S(1)}, u32[]{:S(2)}, u32[]{:S(2)}) %collective-permute-start.34) | collective-permute-done | bytes 131104 | tf_op jit(solution)/shard_map/ppermute | solution.py:92
  91.9 1.4 %collective-permute-done.31 = bf16[32,2048]{1,0:T(8,128)(2,1)S(1)} collective-permute-done((bf16[32,2048]{1,0:T(8,128)(2,1)S(1)}, bf16[32,2048]{1,0:T(8,128)(2,1)S(1)}, u32[]{:S(2)}, u32[]{:S(2)}) %collective-permute-start.31) | collective-permute-done | bytes 131104 | tf_op jit(solution)/shard_map/ppermute | solution.py:92
  95.1 2.4 %collective-permute-start.37 = (bf16[32,2048]{1,0:T(8,128)(2,1)S(1)}, bf16[32,2048]{1,0:T(8,128)(2,1)S(1)}, u32[]{:S(2)}, u32[]{:S(2)}) collective-permute-start(bf16[32,2048]{1,0:T(8,128)(2,1)S(1)} %get-tuple-element.142), channel_id=1, source_target_pairs={{8,0},{9,1},{10,2},{11,3},{12,4},{13,5},{14,6},{15,7},{0,8},{1,9},... | collective-permute-start | bytes 393224 | tf_op jit(solution)/shard_map/ppermute | solution.py:92
  97.5 1.8 %collective-permute-done.36 = bf16[32,2048]{1,0:T(8,128)(2,1)S(1)} collective-permute-done((bf16[32,2048]{1,0:T(8,128)(2,1)S(1)}, bf16[32,2048]{1,0:T(8,128)(2,1)S(1)}, u32[]{:S(2)}, u32[]{:S(2)}) %collective-permute-start.36) | collective-permute-done | bytes 131104 | tf_op jit(solution)/shard_map/ppermute | solution.py:92
  99.3 2.3 %collective-permute-done.35 = bf16[32,2048]{1,0:T(8,128)(2,1)S(1)} collective-permute-done((bf16[32,2048]{1,0:T(8,128)(2,1)S(1)}, bf16[32,2048]{1,0:T(8,128)(2,1)S(1)}, u32[]{:S(2)}, u32[]{:S(2)}) %collective-permute-start.35) | collective-permute-done | bytes 131104 | tf_op jit(solution)/shard_map/ppermute | solution.py:92
  (97 shorter events, 33.8 us)
Async XLA Ops:
  1.2 13.8 %collective-permute-start = (bf16[64,1280]{1,0:T(8,128)(2,1)S(1)}, bf16[64,1280]{1,0:T(8,128)(2,1)S(1)}, u32[]{:S(2)}, u32[]{:S(2)}) collective-permute-start(bf16[64,1280]{1,0:T(8,128)(2,1)S(1)} %get-tuple-element.73._.refs_0_), channel_id=1, source_target_pairs={{16,0},{17,1},{18,2},{19,3},{20,4},{21,5},{22,6},{23,7},{24,8},{25... | collective-permute-start | bytes 491528 | tf_op jit(solution)/shard_map/ppermute | solution.py:92
  5.3 9.7 %collective-permute-start.1 = (bf16[64,1280]{1,0:T(8,128)(2,1)S(1)}, bf16[64,1280]{1,0:T(8,128)(2,1)S(1)}, u32[]{:S(2)}, u32[]{:S(2)}) collective-permute-start(bf16[64,1280]{1,0:T(8,128)(2,1)S(1)} %get-tuple-element.73._.refs_0_), channel_id=1, source_target_pairs={{4,0},{9,1},{6,2},{11,3},{0,4},{13,5},{2,6},{15,7},{12,8},{1,9},{1... | collective-permute-start | bytes 491528 | tf_op jit(solution)/shard_map/ppermute | solution.py:92
  6.8 8.2 %collective-permute-start.2 = (bf16[64,1280]{1,0:T(8,128)(2,1)S(1)}, bf16[64,1280]{1,0:T(8,128)(2,1)S(1)}, u32[]{:S(2)}, u32[]{:S(2)}) collective-permute-start(bf16[64,1280]{1,0:T(8,128)(2,1)S(1)} %get-tuple-element.73._.refs_0_), channel_id=1, source_target_pairs={{8,0},{5,1},{10,2},{7,3},{12,4},{1,5},{14,6},{3,7},{0,8},{13,9},{2... | collective-permute-start | bytes 491528 | tf_op jit(solution)/shard_map/ppermute | solution.py:92
  8.4 6.6 %collective-permute-start.3 = (bf16[4,16,640]{2,1,0:T(8,128)(2,1)S(1)}, bf16[4,16,640]{2,1,0:T(8,128)(2,1)S(1)}, u32[]{:S(2)}, u32[]{:S(2)}) collective-permute-start(bf16[4,16,640]{2,1,0:T(8,128)(2,1)S(1)} %get-tuple-element.74), channel_id=1, source_target_pairs={{8,0},{5,1},{10,2},{7,3},{12,4},{1,5},{14,6},{3,7},{0,8},{13,9},{2... | collective-permute-start | bytes 245768 | tf_op jit(solution)/shard_map/ppermute | solution.py:92
  15.0 9.7 %collective-permute-start.7 = (bf16[2048,768]{1,0:T(8,128)(2,1)S(1)}, bf16[2048,768]{1,0:T(8,128)(2,1)S(1)}, u32[]{:S(2)}, u32[]{:S(2)}) collective-permute-start(bf16[2048,768]{1,0:T(8,128)(2,1)S(1)} %get-tuple-element.82), channel_id=1, source_target_pairs={{0,1},{1,0},{2,3},{3,2},{4,5},{5,4},{6,7},{7,6},{8,9},{9,8},{10,11... | collective-permute-start | bytes 9437192 | tf_op jit(solution)/shard_map/ppermute | solution.py:25
  15.0 9.6 %collective-permute-start.5 = (bf16[64,1280]{1,0:T(8,128)(2,1)S(1)}, bf16[64,1280]{1,0:T(8,128)(2,1)S(1)}, u32[]{:S(2)}, u32[]{:S(2)}) collective-permute-start(bf16[64,1280]{1,0:T(8,128)(2,1)S(1)} %collective-permute-done.refs_1_), channel_id=1, source_target_pairs={{8,0},{5,1},{10,2},{7,3},{12,4},{1,5},{14,6},{3,7},{0,8},{13,9},{2... | collective-permute-start | bytes 491528 | tf_op jit(solution)/shard_map/ppermute | solution.py:92
  15.8 8.8 %collective-permute-start.4 = (bf16[128,1280]{1,0:T(8,128)(2,1)S(1)}, bf16[128,1280]{1,0:T(8,128)(2,1)S(1)}, u32[]{:S(2)}, u32[]{:S(2)}) collective-permute-start(bf16[128,1280]{1,0:T(8,128)(2,1)S(1)} %pad_maximum_fusion), channel_id=1, source_target_pairs={{4,0},{9,1},{6,2},{11,3},{0,4},{13,5},{2,6},{15,7},{12,8},{1,9},{1... | collective-permute-start | bytes 983048 | tf_op jit(solution)/shard_map/ppermute | solution.py:92
  17.4 7.2 %collective-permute-start.6 = (bf16[4,16,640]{2,1,0:T(8,128)(2,1)S(1)}, bf16[4,16,640]{2,1,0:T(8,128)(2,1)S(1)}, u32[]{:S(2)}, u32[]{:S(2)}) collective-permute-start(bf16[4,16,640]{2,1,0:T(8,128)(2,1)S(1)} %pad_maximum_fusion.6), channel_id=1, source_target_pairs={{4,0},{9,1},{6,2},{11,3},{0,4},{13,5},{2,6},{15,7},{12,8},{1,9},{1... | collective-permute-start | bytes 245768 | tf_op jit(solution)/shard_map/ppermute | solution.py:92
  24.6 7.0 %collective-permute-start.10 = (bf16[384,2048]{1,0:T(8,128)(2,1)S(1)}, bf16[384,2048]{1,0:T(8,128)(2,1)S(1)}, u32[]{:S(2)}, u32[]{:S(2)}) collective-permute-start(bf16[384,2048]{1,0:T(8,128)(2,1)S(1)} %get-tuple-element.88), channel_id=1, source_target_pairs={{0,1},{1,0},{2,3},{3,2},{4,5},{5,4},{6,7},{7,6},{8,9},{9,8},{10,11... | collective-permute-start | bytes 4718600 | tf_op jit(solution)/shard_map/ppermute | solution.py:25
  25.8 5.8 %collective-permute-start.9 = (bf16[64,1280]{1,0:T(8,128)(2,1)S(1)}, bf16[64,1280]{1,0:T(8,128)(2,1)S(1)}, u32[]{:S(2)}, u32[]{:S(2)}) collective-permute-start(bf16[64,1280]{1,0:T(8,128)(2,1)S(1)} %collective-permute-done.5.refs_5_), channel_id=1, source_target_pairs={{4,0},{9,1},{6,2},{11,3},{0,4},{13,5},{2,6},{15,7},{12,8},{1,9},{1... | collective-permute-start | bytes 491528 | tf_op jit(solution)/shard_map/ppermute | solution.py:92
  26.9 7.2 %collective-permute-start.11 = (bf16[4,16,640]{2,1,0:T(8,128)(2,1)S(1)}, bf16[4,16,640]{2,1,0:T(8,128)(2,1)S(1)}, u32[]{:S(2)}, u32[]{:S(2)}) collective-permute-start(bf16[4,16,640]{2,1,0:T(8,128)(2,1)S(1)} %pad_maximum_fusion.7), channel_id=1, source_target_pairs={{16,0},{17,1},{18,2},{19,3},{20,4},{21,5},{22,6},{23,7},{24,8},{25... | collective-permute-start | bytes 245768 | tf_op jit(solution)/shard_map/ppermute | solution.py:92
  35.9 6.0 %collective-permute-start.13 = (bf16[288,256]{1,0:T(8,128)(2,1)S(1)}, bf16[288,256]{1,0:T(8,128)(2,1)S(1)}, u32[]{:S(2)}, u32[]{:S(2)}) collective-permute-start(bf16[288,256]{1,0:T(8,128)(2,1)S(1)} %pad_maximum_fusion.5), channel_id=1, source_target_pairs={{0,2},{1,3},{2,0},{3,1},{4,6},{5,7},{6,4},{7,5},{8,10},{9,11},{10,... | collective-permute-start | bytes 442376 | tf_op jit(solution)/shard_map/ppermute | solution.py:25
  42.0 8.5 %collective-permute-start.14 = (bf16[256,256]{1,0:T(8,128)(2,1)S(1)}, bf16[256,256]{1,0:T(8,128)(2,1)S(1)}, u32[]{:S(2)}, u32[]{:S(2)}) collective-permute-start(bf16[256,256]{1,0:T(8,128)(2,1)S(1)} %add_convert_fusion.6.refs_0_.refs_6_), channel_id=1, source_target_pairs={{16,0},{17,1},{18,2},{19,3},{20,4},{21,5},{22,6},{23,7},{24,8},{25... | collective-permute-start | bytes 393224 | tf_op jit(solution)/shard_map/ppermute | solution.py:92
  43.3 7.2 %collective-permute-start.15 = (bf16[256,256]{1,0:T(8,128)(2,1)S(1)}, bf16[256,256]{1,0:T(8,128)(2,1)S(1)}, u32[]{:S(2)}, u32[]{:S(2)}) collective-permute-start(bf16[256,256]{1,0:T(8,128)(2,1)S(1)} %add_convert_fusion.6.refs_0_.refs_6_), channel_id=1, source_target_pairs={{6,0},{7,1},{4,2},{5,3},{2,4},{3,5},{0,6},{1,7},{14,8},{15,9},{12,... | collective-permute-start | bytes 393224 | tf_op jit(solution)/shard_map/ppermute | solution.py:92
  45.1 6.1 %collective-permute-start.16 = (bf16[256,256]{1,0:T(8,128)(2,1)S(1)}, bf16[256,256]{1,0:T(8,128)(2,1)S(1)}, u32[]{:S(2)}, u32[]{:S(2)}) collective-permute-start(bf16[256,256]{1,0:T(8,128)(2,1)S(1)} %add_convert_fusion.6.refs_0_.refs_6_), channel_id=1, source_target_pairs={{8,0},{9,1},{10,2},{11,3},{12,4},{13,5},{14,6},{15,7},{0,8},{1,9},... | collective-permute-start | bytes 393224 | tf_op jit(solution)/shard_map/ppermute | solution.py:92
  51.9 10.6 %collective-permute-start.20 = (bf16[512,256]{1,0:T(8,128)(2,1)S(1)}, bf16[512,256]{1,0:T(8,128)(2,1)S(1)}, u32[]{:S(2)}, u32[]{:S(2)}) collective-permute-start(bf16[512,256]{1,0:T(8,128)(2,1)S(1)} %constant_dynamic-update-slice_fusion), channel_id=1, source_target_pairs={{2,0},{5,1},{0,2},{7,3},{6,4},{1,5},{4,6},{3,7},{10,8},{13,9},{8,1... | collective-permute-start | bytes 786440 | tf_op jit(solution)/shard_map/ppermute | solution.py:92
  53.5 9.1 %collective-permute-start.21 = (bf16[512,256]{1,0:T(8,128)(2,1)S(1)}, bf16[512,256]{1,0:T(8,128)(2,1)S(1)}, u32[]{:S(2)}, u32[]{:S(2)}) collective-permute-start(bf16[512,256]{1,0:T(8,128)(2,1)S(1)} %constant_dynamic-update-slice_fusion), channel_id=1, source_target_pairs={{4,0},{3,1},{6,2},{1,3},{0,4},{7,5},{2,6},{5,7},{12,8},{11,9},{14,... | collective-permute-start | bytes 786440 | tf_op jit(solution)/shard_map/ppermute | solution.py:92
  54.6 7.4 %collective-permute-start.19 = (bf16[256,256]{1,0:T(8,128)(2,1)S(1)}, bf16[256,256]{1,0:T(8,128)(2,1)S(1)}, u32[]{:S(2)}, u32[]{:S(2)}) collective-permute-start(bf16[256,256]{1,0:T(8,128)(2,1)S(1)} %collective-permute-done.15.refs_2_), channel_id=1, source_target_pairs={{16,0},{17,1},{18,2},{19,3},{20,4},{21,5},{22,6},{23,7},{24,8},{25... | collective-permute-start | bytes 393224 | tf_op jit(solution)/shard_map/ppermute | solution.py:92
  56.4 6.1 %collective-permute-start.22 = (bf16[256,256]{1,0:T(8,128)(2,1)S(1)}, bf16[256,256]{1,0:T(8,128)(2,1)S(1)}, u32[]{:S(2)}, u32[]{:S(2)}) collective-permute-start(bf16[256,256]{1,0:T(8,128)(2,1)S(1)} %collective-permute-done.14.refs_1_.refs_7_), channel_id=1, source_target_pairs={{8,0},{9,1},{10,2},{11,3},{12,4},{13,5},{14,6},{15,7},{0,8},{1,9},... | collective-permute-start | bytes 393224 | tf_op jit(solution)/shard_map/ppermute | solution.py:92
  62.6 6.4 %collective-permute-start.23 = (bf16[512,256]{1,0:T(8,128)(2,1)S(1)}, bf16[512,256]{1,0:T(8,128)(2,1)S(1)}, u32[]{:S(2)}, u32[]{:S(2)}) collective-permute-start(bf16[512,256]{1,0:T(8,128)(2,1)S(1)} %pad_maximum_fusion.1), channel_id=1, source_target_pairs={{4,0},{3,1},{6,2},{1,3},{0,4},{7,5},{2,6},{5,7},{12,8},{11,9},{14,... | collective-permute-start | bytes 786440 | tf_op jit(solution)/shard_map/ppermute | solution.py:92
  71.7 5.9 %collective-permute-start.30 = (bf16[256,1664]{1,0:T(8,128)(2,1)S(1)}, bf16[256,1664]{1,0:T(8,128)(2,1)S(1)}, u32[]{:S(2)}, u32[]{:S(2)}) collective-permute-start(bf16[256,1664]{1,0:T(8,128)(2,1)S(1)} %experts_in_second.3.refs_5_.act_ref), channel_id=1, source_target_pairs={{0,1},{1,0},{2,3},{3,2},{4,5},{5,4},{6,7},{7,6},{8,9},{9,8},{10,11... | collective-permute-start | bytes 2555912 | tf_op jit(solution)/shard_map/ppermute | solution.py:25
  74.5 7.8 %collective-permute-start.27 = (bf16[64,2048]{1,0:T(8,128)(2,1)S(1)}, bf16[64,2048]{1,0:T(8,128)(2,1)S(1)}, u32[]{:S(2)}, u32[]{:S(2)}) collective-permute-start(bf16[64,2048]{1,0:T(8,128)(2,1)S(1)} %pad_maximum_fusion.2), channel_id=1, source_target_pairs={{4,0},{3,1},{6,2},{1,3},{0,4},{7,5},{2,6},{5,7},{12,8},{11,9},{14,... | collective-permute-start | bytes 786440 | tf_op jit(solution)/shard_map/ppermute | solution.py:92
  75.4 5.7 %collective-permute-start.28 = (bf16[32,2048]{1,0:T(8,128)(2,1)S(1)}, bf16[32,2048]{1,0:T(8,128)(2,1)S(1)}, u32[]{:S(2)}, u32[]{:S(2)}) collective-permute-start(bf16[32,2048]{1,0:T(8,128)(2,1)S(1)} %get-tuple-element.112), channel_id=1, source_target_pairs={{8,0},{9,1},{10,2},{11,3},{12,4},{13,5},{14,6},{15,7},{0,8},{1,9},... | collective-permute-start | bytes 393224 | tf_op jit(solution)/shard_map/ppermute | solution.py:92
  82.4 11.0 %collective-permute-start.33 = (bf16[64,2048]{1,0:T(8,128)(2,1)S(1)}, bf16[64,2048]{1,0:T(8,128)(2,1)S(1)}, u32[]{:S(2)}, u32[]{:S(2)}) collective-permute-start(bf16[64,2048]{1,0:T(8,128)(2,1)S(1)} %pad_maximum_fusion.4), channel_id=1, source_target_pairs={{4,0},{3,1},{6,2},{1,3},{0,4},{7,5},{2,6},{5,7},{12,8},{11,9},{14,... | collective-permute-start | bytes 786440 | tf_op jit(solution)/shard_map/ppermute | solution.py:92
  83.4 10.0 %collective-permute-start.32 = (bf16[64,2048]{1,0:T(8,128)(2,1)S(1)}, bf16[64,2048]{1,0:T(8,128)(2,1)S(1)}, u32[]{:S(2)}, u32[]{:S(2)}) collective-permute-start(bf16[64,2048]{1,0:T(8,128)(2,1)S(1)} %pad_maximum_fusion.3), channel_id=1, source_target_pairs={{2,0},{5,1},{0,2},{7,3},{6,4},{1,5},{4,6},{3,7},{10,8},{13,9},{8,1... | collective-permute-start | bytes 786440 | tf_op jit(solution)/shard_map/ppermute | solution.py:92
  84.7 6.1 %collective-permute-start.34 = (bf16[32,2048]{1,0:T(8,128)(2,1)S(1)}, bf16[32,2048]{1,0:T(8,128)(2,1)S(1)}, u32[]{:S(2)}, u32[]{:S(2)}) collective-permute-start(bf16[32,2048]{1,0:T(8,128)(2,1)S(1)} %get-tuple-element.143), channel_id=1, source_target_pairs={{8,0},{9,1},{10,2},{11,3},{12,4},{13,5},{14,6},{15,7},{0,8},{1,9},... | collective-permute-start | bytes 393224 | tf_op jit(solution)/shard_map/ppermute | solution.py:92
  85.6 7.7 %collective-permute-start.31 = (bf16[32,2048]{1,0:T(8,128)(2,1)S(1)}, bf16[32,2048]{1,0:T(8,128)(2,1)S(1)}, u32[]{:S(2)}, u32[]{:S(2)}) collective-permute-start(bf16[32,2048]{1,0:T(8,128)(2,1)S(1)} %add_convert_fusion.5), channel_id=1, source_target_pairs={{16,0},{17,1},{18,2},{19,3},{20,4},{21,5},{22,6},{23,7},{24,8},{25... | collective-permute-start | bytes 393224 | tf_op jit(solution)/shard_map/ppermute | solution.py:92
  87.0 10.5 %collective-permute-start.38 = (bf16[32,2048]{1,0:T(8,128)(2,1)S(1)}, bf16[32,2048]{1,0:T(8,128)(2,1)S(1)}, u32[]{:S(2)}, u32[]{:S(2)}) collective-permute-start(bf16[32,2048]{1,0:T(8,128)(2,1)S(1)} %get-tuple-element.139), channel_id=1, source_target_pairs={{2,0},{5,1},{0,2},{7,3},{6,4},{1,5},{4,6},{3,7},{10,8},{13,9},{8,1... | collective-permute-start | bytes 393224 | tf_op jit(solution)/shard_map/ppermute | solution.py:92
  90.8 6.7 %collective-permute-start.39 = (bf16[32,2048]{1,0:T(8,128)(2,1)S(1)}, bf16[32,2048]{1,0:T(8,128)(2,1)S(1)}, u32[]{:S(2)}, u32[]{:S(2)}) collective-permute-start(bf16[32,2048]{1,0:T(8,128)(2,1)S(1)} %get-tuple-element.140), channel_id=1, source_target_pairs={{4,0},{3,1},{6,2},{1,3},{0,4},{7,5},{2,6},{5,7},{12,8},{11,9},{14,... | collective-permute-start | bytes 393224 | tf_op jit(solution)/shard_map/ppermute | solution.py:92
  93.4 5.9 %collective-permute-start.36 = (bf16[32,2048]{1,0:T(8,128)(2,1)S(1)}, bf16[32,2048]{1,0:T(8,128)(2,1)S(1)}, u32[]{:S(2)}, u32[]{:S(2)}) collective-permute-start(bf16[32,2048]{1,0:T(8,128)(2,1)S(1)} %add_convert_fusion.1), channel_id=1, source_target_pairs={{6,0},{7,1},{4,2},{5,3},{2,4},{3,5},{0,6},{1,7},{14,8},{15,9},{12,... | collective-permute-start | bytes 393224 | tf_op jit(solution)/shard_map/ppermute | solution.py:92
  94.9 6.7 %collective-permute-start.35 = (bf16[32,2048]{1,0:T(8,128)(2,1)S(1)}, bf16[32,2048]{1,0:T(8,128)(2,1)S(1)}, u32[]{:S(2)}, u32[]{:S(2)}) collective-permute-start(bf16[32,2048]{1,0:T(8,128)(2,1)S(1)} %get-tuple-element.141), channel_id=1, source_target_pairs={{16,0},{17,1},{18,2},{19,3},{20,4},{21,5},{22,6},{23,7},{24,8},{25... | collective-permute-start | bytes 393224 | tf_op jit(solution)/shard_map/ppermute | solution.py:92
  95.1 6.7 %collective-permute-start.37 = (bf16[32,2048]{1,0:T(8,128)(2,1)S(1)}, bf16[32,2048]{1,0:T(8,128)(2,1)S(1)}, u32[]{:S(2)}, u32[]{:S(2)}) collective-permute-start(bf16[32,2048]{1,0:T(8,128)(2,1)S(1)} %get-tuple-element.142), channel_id=1, source_target_pairs={{8,0},{9,1},{10,2},{11,3},{12,4},{13,5},{14,6},{15,7},{0,8},{1,9},... | collective-permute-start | bytes 393224 | tf_op jit(solution)/shard_map/ppermute | solution.py:92
  (12 other events, 97.4 us)

commit v11 on v10

--- a/solution.py
+++ b/solution.py
@@ -399,14 +399,15 @@
         return
     cols = weight_ref.shape[1] // 2
     per_x = 2 * ctx_count * tok
-    for x_off in range(x_count):
-        rows = pl.ds(x_off * per_x, per_x)
-        for which in (1, 0):
-            side = lax.bitwise_xor(my_core, which)
-            weight = weight_ref[:, pl.ds(pl.multiple_of(side * cols, cols), cols)]
-            part = jnp.dot(att_ref[rows, :], weight, preferred_element_type=jnp.float32)
-            out_ref = give_ref if which else keep_refs[x_off]
-            out_ref[pl.ds(x_off * per_x if which else 0, per_x), :] = part.astype(out_ref.dtype)
+    for which in (1, 0):
+        side = lax.bitwise_xor(my_core, which)
+        weight = weight_ref[:, pl.ds(pl.multiple_of(side * cols, cols), cols)]
+        part = jnp.dot(att_ref[...], weight, preferred_element_type=jnp.float32)
+        if which:
+            give_ref[...] = part.astype(give_ref.dtype)
+        else:
+            for x_off, keep_ref in enumerate(keep_refs):
+                keep_ref[...] = part[x_off * per_x : (x_off + 1) * per_x]
 
 
 def finish_kernel(plan, ctx_ref, exp_ref, keep_in, give_in, *refs):

time: 104 us -> 104 us (level)
  no operation moved by 1% of the time
where the time goes in v11:
time: 104 us
  starting transfers between devices  45.1 us (43%)
  waiting for transfers between devices  37 us (36%)
  Pallas kernels  20.2 us (19%)
    ppermute x34, starting transfers between devices, follow(): return lax.ppermute(array, ('ctx', 'exp'), pairs)  41.5 us
    ppermute x34, waiting for transfers between devices, follow(): return lax.ppermute(array, ('ctx', 'exp'), pairs)  29.5 us
    ppermute x7, waiting for transfers between devices, from_offset(): lax.ppermute(array, 'exp', [(i, i ^ offset) for i in range(lax.axis_size(...  7.52 us
    pallas_call x2, Pallas kernels, attend(): pl.pallas_call(functools.partial(attend_kernel, (ctx_count, exp_count, to...  5.34 us
    pallas_call x2, Pallas kernels, shards(): pl.pallas_call(functools.partial(experts_out_kernel, (ctx_count, exp_coun...  3.63 us
    ppermute x7, starting transfers between devices, from_offset(): lax.ppermute(array, 'exp', [(i, i ^ offset) for i in range(lax.axis_size(...  3.61 us
    pallas_call x1, Pallas kernels, deq_in(): pl.pallas_call(functools.partial(deq_in_kernel, ctx_count), in_specs=[pl....  3 us
    pallas_call x2, Pallas kernels, shards(): pl.pallas_call(functools.partial(experts_in_second, (ctx_count, x_count,...  2.59 us
  transfers between devices with their start and end apart: 41, of which 24 were waited for; matrix products, arithmetic and copies ran while one was open for 0% of the time, Pallas kernels for 17%

profile of v11, /device:TPU:0, one launch (start us, length us, event | category | flops | bytes accessed | tf_op | source)
XLA Modules:
  0.0 104.2 jit_solution(6166578519923074723)
XLA Ops:
  1.2 4.1 %collective-permute-start = (bf16[64,1280]{1,0:T(8,128)(2,1)S(1)}, bf16[64,1280]{1,0:T(8,128)(2,1)S(1)}, u32[]{:S(2)}, u32[]{:S(2)}) collective-permute-start(bf16[64,1280]{1,0:T(8,128)(2,1)S(1)} %get-tuple-element.73._.refs_0_), channel_id=1, source_target_pairs={{16,0},{17,1},{18,2},{19,3},{20,4},{21,5},{22,6},{23,7},{24,8},{25... | collective-permute-start | bytes 491528 | tf_op jit(solution)/shard_map/ppermute | solution.py:92
  5.3 1.5 %collective-permute-start.1 = (bf16[64,1280]{1,0:T(8,128)(2,1)S(1)}, bf16[64,1280]{1,0:T(8,128)(2,1)S(1)}, u32[]{:S(2)}, u32[]{:S(2)}) collective-permute-start(bf16[64,1280]{1,0:T(8,128)(2,1)S(1)} %get-tuple-element.73._.refs_0_), channel_id=1, source_target_pairs={{4,0},{9,1},{6,2},{11,3},{0,4},{13,5},{2,6},{15,7},{12,8},{1,9},{1... | collective-permute-start | bytes 491528 | tf_op jit(solution)/shard_map/ppermute | solution.py:92
  6.8 1.6 %collective-permute-start.2 = (bf16[64,1280]{1,0:T(8,128)(2,1)S(1)}, bf16[64,1280]{1,0:T(8,128)(2,1)S(1)}, u32[]{:S(2)}, u32[]{:S(2)}) collective-permute-start(bf16[64,1280]{1,0:T(8,128)(2,1)S(1)} %get-tuple-element.73._.refs_0_), channel_id=1, source_target_pairs={{8,0},{5,1},{10,2},{7,3},{12,4},{1,5},{14,6},{3,7},{0,8},{13,9},{2... | collective-permute-start | bytes 491528 | tf_op jit(solution)/shard_map/ppermute | solution.py:92
  8.8 3.0 %dequant_in.1 = (bf16[2048,768]{1,0:T(8,128)(2,1)S(1)}, bf16[2048,768]{1,0:T(8,128)(2,1)S(1)}) custom-call(s32[1]{0:T(128)} %bitcast.1.exp_ref, s32[3,1,32]{2,1,0:T(1,128)} %bitcast.25, s32[3,1,32]{2,1,0:T(1,128)} %bitcast.26, bf16[1,4096,384]{2,1,0:T(8,128)(2,1)} %gate_hbm.1, bf16[1,4096,384]{2,1,0:T(8,128)(2,1)} %up_hbm.1, ...), custom_call_target="tpu_custom_call" | custom-call | flops 3145728 | bytes 12582912 | tf_op jit(solution)/shard_map/dequant_in/pallas_call | solution.py:269
  11.8 3.1 %collective-permute-done.3._.refs_1_ = bf16[4,16,640]{2,1,0:T(8,128)(2,1)S(1)} collective-permute-done((bf16[4,16,640]{2,1,0:T(8,128)(2,1)S(1)}, bf16[4,16,640]{2,1,0:T(8,128)(2,1)S(1)}, u32[]{:S(2)}, u32[]{:S(2)}) %collective-permute-start.3) | collective-permute-done | bytes 81952 | tf_op jit(solution)/shard_map/ppermute | solution.py:92
  15.8 1.6 %collective-permute-start.4 = (bf16[128,1280]{1,0:T(8,128)(2,1)S(1)}, bf16[128,1280]{1,0:T(8,128)(2,1)S(1)}, u32[]{:S(2)}, u32[]{:S(2)}) collective-permute-start(bf16[128,1280]{1,0:T(8,128)(2,1)S(1)} %pad_maximum_fusion), channel_id=1, source_target_pairs={{4,0},{9,1},{6,2},{11,3},{0,4},{13,5},{2,6},{15,7},{12,8},{1,9},{1... | collective-permute-start | bytes 983048 | tf_op jit(solution)/shard_map/ppermute | solution.py:92
  18.0 1.7 %collective-permute-start.8 = (bf16[64,256]{1,0:T(8,128)(2,1)S(1)}, bf16[64,256]{1,0:T(8,128)(2,1)S(1)}, u32[]{:S(2)}, u32[]{:S(2)}) collective-permute-start(bf16[64,256]{1,0:T(8,128)(2,1)S(1)} %slice.75), channel_id=1, source_target_pairs={{12,0},{13,1},{14,2},{15,3},{8,4},{9,5},{10,6},{11,7},{4,8},{5,9},... | collective-permute-start | bytes 98312 | tf_op jit(solution)/shard_map/ppermute | solution.py:92
  19.7 2.1 %dequant_down.1 = (bf16[384,2048]{1,0:T(8,128)(2,1)S(1)}, bf16[384,2048]{1,0:T(8,128)(2,1)S(1)}) custom-call(s32[1]{0:T(128)} %bitcast.1.exp_ref, s32[3,1,32]{2,1,0:T(1,128)} %bitcast.27, bf16[1,384,4096]{2,1,0:T(8,128)(2,1)} %down_hbm.1, bf16[4,16,640]{2,1,0:T(8,128)(2,1)S(1)} %collective-permute-done.3._.refs_1_), custom_call_target="tpu_custom_call" | custom-call | flops 1572864 | bytes 6291456 | tf_op jit(solution)/shard_map/dequant_down/pallas_call | solution.py:318
  26.9 1.4 %collective-permute-start.11 = (bf16[4,16,640]{2,1,0:T(8,128)(2,1)S(1)}, bf16[4,16,640]{2,1,0:T(8,128)(2,1)S(1)}, u32[]{:S(2)}, u32[]{:S(2)}) collective-permute-start(bf16[4,16,640]{2,1,0:T(8,128)(2,1)S(1)} %pad_maximum_fusion.7), channel_id=1, source_target_pairs={{16,0},{17,1},{18,2},{19,3},{20,4},{21,5},{22,6},{23,7},{24,8},{25... | collective-permute-start | bytes 245768 | tf_op jit(solution)/shard_map/ppermute | solution.py:92
  28.3 3.2 %attend.2.refs_7_ = bf16[512,1024]{1,0:T(8,128)(2,1)S(1)} custom-call(s32[1]{0:T(128)} %bitcast.ctx_ref, s32[1]{0:T(128)} %bitcast.1.exp_ref, s32[8]{0:T(128)S(1)} %copy-done.2, bf16[64,1280]{1,0:T(8,128)(2,1)S(1)} %get-tuple-element.73._.refs_0_, bf16[64,1280]{1,0:T(8,128)(2,1)S(1)} %collective-permute-done.refs_1_, ...), custom_call_target="tpu_custom_call" | custom-call | flops 939524096 | bytes 4194304 | tf_op jit(solution)/shard_map/attend/pallas_call | solution.py:712
  31.6 2.1 %attend.3 = (f32[256,256]{1,0:T(8,128)S(1)}, f32[256,256]{1,0:T(8,128)S(1)}, bf16[512,256]{1,0:T(8,128)(2,1)S(1)}) custom-call(s32[1]{0:T(128)} %bitcast.ctx_ref, s32[1]{0:T(128)} %bitcast.1.exp_ref, s32[8]{0:T(128)S(1)} %copy-done.2, bf16[64,1280]{1,0:T(8,128)(2,1)S(1)} %get-tuple-element.73._.refs_0_, bf16[64,1280]{1,0:T(8,128)(2,1)S(1)} %collective-permute-done.refs_1_, ...), custom_call_target="tpu_custom_call" | custom-call | flops 671088640 | bytes 4194304 | tf_op jit(solution)/shard_map/attend/pallas_call | solution.py:712
  34.4 1.5 %collective-permute-done.12.refs_1_ = bf16[544,256]{1,0:T(8,128)(2,1)S(1)} collective-permute-done((bf16[544,256]{1,0:T(8,128)(2,1)S(1)}, bf16[544,256]{1,0:T(8,128)(2,1)S(1)}, u32[]{:S(2)}, u32[]{:S(2)}) %collective-permute-start.12) | collective-permute-done | bytes 278560 | tf_op jit(solution)/shard_map/ppermute | solution.py:25
  35.9 1.6 %collective-permute-start.13 = (bf16[288,256]{1,0:T(8,128)(2,1)S(1)}, bf16[288,256]{1,0:T(8,128)(2,1)S(1)}, u32[]{:S(2)}, u32[]{:S(2)}) collective-permute-start(bf16[288,256]{1,0:T(8,128)(2,1)S(1)} %pad_maximum_fusion.5), channel_id=1, source_target_pairs={{0,2},{1,3},{2,0},{3,1},{4,6},{5,7},{6,4},{7,5},{8,10},{9,11},{10,... | collective-permute-start | bytes 442376 | tf_op jit(solution)/shard_map/ppermute | solution.py:25
  37.6 4.3 %collective-permute-done.13.refs_2_ = bf16[288,256]{1,0:T(8,128)(2,1)S(1)} collective-permute-done((bf16[288,256]{1,0:T(8,128)(2,1)S(1)}, bf16[288,256]{1,0:T(8,128)(2,1)S(1)}, u32[]{:S(2)}, u32[]{:S(2)}) %collective-permute-start.13) | collective-permute-done | bytes 147488 | tf_op jit(solution)/shard_map/ppermute | solution.py:25
  43.3 1.9 %collective-permute-start.15 = (bf16[256,256]{1,0:T(8,128)(2,1)S(1)}, bf16[256,256]{1,0:T(8,128)(2,1)S(1)}, u32[]{:S(2)}, u32[]{:S(2)}) collective-permute-start(bf16[256,256]{1,0:T(8,128)(2,1)S(1)} %add_convert_fusion.6.refs_0_.refs_6_), channel_id=1, source_target_pairs={{6,0},{7,1},{4,2},{5,3},{2,4},{3,5},{0,6},{1,7},{14,8},{15,9},{12,... | collective-permute-start | bytes 393224 | tf_op jit(solution)/shard_map/ppermute | solution.py:92
  48.1 2.4 %collective-permute-done.14.refs_1_.refs_7_ = bf16[256,256]{1,0:T(8,128)(2,1)S(1)} collective-permute-done((bf16[256,256]{1,0:T(8,128)(2,1)S(1)}, bf16[256,256]{1,0:T(8,128)(2,1)S(1)}, u32[]{:S(2)}, u32[]{:S(2)}) %collective-permute-start.14) | collective-permute-done | bytes 131104 | tf_op jit(solution)/shard_map/ppermute | solution.py:92
  51.9 1.6 %collective-permute-start.20 = (bf16[512,256]{1,0:T(8,128)(2,1)S(1)}, bf16[512,256]{1,0:T(8,128)(2,1)S(1)}, u32[]{:S(2)}, u32[]{:S(2)}) collective-permute-start(bf16[512,256]{1,0:T(8,128)(2,1)S(1)} %constant_dynamic-update-slice_fusion), channel_id=1, source_target_pairs={{2,0},{5,1},{0,2},{7,3},{6,4},{1,5},{4,6},{3,7},{10,8},{13,9},{8,1... | collective-permute-start | bytes 786440 | tf_op jit(solution)/shard_map/ppermute | solution.py:92
  54.6 1.8 %collective-permute-start.19 = (bf16[256,256]{1,0:T(8,128)(2,1)S(1)}, bf16[256,256]{1,0:T(8,128)(2,1)S(1)}, u32[]{:S(2)}, u32[]{:S(2)}) collective-permute-start(bf16[256,256]{1,0:T(8,128)(2,1)S(1)} %collective-permute-done.15.refs_2_), channel_id=1, source_target_pairs={{16,0},{17,1},{18,2},{19,3},{20,4},{21,5},{22,6},{23,7},{24,8},{25... | collective-permute-start | bytes 393224 | tf_op jit(solution)/shard_map/ppermute | solution.py:92
  57.1 4.9 %collective-permute-done.19.refs_5_ = bf16[256,256]{1,0:T(8,128)(2,1)S(1)} collective-permute-done((bf16[256,256]{1,0:T(8,128)(2,1)S(1)}, bf16[256,256]{1,0:T(8,128)(2,1)S(1)}, u32[]{:S(2)}, u32[]{:S(2)}) %collective-permute-start.19) | collective-permute-done | bytes 131104 | tf_op jit(solution)/shard_map/ppermute | solution.py:92
  64.2 2.1 %experts_in_first.1 = (f32[512,1536]{1,0:T(8,128)S(1)}, f32[512,1]{1,0:T(8,128)S(1)}) custom-call(s32[1]{0:T(128)} %bitcast.ctx_ref, s32[1]{0:T(128)} %bitcast.1.exp_ref, bf16[256,256]{1,0:T(8,128)(2,1)S(1)} %add_convert_fusion.6.refs_0_.refs_6_, bf16[256,256]{1,0:T(8,128)(2,1)S(1)} %collective-permute-done.14.refs_1_.refs_7_, ...), custom_call_target="tpu_custom_call" | custom-call | flops 1610612736 | bytes 8388608 | tf_op jit(solution)/shard_map/experts_in_first/pallas_call | solution.py:785
  66.4 2.2 %collective-permute-done.24.refs_5_ = bf16[256,256]{1,0:T(8,128)(2,1)S(1)} collective-permute-done((bf16[256,256]{1,0:T(8,128)(2,1)S(1)}, bf16[256,256]{1,0:T(8,128)(2,1)S(1)}, u32[]{:S(2)}, u32[]{:S(2)}) %collective-permute-start.24) | collective-permute-done | bytes 131104 | tf_op jit(solution)/shard_map/ppermute | solution.py:92
  70.3 1.4 %experts_in_second.3.refs_5_.act_ref = bf16[256,1664]{1,0:T(8,128)(2,1)S(1)} custom-call(s32[1]{0:T(128)} %bitcast.ctx_ref, s32[1]{0:T(128)} %bitcast.1.exp_ref, bf16[256,256]{1,0:T(8,128)(2,1)S(1)} %collective-permute-done.16.refs_0_.refs_8_, bf16[512,256]{1,0:T(8,128)(2,1)S(1)} %collective-permute-done.20.refs_6_.refs_1_.refs_11_, ...), custom_call_target="tpu_custom_call" | custom-call | flops 805306368 | bytes 8388608 | tf_op jit(solution)/shard_map/experts_in_second/pallas_call | solution.py:803
  72.7 1.8 %experts_out.2 = (f32[32,2048]{1,0:T(8,128)S(1)}, f32[32,2048]{1,0:T(8,128)S(1)}, bf16[32,2048]{1,0:T(8,128)(2,1)S(1)}, bf16[32,2048]{1,0:T(8,128)(2,1)S(1)}, f3...) custom-call(s32[1]{0:T(128)} %bitcast.ctx_ref, ...), custom_call_target="tpu_custom_call" | custom-call | flops 805306368 | bytes 8388608 | tf_op jit(solution)/shard_map/experts_out/pallas_call | solution.py:840
  76.1 1.5 %collective-permute-start.29 = (bf16[32,2048]{1,0:T(8,128)(2,1)S(1)}, bf16[32,2048]{1,0:T(8,128)(2,1)S(1)}, u32[]{:S(2)}, u32[]{:S(2)}) collective-permute-start(bf16[32,2048]{1,0:T(8,128)(2,1)S(1)} %get-tuple-element.113), channel_id=1, source_target_pairs={{2,0},{5,1},{0,2},{7,3},{6,4},{1,5},{4,6},{3,7},{10,8},{13,9},{8,1... | collective-permute-start | bytes 393224 | tf_op jit(solution)/shard_map/ppermute | solution.py:92
  77.6 1.8 %experts_out.3 = (f32[32,2048]{1,0:T(8,128)S(1)}, bf16[32,2048]{1,0:T(8,128)(2,1)S(1)}, bf16[32,2048]{1,0:T(8,128)(2,1)S(1)}, f32[32,2048]{1,0:T(8,128)S(1)}, f3...) custom-call(s32[1]{0:T(128)} %bitcast.ctx_ref, ...), custom_call_target="tpu_custom_call" | custom-call | flops 805306368 | bytes 8388608 | tf_op jit(solution)/shard_map/experts_out/pallas_call | solution.py:840
  79.4 1.7 %collective-permute-done.28 = bf16[32,2048]{1,0:T(8,128)(2,1)S(1)} collective-permute-done((bf16[32,2048]{1,0:T(8,128)(2,1)S(1)}, bf16[32,2048]{1,0:T(8,128)(2,1)S(1)}, u32[]{:S(2)}, u32[]{:S(2)}) %collective-permute-start.28) | collective-permute-done | bytes 131104 | tf_op jit(solution)/shard_map/ppermute | solution.py:92
  85.6 1.4 %collective-permute-start.31 = (bf16[32,2048]{1,0:T(8,128)(2,1)S(1)}, bf16[32,2048]{1,0:T(8,128)(2,1)S(1)}, u32[]{:S(2)}, u32[]{:S(2)}) collective-permute-start(bf16[32,2048]{1,0:T(8,128)(2,1)S(1)} %add_convert_fusion.5), channel_id=1, source_target_pairs={{16,0},{17,1},{18,2},{19,3},{20,4},{21,5},{22,6},{23,7},{24,8},{25... | collective-permute-start | bytes 393224 | tf_op jit(solution)/shard_map/ppermute | solution.py:92
  88.2 2.6 %collective-permute-done.34 = bf16[32,2048]{1,0:T(8,128)(2,1)S(1)} collective-permute-done((bf16[32,2048]{1,0:T(8,128)(2,1)S(1)}, bf16[32,2048]{1,0:T(8,128)(2,1)S(1)}, u32[]{:S(2)}, u32[]{:S(2)}) %collective-permute-start.34) | collective-permute-done | bytes 131104 | tf_op jit(solution)/shard_map/ppermute | solution.py:92
  91.9 1.4 %collective-permute-done.31 = bf16[32,2048]{1,0:T(8,128)(2,1)S(1)} collective-permute-done((bf16[32,2048]{1,0:T(8,128)(2,1)S(1)}, bf16[32,2048]{1,0:T(8,128)(2,1)S(1)}, u32[]{:S(2)}, u32[]{:S(2)}) %collective-permute-start.31) | collective-permute-done | bytes 131104 | tf_op jit(solution)/shard_map/ppermute | solution.py:92
  95.1 2.4 %collective-permute-start.37 = (bf16[32,2048]{1,0:T(8,128)(2,1)S(1)}, bf16[32,2048]{1,0:T(8,128)(2,1)S(1)}, u32[]{:S(2)}, u32[]{:S(2)}) collective-permute-start(bf16[32,2048]{1,0:T(8,128)(2,1)S(1)} %get-tuple-element.142), channel_id=1, source_target_pairs={{8,0},{9,1},{10,2},{11,3},{12,4},{13,5},{14,6},{15,7},{0,8},{1,9},... | collective-permute-start | bytes 393224 | tf_op jit(solution)/shard_map/ppermute | solution.py:92
  97.5 1.8 %collective-permute-done.36 = bf16[32,2048]{1,0:T(8,128)(2,1)S(1)} collective-permute-done((bf16[32,2048]{1,0:T(8,128)(2,1)S(1)}, bf16[32,2048]{1,0:T(8,128)(2,1)S(1)}, u32[]{:S(2)}, u32[]{:S(2)}) %collective-permute-start.36) | collective-permute-done | bytes 131104 | tf_op jit(solution)/shard_map/ppermute | solution.py:92
  99.3 2.3 %collective-permute-done.35 = bf16[32,2048]{1,0:T(8,128)(2,1)S(1)} collective-permute-done((bf16[32,2048]{1,0:T(8,128)(2,1)S(1)}, bf16[32,2048]{1,0:T(8,128)(2,1)S(1)}, u32[]{:S(2)}, u32[]{:S(2)}) %collective-permute-start.35) | collective-permute-done | bytes 131104 | tf_op jit(solution)/shard_map/ppermute | solution.py:92
  (97 shorter events, 33.8 us)
Async XLA Ops:
  1.2 13.8 %collective-permute-start = (bf16[64,1280]{1,0:T(8,128)(2,1)S(1)}, bf16[64,1280]{1,0:T(8,128)(2,1)S(1)}, u32[]{:S(2)}, u32[]{:S(2)}) collective-permute-start(bf16[64,1280]{1,0:T(8,128)(2,1)S(1)} %get-tuple-element.73._.refs_0_), channel_id=1, source_target_pairs={{16,0},{17,1},{18,2},{19,3},{20,4},{21,5},{22,6},{23,7},{24,8},{25... | collective-permute-start | bytes 491528 | tf_op jit(solution)/shard_map/ppermute | solution.py:92
  5.3 9.7 %collective-permute-start.1 = (bf16[64,1280]{1,0:T(8,128)(2,1)S(1)}, bf16[64,1280]{1,0:T(8,128)(2,1)S(1)}, u32[]{:S(2)}, u32[]{:S(2)}) collective-permute-start(bf16[64,1280]{1,0:T(8,128)(2,1)S(1)} %get-tuple-element.73._.refs_0_), channel_id=1, source_target_pairs={{4,0},{9,1},{6,2},{11,3},{0,4},{13,5},{2,6},{15,7},{12,8},{1,9},{1... | collective-permute-start | bytes 491528 | tf_op jit(solution)/shard_map/ppermute | solution.py:92
  6.8 8.2 %collective-permute-start.2 = (bf16[64,1280]{1,0:T(8,128)(2,1)S(1)}, bf16[64,1280]{1,0:T(8,128)(2,1)S(1)}, u32[]{:S(2)}, u32[]{:S(2)}) collective-permute-start(bf16[64,1280]{1,0:T(8,128)(2,1)S(1)} %get-tuple-element.73._.refs_0_), channel_id=1, source_target_pairs={{8,0},{5,1},{10,2},{7,3},{12,4},{1,5},{14,6},{3,7},{0,8},{13,9},{2... | collective-permute-start | bytes 491528 | tf_op jit(solution)/shard_map/ppermute | solution.py:92
  8.4 6.6 %collective-permute-start.3 = (bf16[4,16,640]{2,1,0:T(8,128)(2,1)S(1)}, bf16[4,16,640]{2,1,0:T(8,128)(2,1)S(1)}, u32[]{:S(2)}, u32[]{:S(2)}) collective-permute-start(bf16[4,16,640]{2,1,0:T(8,128)(2,1)S(1)} %get-tuple-element.74), channel_id=1, source_target_pairs={{8,0},{5,1},{10,2},{7,3},{12,4},{1,5},{14,6},{3,7},{0,8},{13,9},{2... | collective-permute-start | bytes 245768 | tf_op jit(solution)/shard_map/ppermute | solution.py:92
  15.0 9.7 %collective-permute-start.7 = (bf16[2048,768]{1,0:T(8,128)(2,1)S(1)}, bf16[2048,768]{1,0:T(8,128)(2,1)S(1)}, u32[]{:S(2)}, u32[]{:S(2)}) collective-permute-start(bf16[2048,768]{1,0:T(8,128)(2,1)S(1)} %get-tuple-element.82), channel_id=1, source_target_pairs={{0,1},{1,0},{2,3},{3,2},{4,5},{5,4},{6,7},{7,6},{8,9},{9,8},{10,11... | collective-permute-start | bytes 9437192 | tf_op jit(solution)/shard_map/ppermute | solution.py:25
  15.0 9.6 %collective-permute-start.5 = (bf16[64,1280]{1,0:T(8,128)(2,1)S(1)}, bf16[64,1280]{1,0:T(8,128)(2,1)S(1)}, u32[]{:S(2)}, u32[]{:S(2)}) collective-permute-start(bf16[64,1280]{1,0:T(8,128)(2,1)S(1)} %collective-permute-done.refs_1_), channel_id=1, source_target_pairs={{8,0},{5,1},{10,2},{7,3},{12,4},{1,5},{14,6},{3,7},{0,8},{13,9},{2... | collective-permute-start | bytes 491528 | tf_op jit(solution)/shard_map/ppermute | solution.py:92
  15.8 8.8 %collective-permute-start.4 = (bf16[128,1280]{1,0:T(8,128)(2,1)S(1)}, bf16[128,1280]{1,0:T(8,128)(2,1)S(1)}, u32[]{:S(2)}, u32[]{:S(2)}) collective-permute-start(bf16[128,1280]{1,0:T(8,128)(2,1)S(1)} %pad_maximum_fusion), channel_id=1, source_target_pairs={{4,0},{9,1},{6,2},{11,3},{0,4},{13,5},{2,6},{15,7},{12,8},{1,9},{1... | collective-permute-start | bytes 983048 | tf_op jit(solution)/shard_map/ppermute | solution.py:92
  17.4 7.2 %collective-permute-start.6 = (bf16[4,16,640]{2,1,0:T(8,128)(2,1)S(1)}, bf16[4,16,640]{2,1,0:T(8,128)(2,1)S(1)}, u32[]{:S(2)}, u32[]{:S(2)}) collective-permute-start(bf16[4,16,640]{2,1,0:T(8,128)(2,1)S(1)} %pad_maximum_fusion.6), channel_id=1, source_target_pairs={{4,0},{9,1},{6,2},{11,3},{0,4},{13,5},{2,6},{15,7},{12,8},{1,9},{1... | collective-permute-start | bytes 245768 | tf_op jit(solution)/shard_map/ppermute | solution.py:92
  24.6 7.0 %collective-permute-start.10 = (bf16[384,2048]{1,0:T(8,128)(2,1)S(1)}, bf16[384,2048]{1,0:T(8,128)(2,1)S(1)}, u32[]{:S(2)}, u32[]{:S(2)}) collective-permute-start(bf16[384,2048]{1,0:T(8,128)(2,1)S(1)} %get-tuple-element.88), channel_id=1, source_target_pairs={{0,1},{1,0},{2,3},{3,2},{4,5},{5,4},{6,7},{7,6},{8,9},{9,8},{10,11... | collective-permute-start | bytes 4718600 | tf_op jit(solution)/shard_map/ppermute | solution.py:25
  25.8 5.8 %collective-permute-start.9 = (bf16[64,1280]{1,0:T(8,128)(2,1)S(1)}, bf16[64,1280]{1,0:T(8,128)(2,1)S(1)}, u32[]{:S(2)}, u32[]{:S(2)}) collective-permute-start(bf16[64,1280]{1,0:T(8,128)(2,1)S(1)} %collective-permute-done.5.refs_5_), channel_id=1, source_target_pairs={{4,0},{9,1},{6,2},{11,3},{0,4},{13,5},{2,6},{15,7},{12,8},{1,9},{1... | collective-permute-start | bytes 491528 | tf_op jit(solution)/shard_map/ppermute | solution.py:92
  26.9 7.2 %collective-permute-start.11 = (bf16[4,16,640]{2,1,0:T(8,128)(2,1)S(1)}, bf16[4,16,640]{2,1,0:T(8,128)(2,1)S(1)}, u32[]{:S(2)}, u32[]{:S(2)}) collective-permute-start(bf16[4,16,640]{2,1,0:T(8,128)(2,1)S(1)} %pad_maximum_fusion.7), channel_id=1, source_target_pairs={{16,0},{17,1},{18,2},{19,3},{20,4},{21,5},{22,6},{23,7},{24,8},{25... | collective-permute-start | bytes 245768 | tf_op jit(solution)/shard_map/ppermute | solution.py:92
  35.9 6.0 %collective-permute-start.13 = (bf16[288,256]{1,0:T(8,128)(2,1)S(1)}, bf16[288,256]{1,0:T(8,128)(2,1)S(1)}, u32[]{:S(2)}, u32[]{:S(2)}) collective-permute-start(bf16[288,256]{1,0:T(8,128)(2,1)S(1)} %pad_maximum_fusion.5), channel_id=1, source_target_pairs={{0,2},{1,3},{2,0},{3,1},{4,6},{5,7},{6,4},{7,5},{8,10},{9,11},{10,... | collective-permute-start | bytes 442376 | tf_op jit(solution)/shard_map/ppermute | solution.py:25
  42.0 8.5 %collective-permute-start.14 = (bf16[256,256]{1,0:T(8,128)(2,1)S(1)}, bf16[256,256]{1,0:T(8,128)(2,1)S(1)}, u32[]{:S(2)}, u32[]{:S(2)}) collective-permute-start(bf16[256,256]{1,0:T(8,128)(2,1)S(1)} %add_convert_fusion.6.refs_0_.refs_6_), channel_id=1, source_target_pairs={{16,0},{17,1},{18,2},{19,3},{20,4},{21,5},{22,6},{23,7},{24,8},{25... | collective-permute-start | bytes 393224 | tf_op jit(solution)/shard_map/ppermute | solution.py:92
  43.3 7.2 %collective-permute-start.15 = (bf16[256,256]{1,0:T(8,128)(2,1)S(1)}, bf16[256,256]{1,0:T(8,128)(2,1)S(1)}, u32[]{:S(2)}, u32[]{:S(2)}) collective-permute-start(bf16[256,256]{1,0:T(8,128)(2,1)S(1)} %add_convert_fusion.6.refs_0_.refs_6_), channel_id=1, source_target_pairs={{6,0},{7,1},{4,2},{5,3},{2,4},{3,5},{0,6},{1,7},{14,8},{15,9},{12,... | collective-permute-start | bytes 393224 | tf_op jit(solution)/shard_map/ppermute | solution.py:92
  45.1 6.0 %collective-permute-start.16 = (bf16[256,256]{1,0:T(8,128)(2,1)S(1)}, bf16[256,256]{1,0:T(8,128)(2,1)S(1)}, u32[]{:S(2)}, u32[]{:S(2)}) collective-permute-start(bf16[256,256]{1,0:T(8,128)(2,1)S(1)} %add_convert_fusion.6.refs_0_.refs_6_), channel_id=1, source_target_pairs={{8,0},{9,1},{10,2},{11,3},{12,4},{13,5},{14,6},{15,7},{0,8},{1,9},... | collective-permute-start | bytes 393224 | tf_op jit(solution)/shard_map/ppermute | solution.py:92
  51.9 10.6 %collective-permute-start.20 = (bf16[512,256]{1,0:T(8,128)(2,1)S(1)}, bf16[512,256]{1,0:T(8,128)(2,1)S(1)}, u32[]{:S(2)}, u32[]{:S(2)}) collective-permute-start(bf16[512,256]{1,0:T(8,128)(2,1)S(1)} %constant_dynamic-update-slice_fusion), channel_id=1, source_target_pairs={{2,0},{5,1},{0,2},{7,3},{6,4},{1,5},{4,6},{3,7},{10,8},{13,9},{8,1... | collective-permute-start | bytes 786440 | tf_op jit(solution)/shard_map/ppermute | solution.py:92
  53.5 9.1 %collective-permute-start.21 = (bf16[512,256]{1,0:T(8,128)(2,1)S(1)}, bf16[512,256]{1,0:T(8,128)(2,1)S(1)}, u32[]{:S(2)}, u32[]{:S(2)}) collective-permute-start(bf16[512,256]{1,0:T(8,128)(2,1)S(1)} %constant_dynamic-update-slice_fusion), channel_id=1, source_target_pairs={{4,0},{3,1},{6,2},{1,3},{0,4},{7,5},{2,6},{5,7},{12,8},{11,9},{14,... | collective-permute-start | bytes 786440 | tf_op jit(solution)/shard_map/ppermute | solution.py:92
  54.6 7.4 %collective-permute-start.19 = (bf16[256,256]{1,0:T(8,128)(2,1)S(1)}, bf16[256,256]{1,0:T(8,128)(2,1)S(1)}, u32[]{:S(2)}, u32[]{:S(2)}) collective-permute-start(bf16[256,256]{1,0:T(8,128)(2,1)S(1)} %collective-permute-done.15.refs_2_), channel_id=1, source_target_pairs={{16,0},{17,1},{18,2},{19,3},{20,4},{21,5},{22,6},{23,7},{24,8},{25... | collective-permute-start | bytes 393224 | tf_op jit(solution)/shard_map/ppermute | solution.py:92
  56.4 6.1 %collective-permute-start.22 = (bf16[256,256]{1,0:T(8,128)(2,1)S(1)}, bf16[256,256]{1,0:T(8,128)(2,1)S(1)}, u32[]{:S(2)}, u32[]{:S(2)}) collective-permute-start(bf16[256,256]{1,0:T(8,128)(2,1)S(1)} %collective-permute-done.14.refs_1_.refs_7_), channel_id=1, source_target_pairs={{8,0},{9,1},{10,2},{11,3},{12,4},{13,5},{14,6},{15,7},{0,8},{1,9},... | collective-permute-start | bytes 393224 | tf_op jit(solution)/shard_map/ppermute | solution.py:92
  62.6 6.4 %collective-permute-start.23 = (bf16[512,256]{1,0:T(8,128)(2,1)S(1)}, bf16[512,256]{1,0:T(8,128)(2,1)S(1)}, u32[]{:S(2)}, u32[]{:S(2)}) collective-permute-start(bf16[512,256]{1,0:T(8,128)(2,1)S(1)} %pad_maximum_fusion.1), channel_id=1, source_target_pairs={{4,0},{3,1},{6,2},{1,3},{0,4},{7,5},{2,6},{5,7},{12,8},{11,9},{14,... | collective-permute-start | bytes 786440 | tf_op jit(solution)/shard_map/ppermute | solution.py:92
  71.7 5.9 %collective-permute-start.30 = (bf16[256,1664]{1,0:T(8,128)(2,1)S(1)}, bf16[256,1664]{1,0:T(8,128)(2,1)S(1)}, u32[]{:S(2)}, u32[]{:S(2)}) collective-permute-start(bf16[256,1664]{1,0:T(8,128)(2,1)S(1)} %experts_in_second.3.refs_5_.act_ref), channel_id=1, source_target_pairs={{0,1},{1,0},{2,3},{3,2},{4,5},{5,4},{6,7},{7,6},{8,9},{9,8},{10,11... | collective-permute-start | bytes 2555912 | tf_op jit(solution)/shard_map/ppermute | solution.py:25
  74.5 7.8 %collective-permute-start.27 = (bf16[64,2048]{1,0:T(8,128)(2,1)S(1)}, bf16[64,2048]{1,0:T(8,128)(2,1)S(1)}, u32[]{:S(2)}, u32[]{:S(2)}) collective-permute-start(bf16[64,2048]{1,0:T(8,128)(2,1)S(1)} %pad_maximum_fusion.2), channel_id=1, source_target_pairs={{4,0},{3,1},{6,2},{1,3},{0,4},{7,5},{2,6},{5,7},{12,8},{11,9},{14,... | collective-permute-start | bytes 786440 | tf_op jit(solution)/shard_map/ppermute | solution.py:92
  75.4 5.7 %collective-permute-start.28 = (bf16[32,2048]{1,0:T(8,128)(2,1)S(1)}, bf16[32,2048]{1,0:T(8,128)(2,1)S(1)}, u32[]{:S(2)}, u32[]{:S(2)}) collective-permute-start(bf16[32,2048]{1,0:T(8,128)(2,1)S(1)} %get-tuple-element.112), channel_id=1, source_target_pairs={{8,0},{9,1},{10,2},{11,3},{12,4},{13,5},{14,6},{15,7},{0,8},{1,9},... | collective-permute-start | bytes 393224 | tf_op jit(solution)/shard_map/ppermute | solution.py:92
  82.4 11.0 %collective-permute-start.33 = (bf16[64,2048]{1,0:T(8,128)(2,1)S(1)}, bf16[64,2048]{1,0:T(8,128)(2,1)S(1)}, u32[]{:S(2)}, u32[]{:S(2)}) collective-permute-start(bf16[64,2048]{1,0:T(8,128)(2,1)S(1)} %pad_maximum_fusion.4), channel_id=1, source_target_pairs={{4,0},{3,1},{6,2},{1,3},{0,4},{7,5},{2,6},{5,7},{12,8},{11,9},{14,... | collective-permute-start | bytes 786440 | tf_op jit(solution)/shard_map/ppermute | solution.py:92
  83.4 10.0 %collective-permute-start.32 = (bf16[64,2048]{1,0:T(8,128)(2,1)S(1)}, bf16[64,2048]{1,0:T(8,128)(2,1)S(1)}, u32[]{:S(2)}, u32[]{:S(2)}) collective-permute-start(bf16[64,2048]{1,0:T(8,128)(2,1)S(1)} %pad_maximum_fusion.3), channel_id=1, source_target_pairs={{2,0},{5,1},{0,2},{7,3},{6,4},{1,5},{4,6},{3,7},{10,8},{13,9},{8,1... | collective-permute-start | bytes 786440 | tf_op jit(solution)/shard_map/ppermute | solution.py:92
  84.7 6.1 %collective-permute-start.34 = (bf16[32,2048]{1,0:T(8,128)(2,1)S(1)}, bf16[32,2048]{1,0:T(8,128)(2,1)S(1)}, u32[]{:S(2)}, u32[]{:S(2)}) collective-permute-start(bf16[32,2048]{1,0:T(8,128)(2,1)S(1)} %get-tuple-element.143), channel_id=1, source_target_pairs={{8,0},{9,1},{10,2},{11,3},{12,4},{13,5},{14,6},{15,7},{0,8},{1,9},... | collective-permute-start | bytes 393224 | tf_op jit(solution)/shard_map/ppermute | solution.py:92
  85.6 7.7 %collective-permute-start.31 = (bf16[32,2048]{1,0:T(8,128)(2,1)S(1)}, bf16[32,2048]{1,0:T(8,128)(2,1)S(1)}, u32[]{:S(2)}, u32[]{:S(2)}) collective-permute-start(bf16[32,2048]{1,0:T(8,128)(2,1)S(1)} %add_convert_fusion.5), channel_id=1, source_target_pairs={{16,0},{17,1},{18,2},{19,3},{20,4},{21,5},{22,6},{23,7},{24,8},{25... | collective-permute-start | bytes 393224 | tf_op jit(solution)/shard_map/ppermute | solution.py:92
  87.0 10.5 %collective-permute-start.38 = (bf16[32,2048]{1,0:T(8,128)(2,1)S(1)}, bf16[32,2048]{1,0:T(8,128)(2,1)S(1)}, u32[]{:S(2)}, u32[]{:S(2)}) collective-permute-start(bf16[32,2048]{1,0:T(8,128)(2,1)S(1)} %get-tuple-element.139), channel_id=1, source_target_pairs={{2,0},{5,1},{0,2},{7,3},{6,4},{1,5},{4,6},{3,7},{10,8},{13,9},{8,1... | collective-permute-start | bytes 393224 | tf_op jit(solution)/shard_map/ppermute | solution.py:92
  90.8 6.7 %collective-permute-start.39 = (bf16[32,2048]{1,0:T(8,128)(2,1)S(1)}, bf16[32,2048]{1,0:T(8,128)(2,1)S(1)}, u32[]{:S(2)}, u32[]{:S(2)}) collective-permute-start(bf16[32,2048]{1,0:T(8,128)(2,1)S(1)} %get-tuple-element.140), channel_id=1, source_target_pairs={{4,0},{3,1},{6,2},{1,3},{0,4},{7,5},{2,6},{5,7},{12,8},{11,9},{14,... | collective-permute-start | bytes 393224 | tf_op jit(solution)/shard_map/ppermute | solution.py:92
  93.4 5.9 %collective-permute-start.36 = (bf16[32,2048]{1,0:T(8,128)(2,1)S(1)}, bf16[32,2048]{1,0:T(8,128)(2,1)S(1)}, u32[]{:S(2)}, u32[]{:S(2)}) collective-permute-start(bf16[32,2048]{1,0:T(8,128)(2,1)S(1)} %add_convert_fusion.1), channel_id=1, source_target_pairs={{6,0},{7,1},{4,2},{5,3},{2,4},{3,5},{0,6},{1,7},{14,8},{15,9},{12,... | collective-permute-start | bytes 393224 | tf_op jit(solution)/shard_map/ppermute | solution.py:92
  94.9 6.7 %collective-permute-start.35 = (bf16[32,2048]{1,0:T(8,128)(2,1)S(1)}, bf16[32,2048]{1,0:T(8,128)(2,1)S(1)}, u32[]{:S(2)}, u32[]{:S(2)}) collective-permute-start(bf16[32,2048]{1,0:T(8,128)(2,1)S(1)} %get-tuple-element.141), channel_id=1, source_target_pairs={{16,0},{17,1},{18,2},{19,3},{20,4},{21,5},{22,6},{23,7},{24,8},{25... | collective-permute-start | bytes 393224 | tf_op jit(solution)/shard_map/ppermute | solution.py:92
  95.1 6.7 %collective-permute-start.37 = (bf16[32,2048]{1,0:T(8,128)(2,1)S(1)}, bf16[32,2048]{1,0:T(8,128)(2,1)S(1)}, u32[]{:S(2)}, u32[]{:S(2)}) collective-permute-start(bf16[32,2048]{1,0:T(8,128)(2,1)S(1)} %get-tuple-element.142), channel_id=1, source_target_pairs={{8,0},{9,1},{10,2},{11,3},{12,4},{13,5},{14,6},{15,7},{0,8},{1,9},... | collective-permute-start | bytes 393224 | tf_op jit(solution)/shard_map/ppermute | solution.py:92
  (12 other events, 97.4 us)

commit v12 on v11

--- a/solution.py
+++ b/solution.py
@@ -573,6 +573,15 @@
                 cols = state.shape[1]
                 at = pl.ds(pl.multiple_of(lax.bitwise_xor(my_ctx, c_off) * cols, cols), cols)
                 ref[:, at] = ref[:, at] + state
+
+
+def join_kernel(ctx_count, exp_ref, mine_ref, came_ref, out_ref):
+    core = lax.bitwise_and(exp_ref[0], 1)
+    cols = mine_ref.shape[1] // ctx_count
+    for c in range(ctx_count):
+        for which, ref in enumerate((mine_ref, came_ref)):
+            at = pl.multiple_of((2 * c + lax.bitwise_xor(core, which)) * cols, cols)
+            out_ref[:, pl.ds(at, cols)] = ref[:, c * cols : (c + 1) * cols]
 
 
 def shards(
@@ -893,10 +902,13 @@
     core = lax.bitwise_and(my_exp[0], 1)
     mine = jnp.where(core == 0, total[:tok], total[tok:]).astype(bf16)
     came = from_offset(jnp.where(core == 0, total[tok:], total[:tok]).astype(bf16), 1)
-    mine = mine.reshape(tok, ctx_count, 1, cols)
-    came = came.reshape(tok, ctx_count, 1, cols)
-    result = jnp.where(core == 0, jnp.concatenate([mine, came], axis=2), jnp.concatenate([came, mine], axis=2))
-    return result.reshape(tok, model_width)
+    return pl.pallas_call(
+        functools.partial(join_kernel, ctx_count),
+        in_specs=[smem, vmem, vmem],
+        out_specs=vmem,
+        out_shape=jax.ShapeDtypeStruct((tok, model_width), bf16),
+        name="join",
+    )(my_exp, mine, came)
 
 
 def solution(mesh):

time: 104 us -> 106 us (1.019)
  Pallas kernels: 20.2 us -> 21.7 us
    pallas_call x0 -> x1, Pallas kernels: none -> 1.54 us  [shards(): pl.pallas_call(functools.partial(join_kernel, ctx_count), in_specs=[smem,...]
where the time goes in v12:
time: 106 us
  starting transfers between devices  45.1 us (43%)
  waiting for transfers between devices  37.1 us (35%)
  Pallas kernels  21.7 us (20%)
  other arithmetic  1.19 us (1%)
    ppermute x34, starting transfers between devices, follow(): return lax.ppermute(array, ('ctx', 'exp'), pairs)  41.5 us
    ppermute x34, waiting for transfers between devices, follow(): return lax.ppermute(array, ('ctx', 'exp'), pairs)  29.5 us
    ppermute x7, waiting for transfers between devices, from_offset(): lax.ppermute(array, 'exp', [(i, i ^ offset) for i in range(lax.axis_size(...  7.55 us
    pallas_call x2, Pallas kernels, attend(): pl.pallas_call(functools.partial(attend_kernel, (ctx_count, exp_count, to...  5.34 us
    pallas_call x2, Pallas kernels, shards(): pl.pallas_call(functools.partial(experts_out_kernel, (ctx_count, exp_coun...  3.63 us
    ppermute x7, starting transfers between devices, from_offset(): lax.ppermute(array, 'exp', [(i, i ^ offset) for i in range(lax.axis_size(...  3.54 us
    pallas_call x1, Pallas kernels, deq_in(): pl.pallas_call(functools.partial(deq_in_kernel, ctx_count), in_specs=[pl....  3 us
    pallas_call x2, Pallas kernels, shards(): pl.pallas_call(functools.partial(experts_in_second, (ctx_count, x_count,...  2.59 us
  transfers between devices with their start and end apart: 41, of which 24 were waited for; matrix products, arithmetic and copies ran while one was open for 0% of the time, Pallas kernels for 17%

profile of v12, /device:TPU:0, one launch (start us, length us, event | category | flops | bytes accessed | tf_op | source)
XLA Modules:
  0.0 106.0 jit_solution(12414339014686075333)
XLA Ops:
  1.2 4.1 %collective-permute-start = (bf16[64,1280]{1,0:T(8,128)(2,1)S(1)}, bf16[64,1280]{1,0:T(8,128)(2,1)S(1)}, u32[]{:S(2)}, u32[]{:S(2)}) collective-permute-start(bf16[64,1280]{1,0:T(8,128)(2,1)S(1)} %get-tuple-element.73._.refs_0_), channel_id=1, source_target_pairs={{16,0},{17,1},{18,2},{19,3},{20,4},{21,5},{22,6},{23,7},{24,8},{25... | collective-permute-start | bytes 491528 | tf_op jit(solution)/shard_map/ppermute | solution.py:92
  5.3 1.5 %collective-permute-start.1 = (bf16[64,1280]{1,0:T(8,128)(2,1)S(1)}, bf16[64,1280]{1,0:T(8,128)(2,1)S(1)}, u32[]{:S(2)}, u32[]{:S(2)}) collective-permute-start(bf16[64,1280]{1,0:T(8,128)(2,1)S(1)} %get-tuple-element.73._.refs_0_), channel_id=1, source_target_pairs={{4,0},{9,1},{6,2},{11,3},{0,4},{13,5},{2,6},{15,7},{12,8},{1,9},{1... | collective-permute-start | bytes 491528 | tf_op jit(solution)/shard_map/ppermute | solution.py:92
  6.8 1.6 %collective-permute-start.2 = (bf16[64,1280]{1,0:T(8,128)(2,1)S(1)}, bf16[64,1280]{1,0:T(8,128)(2,1)S(1)}, u32[]{:S(2)}, u32[]{:S(2)}) collective-permute-start(bf16[64,1280]{1,0:T(8,128)(2,1)S(1)} %get-tuple-element.73._.refs_0_), channel_id=1, source_target_pairs={{8,0},{5,1},{10,2},{7,3},{12,4},{1,5},{14,6},{3,7},{0,8},{13,9},{2... | collective-permute-start | bytes 491528 | tf_op jit(solution)/shard_map/ppermute | solution.py:92
  8.8 3.0 %dequant_in.1 = (bf16[2048,768]{1,0:T(8,128)(2,1)S(1)}, bf16[2048,768]{1,0:T(8,128)(2,1)S(1)}) custom-call(s32[1]{0:T(128)} %bitcast.exp_ref, s32[3,1,32]{2,1,0:T(1,128)} %bitcast.13, s32[3,1,32]{2,1,0:T(1,128)} %bitcast.14, bf16[1,4096,384]{2,1,0:T(8,128)(2,1)} %gate_hbm.1, bf16[1,4096,384]{2,1,0:T(8,128)(2,1)} %up_hbm.1, ...), custom_call_target="tpu_custom_call" | custom-call | flops 3145728 | bytes 12582912 | tf_op jit(solution)/shard_map/dequant_in/pallas_call | solution.py:269
  11.8 3.1 %collective-permute-done.3._.refs_1_ = bf16[4,16,640]{2,1,0:T(8,128)(2,1)S(1)} collective-permute-done((bf16[4,16,640]{2,1,0:T(8,128)(2,1)S(1)}, bf16[4,16,640]{2,1,0:T(8,128)(2,1)S(1)}, u32[]{:S(2)}, u32[]{:S(2)}) %collective-permute-start.3) | collective-permute-done | bytes 81952 | tf_op jit(solution)/shard_map/ppermute | solution.py:92
  15.8 1.6 %collective-permute-start.4 = (bf16[128,1280]{1,0:T(8,128)(2,1)S(1)}, bf16[128,1280]{1,0:T(8,128)(2,1)S(1)}, u32[]{:S(2)}, u32[]{:S(2)}) collective-permute-start(bf16[128,1280]{1,0:T(8,128)(2,1)S(1)} %pad_maximum_fusion), channel_id=1, source_target_pairs={{4,0},{9,1},{6,2},{11,3},{0,4},{13,5},{2,6},{15,7},{12,8},{1,9},{1... | collective-permute-start | bytes 983048 | tf_op jit(solution)/shard_map/ppermute | solution.py:92
  18.0 1.7 %collective-permute-start.8 = (bf16[64,256]{1,0:T(8,128)(2,1)S(1)}, bf16[64,256]{1,0:T(8,128)(2,1)S(1)}, u32[]{:S(2)}, u32[]{:S(2)}) collective-permute-start(bf16[64,256]{1,0:T(8,128)(2,1)S(1)} %slice.75), channel_id=1, source_target_pairs={{12,0},{13,1},{14,2},{15,3},{8,4},{9,5},{10,6},{11,7},{4,8},{5,9},... | collective-permute-start | bytes 98312 | tf_op jit(solution)/shard_map/ppermute | solution.py:92
  19.7 2.1 %dequant_down.1 = (bf16[384,2048]{1,0:T(8,128)(2,1)S(1)}, bf16[384,2048]{1,0:T(8,128)(2,1)S(1)}) custom-call(s32[1]{0:T(128)} %bitcast.exp_ref, s32[3,1,32]{2,1,0:T(1,128)} %bitcast.15, bf16[1,384,4096]{2,1,0:T(8,128)(2,1)} %down_hbm.1, bf16[4,16,640]{2,1,0:T(8,128)(2,1)S(1)} %collective-permute-done.3._.refs_1_), custom_call_target="tpu_custom_call" | custom-call | flops 1572864 | bytes 6291456 | tf_op jit(solution)/shard_map/dequant_down/pallas_call | solution.py:318
  26.9 1.4 %collective-permute-start.11 = (bf16[4,16,640]{2,1,0:T(8,128)(2,1)S(1)}, bf16[4,16,640]{2,1,0:T(8,128)(2,1)S(1)}, u32[]{:S(2)}, u32[]{:S(2)}) collective-permute-start(bf16[4,16,640]{2,1,0:T(8,128)(2,1)S(1)} %pad_maximum_fusion.7), channel_id=1, source_target_pairs={{16,0},{17,1},{18,2},{19,3},{20,4},{21,5},{22,6},{23,7},{24,8},{25... | collective-permute-start | bytes 245768 | tf_op jit(solution)/shard_map/ppermute | solution.py:92
  28.3 3.2 %attend.2.refs_7_ = bf16[512,1024]{1,0:T(8,128)(2,1)S(1)} custom-call(s32[1]{0:T(128)} %bitcast.1.ctx_ref, s32[1]{0:T(128)} %bitcast.exp_ref, s32[8]{0:T(128)S(1)} %copy-done.2, bf16[64,1280]{1,0:T(8,128)(2,1)S(1)} %get-tuple-element.73._.refs_0_, bf16[64,1280]{1,0:T(8,128)(2,1)S(1)} %collective-permute-done.refs_1_, ...), custom_call_target="tpu_custom_call" | custom-call | flops 939524096 | bytes 4194304 | tf_op jit(solution)/shard_map/attend/pallas_call | solution.py:721
  31.6 2.1 %attend.3 = (f32[256,256]{1,0:T(8,128)S(1)}, f32[256,256]{1,0:T(8,128)S(1)}, bf16[512,256]{1,0:T(8,128)(2,1)S(1)}) custom-call(s32[1]{0:T(128)} %bitcast.1.ctx_ref, s32[1]{0:T(128)} %bitcast.exp_ref, s32[8]{0:T(128)S(1)} %copy-done.2, bf16[64,1280]{1,0:T(8,128)(2,1)S(1)} %get-tuple-element.73._.refs_0_, bf16[64,1280]{1,0:T(8,128)(2,1)S(1)} %collective-permute-done.refs_1_, ...), custom_call_target="tpu_custom_call" | custom-call | flops 671088640 | bytes 4194304 | tf_op jit(solution)/shard_map/attend/pallas_call | solution.py:721
  34.4 1.5 %collective-permute-done.12.refs_1_ = bf16[544,256]{1,0:T(8,128)(2,1)S(1)} collective-permute-done((bf16[544,256]{1,0:T(8,128)(2,1)S(1)}, bf16[544,256]{1,0:T(8,128)(2,1)S(1)}, u32[]{:S(2)}, u32[]{:S(2)}) %collective-permute-start.12) | collective-permute-done | bytes 278560 | tf_op jit(solution)/shard_map/ppermute | solution.py:25
  35.9 1.6 %collective-permute-start.13 = (bf16[288,256]{1,0:T(8,128)(2,1)S(1)}, bf16[288,256]{1,0:T(8,128)(2,1)S(1)}, u32[]{:S(2)}, u32[]{:S(2)}) collective-permute-start(bf16[288,256]{1,0:T(8,128)(2,1)S(1)} %pad_maximum_fusion.5), channel_id=1, source_target_pairs={{0,2},{1,3},{2,0},{3,1},{4,6},{5,7},{6,4},{7,5},{8,10},{9,11},{10,... | collective-permute-start | bytes 442376 | tf_op jit(solution)/shard_map/ppermute | solution.py:25
  37.6 4.3 %collective-permute-done.13.refs_2_ = bf16[288,256]{1,0:T(8,128)(2,1)S(1)} collective-permute-done((bf16[288,256]{1,0:T(8,128)(2,1)S(1)}, bf16[288,256]{1,0:T(8,128)(2,1)S(1)}, u32[]{:S(2)}, u32[]{:S(2)}) %collective-permute-start.13) | collective-permute-done | bytes 147488 | tf_op jit(solution)/shard_map/ppermute | solution.py:25
  43.3 1.9 %collective-permute-start.15 = (bf16[256,256]{1,0:T(8,128)(2,1)S(1)}, bf16[256,256]{1,0:T(8,128)(2,1)S(1)}, u32[]{:S(2)}, u32[]{:S(2)}) collective-permute-start(bf16[256,256]{1,0:T(8,128)(2,1)S(1)} %add_convert_fusion.6.refs_0_.refs_6_), channel_id=1, source_target_pairs={{6,0},{7,1},{4,2},{5,3},{2,4},{3,5},{0,6},{1,7},{14,8},{15,9},{12,... | collective-permute-start | bytes 393224 | tf_op jit(solution)/shard_map/ppermute | solution.py:92
  48.1 2.4 %collective-permute-done.14.refs_1_.refs_7_ = bf16[256,256]{1,0:T(8,128)(2,1)S(1)} collective-permute-done((bf16[256,256]{1,0:T(8,128)(2,1)S(1)}, bf16[256,256]{1,0:T(8,128)(2,1)S(1)}, u32[]{:S(2)}, u32[]{:S(2)}) %collective-permute-start.14) | collective-permute-done | bytes 131104 | tf_op jit(solution)/shard_map/ppermute | solution.py:92
  51.9 1.6 %collective-permute-start.20 = (bf16[512,256]{1,0:T(8,128)(2,1)S(1)}, bf16[512,256]{1,0:T(8,128)(2,1)S(1)}, u32[]{:S(2)}, u32[]{:S(2)}) collective-permute-start(bf16[512,256]{1,0:T(8,128)(2,1)S(1)} %constant_dynamic-update-slice_fusion), channel_id=1, source_target_pairs={{2,0},{5,1},{0,2},{7,3},{6,4},{1,5},{4,6},{3,7},{10,8},{13,9},{8,1... | collective-permute-start | bytes 786440 | tf_op jit(solution)/shard_map/ppermute | solution.py:92
  54.6 1.8 %collective-permute-start.19 = (bf16[256,256]{1,0:T(8,128)(2,1)S(1)}, bf16[256,256]{1,0:T(8,128)(2,1)S(1)}, u32[]{:S(2)}, u32[]{:S(2)}) collective-permute-start(bf16[256,256]{1,0:T(8,128)(2,1)S(1)} %collective-permute-done.15.refs_2_), channel_id=1, source_target_pairs={{16,0},{17,1},{18,2},{19,3},{20,4},{21,5},{22,6},{23,7},{24,8},{25... | collective-permute-start | bytes 393224 | tf_op jit(solution)/shard_map/ppermute | solution.py:92
  57.1 4.9 %collective-permute-done.19.refs_5_ = bf16[256,256]{1,0:T(8,128)(2,1)S(1)} collective-permute-done((bf16[256,256]{1,0:T(8,128)(2,1)S(1)}, bf16[256,256]{1,0:T(8,128)(2,1)S(1)}, u32[]{:S(2)}, u32[]{:S(2)}) %collective-permute-start.19) | collective-permute-done | bytes 131104 | tf_op jit(solution)/shard_map/ppermute | solution.py:92
  64.2 2.1 %experts_in_first.1 = (f32[512,1536]{1,0:T(8,128)S(1)}, f32[512,1]{1,0:T(8,128)S(1)}) custom-call(s32[1]{0:T(128)} %bitcast.1.ctx_ref, s32[1]{0:T(128)} %bitcast.exp_ref, bf16[256,256]{1,0:T(8,128)(2,1)S(1)} %add_convert_fusion.6.refs_0_.refs_6_, bf16[256,256]{1,0:T(8,128)(2,1)S(1)} %collective-permute-done.14.refs_1_.refs_7_, ...), custom_call_target="tpu_custom_call" | custom-call | flops 1610612736 | bytes 8388608 | tf_op jit(solution)/shard_map/experts_in_first/pallas_call | solution.py:794
  66.4 2.2 %collective-permute-done.24.refs_5_ = bf16[256,256]{1,0:T(8,128)(2,1)S(1)} collective-permute-done((bf16[256,256]{1,0:T(8,128)(2,1)S(1)}, bf16[256,256]{1,0:T(8,128)(2,1)S(1)}, u32[]{:S(2)}, u32[]{:S(2)}) %collective-permute-start.24) | collective-permute-done | bytes 131104 | tf_op jit(solution)/shard_map/ppermute | solution.py:92
  72.7 1.8 %experts_out.2 = (f32[32,2048]{1,0:T(8,128)S(1)}, f32[32,2048]{1,0:T(8,128)S(1)}, bf16[32,2048]{1,0:T(8,128)(2,1)S(1)}, bf16[32,2048]{1,0:T(8,128)(2,1)S(1)}, f3...) custom-call(s32[1]{0:T(128)} %bitcast.1.ctx_ref, ...), custom_call_target="tpu_custom_call" | custom-call | flops 805306368 | bytes 8388608 | tf_op jit(solution)/shard_map/experts_out/pallas_call | solution.py:849
  76.1 1.5 %collective-permute-start.29 = (bf16[32,2048]{1,0:T(8,128)(2,1)S(1)}, bf16[32,2048]{1,0:T(8,128)(2,1)S(1)}, u32[]{:S(2)}, u32[]{:S(2)}) collective-permute-start(bf16[32,2048]{1,0:T(8,128)(2,1)S(1)} %get-tuple-element.113), channel_id=1, source_target_pairs={{2,0},{5,1},{0,2},{7,3},{6,4},{1,5},{4,6},{3,7},{10,8},{13,9},{8,1... | collective-permute-start | bytes 393224 | tf_op jit(solution)/shard_map/ppermute | solution.py:92
  77.6 1.8 %experts_out.3 = (f32[32,2048]{1,0:T(8,128)S(1)}, bf16[32,2048]{1,0:T(8,128)(2,1)S(1)}, bf16[32,2048]{1,0:T(8,128)(2,1)S(1)}, f32[32,2048]{1,0:T(8,128)S(1)}, f3...) custom-call(s32[1]{0:T(128)} %bitcast.1.ctx_ref, ...), custom_call_target="tpu_custom_call" | custom-call | flops 805306368 | bytes 8388608 | tf_op jit(solution)/shard_map/experts_out/pallas_call | solution.py:849
  79.4 1.7 %collective-permute-done.28 = bf16[32,2048]{1,0:T(8,128)(2,1)S(1)} collective-permute-done((bf16[32,2048]{1,0:T(8,128)(2,1)S(1)}, bf16[32,2048]{1,0:T(8,128)(2,1)S(1)}, u32[]{:S(2)}, u32[]{:S(2)}) %collective-permute-start.28) | collective-permute-done | bytes 131104 | tf_op jit(solution)/shard_map/ppermute | solution.py:92
  85.6 1.4 %collective-permute-start.31 = (bf16[32,2048]{1,0:T(8,128)(2,1)S(1)}, bf16[32,2048]{1,0:T(8,128)(2,1)S(1)}, u32[]{:S(2)}, u32[]{:S(2)}) collective-permute-start(bf16[32,2048]{1,0:T(8,128)(2,1)S(1)} %add_convert_fusion.5), channel_id=1, source_target_pairs={{16,0},{17,1},{18,2},{19,3},{20,4},{21,5},{22,6},{23,7},{24,8},{25... | collective-permute-start | bytes 393224 | tf_op jit(solution)/shard_map/ppermute | solution.py:92
  88.2 2.6 %collective-permute-done.34 = bf16[32,2048]{1,0:T(8,128)(2,1)S(1)} collective-permute-done((bf16[32,2048]{1,0:T(8,128)(2,1)S(1)}, bf16[32,2048]{1,0:T(8,128)(2,1)S(1)}, u32[]{:S(2)}, u32[]{:S(2)}) %collective-permute-start.34) | collective-permute-done | bytes 131104 | tf_op jit(solution)/shard_map/ppermute | solution.py:92
  91.9 1.4 %collective-permute-done.31 = bf16[32,2048]{1,0:T(8,128)(2,1)S(1)} collective-permute-done((bf16[32,2048]{1,0:T(8,128)(2,1)S(1)}, bf16[32,2048]{1,0:T(8,128)(2,1)S(1)}, u32[]{:S(2)}, u32[]{:S(2)}) %collective-permute-start.31) | collective-permute-done | bytes 131104 | tf_op jit(solution)/shard_map/ppermute | solution.py:92
  95.1 2.4 %collective-permute-start.37 = (bf16[32,2048]{1,0:T(8,128)(2,1)S(1)}, bf16[32,2048]{1,0:T(8,128)(2,1)S(1)}, u32[]{:S(2)}, u32[]{:S(2)}) collective-permute-start(bf16[32,2048]{1,0:T(8,128)(2,1)S(1)} %get-tuple-element.142), channel_id=1, source_target_pairs={{8,0},{9,1},{10,2},{11,3},{12,4},{13,5},{14,6},{15,7},{0,8},{1,9},... | collective-permute-start | bytes 393224 | tf_op jit(solution)/shard_map/ppermute | solution.py:92
  97.5 1.8 %collective-permute-done.36 = bf16[32,2048]{1,0:T(8,128)(2,1)S(1)} collective-permute-done((bf16[32,2048]{1,0:T(8,128)(2,1)S(1)}, bf16[32,2048]{1,0:T(8,128)(2,1)S(1)}, u32[]{:S(2)}, u32[]{:S(2)}) %collective-permute-start.36) | collective-permute-done | bytes 131104 | tf_op jit(solution)/shard_map/ppermute | solution.py:92
  99.3 2.3 %collective-permute-done.35 = bf16[32,2048]{1,0:T(8,128)(2,1)S(1)} collective-permute-done((bf16[32,2048]{1,0:T(8,128)(2,1)S(1)}, bf16[32,2048]{1,0:T(8,128)(2,1)S(1)}, u32[]{:S(2)}, u32[]{:S(2)}) %collective-permute-start.35) | collective-permute-done | bytes 131104 | tf_op jit(solution)/shard_map/ppermute | solution.py:92
  104.5 1.5 %join.1 = bf16[16,4096]{1,0:T(8,128)(2,1)} custom-call(s32[1]{0:T(128)} %bitcast.exp_ref, bf16[16,2048]{1,0:T(8,128)(2,1)} %get-tuple-element.146.mine_ref, bf16[16,2048]{1,0:T(8,128)(2,1)} %copy-done.3), custom_call_target="tpu_custom_call" | custom-call | tf_op jit(solution)/shard_map/join/pallas_call | solution.py:905
  (95 shorter events, 35.5 us)
Async XLA Ops:
  1.2 13.8 %collective-permute-start = (bf16[64,1280]{1,0:T(8,128)(2,1)S(1)}, bf16[64,1280]{1,0:T(8,128)(2,1)S(1)}, u32[]{:S(2)}, u32[]{:S(2)}) collective-permute-start(bf16[64,1280]{1,0:T(8,128)(2,1)S(1)} %get-tuple-element.73._.refs_0_), channel_id=1, source_target_pairs={{16,0},{17,1},{18,2},{19,3},{20,4},{21,5},{22,6},{23,7},{24,8},{25... | collective-permute-start | bytes 491528 | tf_op jit(solution)/shard_map/ppermute | solution.py:92
  5.3 9.7 %collective-permute-start.1 = (bf16[64,1280]{1,0:T(8,128)(2,1)S(1)}, bf16[64,1280]{1,0:T(8,128)(2,1)S(1)}, u32[]{:S(2)}, u32[]{:S(2)}) collective-permute-start(bf16[64,1280]{1,0:T(8,128)(2,1)S(1)} %get-tuple-element.73._.refs_0_), channel_id=1, source_target_pairs={{4,0},{9,1},{6,2},{11,3},{0,4},{13,5},{2,6},{15,7},{12,8},{1,9},{1... | collective-permute-start | bytes 491528 | tf_op jit(solution)/shard_map/ppermute | solution.py:92
  6.8 8.2 %collective-permute-start.2 = (bf16[64,1280]{1,0:T(8,128)(2,1)S(1)}, bf16[64,1280]{1,0:T(8,128)(2,1)S(1)}, u32[]{:S(2)}, u32[]{:S(2)}) collective-permute-start(bf16[64,1280]{1,0:T(8,128)(2,1)S(1)} %get-tuple-element.73._.refs_0_), channel_id=1, source_target_pairs={{8,0},{5,1},{10,2},{7,3},{12,4},{1,5},{14,6},{3,7},{0,8},{13,9},{2... | collective-permute-start | bytes 491528 | tf_op jit(solution)/shard_map/ppermute | solution.py:92
  8.4 6.6 %collective-permute-start.3 = (bf16[4,16,640]{2,1,0:T(8,128)(2,1)S(1)}, bf16[4,16,640]{2,1,0:T(8,128)(2,1)S(1)}, u32[]{:S(2)}, u32[]{:S(2)}) collective-permute-start(bf16[4,16,640]{2,1,0:T(8,128)(2,1)S(1)} %get-tuple-element.74), channel_id=1, source_target_pairs={{8,0},{5,1},{10,2},{7,3},{12,4},{1,5},{14,6},{3,7},{0,8},{13,9},{2... | collective-permute-start | bytes 245768 | tf_op jit(solution)/shard_map/ppermute | solution.py:92
  15.0 9.7 %collective-permute-start.7 = (bf16[2048,768]{1,0:T(8,128)(2,1)S(1)}, bf16[2048,768]{1,0:T(8,128)(2,1)S(1)}, u32[]{:S(2)}, u32[]{:S(2)}) collective-permute-start(bf16[2048,768]{1,0:T(8,128)(2,1)S(1)} %get-tuple-element.82), channel_id=1, source_target_pairs={{0,1},{1,0},{2,3},{3,2},{4,5},{5,4},{6,7},{7,6},{8,9},{9,8},{10,11... | collective-permute-start | bytes 9437192 | tf_op jit(solution)/shard_map/ppermute | solution.py:25
  15.0 9.6 %collective-permute-start.5 = (bf16[64,1280]{1,0:T(8,128)(2,1)S(1)}, bf16[64,1280]{1,0:T(8,128)(2,1)S(1)}, u32[]{:S(2)}, u32[]{:S(2)}) collective-permute-start(bf16[64,1280]{1,0:T(8,128)(2,1)S(1)} %collective-permute-done.refs_1_), channel_id=1, source_target_pairs={{8,0},{5,1},{10,2},{7,3},{12,4},{1,5},{14,6},{3,7},{0,8},{13,9},{2... | collective-permute-start | bytes 491528 | tf_op jit(solution)/shard_map/ppermute | solution.py:92
  15.8 8.8 %collective-permute-start.4 = (bf16[128,1280]{1,0:T(8,128)(2,1)S(1)}, bf16[128,1280]{1,0:T(8,128)(2,1)S(1)}, u32[]{:S(2)}, u32[]{:S(2)}) collective-permute-start(bf16[128,1280]{1,0:T(8,128)(2,1)S(1)} %pad_maximum_fusion), channel_id=1, source_target_pairs={{4,0},{9,1},{6,2},{11,3},{0,4},{13,5},{2,6},{15,7},{12,8},{1,9},{1... | collective-permute-start | bytes 983048 | tf_op jit(solution)/shard_map/ppermute | solution.py:92
  17.4 7.2 %collective-permute-start.6 = (bf16[4,16,640]{2,1,0:T(8,128)(2,1)S(1)}, bf16[4,16,640]{2,1,0:T(8,128)(2,1)S(1)}, u32[]{:S(2)}, u32[]{:S(2)}) collective-permute-start(bf16[4,16,640]{2,1,0:T(8,128)(2,1)S(1)} %pad_maximum_fusion.6), channel_id=1, source_target_pairs={{4,0},{9,1},{6,2},{11,3},{0,4},{13,5},{2,6},{15,7},{12,8},{1,9},{1... | collective-permute-start | bytes 245768 | tf_op jit(solution)/shard_map/ppermute | solution.py:92
  24.6 7.0 %collective-permute-start.10 = (bf16[384,2048]{1,0:T(8,128)(2,1)S(1)}, bf16[384,2048]{1,0:T(8,128)(2,1)S(1)}, u32[]{:S(2)}, u32[]{:S(2)}) collective-permute-start(bf16[384,2048]{1,0:T(8,128)(2,1)S(1)} %get-tuple-element.88), channel_id=1, source_target_pairs={{0,1},{1,0},{2,3},{3,2},{4,5},{5,4},{6,7},{7,6},{8,9},{9,8},{10,11... | collective-permute-start | bytes 4718600 | tf_op jit(solution)/shard_map/ppermute | solution.py:25
  25.8 5.8 %collective-permute-start.9 = (bf16[64,1280]{1,0:T(8,128)(2,1)S(1)}, bf16[64,1280]{1,0:T(8,128)(2,1)S(1)}, u32[]{:S(2)}, u32[]{:S(2)}) collective-permute-start(bf16[64,1280]{1,0:T(8,128)(2,1)S(1)} %collective-permute-done.5.refs_5_), channel_id=1, source_target_pairs={{4,0},{9,1},{6,2},{11,3},{0,4},{13,5},{2,6},{15,7},{12,8},{1,9},{1... | collective-permute-start | bytes 491528 | tf_op jit(solution)/shard_map/ppermute | solution.py:92
  26.9 7.2 %collective-permute-start.11 = (bf16[4,16,640]{2,1,0:T(8,128)(2,1)S(1)}, bf16[4,16,640]{2,1,0:T(8,128)(2,1)S(1)}, u32[]{:S(2)}, u32[]{:S(2)}) collective-permute-start(bf16[4,16,640]{2,1,0:T(8,128)(2,1)S(1)} %pad_maximum_fusion.7), channel_id=1, source_target_pairs={{16,0},{17,1},{18,2},{19,3},{20,4},{21,5},{22,6},{23,7},{24,8},{25... | collective-permute-start | bytes 245768 | tf_op jit(solution)/shard_map/ppermute | solution.py:92
  35.9 6.0 %collective-permute-start.13 = (bf16[288,256]{1,0:T(8,128)(2,1)S(1)}, bf16[288,256]{1,0:T(8,128)(2,1)S(1)}, u32[]{:S(2)}, u32[]{:S(2)}) collective-permute-start(bf16[288,256]{1,0:T(8,128)(2,1)S(1)} %pad_maximum_fusion.5), channel_id=1, source_target_pairs={{0,2},{1,3},{2,0},{3,1},{4,6},{5,7},{6,4},{7,5},{8,10},{9,11},{10,... | collective-permute-start | bytes 442376 | tf_op jit(solution)/shard_map/ppermute | solution.py:25
  42.0 8.5 %collective-permute-start.14 = (bf16[256,256]{1,0:T(8,128)(2,1)S(1)}, bf16[256,256]{1,0:T(8,128)(2,1)S(1)}, u32[]{:S(2)}, u32[]{:S(2)}) collective-permute-start(bf16[256,256]{1,0:T(8,128)(2,1)S(1)} %add_convert_fusion.6.refs_0_.refs_6_), channel_id=1, source_target_pairs={{16,0},{17,1},{18,2},{19,3},{20,4},{21,5},{22,6},{23,7},{24,8},{25... | collective-permute-start | bytes 393224 | tf_op jit(solution)/shard_map/ppermute | solution.py:92
  43.3 7.2 %collective-permute-start.15 = (bf16[256,256]{1,0:T(8,128)(2,1)S(1)}, bf16[256,256]{1,0:T(8,128)(2,1)S(1)}, u32[]{:S(2)}, u32[]{:S(2)}) collective-permute-start(bf16[256,256]{1,0:T(8,128)(2,1)S(1)} %add_convert_fusion.6.refs_0_.refs_6_), channel_id=1, source_target_pairs={{6,0},{7,1},{4,2},{5,3},{2,4},{3,5},{0,6},{1,7},{14,8},{15,9},{12,... | collective-permute-start | bytes 393224 | tf_op jit(solution)/shard_map/ppermute | solution.py:92
  45.1 6.0 %collective-permute-start.16 = (bf16[256,256]{1,0:T(8,128)(2,1)S(1)}, bf16[256,256]{1,0:T(8,128)(2,1)S(1)}, u32[]{:S(2)}, u32[]{:S(2)}) collective-permute-start(bf16[256,256]{1,0:T(8,128)(2,1)S(1)} %add_convert_fusion.6.refs_0_.refs_6_), channel_id=1, source_target_pairs={{8,0},{9,1},{10,2},{11,3},{12,4},{13,5},{14,6},{15,7},{0,8},{1,9},... | collective-permute-start | bytes 393224 | tf_op jit(solution)/shard_map/ppermute | solution.py:92
  51.9 10.6 %collective-permute-start.20 = (bf16[512,256]{1,0:T(8,128)(2,1)S(1)}, bf16[512,256]{1,0:T(8,128)(2,1)S(1)}, u32[]{:S(2)}, u32[]{:S(2)}) collective-permute-start(bf16[512,256]{1,0:T(8,128)(2,1)S(1)} %constant_dynamic-update-slice_fusion), channel_id=1, source_target_pairs={{2,0},{5,1},{0,2},{7,3},{6,4},{1,5},{4,6},{3,7},{10,8},{13,9},{8,1... | collective-permute-start | bytes 786440 | tf_op jit(solution)/shard_map/ppermute | solution.py:92
  53.5 9.1 %collective-permute-start.21 = (bf16[512,256]{1,0:T(8,128)(2,1)S(1)}, bf16[512,256]{1,0:T(8,128)(2,1)S(1)}, u32[]{:S(2)}, u32[]{:S(2)}) collective-permute-start(bf16[512,256]{1,0:T(8,128)(2,1)S(1)} %constant_dynamic-update-slice_fusion), channel_id=1, source_target_pairs={{4,0},{3,1},{6,2},{1,3},{0,4},{7,5},{2,6},{5,7},{12,8},{11,9},{14,... | collective-permute-start | bytes 786440 | tf_op jit(solution)/shard_map/ppermute | solution.py:92
  54.6 7.4 %collective-permute-start.19 = (bf16[256,256]{1,0:T(8,128)(2,1)S(1)}, bf16[256,256]{1,0:T(8,128)(2,1)S(1)}, u32[]{:S(2)}, u32[]{:S(2)}) collective-permute-start(bf16[256,256]{1,0:T(8,128)(2,1)S(1)} %collective-permute-done.15.refs_2_), channel_id=1, source_target_pairs={{16,0},{17,1},{18,2},{19,3},{20,4},{21,5},{22,6},{23,7},{24,8},{25... | collective-permute-start | bytes 393224 | tf_op jit(solution)/shard_map/ppermute | solution.py:92
  56.4 6.1 %collective-permute-start.22 = (bf16[256,256]{1,0:T(8,128)(2,1)S(1)}, bf16[256,256]{1,0:T(8,128)(2,1)S(1)}, u32[]{:S(2)}, u32[]{:S(2)}) collective-permute-start(bf16[256,256]{1,0:T(8,128)(2,1)S(1)} %collective-permute-done.14.refs_1_.refs_7_), channel_id=1, source_target_pairs={{8,0},{9,1},{10,2},{11,3},{12,4},{13,5},{14,6},{15,7},{0,8},{1,9},... | collective-permute-start | bytes 393224 | tf_op jit(solution)/shard_map/ppermute | solution.py:92
  62.6 6.4 %collective-permute-start.23 = (bf16[512,256]{1,0:T(8,128)(2,1)S(1)}, bf16[512,256]{1,0:T(8,128)(2,1)S(1)}, u32[]{:S(2)}, u32[]{:S(2)}) collective-permute-start(bf16[512,256]{1,0:T(8,128)(2,1)S(1)} %pad_maximum_fusion.1), channel_id=1, source_target_pairs={{4,0},{3,1},{6,2},{1,3},{0,4},{7,5},{2,6},{5,7},{12,8},{11,9},{14,... | collective-permute-start | bytes 786440 | tf_op jit(solution)/shard_map/ppermute | solution.py:92
  71.7 5.9 %collective-permute-start.30 = (bf16[256,1664]{1,0:T(8,128)(2,1)S(1)}, bf16[256,1664]{1,0:T(8,128)(2,1)S(1)}, u32[]{:S(2)}, u32[]{:S(2)}) collective-permute-start(bf16[256,1664]{1,0:T(8,128)(2,1)S(1)} %experts_in_second.3.refs_5_.act_ref), channel_id=1, source_target_pairs={{0,1},{1,0},{2,3},{3,2},{4,5},{5,4},{6,7},{7,6},{8,9},{9,8},{10,11... | collective-permute-start | bytes 2555912 | tf_op jit(solution)/shard_map/ppermute | solution.py:25
  74.5 7.8 %collective-permute-start.27 = (bf16[64,2048]{1,0:T(8,128)(2,1)S(1)}, bf16[64,2048]{1,0:T(8,128)(2,1)S(1)}, u32[]{:S(2)}, u32[]{:S(2)}) collective-permute-start(bf16[64,2048]{1,0:T(8,128)(2,1)S(1)} %pad_maximum_fusion.2), channel_id=1, source_target_pairs={{4,0},{3,1},{6,2},{1,3},{0,4},{7,5},{2,6},{5,7},{12,8},{11,9},{14,... | collective-permute-start | bytes 786440 | tf_op jit(solution)/shard_map/ppermute | solution.py:92
  75.4 5.7 %collective-permute-start.28 = (bf16[32,2048]{1,0:T(8,128)(2,1)S(1)}, bf16[32,2048]{1,0:T(8,128)(2,1)S(1)}, u32[]{:S(2)}, u32[]{:S(2)}) collective-permute-start(bf16[32,2048]{1,0:T(8,128)(2,1)S(1)} %get-tuple-element.112), channel_id=1, source_target_pairs={{8,0},{9,1},{10,2},{11,3},{12,4},{13,5},{14,6},{15,7},{0,8},{1,9},... | collective-permute-start | bytes 393224 | tf_op jit(solution)/shard_map/ppermute | solution.py:92
  82.4 11.0 %collective-permute-start.33 = (bf16[64,2048]{1,0:T(8,128)(2,1)S(1)}, bf16[64,2048]{1,0:T(8,128)(2,1)S(1)}, u32[]{:S(2)}, u32[]{:S(2)}) collective-permute-start(bf16[64,2048]{1,0:T(8,128)(2,1)S(1)} %pad_maximum_fusion.4), channel_id=1, source_target_pairs={{4,0},{3,1},{6,2},{1,3},{0,4},{7,5},{2,6},{5,7},{12,8},{11,9},{14,... | collective-permute-start | bytes 786440 | tf_op jit(solution)/shard_map/ppermute | solution.py:92
  83.4 10.0 %collective-permute-start.32 = (bf16[64,2048]{1,0:T(8,128)(2,1)S(1)}, bf16[64,2048]{1,0:T(8,128)(2,1)S(1)}, u32[]{:S(2)}, u32[]{:S(2)}) collective-permute-start(bf16[64,2048]{1,0:T(8,128)(2,1)S(1)} %pad_maximum_fusion.3), channel_id=1, source_target_pairs={{2,0},{5,1},{0,2},{7,3},{6,4},{1,5},{4,6},{3,7},{10,8},{13,9},{8,1... | collective-permute-start | bytes 786440 | tf_op jit(solution)/shard_map/ppermute | solution.py:92
  84.7 6.1 %collective-permute-start.34 = (bf16[32,2048]{1,0:T(8,128)(2,1)S(1)}, bf16[32,2048]{1,0:T(8,128)(2,1)S(1)}, u32[]{:S(2)}, u32[]{:S(2)}) collective-permute-start(bf16[32,2048]{1,0:T(8,128)(2,1)S(1)} %get-tuple-element.143), channel_id=1, source_target_pairs={{8,0},{9,1},{10,2},{11,3},{12,4},{13,5},{14,6},{15,7},{0,8},{1,9},... | collective-permute-start | bytes 393224 | tf_op jit(solution)/shard_map/ppermute | solution.py:92
  85.6 7.7 %collective-permute-start.31 = (bf16[32,2048]{1,0:T(8,128)(2,1)S(1)}, bf16[32,2048]{1,0:T(8,128)(2,1)S(1)}, u32[]{:S(2)}, u32[]{:S(2)}) collective-permute-start(bf16[32,2048]{1,0:T(8,128)(2,1)S(1)} %add_convert_fusion.5), channel_id=1, source_target_pairs={{16,0},{17,1},{18,2},{19,3},{20,4},{21,5},{22,6},{23,7},{24,8},{25... | collective-permute-start | bytes 393224 | tf_op jit(solution)/shard_map/ppermute | solution.py:92
  87.0 10.5 %collective-permute-start.38 = (bf16[32,2048]{1,0:T(8,128)(2,1)S(1)}, bf16[32,2048]{1,0:T(8,128)(2,1)S(1)}, u32[]{:S(2)}, u32[]{:S(2)}) collective-permute-start(bf16[32,2048]{1,0:T(8,128)(2,1)S(1)} %get-tuple-element.139), channel_id=1, source_target_pairs={{2,0},{5,1},{0,2},{7,3},{6,4},{1,5},{4,6},{3,7},{10,8},{13,9},{8,1... | collective-permute-start | bytes 393224 | tf_op jit(solution)/shard_map/ppermute | solution.py:92
  90.8 6.7 %collective-permute-start.39 = (bf16[32,2048]{1,0:T(8,128)(2,1)S(1)}, bf16[32,2048]{1,0:T(8,128)(2,1)S(1)}, u32[]{:S(2)}, u32[]{:S(2)}) collective-permute-start(bf16[32,2048]{1,0:T(8,128)(2,1)S(1)} %get-tuple-element.140), channel_id=1, source_target_pairs={{4,0},{3,1},{6,2},{1,3},{0,4},{7,5},{2,6},{5,7},{12,8},{11,9},{14,... | collective-permute-start | bytes 393224 | tf_op jit(solution)/shard_map/ppermute | solution.py:92
  93.4 5.9 %collective-permute-start.36 = (bf16[32,2048]{1,0:T(8,128)(2,1)S(1)}, bf16[32,2048]{1,0:T(8,128)(2,1)S(1)}, u32[]{:S(2)}, u32[]{:S(2)}) collective-permute-start(bf16[32,2048]{1,0:T(8,128)(2,1)S(1)} %add_convert_fusion.1), channel_id=1, source_target_pairs={{6,0},{7,1},{4,2},{5,3},{2,4},{3,5},{0,6},{1,7},{14,8},{15,9},{12,... | collective-permute-start | bytes 393224 | tf_op jit(solution)/shard_map/ppermute | solution.py:92
  94.9 6.7 %collective-permute-start.35 = (bf16[32,2048]{1,0:T(8,128)(2,1)S(1)}, bf16[32,2048]{1,0:T(8,128)(2,1)S(1)}, u32[]{:S(2)}, u32[]{:S(2)}) collective-permute-start(bf16[32,2048]{1,0:T(8,128)(2,1)S(1)} %get-tuple-element.141), channel_id=1, source_target_pairs={{16,0},{17,1},{18,2},{19,3},{20,4},{21,5},{22,6},{23,7},{24,8},{25... | collective-permute-start | bytes 393224 | tf_op jit(solution)/shard_map/ppermute | solution.py:92
  95.1 6.7 %collective-permute-start.37 = (bf16[32,2048]{1,0:T(8,128)(2,1)S(1)}, bf16[32,2048]{1,0:T(8,128)(2,1)S(1)}, u32[]{:S(2)}, u32[]{:S(2)}) collective-permute-start(bf16[32,2048]{1,0:T(8,128)(2,1)S(1)} %get-tuple-element.142), channel_id=1, source_target_pairs={{8,0},{9,1},{10,2},{11,3},{12,4},{13,5},{14,6},{15,7},{0,8},{1,9},... | collective-permute-start | bytes 393224 | tf_op jit(solution)/shard_map/ppermute | solution.py:92
  (13 other events, 98.0 us)
